TPU v7x, 256 devices: a whole 4x4x8 slice. The times are simulated.
256 devices in a mesh: chan: 16 (over z, core), row: 4 (over x), col: 4 (over y).
Axes of the slice: x: 4, y: 4, z: 8, core: 2. Of those that a mesh axis runs over, the one named last changes fastest.
Arguments:
- voltages: bfloat16 [2, 1024, 131072], P(None, 'chan', ('row', 'col')), may hold values from -6 to 6
- input_flags: int32 [1024], P('chan'), may hold values 0 or 1
- channel_order: int32 [128], replicated, may hold values from 0 to 127, each once
- beam_weights: bfloat16 [2, 128, 256, 1024], P(None, 'chan', 'col'), may hold values from -0.1875 to 0.1875
Outputs:
- visibility: float32 [2, 128, 1024, 1024], P(None, 'chan', 'row', 'col')
- beam_power: float32 [128, 256, 128], P('chan', 'col', 'row')
Inputs may be any that keep to these rules, and one draw needn't show every extreme that they name: `channel_order`: every fine channel appears exactly once.
All inputs are finite; a program needn't handle non-finite values. No bound on the sum of `input_flags` on one device may be relied on, other than what follows from the above.
Results may differ from a plain program's by a relative error of at most 0.005.
Values may be sent and summed in bfloat16 or wider, within the bound.
No kernel may reach another device: no remote copies, remote signals or barrier semaphores. Data moves between devices by JAX's collectives and lax.ppermute only.
A program may use at most 128 MiB of HBM per device.

v0:
```python
import math

import jax
import jax.numpy as jnp
from jax import lax
from jax.sharding import PartitionSpec as P

NCH = 128
TAPS = 4
INTEG = 8


def passed_along(value, axis, steps):
    count = lax.axis_size(axis)
    initial, last = (max(0, -steps), min(count, count - steps))
    return lax.ppermute(value, axis, [(source, source + steps) for source in range(initial, last)])


def prototype(taps, length):
    position = jnp.arange(taps * length, dtype=jnp.float32) + 0.5
    offset = position / length - taps / 2.0
    window = 0.5 - 0.5 * jnp.cos(2.0 * math.pi * position / (taps * length))
    return (jnp.sin(math.pi * offset) / (math.pi * offset) * window).reshape(taps, length)


def dft_tables(channel_rows, length):
    sample_index = jnp.arange(length, dtype=jnp.int32)
    product = channel_rows[:, None] * sample_index[None, :] % length
    angle = 2.0 * math.pi / length * product.astype(jnp.float32)
    factor = 1.0 / math.sqrt(length)
    cosine = jnp.cos(angle) * factor
    sine = jnp.sin(angle) * factor
    real_rows = jnp.stack([cosine, sine], axis=1)
    imag_rows = jnp.stack([-sine, cosine], axis=1)
    return jnp.stack([real_rows, imag_rows], axis=1).astype(jnp.bfloat16)


def to_frames(gathered, frames, outer, inner, swapped):
    chans = gathered.shape[0]
    width = gathered.shape[1]
    split = gathered.reshape(chans, width, outer, inner, 2, frames)
    if swapped:
        order = jnp.transpose(split, (0, 4, 1, 3, 2, 5))
    else:
        order = jnp.transpose(split, (0, 4, 1, 2, 3, 5))
    return order.reshape(chans, 2, width, outer * inner * frames)


def correlate_one(left_block, right_block, frame_count):
    left_re = left_block[0]
    left_im = left_block[1]
    right_re = right_block[0]
    right_im = right_block[1]
    dims = (((1,), (1,)), ((), ()))
    vis_re = lax.dot_general(left_re, right_re, dims, preferred_element_type=jnp.float32)
    vis_re = vis_re + lax.dot_general(left_im, right_im, dims, preferred_element_type=jnp.float32)
    vis_im = lax.dot_general(left_im, right_re, dims, preferred_element_type=jnp.float32)
    vis_im = vis_im - lax.dot_general(left_re, right_im, dims, preferred_element_type=jnp.float32)
    return jnp.stack([vis_re, vis_im]) / frame_count


def correlate(left_view, right_view, frame_count):
    result = lax.map(
        lambda items: correlate_one(items[0], items[1], frame_count), (left_view, right_view)
    )
    return jnp.transpose(result, (1, 0, 2, 3))


def beams_one(weights, block):
    w_real = weights[0]
    w_imag = weights[1]
    x_real = block[0]
    x_imag = block[1]
    beam_re = jnp.dot(w_real, x_real, preferred_element_type=jnp.float32) - jnp.dot(
        w_imag, x_imag, preferred_element_type=jnp.float32
    )
    beam_im = jnp.dot(w_real, x_imag, preferred_element_type=jnp.float32) + jnp.dot(
        w_imag, x_real, preferred_element_type=jnp.float32
    )
    return jnp.stack([beam_re, beam_im], axis=1)


def form_beams(weights, view):
    by_channel = jnp.transpose(weights, (1, 0, 2, 3))
    return lax.map(lambda items: beams_one(items[0], items[1]), (by_channel, view))


def integrate(voltage):
    power = voltage[:, :, 0] * voltage[:, :, 0] + voltage[:, :, 1] * voltage[:, :, 1]
    return power.reshape(power.shape[0], power.shape[1], -1, INTEG).mean(axis=-1)


def on_device(voltages, input_flags, channel_order, beam_weights):
    masked = voltages * input_flags.astype(jnp.bfloat16)[None, :, None]
    local_inputs = masked.shape[1]
    frames = masked.shape[2] // NCH
    history = passed_along(masked[:, :, masked.shape[2] - (TAPS - 1) * NCH :], ("row", "col"), 1)
    joined = jnp.concatenate([history, masked], axis=2)
    blocks = joined.reshape(2, local_inputs, frames + TAPS - 1, NCH)
    coeffs = prototype(TAPS, NCH)
    filtered = jnp.zeros((2, local_inputs, frames, NCH), jnp.float32)
    for tap_index in range(TAPS):
        filtered = filtered + coeffs[tap_index] * blocks[
            :, :, tap_index : tap_index + frames
        ].astype(jnp.float32)
    filtered = filtered.astype(jnp.bfloat16)
    tables = dft_tables(channel_order, NCH)
    spectrum = jnp.einsum(
        "kqpn,pifn->kiqf",
        tables.astype(jnp.float32),
        filtered.astype(jnp.float32),
        precision=lax.Precision.HIGHEST,
    ).astype(jnp.bfloat16)
    spectrum = spectrum.reshape(NCH, local_inputs, 2 * frames)
    turned = lax.all_to_all(spectrum, "chan", split_axis=0, concat_axis=1, tiled=True)
    row_count = lax.axis_size("row")
    col_count = lax.axis_size("col")
    total_frames = frames * row_count * col_count
    row_turned = lax.all_to_all(turned, "row", split_axis=1, concat_axis=2, tiled=True)
    row_all = lax.all_gather(row_turned, "col", axis=2, tiled=True)
    col_turned = lax.all_to_all(turned, "col", split_axis=1, concat_axis=2, tiled=True)
    col_all = lax.all_gather(col_turned, "row", axis=2, tiled=True)
    row_view = to_frames(row_all, frames, col_count, row_count, True)
    col_view = to_frames(col_all, frames, row_count, col_count, False)
    visibility = correlate(row_view, col_view, total_frames)
    weights_all = lax.all_gather(beam_weights, "col", axis=2, tiled=True)
    local_view = to_frames(turned, frames, 1, 1, False)
    voltage = form_beams(weights_all, local_view)
    own_power = integrate(voltage)
    beam_power = lax.all_to_all(own_power, "col", split_axis=1, concat_axis=2, tiled=True)
    return (visibility, beam_power)


def solution(mesh):
    placed = (P(None, "chan", ("row", "col")), P("chan"), P(), P(None, "chan", "col", None))
    return jax.shard_map(
        on_device,
        mesh=mesh,
        in_specs=placed,
        out_specs=(P(None, "chan", "row", "col"), P("chan", "col", "row")),
        check_vma=False,
    )
```

profile of v0, /device:TPU:6, one launch (start us, length us, event | category | flops | bytes accessed | tf_op | source)
XLA Modules:
  0.0 379.0 jit_solution(13074412486855546821)
XLA Ops:
  7.2 3.3 copy.87
  10.9 3.5 collective-permute-start
  14.8 4.7 %collective-permute-done = bf16[2,64,384]{2,1,0:T(8,128)(2,1)S(1)} collective-permute-done((bf16[2,64,384]{2,1,0:T(8,128)(2,1)S(1)}, bf16[2,64,384]{2,1,0:T(8,128)(2,1)S(1)}, u32[]{:S(2)}, u32[]{:S(2)}) %collective-permute-start) | collective-permute-done | bytes 98336 | tf_op jit(solution)/shard_map/ppermute | solution.py:16
  19.7 2.5 reshape.215
  22.2 6.9 %bitcast_convert_fusion = bf16[64,64,128,2]{2,1,3,0:T(8,128)(2,1)S(1)} fusion(bf16[128,1,2,128]{3,0,2,1:T(8,128)(2,1)S(1)} %get-tuple-element.105, bf16[128,1,2,128]{3,0,2,1:T(8,128)(2,1)S(1)} %get-tuple-element.104, bf16[2,64,67,128]{3,2,1,0:T(8,128)(2,1)} %reshape.215, f32[128]{0:T(128)S(1)} %get-tuple-element.107, f32[128]{0:T(128)S(1)} %get-tuple-element.108, ...), kind=kOutput, calls=%fused_computation.33 | convolution fusion | flops 550764544 | bytes 10618880 | tf_op jit(solution)/shard_map/kqpn,pifn->kiqf/dot_general | solution.py:108
  29.0 2.8 copy.74
  31.8 59.0 %all_to_all.72 = bf16[128,64,128]{2,1,0:T(8,128)(2,1)S(1)} all-to-all(bf16[128,64,128]{2,1,0:T(8,128)(2,1)} %copy.74), channel_id=1, replica_groups=mesh['chan'=16,'row'=4,'col'=4] {'chan'}, dimensions={0} | all-to-all | bytes 4194304 | tf_op jit(solution)/shard_map/all_to_all | solution.py:115
  91.0 1.4 copy.76
  93.7 29.9 %all_to_all.73 = bf16[8,1024,128]{2,0,1:T(8,128)(2,1)} all-to-all(bf16[8,1024,128]{2,0,1:T(8,128)(2,1)S(1)} %copy.76), channel_id=1, replica_groups=mesh['chan'=16,'row'=4,'col'=4] {'row'}, dimensions={1} | all-to-all | bytes 4194304 | tf_op jit(solution)/shard_map/all_to_all | solution.py:119
  123.6 4.3 %copy.78 = bf16[8,256,4,128]{1,3,2,0:T(8,128)(2,1)} copy(bf16[8,256,4,128]{3,0,1,2:T(8,128)(2,1)} %bitcast.171) | data formatting | bytes 4194304 | tf_op jit(solution)/shard_map/all_to_all | solution.py:119
  128.0 50.1 %all_to_all.74 = bf16[8,1024,128]{2,0,1:T(8,128)(2,1)} all-to-all(bf16[8,1024,128]{2,0,1:T(8,128)(2,1)} %copy-done), channel_id=1, replica_groups=mesh['chan'=16,'row'=4,'col'=4] {'col'}, dimensions={1} | all-to-all | bytes 4194304 | tf_op jit(solution)/shard_map/all_to_all | solution.py:121
  178.1 4.3 %copy.82 = bf16[8,256,4,128]{1,3,2,0:T(8,128)(2,1)} copy(bf16[8,256,4,128]{3,0,1,2:T(8,128)(2,1)} %bitcast.169) | data formatting | bytes 4194304 | tf_op jit(solution)/shard_map/all_to_all | solution.py:121
  182.5 4.2 %copy.88 = bf16[8,16,64,128]{2,1,3,0:T(8,128)(2,1)} copy(bf16[8,16,64,128]{3,2,0,1:T(8,128)(2,1)S(1)} %bitcast.162) | data formatting | bytes 4194304 | tf_op jit(solution)/shard_map/all_to_all | solution.py:115
  186.7 5.5 %reshape.221 = bf16[8,1024,1,1,2,64]{1,5,4,0,3,2:T(8,128)(2,1)S(1)} reshape(bf16[8,16,64,128]{2,1,3,0:T(8,128)(2,1)} %copy.88) | data formatting | bytes 4194304 | tf_op jit(solution)/shard_map/reshape | solution.py:41
  192.2 43.0 %while.21 = (s32[]{:T(128)}, f32[8,256,2,64]{1,3,2,0:T(8,128)S(1)}, bf16[8,2,256,1024]{3,2,1,0:T(8,128)(2,1)}, bf16[8,2,1024,64]{2,3,1,0:T(8,128)(2,1)S(1)}, s32[]{:T(128)}, /*index=5*/s32[]{:T(128)}, s32[]{}) while((s32[]{:T(128)}, f32[8,256,2,64]{1,3,2,0:T(8,128)S(1)}, bf16[8,2,256,1024]{3,2,1,0:T(8,128)(2,1)}, ...), condition=%wide.region_3.4_spmd, body=%wide.region_2.3_spmd.sunk | while | flops 134283264 | bytes 3282021 | solution.py:85
  193.5 1.3 fusion.51
  194.9 1.3 fusion.52
  198.9 1.3 fusion.51
  200.3 1.3 fusion.52
  204.3 1.3 fusion.51
  205.6 1.3 fusion.52
  207.0 1.3 fusion.53
  220.4 1.3 fusion.51
  225.8 1.3 fusion.51
  232.5 1.3 fusion.52
  233.8 1.4 fusion.53
  237.0 3.5 all-to-all-start.3
  240.5 5.4 %all-to-all-done.3 = f32[4,1,4096]{2,1,0:T(1,128)S(1)} async-done(((f32[4,1,4096]{2,1,0:T(1,128)}), f32[4,1,4096]{2,1,0:T(1,128)S(1)}, u32[]{:S(2)}, u32[]{:S(2)}) %all-to-all-start.3) | async-done | bytes 65568 | tf_op jit(solution)/shard_map/all_to_all | solution.py:130
  248.9 8.3 %copy.79 = bf16[8,2,256,4,4,64]{2,5,4,3,1,0:T(8,128)(2,1)} copy(bf16[8,2,256,4,4,64]{2,5,1,3,4,0:T(8,128)(2,1)} %bitcast.165) | data formatting | bytes 16777216 | tf_op jit(solution)/shard_map/transpose | solution.py:43
  257.2 50.9 %all-gather.6.cloned.1.call-done = bf16[8,256,2048]{1,2,0:T(8,128)(2,1)} async-done(((bf16[8,256,512]{1,2,0:T(8,128)(2,1)}), bf16[8,256,2048]{1,2,0:T(8,128)(2,1)}) %all-gather.6.cloned.1.call-update) | async-done | bytes 8388624 | tf_op jit(solution)/shard_map/all_gather | solution.py:122
  308.1 8.3 %copy.83 = bf16[8,2,256,4,4,64]{2,5,4,3,1,0:T(8,128)(2,1)} copy(bf16[8,2,256,4,4,64]{2,5,1,4,3,0:T(8,128)(2,1)} %bitcast.166) | data formatting | bytes 16777216 | tf_op jit(solution)/shard_map/transpose | solution.py:45
  316.3 56.2 %while.20 = (s32[]{:T(128)}, f32[8,2,256,256]{3,2,0,1:T(8,128)}, bf16[8,2,256,1024]{2,3,1,0:T(8,128)(2,1)}, bf16[8,2,256,1024]{2,3,1,0:T(8,128)(2,1)}, s32[]{:T(128)}, /*index=5*/s32[]{:T(128)}, s32[]{}) while((s32[]{:T(128)}, f32[8,2,256,256]{3,2,0,1:T(8,128)}, bf16[8,2,256,1024]{2,3,1,0:T(8,128)(2,1)}, bf16[8,2,256,1024]{2,3,1,0:T(8,128)(2,1)}, ...), condition=%wide.region_1.2_spmd, body=%wide.region_0.1_spmd.sunk | while | flops 537264128 | bytes 6821473 | solution.py:63
  316.3 1.5 fusion.45
  317.9 1.5 fusion.46
  319.4 1.5 fusion.47
  321.0 1.5 fusion.48
  323.4 1.5 fusion.45
  324.9 1.5 fusion.46
  326.5 1.5 fusion.47
  328.0 1.5 fusion.48
  330.4 1.5 fusion.45
  331.9 1.5 fusion.46
  333.5 1.5 fusion.47
  335.0 1.5 fusion.48
  337.4 1.5 fusion.45
  338.9 1.5 fusion.46
  340.5 1.5 fusion.47
  342.0 1.5 fusion.48
  344.4 1.5 fusion.45
  346.0 1.5 fusion.46
  347.5 1.5 fusion.47
  349.1 1.5 fusion.48
  351.4 1.5 fusion.45
  353.0 1.5 fusion.46
  354.5 1.5 fusion.47
  356.1 1.5 fusion.48
  358.5 1.5 fusion.45
  360.0 1.5 fusion.46
  361.5 1.5 fusion.47
  363.1 1.5 fusion.48
  365.5 1.5 fusion.45
  367.0 1.5 fusion.46
  368.6 1.5 fusion.47
  370.1 1.5 fusion.48
  (73 shorter events, 42.0 us)
Async XLA Ops:
  7.2 3.4 copy-start.3
  7.2 3.4 copy-start.1
  7.2 185.0 %all-gather.8.cloned.1.call-start = ((), (), s32[]{:S(2)}) async-start(), calls=%async_computation.6 | async-start | bytes 10485760 | tf_op jit(solution)/shard_map/all_gather | solution.py:126
  10.5 3.9 %copy-start.2 = (s32[128]{0:T(128)S(1)}, s32[128]{0:T(128)}, u32[]{:S(2)}) copy-start(s32[128]{0:T(128)} %param.10) | copy-start | bytes 1540
  10.5 238.3 %all-gather.4.cloned.1.call-start = ((), (), s32[]{:S(2)}) async-start(), calls=%async_computation.4 | async-start | bytes 10485760 | tf_op jit(solution)/shard_map/all_gather | solution.py:120
  10.9 8.6 %collective-permute-start = (bf16[2,64,384]{2,1,0:T(8,128)(2,1)S(1)}, bf16[2,64,384]{2,1,0:T(8,128)(2,1)S(1)}, u32[]{:S(2)}, u32[]{:S(2)}) collective-permute-start(bf16[2,64,384]{2,1,0:T(8,128)(2,1)S(1)} %slice.82), channel_id=1, source_target_pairs={{0,1},{1,2},{2,3},{3,4},{4,5},{5,6},{6,7},{7,8},{8,9},{9,10},{10,1... | collective-permute-start | bytes 294920 | tf_op jit(solution)/shard_map/ppermute | solution.py:16
  92.4 1.3 copy-start
  128.0 180.1 %all-gather.6.cloned.1.call-start = ((), (), s32[]{:S(2)}) async-start(), calls=%async_computation.5 | async-start | bytes 10485760 | tf_op jit(solution)/shard_map/all_gather | solution.py:122
  237.0 8.9 %all-to-all-start.3 = ((f32[4,1,4096]{2,1,0:T(1,128)}), f32[4,1,4096]{2,1,0:T(1,128)S(1)}, u32[]{:S(2)}, u32[]{:S(2)}) async-start(f32[4,1,4096]{2,1,0:T(1,128)} %reshape.226), calls=%async_computation.3 | async-start | bytes 131072 | tf_op jit(solution)/shard_map/all_to_all | solution.py:130
Sparse Core Ops, SparseCore 0:
  10.7 88.5 all-gather.7
  128.1 98.6 all-gather.3
  228.6 79.3 all-gather.5
where the time goes:
time: 384 us; the launch traced here: 379 us
  blocking collectives  139 us (36%)
  matrix products  98.8 us (26%)
  waiting for transfers between devices  61 us (16%)
  local copies, waits for them, and re-layouts  50 us (13%)
  between operations  13.9 us (4%)
  other arithmetic  8.62 us (2%)
  starting transfers between devices  7.07 us (2%)
    all_to_all x1, blocking collectives, on_device(): lax.all_to_all(spectrum, 'chan', split_axis=0, concat_axis=1, tiled=True)  59 us
    all_gather x1, waiting for transfers between devices, on_device(): col_all = lax.all_gather(col_turned, 'row', axis=2, tiled=True)  50.9 us
    all_to_all x1, blocking collectives, on_device(): lax.all_to_all(turned, 'col', split_axis=1, concat_axis=2, tiled=True)  50.1 us
    all_to_all x1, blocking collectives, on_device(): lax.all_to_all(turned, 'row', split_axis=1, concat_axis=2, tiled=True)  29.9 us
    dot_general x8, matrix products, correlate_one(): lax.dot_general(left_im, right_im, dims, preferred_element_type=jnp.float32)  12.3 us
    dot_general x8, matrix products, correlate_one(): lax.dot_general(left_re, right_im, dims, preferred_element_type=jnp.float32)  12.3 us
    dot_general x8, matrix products, correlate_one(): lax.dot_general(left_re, right_re, dims, preferred_element_type=jnp.float32)  12.3 us
    dot_general x8, matrix products, correlate_one(): lax.dot_general(left_im, right_re, dims, preferred_element_type=jnp.float32)  12.3 us
  transfers between devices with their start and end apart: 5, of which 3 were waited for; matrix products, arithmetic and copies ran while one was open for 23% of the time, Pallas kernels for 0%

commit v1 on v0

v1 whole, which is shorter than its diff:
```python
import functools
import math

import jax
import jax.numpy as jnp
import numpy as np
from jax import lax
from jax.experimental import pallas as pl
from jax.experimental.pallas import tpu as pltpu
from jax.sharding import PartitionSpec as P

NCH = 128
TAPS = 4
INTEG = 8
CHUNKS = (4, 4)

F32 = jnp.float32
BF16 = jnp.bfloat16


def prototype(taps, length):
    position = np.arange(taps * length, dtype=np.float32) + np.float32(0.5)
    offset = position / np.float32(length) - np.float32(taps / 2.0)
    window = 0.5 - 0.5 * np.cos(2.0 * math.pi * position.astype(np.float64) / (taps * length))
    sinc = np.sin(math.pi * offset.astype(np.float64)) / (math.pi * offset.astype(np.float64))
    return (sinc * window).astype(np.float32).reshape(taps, length)


def dft_table(length):
    index = np.arange(length)
    angle = 2.0 * math.pi / length * (index[:, None] * index[None, :] % length)
    factor = 1.0 / math.sqrt(length)
    table = np.concatenate([np.cos(angle) * factor, np.sin(angle) * factor], axis=1)
    return table.astype(np.float32).astype(jnp.bfloat16)


def passed_along(value, axis, steps):
    count = lax.axis_size(axis)
    initial, last = (max(0, -steps), min(count, count - steps))
    return lax.ppermute(value, axis, [(source, source + steps) for source in range(initial, last)])


def spectrum_kernel(chunks, v_ref, halo_ref, flags_ref, order_ref, coeff_ref, table_ref, *rest):
    outs, (filt_ref, spec_ref) = rest[: len(chunks)], rest[len(chunks) :]
    inputs = v_ref.shape[1]
    frames = v_ref.shape[2] // NCH
    eye = lax.broadcasted_iota(jnp.int32, (inputs, inputs), 0) == lax.broadcasted_iota(
        jnp.int32, (inputs, inputs), 1
    )
    flags = jnp.where(eye, flags_ref[...].astype(F32), 0.0)
    mask = jnp.broadcast_to(jnp.sum(flags, axis=1, keepdims=True), (inputs, NCH))
    taps = [jnp.broadcast_to(coeff_ref[t : t + 1, :], (inputs, NCH)) for t in range(TAPS)]

    for part in range(2):
        past = tuple(
            halo_ref[part, :, t * NCH : (t + 1) * NCH].astype(F32) * mask for t in range(TAPS - 1)
        )

        def frame_step(f, past, part=part):
            lanes = pl.ds(pl.multiple_of(f * NCH, NCH), NCH)
            now = v_ref[part, :, lanes].astype(F32) * mask
            window = past + (now,)
            total = taps[0] * window[0]
            for t in range(1, TAPS):
                total = total + taps[t] * window[t]
            filt_ref[part, pl.ds(f, inputs, stride=frames), :] = total
            return window[1:]

        lax.fori_loop(0, frames, frame_step, past, unroll=4)

    onehot = (
        lax.broadcasted_iota(jnp.int32, (NCH, NCH), 0) == jnp.broadcast_to(order_ref[...], (NCH, NCH))
    )
    rows = lax.dot_general(
        onehot.astype(BF16), table_ref[...], (((0,), (0,)), ((), ())), preferred_element_type=F32
    ).astype(BF16)

    def input_step(pair, carry):
        blocks = []
        for which in range(2):
            i = pair * 2 + which
            at = pl.ds(pl.multiple_of(i * frames, frames), frames)
            re = filt_ref[0, at, :].astype(BF16)
            im = filt_ref[1, at, :].astype(BF16)
            blocks.append(jnp.concatenate([re, im], axis=1))
            blocks.append(jnp.concatenate([im, -re], axis=1))
        right = jnp.concatenate(blocks, axis=0)
        result = lax.dot_general(
            rows, right, (((1,), (1,)), ((), ())), preferred_element_type=F32
        )
        for which in range(2):
            spec_ref[pl.ds(pair * 2 + which, NCH, stride=inputs), :] = result[
                :, which * NCH : (which + 1) * NCH
            ]
        return carry

    lax.fori_loop(0, inputs // 2, input_step, 0, unroll=2)

    per_block = sum(chunks)
    blocks = NCH // per_block

    def copy_step(block, carry):
        first = 0
        for out, size in zip(outs, chunks):
            for k in range(size):
                at = pl.multiple_of((block * per_block + first + k) * inputs, inputs)
                out[block, k] = spec_ref[pl.ds(at, inputs), :].astype(BF16)
            first += size
        return carry

    lax.fori_loop(0, blocks, copy_step, 0)


def spectra(voltages, halo, flags, order, chunks):
    inputs = voltages.shape[1]
    frames = voltages.shape[2] // NCH
    blocks = NCH // sum(chunks)
    vmem = pl.BlockSpec(memory_space=pltpu.VMEM)
    return pl.pallas_call(
        functools.partial(spectrum_kernel, chunks),
        out_shape=[jax.ShapeDtypeStruct((blocks, size, inputs, 2 * frames), BF16) for size in chunks],
        in_specs=[vmem] * 6,
        out_specs=[vmem] * len(chunks),
        scratch_shapes=[
            pltpu.VMEM((2, inputs * frames, NCH), F32),
            pltpu.VMEM((NCH * inputs, 2 * frames), F32),
        ],
        compiler_params=pltpu.CompilerParams(vmem_limit_bytes=40 * 2**20),
        cost_estimate=pl.CostEstimate(
            flops=2 * 2 * NCH * NCH * 2 * inputs * frames,
            bytes_accessed=8 * 2**20,
            transcendentals=0,
        ),
    )(
        voltages,
        halo,
        flags.reshape(1, inputs),
        order.reshape(1, NCH),
        jnp.asarray(prototype(TAPS, NCH)),
        jnp.asarray(dft_table(NCH)),
    )


def product_kernel(col_ref, own_ref, prev_ref, next_ref, far_lo_ref, far_hi_ref, w_ref, vis_ref, beam_ref, x_ref, r_ref):
    col = col_ref[0]
    blocks, _, inputs, lanes = own_ref.shape
    half = blocks // 2
    total = blocks * inputs
    groups = vis_ref.shape[0]
    panel = total // groups
    for s, ref in enumerate((own_ref, prev_ref, next_ref)):
        x_ref[:, s * lanes : (s + 1) * lanes] = ref[:, 0].reshape(total, lanes)
    x_ref[: half * inputs, 3 * lanes :] = far_lo_ref[:, 0].reshape(half * inputs, lanes)
    x_ref[half * inputs :, 3 * lanes :] = far_hi_ref[:, 0].reshape(half * inputs, lanes)
    mine = x_ref[pl.ds(pl.multiple_of(col * panel, panel), panel), :]
    r_ref[:panel] = mine
    first = lax.broadcasted_iota(jnp.int32, (panel, lanes), 1) < lanes // 2
    for s in range(4):
        turned = pltpu.roll(mine[:, s * lanes : (s + 1) * lanes].astype(F32), lanes // 2, axis=1)
        r_ref[panel:, s * lanes : (s + 1) * lanes] = jnp.where(first, -turned, turned).astype(BF16)
    scale = 1.0 / (NCH * 8)
    for g in range(groups):
        result = lax.dot_general(
            x_ref[g * panel : (g + 1) * panel],
            r_ref[...],
            (((1,), (1,)), ((), ())),
            preferred_element_type=F32,
        )
        result = (result * scale).astype(BF16)
        vis_ref[g, 0, 0] = result[:, :panel]
        vis_ref[g, 1, 0] = result[:, panel:]
    beams = w_ref.shape[2]
    weights = w_ref[:, 0].reshape(2 * beams, total)
    parts = lax.dot_general(
        weights, x_ref[...], (((1,), (0,)), ((), ())), preferred_element_type=F32
    )
    first = lax.broadcasted_iota(jnp.int32, (beams, lanes), 1) < lanes // 2
    bins = lanes // 2 // INTEG
    power = jnp.zeros((beams, 4 * bins), F32)
    for s, shift in enumerate((0, 3, 1, 2)):
        piece = parts[:, s * lanes : (s + 1) * lanes]
        turned = pltpu.roll(piece[beams:], lanes // 2, axis=1)
        value = piece[:beams] + jnp.where(first, -turned, turned)
        lane = lax.broadcasted_iota(jnp.int32, (lanes, 4 * bins), 0)
        place = lax.broadcasted_iota(jnp.int32, (lanes, 4 * bins), 1)
        source = lax.rem(col + shift, 4)
        wanted = source * bins + lax.rem(lane, lanes // 2) // INTEG
        pool = jnp.where(place == wanted, 1.0 / INTEG, 0.0).astype(F32)
        power = power + lax.dot_general(
            value * value,
            pool,
            (((1,), (0,)), ((), ())),
            precision=lax.Precision.HIGHEST,
            preferred_element_type=F32,
        )
    beam_ref[0] = power


def products(col, slots, weights, first):
    own = slots[0]
    blocks, size, inputs, lanes = own.shape
    beams = weights.shape[2]
    total = blocks * inputs
    panel = total // 4
    bins = 4 * (lanes // 2 // INTEG)

    def data(count):
        return pl.BlockSpec((count, 1, inputs, lanes), lambda k, c: (0, k, 0, 0))

    return pl.pallas_call(
        product_kernel,
        out_shape=[
            jax.ShapeDtypeStruct((4, 2, size, panel, panel), BF16),
            jax.ShapeDtypeStruct((size, beams, bins), F32),
        ],
        grid_spec=pltpu.PrefetchScalarGridSpec(
            num_scalar_prefetch=1,
            grid=(size,),
            in_specs=[
                data(blocks),
                data(blocks),
                data(blocks),
                data(blocks // 2),
                data(blocks // 2),
                pl.BlockSpec((2, 1, beams, total), lambda k, c: (0, first + k, 0, 0)),
            ],
            out_specs=[
                pl.BlockSpec((4, 2, 1, panel, panel), lambda k, c: (0, 0, k, 0, 0)),
                pl.BlockSpec((1, beams, bins), lambda k, c: (k, 0, 0)),
            ],
            scratch_shapes=[
                pltpu.VMEM((total, 4 * lanes), BF16),
                pltpu.VMEM((2 * panel, 4 * lanes), BF16),
            ],
        ),
        compiler_params=pltpu.CompilerParams(vmem_limit_bytes=40 * 2**20),
        cost_estimate=pl.CostEstimate(
            flops=2 * size * total * 4 * lanes * (2 * panel + 2 * beams),
            bytes_accessed=size * (2 * total * 4 * lanes + 4 * total * panel * 2),
            transcendentals=0,
        ),
    )(col, *slots, weights)


def gathered(block):
    count = lax.axis_size("col")
    up = [(i, (i + 1) % count) for i in range(count)]
    down = [(i, (i - 1) % count) for i in range(count)]
    half = block.shape[0] // 2
    from_prev = lax.ppermute(block, "col", up)
    from_next = lax.ppermute(block, "col", down)
    far_lo = lax.ppermute(from_prev[:half], "col", up)
    far_hi = lax.ppermute(from_next[half:], "col", down)
    return (block, from_prev, from_next, far_lo, far_hi)


def on_device(voltages, input_flags, channel_order, beam_weights):
    history = passed_along(voltages[:, :, voltages.shape[2] - (TAPS - 1) * NCH :], ("row", "col"), 1)
    flags = input_flags
    pieces = spectra(voltages, history, flags, channel_order, CHUNKS)
    col = lax.axis_index("col").astype(jnp.int32).reshape(1)
    vis = []
    power = []
    first = 0
    for piece, size in zip(pieces, CHUNKS):
        turned = lax.all_to_all(piece, "chan", split_axis=0, concat_axis=0, tiled=True)
        partial, beam = products(col, gathered(turned), beam_weights, first)
        summed = lax.psum_scatter(partial, "row", scatter_dimension=0, tiled=True)
        vis.append(summed[0].astype(F32))
        power.append(beam)
        first += size
    return (jnp.concatenate(vis, axis=1), jnp.concatenate(power, axis=0))


def solution(mesh):
    placed = (P(None, "chan", ("row", "col")), P("chan"), P(), P(None, "chan", "col", None))
    return jax.shard_map(
        on_device,
        mesh=mesh,
        in_specs=placed,
        out_specs=(P(None, "chan", "row", "col"), P("chan", "col", "row")),
        check_vma=False,
    )
```

time: 384 us -> 264 us (0.69)
  matrix products: 98.8 us -> 0 us
  blocking collectives: 139 us -> 65.6 us
  waiting for transfers between devices: 61 us -> 124 us
  local copies, waits for them, and re-layouts: 50 us -> 15.6 us
  Pallas kernels: 0 us -> 25.7 us
  starting transfers between devices: 7.07 us -> 11.9 us
  other arithmetic: 8.62 us -> 3.85 us
    dot_general x65 -> x0, matrix products: 98.8 us -> none  [the longest x8 12.3 us: correlate_one(): lax.dot_general(left_im, right_im, dims, preferred_element_type=jnp.float32)]
    ppermute x0 -> x8, waiting for transfers between devices: none -> 76.8 us  [the longest x2 46.7 us: gathered(): from_next = lax.ppermute(block, 'col', down)]
    all_to_all x3 -> x2, blocking collectives: 139 us -> 65.6 us  [on_device(): lax.all_to_all(piece, 'chan', split_axis=0, concat_axis=0, tiled=True)]
    all_gather x3 -> x0, waiting for transfers between devices: 50.9 us -> none  [the longest x1 50.9 us: on_device(): col_all = lax.all_gather(col_turned, 'row', axis=2, tiled=True)]
    reduce_scatter x0 -> x2, waiting for transfers between devices: none -> 42 us  [on_device(): summed = lax.psum_scatter(partial, 'row', scatter_dimension=0, tiled=True)]
    pallas_call x0 -> x3, Pallas kernels: none -> 25.7 us  [the longest x2 15 us: products(): pl.pallas_call(product_kernel, out_shape=[jax.ShapeDtypeStruct((4, 2, siz...]
    transpose x2 -> x0, local copies, waits for them, and re-layouts: 16.6 us -> none  [the longest x1 8.29 us: to_frames(): order = jnp.transpose(split, (0, 4, 1, 3, 2, 5))]
    all_to_all x8 -> x0, local copies, waits for them, and re-layouts: 15.9 us -> none  [the longest x3 5.72 us: on_device(): lax.all_to_all(spectrum, 'chan', split_axis=0, concat_axis=1, tiled=True)]
  transfers between devices with their start and end apart: 5 -> 11, of which waited for: 3 -> 9; matrix products, arithmetic and copies ran while one was open for 23% -> 1% of each run, Pallas kernels for 0% -> 3%
where the time goes in v1:
time: 264 us; the launch traced here: 261 us
  waiting for transfers between devices  124 us (47%)
  blocking collectives  65.6 us (25%)
  Pallas kernels  25.7 us (10%)
  local copies, waits for them, and re-layouts  15.6 us (6%)
  between operations  14.1 us (5%)
  starting transfers between devices  11.9 us (5%)
  other arithmetic  3.85 us (1%)
    all_to_all x2, blocking collectives, on_device(): lax.all_to_all(piece, 'chan', split_axis=0, concat_axis=0, tiled=True)  65.6 us
    ppermute x2, waiting for transfers between devices, gathered(): from_next = lax.ppermute(block, 'col', down)  46.7 us
    reduce_scatter x2, waiting for transfers between devices, on_device(): summed = lax.psum_scatter(partial, 'row', scatter_dimension=0, tiled=True)  42 us
    ppermute x2, waiting for transfers between devices, gathered(): far_hi = lax.ppermute(from_next[half:], 'col', down)  23.3 us
    pallas_call x2, Pallas kernels, products(): pl.pallas_call(product_kernel, out_shape=[jax.ShapeDtypeStruct((4, 2, siz...  15 us
    unnamed x23, local copies, waits for them, and re-layouts  12.9 us
    pallas_call x1, Pallas kernels, spectra(): pl.pallas_call(functools.partial(spectrum_kernel, chunks), out_shape=[jax...  10.7 us
    ppermute x2, waiting for transfers between devices, gathered(): far_lo = lax.ppermute(from_prev[:half], 'col', up)  6.71 us
  transfers between devices with their start and end apart: 11, of which 9 were waited for; matrix products, arithmetic and copies ran while one was open for 1% of the time, Pallas kernels for 3%

profile of v1, /device:TPU:6, one launch (start us, length us, event | category | flops | bytes accessed | tf_op | source)
XLA Modules:
  0.0 260.9 jit_solution(10108781577080013107)
XLA Ops:
  7.2 0.0 reduce-scatter.5.cloned.1.call-start
  7.2 0.9 slice.15
  8.1 3.5 %collective-permute-start = (bf16[2,64,384]{2,1,0:T(8,128)(2,1)S(1)}, bf16[2,64,384]{2,1,0:T(8,128)(2,1)S(1)}, u32[]{:S(2)}, u32[]{:S(2)}) collective-permute-start(bf16[2,64,384]{2,1,0:T(8,128)(2,1)S(1)} %slice.15), channel_id=1, source_target_pairs={{0,1},{1,2},{2,3},{3,4},{4,5},{5,6},{6,7},{7,8},{8,9},{9,10},{10,1... | collective-permute-start | bytes 294920 | tf_op jit(solution)/shard_map/ppermute | solution.py:40
  11.6 5.1 %collective-permute-done.halo_ref = bf16[2,64,384]{2,1,0:T(8,128)(2,1)S(1)} collective-permute-done((bf16[2,64,384]{2,1,0:T(8,128)(2,1)S(1)}, bf16[2,64,384]{2,1,0:T(8,128)(2,1)S(1)}, u32[]{:S(2)}, u32[]{:S(2)}) %collective-permute-start) | collective-permute-done | bytes 98336 | tf_op jit(solution)/shard_map/ppermute | solution.py:40
  16.7 0.0 copy-start.2
  16.7 1.6 copy-done.2
  18.3 0.0 copy-start.5
  18.3 0.8 copy-done.5
  19.2 0.0 copy-start.6
  19.2 0.7 copy-done.6
  19.9 0.0 copy-start.7
  19.9 0.7 copy-done.7
  20.5 0.0 copy-start.8
  20.5 0.7 copy-done.8
  21.2 10.7 %shard_map.77 = (bf16[16,4,64,128]{3,2,1,0:T(8,128)(2,1)S(1)}, bf16[16,4,64,128]{3,2,1,0:T(8,128)(2,1)S(1)}) custom-call(bf16[2,64,8192]{2,1,0:T(8,128)(2,1)S(1)} %copy-done.2, bf16[2,64,384]{2,1,0:T(8,128)(2,1)S(1)} %collective-permute-done.halo_ref, s32[1,64]{1,0:T(1,128)S(1)} %bitcast.5, s32[1,128]{1,0:T(1,128)S(1)} %bitcast.6, f32[4,128]{1,0:T(4,128)S(1)} %copy-done.6, ...), custom_call_target="tpu_custom_call" | custom-call | flops 536870912 | bytes 8388608 | tf_op jit(solution)/shard_map/pallas_call | solution.py:119
  31.9 35.6 %all_to_all.10.own_ref = bf16[16,4,64,128]{3,2,1,0:T(8,128)(2,1)S(1)} all-to-all(bf16[16,4,64,128]{3,2,1,0:T(8,128)(2,1)S(1)} %get-tuple-element.10), channel_id=1, replica_groups=mesh['chan'=16,'row'=4,'col'=4] {'chan'}, dimensions={0} | all-to-all | bytes 2097152 | tf_op jit(solution)/shard_map/all_to_all | solution.py:266
  67.5 0.9 collective-permute-start.6
  68.4 1.1 collective-permute-start.5
  69.5 23.3 %collective-permute-done.6.next_ref = bf16[16,4,64,128]{3,2,1,0:T(8,128)(2,1)S(1)} collective-permute-done((bf16[16,4,64,128]{3,2,1,0:T(8,128)(2,1)S(1)}, bf16[16,4,64,128]{3,2,1,0:T(8,128)(2,1)S(1)}, u32[]{:S(2)}, u32[]{:S(2)}) %collective-permute-start.6) | collective-permute-done | bytes 1048608 | tf_op jit(solution)/shard_map/ppermute | solution.py:251
  92.8 0.9 slice.23
  93.7 2.1 collective-permute-start.8
  95.8 0.0 collective-permute-done.5.prev_ref
  95.8 0.9 slice.22
  96.7 0.0 copy-start.3
  96.7 1.0 copy-done.3
  97.6 0.0 collective-permute-start.7
  97.6 11.0 %collective-permute-done.8.far_hi_ref = bf16[8,4,64,128]{3,2,1,0:T(8,128)(2,1)} collective-permute-done((bf16[8,4,64,128]{3,2,1,0:T(8,128)(2,1)}, bf16[8,4,64,128]{3,2,1,0:T(8,128)(2,1)}, u32[]{:S(2)}, u32[]{:S(2)}) %collective-permute-start.8) | collective-permute-done | bytes 524320 | tf_op jit(solution)/shard_map/ppermute | solution.py:253
  108.6 4.6 %collective-permute-done.7.far_lo_ref = bf16[8,4,64,128]{3,2,1,0:T(8,128)(2,1)} collective-permute-done((bf16[8,4,64,128]{3,2,1,0:T(8,128)(2,1)}, bf16[8,4,64,128]{3,2,1,0:T(8,128)(2,1)}, u32[]{:S(2)}, u32[]{:S(2)}) %collective-permute-start.7) | collective-permute-done | bytes 524320 | tf_op jit(solution)/shard_map/ppermute | solution.py:252
  113.2 0.0 copy-start.4
  113.2 1.2 copy-done.4
  114.4 0.0 copy-start.9
  114.4 1.6 copy-done.9
  116.0 8.0 %shard_map.79 = (bf16[4,2,4,256,256]{4,3,2,1,0:T(8,128)(2,1)S(1)}, f32[4,64,32]{2,1,0:T(8,128)S(1)}) custom-call(s32[1]{0:T(128)} %bitcast.col_ref, bf16[16,4,64,128]{3,2,1,0:T(8,128)(2,1)S(1)} %all_to_all.10.own_ref, bf16[16,4,64,128]{3,2,1,0:T(8,128)(2,1)S(1)} %copy-done.4, bf16[16,4,64,128]{3,2,1,0:T(8,128)(2,1)S(1)} %collective-permute-done.6.next_ref, ...), custom_call_target="tpu_custom_call" | custom-call | flops 2684354560 | bytes 12582912 | tf_op jit(solution)/shard_map/pallas_call | solution.py:210
  124.0 0.0 copy-start
  124.0 2.0 copy-done
  126.0 0.0 reduce-scatter.5.cloned.1.call-update
  126.1 0.0 reduce-scatter.3.cloned.1.call-start
  126.1 0.0 copy-start.10
  126.1 30.0 %all_to_all.11.own_ref = bf16[16,4,64,128]{3,2,1,0:T(8,128)(2,1)S(1)} all-to-all(bf16[16,4,64,128]{3,2,1,0:T(8,128)(2,1)S(1)} %get-tuple-element.8), channel_id=1, replica_groups=mesh['chan'=16,'row'=4,'col'=4] {'chan'}, dimensions={0} | all-to-all | bytes 2097152 | tf_op jit(solution)/shard_map/all_to_all | solution.py:266
  156.1 0.0 collective-permute-start.2
  156.1 2.0 collective-permute-start.1
  158.1 23.3 %collective-permute-done.2.next_ref = bf16[16,4,64,128]{3,2,1,0:T(8,128)(2,1)S(1)} collective-permute-done((bf16[16,4,64,128]{3,2,1,0:T(8,128)(2,1)S(1)}, bf16[16,4,64,128]{3,2,1,0:T(8,128)(2,1)S(1)}, u32[]{:S(2)}, u32[]{:S(2)}) %collective-permute-start.2) | collective-permute-done | bytes 1048608 | tf_op jit(solution)/shard_map/ppermute | solution.py:251
  181.5 1.0 collective-permute-start.4
  182.5 0.2 collective-permute-done.1.prev_ref
  182.7 1.2 collective-permute-start.3
  183.9 12.3 %collective-permute-done.4.far_hi_ref = bf16[8,4,64,128]{3,2,1,0:T(8,128)(2,1)S(1)} collective-permute-done((bf16[8,4,64,128]{3,2,1,0:T(8,128)(2,1)S(1)}, bf16[8,4,64,128]{3,2,1,0:T(8,128)(2,1)S(1)}, u32[]{:S(2)}, u32[]{:S(2)}) %collective-permute-start.4) | collective-permute-done | bytes 524320 | tf_op jit(solution)/shard_map/ppermute | solution.py:253
  196.2 2.1 collective-permute-done.3.far_lo_ref
  198.3 0.0 copy-done.10
  198.3 7.1 %shard_map.78 = (bf16[4,2,4,256,256]{4,3,2,1,0:T(8,128)(2,1)S(1)}, f32[4,64,32]{2,1,0:T(8,128)S(1)}) custom-call(s32[1]{0:T(128)} %bitcast.col_ref, bf16[16,4,64,128]{3,2,1,0:T(8,128)(2,1)S(1)} %all_to_all.11.own_ref, bf16[16,4,64,128]{3,2,1,0:T(8,128)(2,1)S(1)} %collective-permute-done.1.prev_ref, ...), custom_call_target="tpu_custom_call" | custom-call | flops 2684354560 | bytes 12582912 | tf_op jit(solution)/shard_map/pallas_call | solution.py:210
  205.4 0.0 copy-start.1
  205.4 1.9 copy-done.1
  207.3 0.0 reduce-scatter.3.cloned.1.call-update
  207.4 0.8 copy.8
  208.2 0.0 reduce-scatter.5.cloned.1.call-done
  208.2 42.0 %reduce-scatter.3.cloned.1.call-done = bf16[1,2,4,256,256]{4,3,2,1,0:T(8,128)(2,1)} async-done(((bf16[4,2,4,256,256]{4,3,2,1,0:T(8,128)(2,1)}), bf16[1,2,4,256,256]{4,3,2,1,0:T(8,128)(2,1)}) %reduce-scatter.3.cloned.1.call-update) | async-done | bytes 1048592 | tf_op jit(solution)/shard_map/reduce_scatter | solution.py:268
  250.2 3.8 %maximum_convert_fusion = f32[2,8,256,256]{3,2,1,0:T(8,128)} fusion(bf16[2,4,256,256]{3,2,1,0:T(8,128)(2,1)} %bitcast.7, bf16[2,4,256,256]{3,2,1,0:T(8,128)(2,1)} %bitcast.8), kind=kLoop, calls=%fused_computation | loop fusion | flops 2097152 | bytes 6291456 | tf_op jit(solution)/shard_map/concatenate | solution.py:272
  (3 shorter events, 0.1 us)
Async XLA Ops:
  7.2 201.0 %reduce-scatter.5.cloned.1.call-start = ((), (), s32[]{:S(2)}) async-start(), calls=%async_computation.5 | async-start | bytes 5242880 | tf_op jit(solution)/shard_map/reduce_scatter | solution.py:268
  8.1 8.6 %collective-permute-start = (bf16[2,64,384]{2,1,0:T(8,128)(2,1)S(1)}, bf16[2,64,384]{2,1,0:T(8,128)(2,1)S(1)}, u32[]{:S(2)}, u32[]{:S(2)}) collective-permute-start(bf16[2,64,384]{2,1,0:T(8,128)(2,1)S(1)} %slice.15), channel_id=1, source_target_pairs={{0,1},{1,2},{2,3},{3,4},{4,5},{5,6},{6,7},{7,8},{8,9},{9,10},{10,1... | collective-permute-start | bytes 294920 | tf_op jit(solution)/shard_map/ppermute | solution.py:40
  16.7 1.6 copy-start.2
  18.3 0.8 copy-start.5
  19.2 0.7 copy-start.6
  19.9 0.7 copy-start.7
  20.5 0.7 copy-start.8
  67.5 25.3 %collective-permute-start.6 = (bf16[16,4,64,128]{3,2,1,0:T(8,128)(2,1)S(1)}, bf16[16,4,64,128]{3,2,1,0:T(8,128)(2,1)S(1)}, u32[]{:S(2)}, u32[]{:S(2)}) collective-permute-start(bf16[16,4,64,128]{3,2,1,0:T(8,128)(2,1)S(1)} %all_to_all.10.own_ref), channel_id=1, source_target_pairs={{0,3},{1,0},{2,1},{3,2},{4,7},{5,4},{6,5},{7,6},{8,11},{9,8},{10,9... | collective-permute-start | bytes 3145736 | tf_op jit(solution)/shard_map/ppermute | solution.py:251
  68.4 27.4 %collective-permute-start.5 = (bf16[16,4,64,128]{3,2,1,0:T(8,128)(2,1)S(1)}, bf16[16,4,64,128]{3,2,1,0:T(8,128)(2,1)S(1)}, u32[]{:S(2)}, u32[]{:S(2)}) collective-permute-start(bf16[16,4,64,128]{3,2,1,0:T(8,128)(2,1)S(1)} %all_to_all.10.own_ref), channel_id=1, source_target_pairs={{0,1},{1,2},{2,3},{3,0},{4,5},{5,6},{6,7},{7,4},{8,9},{9,10},{10,1... | collective-permute-start | bytes 3145736 | tf_op jit(solution)/shard_map/ppermute | solution.py:250
  93.7 15.0 %collective-permute-start.8 = (bf16[8,4,64,128]{3,2,1,0:T(8,128)(2,1)}, bf16[8,4,64,128]{3,2,1,0:T(8,128)(2,1)}, u32[]{:S(2)}, u32[]{:S(2)}) collective-permute-start(bf16[8,4,64,128]{3,2,1,0:T(8,128)(2,1)} %slice.23), channel_id=1, source_target_pairs={{0,3},{1,0},{2,1},{3,2},{4,7},{5,4},{6,5},{7,6},{8,11},{9,8},{10,9... | collective-permute-start | bytes 1572872 | tf_op jit(solution)/shard_map/ppermute | solution.py:253
  96.7 1.0 copy-start.3
  97.6 15.6 %collective-permute-start.7 = (bf16[8,4,64,128]{3,2,1,0:T(8,128)(2,1)}, bf16[8,4,64,128]{3,2,1,0:T(8,128)(2,1)}, u32[]{:S(2)}, u32[]{:S(2)}) collective-permute-start(bf16[8,4,64,128]{3,2,1,0:T(8,128)(2,1)} %slice.22), channel_id=1, source_target_pairs={{0,1},{1,2},{2,3},{3,0},{4,5},{5,6},{6,7},{7,4},{8,9},{9,10},{10,1... | collective-permute-start | bytes 1572872 | tf_op jit(solution)/shard_map/ppermute | solution.py:252
  113.2 1.2 copy-start.4
  114.4 1.6 copy-start.9
  124.0 2.0 copy-start
  126.1 124.1 %reduce-scatter.3.cloned.1.call-start = ((), (), s32[]{:S(2)}) async-start(), calls=%async_computation.4 | async-start | bytes 5242880 | tf_op jit(solution)/shard_map/reduce_scatter | solution.py:268
  126.1 72.2 %copy-start.10 = (bf16[2,8,64,1024]{3,2,1,0:T(8,128)(2,1)S(1)}, bf16[2,8,64,1024]{3,2,1,0:T(8,128)(2,1)}, u32[]{:S(2)}) copy-start(bf16[2,8,64,1024]{3,2,1,0:T(8,128)(2,1)} %w_ref.3) | copy-start | bytes 6291460
  156.1 25.4 %collective-permute-start.2 = (bf16[16,4,64,128]{3,2,1,0:T(8,128)(2,1)S(1)}, bf16[16,4,64,128]{3,2,1,0:T(8,128)(2,1)S(1)}, u32[]{:S(2)}, u32[]{:S(2)}) collective-permute-start(bf16[16,4,64,128]{3,2,1,0:T(8,128)(2,1)S(1)} %all_to_all.11.own_ref), channel_id=1, source_target_pairs={{0,3},{1,0},{2,1},{3,2},{4,7},{5,4},{6,5},{7,6},{8,11},{9,8},{10,9... | collective-permute-start | bytes 3145736 | tf_op jit(solution)/shard_map/ppermute | solution.py:251
  156.1 26.6 %collective-permute-start.1 = (bf16[16,4,64,128]{3,2,1,0:T(8,128)(2,1)S(1)}, bf16[16,4,64,128]{3,2,1,0:T(8,128)(2,1)S(1)}, u32[]{:S(2)}, u32[]{:S(2)}) collective-permute-start(bf16[16,4,64,128]{3,2,1,0:T(8,128)(2,1)S(1)} %all_to_all.11.own_ref), channel_id=1, source_target_pairs={{0,1},{1,2},{2,3},{3,0},{4,5},{5,6},{6,7},{7,4},{8,9},{9,10},{10,1... | collective-permute-start | bytes 3145736 | tf_op jit(solution)/shard_map/ppermute | solution.py:250
  181.5 14.7 %collective-permute-start.4 = (bf16[8,4,64,128]{3,2,1,0:T(8,128)(2,1)S(1)}, bf16[8,4,64,128]{3,2,1,0:T(8,128)(2,1)S(1)}, u32[]{:S(2)}, u32[]{:S(2)}) collective-permute-start(bf16[8,4,64,128]{3,2,1,0:T(8,128)(2,1)S(1)} %slice.21), channel_id=1, source_target_pairs={{0,3},{1,0},{2,1},{3,2},{4,7},{5,4},{6,5},{7,6},{8,11},{9,8},{10,9... | collective-permute-start | bytes 1572872 | tf_op jit(solution)/shard_map/ppermute | solution.py:253
  182.7 15.6 %collective-permute-start.3 = (bf16[8,4,64,128]{3,2,1,0:T(8,128)(2,1)S(1)}, bf16[8,4,64,128]{3,2,1,0:T(8,128)(2,1)S(1)}, u32[]{:S(2)}, u32[]{:S(2)}) collective-permute-start(bf16[8,4,64,128]{3,2,1,0:T(8,128)(2,1)S(1)} %slice.20), channel_id=1, source_target_pairs={{0,1},{1,2},{2,3},{3,0},{4,5},{5,6},{6,7},{7,4},{8,9},{9,10},{10,1... | collective-permute-start | bytes 1572872 | tf_op jit(solution)/shard_map/ppermute | solution.py:252
  205.4 1.9 copy-start.1
Sparse Core Ops, SparseCore 0:
  126.2 41.9 reduce-scatter.4
  207.5 42.6 reduce-scatter.2

commit v2 on v1

v2 whole, which is shorter than its diff:
```python
import functools
import math

import jax
import jax.numpy as jnp
import numpy as np
from jax import lax
from jax.experimental import pallas as pl
from jax.experimental.pallas import tpu as pltpu
from jax.sharding import PartitionSpec as P

NCH = 128
TAPS = 4
INTEG = 8
CHUNKS = (4, 4)

F32 = jnp.float32
BF16 = jnp.bfloat16
VMEM = pl.BlockSpec(memory_space=pltpu.VMEM)
SMEM = pl.BlockSpec(memory_space=pltpu.SMEM)
ANY = pl.BlockSpec(memory_space=pl.ANY)


def cost(micros):
    return pl.CostEstimate(flops=int(micros * 1.1e9), bytes_accessed=1, transcendentals=0)


def limit(mebibytes):
    return pltpu.CompilerParams(vmem_limit_bytes=mebibytes * 2**20)


def prototype(taps, length):
    position = np.arange(taps * length, dtype=np.float32) + np.float32(0.5)
    offset = position / np.float32(length) - np.float32(taps / 2.0)
    window = 0.5 - 0.5 * np.cos(2.0 * math.pi * position.astype(np.float64) / (taps * length))
    sinc = np.sin(math.pi * offset.astype(np.float64)) / (math.pi * offset.astype(np.float64))
    return (sinc * window).astype(np.float32).reshape(taps, length)


def dft_table(length):
    index = np.arange(length)
    angle = 2.0 * math.pi / length * (index[:, None] * index[None, :] % length)
    factor = 1.0 / math.sqrt(length)
    table = np.concatenate([np.cos(angle) * factor, np.sin(angle) * factor], axis=1)
    return table.astype(np.float32).astype(jnp.bfloat16)


def passed_along(value, axis, steps):
    count = lax.axis_size(axis)
    initial, last = (max(0, -steps), min(count, count - steps))
    return lax.ppermute(value, axis, [(source, source + steps) for source in range(initial, last)])


def flag_column(flags, inputs):
    eye = lax.broadcasted_iota(jnp.int32, (inputs, inputs), 0) == lax.broadcasted_iota(
        jnp.int32, (inputs, inputs), 1
    )
    held = jnp.where(eye, flags.astype(F32), 0.0)
    return jnp.broadcast_to(jnp.sum(held, axis=1, keepdims=True), (inputs, NCH))


def filter_kernel(v_hbm, flags_hbm, coeff_hbm, filt_ref, v_ref, flags_ref, coeff_ref, sems):
    copies = [
        pltpu.make_async_copy(src, dst, sems.at[n])
        for n, (src, dst) in enumerate(
            ((v_hbm, v_ref), (flags_hbm, flags_ref), (coeff_hbm, coeff_ref))
        )
    ]
    for copy in copies:
        copy.start()
    for copy in copies:
        copy.wait()
    inputs = v_ref.shape[1]
    frames = v_ref.shape[2] // NCH
    mask = flag_column(flags_ref[...], inputs)
    taps = [jnp.broadcast_to(coeff_ref[t : t + 1, :], (inputs, NCH)) * mask for t in range(TAPS)]
    for part in range(2):

        def frame_step(f, past, part=part):
            lanes = pl.ds(pl.multiple_of(f * NCH, NCH), NCH)
            window = past + (v_ref[part, :, lanes].astype(F32),)
            total = taps[0] * window[0]
            for t in range(1, TAPS):
                total = total + taps[t] * window[t]
            filt_ref[part, pl.ds(f, inputs, stride=frames), :] = total
            return window[1:]

        zero = v_ref[part, :, :NCH].astype(F32) * 0.0
        lax.fori_loop(0, frames, frame_step, (zero,) * (TAPS - 1), unroll=4)


def spectrum_kernel(chunks, filt_ref, halo_ref, flags_hbm, order_hbm, coeff_hbm, table_hbm, *rest):
    outs = rest[: len(chunks)]
    flags_ref, order_ref, coeff_ref, table_ref, corr_ref, spec_ref, sems = rest[len(chunks) :]
    copies = [
        pltpu.make_async_copy(src, dst, sems.at[n])
        for n, (src, dst) in enumerate(
            (
                (flags_hbm, flags_ref),
                (order_hbm, order_ref),
                (coeff_hbm, coeff_ref),
                (table_hbm, table_ref),
            )
        )
    ]
    for copy in copies:
        copy.start()
    for copy in copies:
        copy.wait()
    inputs = halo_ref.shape[1]
    frames = filt_ref.shape[1] // inputs
    rows = 8
    mask = flag_column(flags_ref[...], inputs)
    taps = [jnp.broadcast_to(coeff_ref[t : t + 1, :], (inputs, NCH)) * mask for t in range(TAPS)]
    for part in range(2):
        past = [halo_ref[part, :, t * NCH : (t + 1) * NCH].astype(F32) for t in range(TAPS - 1)]
        for f in range(rows):
            total = jnp.zeros((inputs, NCH), F32)
            for t in range(TAPS - 1 - f):
                total = total + taps[t] * past[f + t]
            corr_ref[part, pl.ds(f, inputs, stride=rows), :] = total
    onehot = lax.broadcasted_iota(jnp.int32, (NCH, NCH), 0) == jnp.broadcast_to(
        order_ref[...], (NCH, NCH)
    )
    table = lax.dot_general(
        onehot.astype(BF16), table_ref[...], (((0,), (0,)), ((), ())), preferred_element_type=F32
    ).astype(BF16)

    def input_step(pair, carry):
        blocks = []
        for which in range(2):
            i = pair * 2 + which
            both = []
            for part in range(2):
                block = filt_ref[part, pl.ds(pl.multiple_of(i * frames, frames), frames), :]
                extra = corr_ref[part, pl.ds(pl.multiple_of(i * rows, rows), rows), :]
                both.append(jnp.concatenate([block[:rows] + extra, block[rows:]], axis=0).astype(BF16))
            re, im = both
            blocks.append(jnp.concatenate([re, im], axis=1))
            blocks.append(jnp.concatenate([im, -re], axis=1))
        right = jnp.concatenate(blocks, axis=0)
        result = lax.dot_general(
            table, right, (((1,), (1,)), ((), ())), preferred_element_type=F32
        )
        for which in range(2):
            spec_ref[pl.ds(pair * 2 + which, NCH, stride=inputs), :] = result[
                :, which * NCH : (which + 1) * NCH
            ]
        return carry

    lax.fori_loop(0, inputs // 2, input_step, 0, unroll=2)
    per_block = sum(chunks)

    def copy_step(block, carry):
        first = 0
        for out, size in zip(outs, chunks):
            for k in range(size):
                at = pl.multiple_of((block * per_block + first + k) * inputs, inputs)
                out[block, k] = spec_ref[pl.ds(at, inputs), :].astype(BF16)
            first += size
        return carry

    lax.fori_loop(0, NCH // per_block, copy_step, 0)


def spectra(voltages, history, flags, order, chunks):
    inputs = voltages.shape[1]
    frames = voltages.shape[2] // NCH
    flags = flags.reshape(1, inputs)
    coeff = jnp.asarray(prototype(TAPS, NCH))
    filtered = pl.pallas_call(
        filter_kernel,
        out_shape=jax.ShapeDtypeStruct((2, inputs * frames, NCH), F32),
        in_specs=[ANY] * 3,
        out_specs=VMEM,
        scratch_shapes=[
            pltpu.VMEM(voltages.shape, BF16),
            pltpu.VMEM((1, inputs), jnp.int32),
            pltpu.VMEM((TAPS, NCH), F32),
            pltpu.SemaphoreType.DMA((3,)),
        ],
        compiler_params=limit(16),
        cost_estimate=cost(5),
    )(voltages, flags, coeff)
    blocks = NCH // sum(chunks)
    return pl.pallas_call(
        functools.partial(spectrum_kernel, chunks),
        out_shape=[jax.ShapeDtypeStruct((blocks, size, inputs, 2 * frames), BF16) for size in chunks],
        in_specs=[VMEM, VMEM] + [ANY] * 4,
        out_specs=[VMEM] * len(chunks),
        scratch_shapes=[
            pltpu.VMEM((1, inputs), jnp.int32),
            pltpu.VMEM((1, NCH), jnp.int32),
            pltpu.VMEM((TAPS, NCH), F32),
            pltpu.VMEM((NCH, 2 * NCH), BF16),
            pltpu.VMEM((2, inputs * 8, NCH), F32),
            pltpu.VMEM((NCH * inputs, 2 * frames), F32),
            pltpu.SemaphoreType.DMA((4,)),
        ],
        compiler_params=limit(16),
        cost_estimate=cost(6),
    )(filtered, history, flags, order.reshape(1, NCH), coeff, jnp.asarray(dft_table(NCH)))


def halves_kernel(count, low_ref, high_ref, *refs):
    outs = refs[-2 - count :]
    half = outs[0].shape[0]
    outs[0][...] = low_ref[:half]
    outs[1][...] = high_ref[half:]
    for n in range(count):
        outs[2 + n][...] = refs[n][...]


def halves(low, high, through=()):
    shape = jax.ShapeDtypeStruct((low.shape[0] // 2,) + low.shape[1:], BF16)
    shapes = [shape, shape] + [jax.ShapeDtypeStruct(x.shape, x.dtype) for x in through]
    return pl.pallas_call(
        functools.partial(halves_kernel, len(through)),
        out_shape=shapes,
        in_specs=[VMEM] * (2 + len(through)),
        out_specs=[VMEM] * len(shapes),
        cost_estimate=cost(1),
    )(low, high, *through)


def panel_of(x_ref, index, panel):
    return x_ref[0, pl.ds(pl.multiple_of(index * panel, panel), panel), :]


def turned_panel(panel, lanes, low_sign):
    first = lax.broadcasted_iota(jnp.int32, (panel.shape[0], lanes), 1) < lanes // 2
    parts = []
    for s in range(panel.shape[1] // lanes):
        part = pltpu.roll(panel[:, s * lanes : (s + 1) * lanes].astype(F32), lanes // 2, axis=1)
        parts.append(jnp.where(first, low_sign * part, -low_sign * part).astype(BF16))
    return jnp.concatenate(parts, axis=1)


def correlated(left, right):
    return lax.dot_general(
        left, right, (((1,), (1,)), ((), ())), preferred_element_type=F32
    ) * (1.0 / (NCH * 8))


def far_kernel(place_ref, own_ref, prev_ref, next_ref, lo_ref, hi_ref, re_ref, im_ref, x_ref, r_ref):
    fixed, ring = place_ref[0], place_ref[1]
    blocks, _, inputs, lanes = own_ref.shape
    half = blocks // 2 * inputs
    total = blocks * inputs
    for s, ref in enumerate((own_ref, prev_ref, next_ref)):
        x_ref[0, :, s * lanes : (s + 1) * lanes] = ref[:, 0].reshape(total, lanes)
    x_ref[0, :half, 3 * lanes :] = lo_ref[:, 0].reshape(half, lanes)
    x_ref[0, half:, 3 * lanes :] = hi_ref[:, 0].reshape(half, lanes)
    panel = re_ref.shape[1]
    mine = panel_of(x_ref, fixed, panel)
    r_ref[0, :panel] = mine
    r_ref[0, panel:] = turned_panel(mine, lanes, -1.0)
    result = correlated(panel_of(x_ref, lax.rem(ring + 2, 4), panel), r_ref[0])
    re_ref[0] = result[:, :panel].astype(BF16)
    im_ref[0] = result[:, panel:].astype(BF16)


def far_products(place, slots):
    own = slots[0]
    blocks, size, inputs, lanes = own.shape
    total = blocks * inputs
    panel = total // 4

    def data(count):
        return pl.BlockSpec((count, 1, inputs, lanes), lambda k, c: (0, k, 0, 0))

    def whole(rows, width):
        return pl.BlockSpec((1, rows, width), lambda k, c: (k, 0, 0))

    def shape(rows, width):
        return jax.ShapeDtypeStruct((size, rows, width), BF16)

    return pl.pallas_call(
        far_kernel,
        out_shape=[
            shape(panel, panel),
            shape(panel, panel),
            shape(total, 4 * lanes),
            shape(2 * panel, 4 * lanes),
        ],
        grid_spec=pltpu.PrefetchScalarGridSpec(
            num_scalar_prefetch=1,
            grid=(size,),
            in_specs=[data(blocks)] * 3 + [data(blocks // 2)] * 2,
            out_specs=[
                whole(panel, panel),
                whole(panel, panel),
                whole(total, 4 * lanes),
                whole(2 * panel, 4 * lanes),
            ],
        ),
        compiler_params=limit(20),
        cost_estimate=cost(4),
    )(place, *slots)


def near_kernel(
    first, place_ref, x_ref, r_ref, w_hbm, own_ref, up_ref, down_ref, beam_ref, w_ref, sem
):
    fixed, ring = place_ref[0], place_ref[1]
    k = pl.program_id(0)
    size = w_ref.shape[1]
    copy = pltpu.make_async_copy(w_hbm.at[:, first : first + size], w_ref, sem)

    @pl.when(k == 0)
    def _():
        copy.start()

    panel = own_ref.shape[2]
    lanes = x_ref.shape[2] // 4
    for step, ref in ((1, up_ref), (3, down_ref), (0, own_ref)):
        result = correlated(panel_of(x_ref, lax.rem(ring + step, 4), panel), r_ref[0])
        ref[0, 0] = result[:, :panel].astype(ref.dtype)
        ref[1, 0] = result[:, panel:].astype(ref.dtype)

    @pl.when(k == 0)
    def _():
        copy.wait()

    beams = w_ref.shape[2]
    weights = w_ref[:, k].reshape(2 * beams, w_ref.shape[3])
    parts = lax.dot_general(
        weights, x_ref[0], (((1,), (0,)), ((), ())), preferred_element_type=F32
    )
    low = lax.broadcasted_iota(jnp.int32, (beams, lanes), 1) < lanes // 2
    bins = lanes // 2 // INTEG
    power = jnp.zeros((4 * bins, beams), F32)
    for s, shift in enumerate((0, 3, 1, 2)):
        piece = parts[:, s * lanes : (s + 1) * lanes]
        turned = pltpu.roll(piece[beams:], lanes // 2, axis=1)
        value = piece[:beams] + jnp.where(low, -turned, turned)
        lane = lax.broadcasted_iota(jnp.int32, (4 * bins, lanes), 1)
        place = lax.broadcasted_iota(jnp.int32, (4 * bins, lanes), 0)
        wanted = lax.rem(fixed + shift, 4) * bins + lax.rem(lane, lanes // 2) // INTEG
        pool = jnp.where(place == wanted, 1.0 / INTEG, 0.0).astype(F32)
        power = power + lax.dot_general(
            pool,
            value * value,
            (((1,), (1,)), ((), ())),
            precision=lax.Precision.HIGHEST,
            preferred_element_type=F32,
        )
    beam_ref[0] = power


def near_products(place, x, r, weights, first):
    size, total, width = x.shape
    panel = total // 4
    beams = weights.shape[2]
    bins = width // 2 // INTEG
    block = pl.BlockSpec((2, 1, panel, panel), lambda k, c: (0, k, 0, 0))
    return pl.pallas_call(
        functools.partial(near_kernel, first),
        out_shape=[
            jax.ShapeDtypeStruct((2, size, panel, panel), F32),
            jax.ShapeDtypeStruct((2, size, panel, panel), BF16),
            jax.ShapeDtypeStruct((2, size, panel, panel), BF16),
            jax.ShapeDtypeStruct((size, bins, beams), F32),
        ],
        grid_spec=pltpu.PrefetchScalarGridSpec(
            num_scalar_prefetch=1,
            grid=(size,),
            in_specs=[
                pl.BlockSpec((1, total, width), lambda k, c: (k, 0, 0)),
                pl.BlockSpec((1, 2 * panel, width), lambda k, c: (k, 0, 0)),
                ANY,
            ],
            out_specs=[block] * 3 + [pl.BlockSpec((1, bins, beams), lambda k, c: (k, 0, 0))],
            scratch_shapes=[
                pltpu.VMEM((2, size) + weights.shape[2:], BF16),
                pltpu.SemaphoreType.DMA,
            ],
        ),
        compiler_params=limit(20),
        cost_estimate=cost(7),
    )(place, x, r, weights)


def add_kernel(up_ref, down_ref, low_ref, high_ref, *refs):
    up_out, down_out = refs[-2:]
    up_out[0, 0] = (up_ref[0, 0].astype(F32) + low_ref[0].astype(F32)).astype(BF16)
    down_out[0, 0] = (down_ref[0, 0].astype(F32) + high_ref[0].astype(F32)).astype(BF16)


def added(up, down, low, high, after=()):
    _, size, panel, _ = up.shape
    real = pl.BlockSpec((1, 1, panel, panel), lambda k: (0, k, 0, 0))
    imag = pl.BlockSpec((1, 1, panel, panel), lambda k: (1, k, 0, 0))
    one = pl.BlockSpec((1, panel, panel), lambda k: (k, 0, 0))
    shape = jax.ShapeDtypeStruct(up.shape, BF16)
    return pl.pallas_call(
        add_kernel,
        out_shape=[shape, shape],
        grid=(size,),
        in_specs=[real, imag, one, one] + [ANY] * len(after),
        out_specs=[real, imag],
        input_output_aliases={0: 0, 1: 1},
        cost_estimate=cost(1),
    )(up, down, low, high, *after)


def final_kernel(own_ref, prev_ref, next_ref, *refs):
    refs[-1][...] = own_ref[...] + prev_ref[...].astype(F32) + next_ref[...].astype(F32)


def finished(own, from_prev, from_next, first, channels, out):
    _, size, panel, _ = own.shape
    block = pl.BlockSpec((1, 1, panel, panel), lambda p, k: (p, k, 0, 0))
    extra = [] if out is None else [out]
    return pl.pallas_call(
        final_kernel,
        out_shape=jax.ShapeDtypeStruct((2, channels, panel, panel), F32),
        grid=(2, size),
        in_specs=[block] * 3 + [ANY] * len(extra),
        out_specs=pl.BlockSpec((1, 1, panel, panel), lambda p, k: (p, first + k, 0, 0)),
        input_output_aliases={3: 0} if extra else {},
        cost_estimate=cost(2),
    )(own, from_prev, from_next, *extra)


def along(value, axis, step):
    count = lax.axis_size(axis)
    return lax.ppermute(value, axis, [(i, (i + step) % count) for i in range(count)])


def both_ways(up, down, axis):
    return along(up, axis, 1), along(down, axis, -1)


def on_device(voltages, input_flags, channel_order, beam_weights):
    history = passed_along(voltages[:, :, voltages.shape[2] - (TAPS - 1) * NCH :], ("row", "col"), 1)
    place = jnp.stack([lax.axis_index("col"), lax.axis_index("row")]).astype(jnp.int32)
    pieces = spectra(voltages, history, input_flags, channel_order, CHUNKS)
    channels = sum(CHUNKS)

    def turn(piece):
        return lax.all_to_all(piece, "chan", split_axis=0, concat_axis=0, tiled=True)

    own0 = turn(pieces[0])
    near0 = both_ways(own0, own0, "col")
    own1 = turn(pieces[1])
    low0, high0, own1 = halves(*near0, [own1])
    far0 = both_ways(low0, high0, "col")
    near1 = both_ways(own1, own1, "col")

    re0, im0, x0, r0 = far_products(place, (own0, *near0, *far0))
    got0 = both_ways(re0, im0, "row")
    mine0, up0, down0, beam0 = near_products(place, x0, r0, beam_weights, 0)
    low1, high1 = halves(*near1)
    far1 = both_ways(low1, high1, "col")
    sent0 = both_ways(*added(up0, down0, *got0), "row")

    re1, im1, x1, r1 = far_products(place, (own1, *near1, *far1))
    got1 = both_ways(re1, im1, "row")
    mine1, up1, down1, beam1 = near_products(place, x1, r1, beam_weights, CHUNKS[0])
    sent1 = both_ways(*added(up1, down1, *got1), "row")

    out = finished(mine0, *sent0, 0, channels, None)
    visibility = finished(mine1, *sent1, CHUNKS[0], channels, out)
    power = jnp.concatenate([beam0, beam1], axis=0)
    return (visibility, jnp.transpose(power, (0, 2, 1)))


def solution(mesh):
    placed = (P(None, "chan", ("row", "col")), P("chan"), P(), P(None, "chan", "col", None))
    return jax.shard_map(
        on_device,
        mesh=mesh,
        in_specs=placed,
        out_specs=(P(None, "chan", "row", "col"), P("chan", "col", "row")),
        check_vma=False,
    )
```

time: 264 us -> 250 us (0.947)
  Pallas kernels: 25.7 us -> 61.6 us
  waiting for transfers between devices: 124 us -> 92.1 us
  blocking collectives: 65.6 us -> 35.6 us
  starting transfers between devices: 11.9 us -> 28.9 us
  between operations: 14.1 us -> 0.81 us
  local copies, waits for them, and re-layouts: 15.6 us -> 28.7 us
  other arithmetic: 3.85 us -> 0.74 us
    reduce_scatter x2 -> x0, waiting for transfers between devices: 42 us -> none  [on_device(): summed = lax.psum_scatter(partial, 'row', scatter_dimension=0, tiled=True)]
    pallas_call x2 -> x11, Pallas kernels: 15 us -> 54.4 us  [the longest x2 15.5 us: near_products(): pl.pallas_call(functools.partial(near_kernel, first), out_shape=[jax.Shap...]
    all_to_all x2 -> x1, blocking collectives: 65.6 us -> 35.6 us  [turn(): lax.all_to_all(piece, 'chan', split_axis=0, concat_axis=0, tiled=True)]
    all_to_all x0 -> x1, waiting for transfers between devices: none -> 24.5 us  [turn(): lax.all_to_all(piece, 'chan', split_axis=0, concat_axis=0, tiled=True)]
    unnamed x23 -> x62, local copies, waits for them, and re-layouts: 12.9 us -> 27.8 us
    ppermute x8 -> x16, starting transfers between devices: 8.35 us -> 21.1 us  [along(): lax.ppermute(value, axis, [(i, (i + step) % count) for i in range(count)])]
    ppermute x8 -> x16, waiting for transfers between devices: 76.8 us -> 67.6 us  [along(): lax.ppermute(value, axis, [(i, (i + step) % count) for i in range(count)])]
    ppermute x1, waiting for transfers between devices: 5.13 us -> 0.01 us  [passed_along(): lax.ppermute(value, axis, [(source, source + steps) for source in range(i...]
  transfers between devices with their start and end apart: 11 -> 18, of which waited for: 9 -> 7; matrix products, arithmetic and copies ran while one was open for 1% -> 0% of each run, Pallas kernels for 3% -> 18%
where the time goes in v2:
time: 250 us; the launch traced here: 248 us
  waiting for transfers between devices  92.1 us (37%)
  Pallas kernels  61.6 us (25%)
  blocking collectives  35.6 us (14%)
  starting transfers between devices  28.9 us (12%)
  local copies, waits for them, and re-layouts  28.7 us (11%)
    ppermute x16, waiting for transfers between devices, along(): lax.ppermute(value, axis, [(i, (i + step) % count) for i in range(count)])  67.6 us
    all_to_all x1, blocking collectives, turn(): lax.all_to_all(piece, 'chan', split_axis=0, concat_axis=0, tiled=True)  35.6 us
    unnamed x62, local copies, waits for them, and re-layouts  27.8 us
    all_to_all x1, waiting for transfers between devices, turn(): lax.all_to_all(piece, 'chan', split_axis=0, concat_axis=0, tiled=True)  24.5 us
    ppermute x16, starting transfers between devices, along(): lax.ppermute(value, axis, [(i, (i + step) % count) for i in range(count)])  21.1 us
    pallas_call x2, Pallas kernels, near_products(): pl.pallas_call(functools.partial(near_kernel, first), out_shape=[jax.Shap...  15.5 us
    pallas_call x2, Pallas kernels, finished(): pl.pallas_call(final_kernel, out_shape=jax.ShapeDtypeStruct((2, channels,...  12.2 us
    pallas_call x2, Pallas kernels, far_products(): pl.pallas_call(far_kernel, out_shape=[shape(panel, panel), shape(panel, p...  8.54 us
  transfers between devices with their start and end apart: 18, of which 7 were waited for; matrix products, arithmetic and copies ran while one was open for 0% of the time, Pallas kernels for 18%

profile of v2, /device:TPU:6, one launch (start us, length us, event | category | flops | bytes accessed | tf_op | source)
XLA Modules:
  0.0 248.5 jit_solution(7171266756659250823)
XLA Ops:
  0.6 0.9 slice.3
  1.5 3.5 %collective-permute-start = (bf16[2,64,384]{2,1,0:T(8,128)(2,1)S(1)}, bf16[2,64,384]{2,1,0:T(8,128)(2,1)S(1)}, u32[]{:S(2)}, u32[]{:S(2)}) collective-permute-start(bf16[2,64,384]{2,1,0:T(8,128)(2,1)S(1)} %slice.3), channel_id=1, source_target_pairs={{0,1},{1,2},{2,3},{3,4},{4,5},{5,6},{6,7},{7,8},{8,9},{9,10},{10,1... | collective-permute-start | bytes 294920 | tf_op jit(solution)/shard_map/ppermute | solution.py:51
  5.0 0.0 copy-start.2
  5.0 1.6 copy-done.2
  6.6 0.7 copy-done.19
  7.3 0.7 copy-done.22
  8.0 5.0 %shard_map.77.filt_ref = f32[2,4096,128]{2,1,0:T(8,128)S(1)} custom-call(bf16[2,64,8192]{2,1,0:T(8,128)(2,1)S(1)} %copy-done.2, s32[1,64]{1,0:T(1,128)S(1)} %bitcast.6, f32[4,128]{1,0:T(4,128)S(1)} %copy-done.22), custom_call_target="tpu_custom_call" | custom-call | flops 5500000256 | bytes 1 | tf_op jit(solution)/shard_map/pallas_call | solution.py:171
  13.0 7.2 %shard_map.78 = (bf16[16,4,64,128]{3,2,1,0:T(8,128)(2,1)S(1)}, bf16[16,4,64,128]{3,2,1,0:T(8,128)(2,1)}) custom-call(f32[2,4096,128]{2,1,0:T(8,128)S(1)} %shard_map.77.filt_ref, bf16[2,64,384]{2,1,0:T(8,128)(2,1)S(1)} %collective-permute-done.halo_ref, s32[1,64]{1,0:T(1,128)S(1)} %bitcast.7, s32[1,128]{1,0:T(1,128)S(1)} %bitcast.8, f32[4,128]{1,0:T(4,128)S(1)} %copy-done.22, ...), custom_call_target="tpu_custom_call" | custom-call | flops 6600000000 | bytes 1 | tf_op jit(solution)/shard_map/pallas_call | solution.py:186
  20.2 35.6 %all_to_all.10.own_ref = bf16[16,4,64,128]{3,2,1,0:T(8,128)(2,1)S(1)} all-to-all(bf16[16,4,64,128]{3,2,1,0:T(8,128)(2,1)S(1)} %get-tuple-element.29), channel_id=1, replica_groups=mesh['chan'=16,'row'=4,'col'=4] {'chan'}, dimensions={0} | all-to-all | bytes 2097152 | tf_op jit(solution)/shard_map/all_to_all | solution.py:442
  55.8 4.4 %all-to-all-start.1 = ((bf16[16,4,64,128]{3,2,1,0:T(8,128)(2,1)}), bf16[16,4,64,128]{3,2,1,0:T(8,128)(2,1)}, u32[]{:S(2)}, u32[]{:S(2)}) async-start(bf16[16,4,64,128]{3,2,1,0:T(8,128)(2,1)} %get-tuple-element.30), calls=%async_computation.1 | async-start | bytes 2097152 | tf_op jit(solution)/shard_map/all_to_all | solution.py:442
  60.2 0.9 collective-permute-start.2
  61.1 1.2 collective-permute-start.1
  62.3 24.5 %all-to-all-done.1.refs_0_ = bf16[16,4,64,128]{3,2,1,0:T(8,128)(2,1)} async-done(((bf16[16,4,64,128]{3,2,1,0:T(8,128)(2,1)}), bf16[16,4,64,128]{3,2,1,0:T(8,128)(2,1)}, u32[]{:S(2)}, u32[]{:S(2)}) %all-to-all-start.1) | async-done | bytes 1048608 | tf_op jit(solution)/shard_map/all_to_all | solution.py:442
  86.8 1.2 collective-permute-done.1.low_ref.prev_ref
  88.0 1.0 copy-done.9
  89.0 3.2 %shard_map.79 = (bf16[8,4,64,128]{3,2,1,0:T(8,128)(2,1)}, bf16[8,4,64,128]{3,2,1,0:T(8,128)(2,1)}, bf16[16,4,64,128]{3,2,1,0:T(8,128)(2,1)}) custom-call(bf16[16,4,64,128]{3,2,1,0:T(8,128)(2,1)} %copy-done.9, bf16[16,4,64,128]{3,2,1,0:T(8,128)(2,1)} %copy-done.7, bf16[16,4,64,128]{3,2,1,0:T(8,128)(2,1)} %all-to-all-done.1.refs_0_), custom_call_target="tpu_custom_call" | custom-call | flops 1100000000 | bytes 1 | tf_op jit(solution)/shard_map/pallas_call | solution.py:217
  92.2 1.4 collective-permute-start.4
  93.6 0.6 collective-permute-start.3
  94.2 1.4 collective-permute-start.11
  95.6 1.8 collective-permute-start.12
  97.5 0.1 pad_add_fusion.place_ref
  97.5 34.3 %collective-permute-done.11.lo_ref = bf16[8,4,64,128]{3,2,1,0:T(8,128)(2,1)S(1)} collective-permute-done((bf16[8,4,64,128]{3,2,1,0:T(8,128)(2,1)}, bf16[8,4,64,128]{3,2,1,0:T(8,128)(2,1)S(1)}, u32[]{:S(2)}, u32[]{:S(2)}) %collective-permute-start.11) | collective-permute-done | bytes 524320 | tf_op jit(solution)/shard_map/ppermute | solution.py:428
  131.9 0.8 copy-done.15
  132.7 0.8 copy-done.17
  133.5 1.2 copy-done.8
  134.7 1.2 copy-done.10
  135.9 1.0 copy-done.16
  137.0 1.0 copy-done.18
  138.0 4.0 %shard_map.84 = (bf16[4,256,256]{2,1,0:T(8,128)(2,1)}, bf16[4,256,256]{2,1,0:T(8,128)(2,1)}, bf16[4,1024,512]{2,1,0:T(8,128)(2,1)S(1)}, bf16[4,512,512]{2,1,0:T(8,128)(2,1)S(1)}) custom-call(s32[2]{0:T(128)S(1)} %pad_add_fusion.place_ref, bf16[16,4,64,128]{3,2,1,0:T(8,128)(2,1)S(1)} %all_to_all.10.own_ref, bf16[16,4,64,128]{3,2,1,0:T(8,128)(2,1)S(1)} %copy-done.10, ...), custom_call_target="tpu_custom_call" | custom-call | flops 4400000000 | bytes 1 | tf_op jit(solution)/shard_map/pallas_call | solution.py:278
  142.0 2.0 copy-done.23
  144.0 1.3 copy-done.25
  145.3 1.9 collective-permute-start.13
  147.2 0.1 collective-permute-start.14
  147.4 1.0 copy-done.5
  148.4 2.6 %shard_map.80 = (bf16[8,4,64,128]{3,2,1,0:T(8,128)(2,1)}, bf16[8,4,64,128]{3,2,1,0:T(8,128)(2,1)}) custom-call(bf16[16,4,64,128]{3,2,1,0:T(8,128)(2,1)} %collective-permute-done.3.low_ref.prev_ref, bf16[16,4,64,128]{3,2,1,0:T(8,128)(2,1)} %copy-done.5), custom_call_target="tpu_custom_call" | custom-call | flops 1100000000 | bytes 1 | tf_op jit(solution)/shard_map/pallas_call | solution.py:217
  150.9 3.2 %collective-permute-start.6 = (bf16[8,4,64,128]{3,2,1,0:T(8,128)(2,1)}, bf16[8,4,64,128]{3,2,1,0:T(8,128)(2,1)}, u32[]{:S(2)}, u32[]{:S(2)}) collective-permute-start(bf16[8,4,64,128]{3,2,1,0:T(8,128)(2,1)} %get-tuple-element.33), channel_id=1, source_target_pairs={{0,3},{1,0},{2,1},{3,2},{4,7},{5,4},{6,5},{7,6},{8,11},{9,8},{10,9... | collective-permute-start | bytes 1572872 | tf_op jit(solution)/shard_map/ppermute | solution.py:428
  154.2 2.2 copy-done.24
  156.3 1.6 copy-done.26
  157.9 7.7 %shard_map.85 = (f32[2,4,256,256]{3,2,1,0:T(8,128)S(1)}, bf16[2,4,256,256]{3,2,1,0:T(8,128)(2,1)S(1)}, bf16[2,4,256,256]{3,2,1,0:T(8,128)(2,1)S(1)}, f32[4,32,64]{2,1,0:T(8,128)S(1)}) custom-call(s32[2]{0:T(128)S(1)} %pad_add_fusion.place_ref, bf16[4,1024,512]{2,1,0:T(8,128)(2,1)S(1)} %copy-done.24, bf16[4,512,512]{2,1,0:T(8,128)(2,1)S(1)} %copy-done.26, ...), custom_call_target="tpu_custom_call" | custom-call | flops 7699999744 | bytes 1 | tf_op jit(solution)/shard_map/pallas_call | solution.py:357
  165.7 1.3 copy-done
  167.0 1.0 copy-done.13
  168.0 1.0 copy-done.14
  169.0 3.7 %shard_map.86 = (bf16[2,4,256,256]{3,2,1,0:T(8,128)(2,1)}, bf16[2,4,256,256]{3,2,1,0:T(8,128)(2,1)}) custom-call(bf16[2,4,256,256]{3,2,1,0:T(8,128)(2,1)} %copy-done.13, bf16[2,4,256,256]{3,2,1,0:T(8,128)(2,1)} %copy-done.14, bf16[4,256,256]{2,1,0:T(8,128)(2,1)} %collective-permute-done.13.low_ref, ...), custom_call_target="tpu_custom_call", output_to_operand_aliasing={{0}: (0, {}), {1}: (1, {})} | custom-call | flops 1100000000 | bytes 1 | tf_op jit(solution)/shard_map/pallas_call | solution.py:396
  172.7 3.1 %collective-permute-start.15 = (bf16[2,4,256,256]{3,2,1,0:T(8,128)(2,1)}, bf16[2,4,256,256]{3,2,1,0:T(8,128)(2,1)}, u32[]{:S(2)}, u32[]{:S(2)}) collective-permute-start(bf16[2,4,256,256]{3,2,1,0:T(8,128)(2,1)} %get-tuple-element.52), channel_id=1, source_target_pairs={{0,4},{4,8},{8,12},{12,0},{1,5},{5,9},{9,13},{13,1},{2,6},{6,10},{... | collective-permute-start | bytes 3145736 | tf_op jit(solution)/shard_map/ppermute | solution.py:428
  175.8 0.0 collective-permute-start.16
  175.8 1.2 copy-done.6
  177.0 4.6 %shard_map.81 = (bf16[4,256,256]{2,1,0:T(8,128)(2,1)S(1)}, bf16[4,256,256]{2,1,0:T(8,128)(2,1)S(1)}, bf16[4,1024,512]{2,1,0:T(8,128)(2,1)S(1)}, bf16[4,512,512]{2,1,0:T(8,128)(2,1)S(1)}) custom-call(s32[2]{0:T(128)S(1)} %pad_add_fusion.place_ref, bf16[16,4,64,128]{3,2,1,0:T(8,128)(2,1)S(1)} %copy-done.4, ...), custom_call_target="tpu_custom_call" | custom-call | flops 4400000000 | bytes 1 | tf_op jit(solution)/shard_map/pallas_call | solution.py:278
  181.6 3.3 %collective-permute-start.7 = (bf16[4,256,256]{2,1,0:T(8,128)(2,1)S(1)}, bf16[4,256,256]{2,1,0:T(8,128)(2,1)S(1)}, u32[]{:S(2)}, u32[]{:S(2)}) collective-permute-start(bf16[4,256,256]{2,1,0:T(8,128)(2,1)S(1)} %get-tuple-element.39), channel_id=1, source_target_pairs={{0,4},{4,8},{8,12},{12,0},{1,5},{5,9},{9,13},{13,1},{2,6},{6,10},{... | collective-permute-start | bytes 1572872 | tf_op jit(solution)/shard_map/ppermute | solution.py:428
  184.9 7.8 %shard_map.82 = (f32[2,4,256,256]{3,2,1,0:T(8,128)S(1)}, bf16[2,4,256,256]{3,2,1,0:T(8,128)(2,1)S(1)}, bf16[2,4,256,256]{3,2,1,0:T(8,128)(2,1)S(1)}, f32[4,32,64]{2,1,0:T(8,128)S(1)}) custom-call(s32[2]{0:T(128)S(1)} %pad_add_fusion.place_ref, bf16[4,1024,512]{2,1,0:T(8,128)(2,1)S(1)} %get-tuple-element.34.x_ref, ...), custom_call_target="tpu_custom_call" | custom-call | flops 7699999744 | bytes 1 | tf_op jit(solution)/shard_map/pallas_call | solution.py:357
  192.7 1.4 copy-done.1
  194.1 1.0 copy-done.11
  195.0 1.0 copy-done.12
  196.1 12.7 %collective-permute-done.7.low_ref = bf16[4,256,256]{2,1,0:T(8,128)(2,1)S(1)} collective-permute-done((bf16[4,256,256]{2,1,0:T(8,128)(2,1)S(1)}, bf16[4,256,256]{2,1,0:T(8,128)(2,1)S(1)}, u32[]{:S(2)}, u32[]{:S(2)}) %collective-permute-start.7) | collective-permute-done | bytes 524320 | tf_op jit(solution)/shard_map/ppermute | solution.py:428
  208.8 3.4 %collective-permute-done.8.high_ref = bf16[4,256,256]{2,1,0:T(8,128)(2,1)S(1)} collective-permute-done((bf16[4,256,256]{2,1,0:T(8,128)(2,1)S(1)}, bf16[4,256,256]{2,1,0:T(8,128)(2,1)S(1)}, u32[]{:S(2)}, u32[]{:S(2)}) %collective-permute-start.8) | collective-permute-done | bytes 524320 | tf_op jit(solution)/shard_map/ppermute | solution.py:428
  212.2 0.8 copy-done.30
  213.0 3.6 %shard_map.83 = (bf16[2,4,256,256]{3,2,1,0:T(8,128)(2,1)}, bf16[2,4,256,256]{3,2,1,0:T(8,128)(2,1)}) custom-call(bf16[2,4,256,256]{3,2,1,0:T(8,128)(2,1)} %copy-done.11, bf16[2,4,256,256]{3,2,1,0:T(8,128)(2,1)} %copy-done.12, bf16[4,256,256]{2,1,0:T(8,128)(2,1)} %copy-done.29, ...), custom_call_target="tpu_custom_call", output_to_operand_aliasing={{0}: (0, {}), {1}: (1, {})} | custom-call | flops 1100000000 | bytes 1 | tf_op jit(solution)/shard_map/pallas_call | solution.py:396
  216.7 0.4 collective-permute-start.9
  217.1 1.6 collective-permute-start.10
  218.7 0.7 maximum_bitcast_fusion
  219.4 6.1 %shard_map.87.refs_0_ = f32[2,8,256,256]{3,2,1,0:T(8,128)} custom-call(f32[2,4,256,256]{3,2,1,0:T(8,128)} %copy-done, bf16[2,4,256,256]{3,2,1,0:T(8,128)(2,1)} %collective-permute-done.15.prev_ref, bf16[2,4,256,256]{3,2,1,0:T(8,128)(2,1)} %collective-permute-done.16.next_ref), custom_call_target="tpu_custom_call" | custom-call | flops 2200000000 | bytes 1 | tf_op jit(solution)/shard_map/pallas_call | solution.py:415
  225.5 14.3 %collective-permute-done.9.prev_ref = bf16[2,4,256,256]{3,2,1,0:T(8,128)(2,1)S(1)} collective-permute-done((bf16[2,4,256,256]{3,2,1,0:T(8,128)(2,1)}, bf16[2,4,256,256]{3,2,1,0:T(8,128)(2,1)S(1)}, u32[]{:S(2)}, u32[]{:S(2)}) %collective-permute-start.9) | collective-permute-done | bytes 1048608 | tf_op jit(solution)/shard_map/ppermute | solution.py:428
  239.7 1.6 collective-permute-done.10.next_ref
  241.4 1.0 copy-done.28
  242.4 6.1 %shard_map.88 = f32[2,8,256,256]{3,2,1,0:T(8,128)} custom-call(f32[2,4,256,256]{3,2,1,0:T(8,128)} %copy-done.1, bf16[2,4,256,256]{3,2,1,0:T(8,128)(2,1)} %copy-done.27, bf16[2,4,256,256]{3,2,1,0:T(8,128)(2,1)} %copy-done.28, f32[2,8,256,256]{3,2,1,0:T(8,128)} %shard_map.87.refs_0_), custom_call_target="tpu_custom_call", output_to_operand_aliasing={{}: (3, {})} | custom-call | flops 2200000000 | bytes 1 | tf_op jit(solution)/shard_map/pallas_call | solution.py:415
  (50 shorter events, 0.1 us)
Async XLA Ops:
  1.5 11.4 %collective-permute-start = (bf16[2,64,384]{2,1,0:T(8,128)(2,1)S(1)}, bf16[2,64,384]{2,1,0:T(8,128)(2,1)S(1)}, u32[]{:S(2)}, u32[]{:S(2)}) collective-permute-start(bf16[2,64,384]{2,1,0:T(8,128)(2,1)S(1)} %slice.3), channel_id=1, source_target_pairs={{0,1},{1,2},{2,3},{3,4},{4,5},{5,6},{6,7},{7,8},{8,9},{9,10},{10,1... | collective-permute-start | bytes 294920 | tf_op jit(solution)/shard_map/ppermute | solution.py:51
  5.0 1.6 copy-start.2
  6.6 0.7 copy-start.19
  7.3 0.7 copy-start.22
  8.0 5.0 %copy-start.20 = (s32[128]{0:T(128)S(1)}, s32[128]{0:T(128)}, u32[]{:S(2)}) copy-start(s32[128]{0:T(128)} %param.8) | copy-start | bytes 1540
  8.0 5.0 %copy-start.21 = (bf16[128,256]{1,0:T(8,128)(2,1)S(1)}, bf16[128,256]{1,0:T(8,128)(2,1)}, u32[]{:S(2)}) copy-start(bf16[128,256]{1,0:T(8,128)(2,1)} %constant.12.clone.table_hbm) | copy-start | bytes 196612
  55.8 30.9 %all-to-all-start.1 = ((bf16[16,4,64,128]{3,2,1,0:T(8,128)(2,1)}), bf16[16,4,64,128]{3,2,1,0:T(8,128)(2,1)}, u32[]{:S(2)}, u32[]{:S(2)}) async-start(bf16[16,4,64,128]{3,2,1,0:T(8,128)(2,1)} %get-tuple-element.30), calls=%async_computation.1 | async-start | bytes 2097152 | tf_op jit(solution)/shard_map/all_to_all | solution.py:442
  60.2 26.6 %collective-permute-start.2 = (bf16[16,4,64,128]{3,2,1,0:T(8,128)(2,1)S(1)}, bf16[16,4,64,128]{3,2,1,0:T(8,128)(2,1)S(1)}, u32[]{:S(2)}, u32[]{:S(2)}) collective-permute-start(bf16[16,4,64,128]{3,2,1,0:T(8,128)(2,1)S(1)} %all_to_all.10.own_ref), channel_id=1, source_target_pairs={{0,3},{1,0},{2,1},{3,2},{4,7},{5,4},{6,5},{7,6},{8,11},{9,8},{10,9... | collective-permute-start | bytes 3145736 | tf_op jit(solution)/shard_map/ppermute | solution.py:428
  61.1 26.9 %collective-permute-start.1 = (bf16[16,4,64,128]{3,2,1,0:T(8,128)(2,1)S(1)}, bf16[16,4,64,128]{3,2,1,0:T(8,128)(2,1)S(1)}, u32[]{:S(2)}, u32[]{:S(2)}) collective-permute-start(bf16[16,4,64,128]{3,2,1,0:T(8,128)(2,1)S(1)} %all_to_all.10.own_ref), channel_id=1, source_target_pairs={{0,1},{1,2},{2,3},{3,0},{4,5},{5,6},{6,7},{7,4},{8,9},{9,10},{10,1... | collective-permute-start | bytes 3145736 | tf_op jit(solution)/shard_map/ppermute | solution.py:428
  86.8 1.2 copy-start.7
  88.0 1.0 copy-start.9
  92.2 55.2 %collective-permute-start.4 = (bf16[16,4,64,128]{3,2,1,0:T(8,128)(2,1)}, bf16[16,4,64,128]{3,2,1,0:T(8,128)(2,1)S(1)}, u32[]{:S(2)}, u32[]{:S(2)}) collective-permute-start(bf16[16,4,64,128]{3,2,1,0:T(8,128)(2,1)} %get-tuple-element.31.own_ref), channel_id=1, source_target_pairs={{0,3},{1,0},{2,1},{3,2},{4,7},{5,4},{6,5},{7,6},{8,11},{9,8},{10,9... | collective-permute-start | bytes 3145736 | tf_op jit(solution)/shard_map/ppermute | solution.py:428
  93.6 53.7 %collective-permute-start.3 = (bf16[16,4,64,128]{3,2,1,0:T(8,128)(2,1)}, bf16[16,4,64,128]{3,2,1,0:T(8,128)(2,1)}, u32[]{:S(2)}, u32[]{:S(2)}) collective-permute-start(bf16[16,4,64,128]{3,2,1,0:T(8,128)(2,1)} %get-tuple-element.31.own_ref), channel_id=1, source_target_pairs={{0,1},{1,2},{2,3},{3,0},{4,5},{5,6},{6,7},{7,4},{8,9},{9,10},{10,1... | collective-permute-start | bytes 3145736 | tf_op jit(solution)/shard_map/ppermute | solution.py:428
  94.2 37.6 %collective-permute-start.11 = (bf16[8,4,64,128]{3,2,1,0:T(8,128)(2,1)}, bf16[8,4,64,128]{3,2,1,0:T(8,128)(2,1)S(1)}, u32[]{:S(2)}, u32[]{:S(2)}) collective-permute-start(bf16[8,4,64,128]{3,2,1,0:T(8,128)(2,1)} %get-tuple-element.43), channel_id=1, source_target_pairs={{0,1},{1,2},{2,3},{3,0},{4,5},{5,6},{6,7},{7,4},{8,9},{9,10},{10,1... | collective-permute-start | bytes 1572872 | tf_op jit(solution)/shard_map/ppermute | solution.py:428
  95.6 37.0 %collective-permute-start.12 = (bf16[8,4,64,128]{3,2,1,0:T(8,128)(2,1)}, bf16[8,4,64,128]{3,2,1,0:T(8,128)(2,1)S(1)}, u32[]{:S(2)}, u32[]{:S(2)}) collective-permute-start(bf16[8,4,64,128]{3,2,1,0:T(8,128)(2,1)} %get-tuple-element.44), channel_id=1, source_target_pairs={{0,3},{1,0},{2,1},{3,2},{4,7},{5,4},{6,5},{7,6},{8,11},{9,8},{10,9... | collective-permute-start | bytes 1572872 | tf_op jit(solution)/shard_map/ppermute | solution.py:428
  131.9 0.8 copy-start.15
  132.7 0.8 copy-start.17
  133.5 1.2 copy-start.8
  134.7 1.2 copy-start.10
  135.9 1.0 copy-start.16
  137.0 1.0 copy-start.18
  142.0 2.0 copy-start.23
  144.0 1.3 copy-start.25
  145.3 8.8 %copy-start.3 = (bf16[2,8,64,1024]{3,2,1,0:T(8,128)(2,1)S(1)}, bf16[2,8,64,1024]{3,2,1,0:T(8,128)(2,1)}, u32[]{:S(2)}) copy-start(bf16[2,8,64,1024]{3,2,1,0:T(8,128)(2,1)} %w_hbm.3) | copy-start | bytes 6291460
  145.3 23.6 %collective-permute-start.13 = (bf16[4,256,256]{2,1,0:T(8,128)(2,1)}, bf16[4,256,256]{2,1,0:T(8,128)(2,1)}, u32[]{:S(2)}, u32[]{:S(2)}) collective-permute-start(bf16[4,256,256]{2,1,0:T(8,128)(2,1)} %get-tuple-element.50), channel_id=1, source_target_pairs={{0,4},{4,8},{8,12},{12,0},{1,5},{5,9},{9,13},{13,1},{2,6},{6,10},{... | collective-permute-start | bytes 1572872 | tf_op jit(solution)/shard_map/ppermute | solution.py:428
  147.2 21.8 %collective-permute-start.14 = (bf16[4,256,256]{2,1,0:T(8,128)(2,1)}, bf16[4,256,256]{2,1,0:T(8,128)(2,1)}, u32[]{:S(2)}, u32[]{:S(2)}) collective-permute-start(bf16[4,256,256]{2,1,0:T(8,128)(2,1)} %get-tuple-element.51), channel_id=1, source_target_pairs={{0,12},{4,0},{8,4},{12,8},{1,13},{5,1},{9,5},{13,9},{2,14},{6,2},{... | collective-permute-start | bytes 1572872 | tf_op jit(solution)/shard_map/ppermute | solution.py:428
  147.4 1.0 copy-start.5
  150.9 24.9 %collective-permute-start.5 = (bf16[8,4,64,128]{3,2,1,0:T(8,128)(2,1)}, bf16[8,4,64,128]{3,2,1,0:T(8,128)(2,1)}, u32[]{:S(2)}, u32[]{:S(2)}) collective-permute-start(bf16[8,4,64,128]{3,2,1,0:T(8,128)(2,1)} %get-tuple-element.32), channel_id=1, source_target_pairs={{0,1},{1,2},{2,3},{3,0},{4,5},{5,6},{6,7},{7,4},{8,9},{9,10},{10,1... | collective-permute-start | bytes 1572872 | tf_op jit(solution)/shard_map/ppermute | solution.py:428
  150.9 24.9 %collective-permute-start.6 = (bf16[8,4,64,128]{3,2,1,0:T(8,128)(2,1)}, bf16[8,4,64,128]{3,2,1,0:T(8,128)(2,1)}, u32[]{:S(2)}, u32[]{:S(2)}) collective-permute-start(bf16[8,4,64,128]{3,2,1,0:T(8,128)(2,1)} %get-tuple-element.33), channel_id=1, source_target_pairs={{0,3},{1,0},{2,1},{3,2},{4,7},{5,4},{6,5},{7,6},{8,11},{9,8},{10,9... | collective-permute-start | bytes 1572872 | tf_op jit(solution)/shard_map/ppermute | solution.py:428
  154.2 2.2 copy-start.24
  156.3 1.6 copy-start.26
  165.7 1.3 copy-start
  167.0 1.0 copy-start.13
  168.0 1.0 copy-start.14
  169.0 6.8 %copy-start.4 = (bf16[16,4,64,128]{3,2,1,0:T(8,128)(2,1)S(1)}, bf16[16,4,64,128]{3,2,1,0:T(8,128)(2,1)}, u32[]{:S(2)}) copy-start(bf16[16,4,64,128]{3,2,1,0:T(8,128)(2,1)} %get-tuple-element.31.own_ref) | copy-start | bytes 3145732
  172.7 46.7 %collective-permute-start.15 = (bf16[2,4,256,256]{3,2,1,0:T(8,128)(2,1)}, bf16[2,4,256,256]{3,2,1,0:T(8,128)(2,1)}, u32[]{:S(2)}, u32[]{:S(2)}) collective-permute-start(bf16[2,4,256,256]{3,2,1,0:T(8,128)(2,1)} %get-tuple-element.52), channel_id=1, source_target_pairs={{0,4},{4,8},{8,12},{12,0},{1,5},{5,9},{9,13},{13,1},{2,6},{6,10},{... | collective-permute-start | bytes 3145736 | tf_op jit(solution)/shard_map/ppermute | solution.py:428
  175.8 43.6 %collective-permute-start.16 = (bf16[2,4,256,256]{3,2,1,0:T(8,128)(2,1)}, bf16[2,4,256,256]{3,2,1,0:T(8,128)(2,1)}, u32[]{:S(2)}, u32[]{:S(2)}) collective-permute-start(bf16[2,4,256,256]{3,2,1,0:T(8,128)(2,1)} %get-tuple-element.53), channel_id=1, source_target_pairs={{0,12},{4,0},{8,4},{12,8},{1,13},{5,1},{9,5},{13,9},{2,14},{6,2},{... | collective-permute-start | bytes 3145736 | tf_op jit(solution)/shard_map/ppermute | solution.py:428
  175.8 1.2 copy-start.6
  181.6 27.2 %collective-permute-start.7 = (bf16[4,256,256]{2,1,0:T(8,128)(2,1)S(1)}, bf16[4,256,256]{2,1,0:T(8,128)(2,1)S(1)}, u32[]{:S(2)}, u32[]{:S(2)}) collective-permute-start(bf16[4,256,256]{2,1,0:T(8,128)(2,1)S(1)} %get-tuple-element.39), channel_id=1, source_target_pairs={{0,4},{4,8},{8,12},{12,0},{1,5},{5,9},{9,13},{13,1},{2,6},{6,10},{... | collective-permute-start | bytes 1572872 | tf_op jit(solution)/shard_map/ppermute | solution.py:428
  184.9 27.3 %collective-permute-start.8 = (bf16[4,256,256]{2,1,0:T(8,128)(2,1)S(1)}, bf16[4,256,256]{2,1,0:T(8,128)(2,1)S(1)}, u32[]{:S(2)}, u32[]{:S(2)}) collective-permute-start(bf16[4,256,256]{2,1,0:T(8,128)(2,1)S(1)} %get-tuple-element.40), channel_id=1, source_target_pairs={{0,12},{4,0},{8,4},{12,8},{1,13},{5,1},{9,5},{13,9},{2,14},{6,2},{... | collective-permute-start | bytes 1572872 | tf_op jit(solution)/shard_map/ppermute | solution.py:428
  192.7 1.4 copy-start.1
  194.1 1.0 copy-start.11
  195.0 1.0 copy-start.12
  208.8 3.4 %copy-start.29 = (bf16[4,256,256]{2,1,0:T(8,128)(2,1)}, bf16[4,256,256]{2,1,0:T(8,128)(2,1)S(1)}, u32[]{:S(2)}) copy-start(bf16[4,256,256]{2,1,0:T(8,128)(2,1)S(1)} %collective-permute-done.7.low_ref) | copy-start | bytes 1572868
  212.2 0.8 copy-start.30
  216.7 23.1 %collective-permute-start.9 = (bf16[2,4,256,256]{3,2,1,0:T(8,128)(2,1)}, bf16[2,4,256,256]{3,2,1,0:T(8,128)(2,1)S(1)}, u32[]{:S(2)}, u32[]{:S(2)}) collective-permute-start(bf16[2,4,256,256]{3,2,1,0:T(8,128)(2,1)} %get-tuple-element.41), channel_id=1, source_target_pairs={{0,4},{4,8},{8,12},{12,0},{1,5},{5,9},{9,13},{13,1},{2,6},{6,10},{... | collective-permute-start | bytes 3145736 | tf_op jit(solution)/shard_map/ppermute | solution.py:428
  217.1 24.3 %collective-permute-start.10 = (bf16[2,4,256,256]{3,2,1,0:T(8,128)(2,1)}, bf16[2,4,256,256]{3,2,1,0:T(8,128)(2,1)S(1)}, u32[]{:S(2)}, u32[]{:S(2)}) collective-permute-start(bf16[2,4,256,256]{3,2,1,0:T(8,128)(2,1)} %get-tuple-element.42), channel_id=1, source_target_pairs={{0,12},{4,0},{8,4},{12,8},{1,13},{5,1},{9,5},{13,9},{2,14},{6,2},{... | collective-permute-start | bytes 3145736 | tf_op jit(solution)/shard_map/ppermute | solution.py:428
  239.7 1.6 copy-start.27
  241.4 1.0 copy-start.28

commit v3 on v2

--- a/solution.py
+++ b/solution.py
@@ -19,10 +19,15 @@
 VMEM = pl.BlockSpec(memory_space=pltpu.VMEM)
 SMEM = pl.BlockSpec(memory_space=pltpu.SMEM)
 ANY = pl.BlockSpec(memory_space=pl.ANY)
+HBM = pl.BlockSpec(memory_space=pltpu.HBM)
 
 
 def cost(micros):
     return pl.CostEstimate(flops=int(micros * 1.1e9), bytes_accessed=1, transcendentals=0)
+
+
+def in_hbm(value):
+    return pltpu.with_memory_space_constraint(value, pltpu.HBM)
 
 
 def limit(mebibytes):
@@ -171,7 +176,7 @@
     filtered = pl.pallas_call(
         filter_kernel,
         out_shape=jax.ShapeDtypeStruct((2, inputs * frames, NCH), F32),
-        in_specs=[ANY] * 3,
+        in_specs=[HBM] * 3,
         out_specs=VMEM,
         scratch_shapes=[
             pltpu.VMEM(voltages.shape, BF16),
@@ -181,12 +186,12 @@
         ],
         compiler_params=limit(16),
         cost_estimate=cost(5),
-    )(voltages, flags, coeff)
+    )(in_hbm(voltages), in_hbm(flags), in_hbm(coeff))
     blocks = NCH // sum(chunks)
     return pl.pallas_call(
         functools.partial(spectrum_kernel, chunks),
         out_shape=[jax.ShapeDtypeStruct((blocks, size, inputs, 2 * frames), BF16) for size in chunks],
-        in_specs=[VMEM, VMEM] + [ANY] * 4,
+        in_specs=[VMEM, VMEM] + [HBM] * 4,
         out_specs=[VMEM] * len(chunks),
         scratch_shapes=[
             pltpu.VMEM((1, inputs), jnp.int32),
@@ -199,28 +204,37 @@
         ],
         compiler_params=limit(16),
         cost_estimate=cost(6),
-    )(filtered, history, flags, order.reshape(1, NCH), coeff, jnp.asarray(dft_table(NCH)))
-
-
-def halves_kernel(count, low_ref, high_ref, *refs):
-    outs = refs[-2 - count :]
-    half = outs[0].shape[0]
-    outs[0][...] = low_ref[:half]
-    outs[1][...] = high_ref[half:]
-    for n in range(count):
-        outs[2 + n][...] = refs[n][...]
-
-
-def halves(low, high, through=()):
-    shape = jax.ShapeDtypeStruct((low.shape[0] // 2,) + low.shape[1:], BF16)
-    shapes = [shape, shape] + [jax.ShapeDtypeStruct(x.shape, x.dtype) for x in through]
-    return pl.pallas_call(
-        functools.partial(halves_kernel, len(through)),
-        out_shape=shapes,
-        in_specs=[VMEM] * (2 + len(through)),
-        out_specs=[VMEM] * len(shapes),
+    )(
+        filtered,
+        history,
+        *[in_hbm(x) for x in (flags, order.reshape(1, NCH), coeff, jnp.asarray(dft_table(NCH)))],
+    )
+
+
+def halves_kernel(low_ref, high_ref, *refs):
+    low_out, high_out, sems = refs[-3:]
+    half = low_out.shape[0]
+    copies = [
+        pltpu.make_async_copy(low_ref.at[:half], low_out, sems.at[0]),
+        pltpu.make_async_copy(high_ref.at[half:], high_out, sems.at[1]),
+    ]
+    for copy in copies:
+        copy.start()
+    for copy in copies:
+        copy.wait()
+
+
+def halves(low, high, after=()):
+    shape = (low.shape[0] // 2,) + low.shape[1:]
+    return pl.pallas_call(
+        halves_kernel,
+        out_shape=[jax.ShapeDtypeStruct(shape, BF16)] * 2,
+        in_specs=[ANY] * (2 + len(after)),
+        out_specs=[ANY] * 2,
+        scratch_shapes=[pltpu.SemaphoreType.DMA((2,))],
+        compiler_params=limit(62),
         cost_estimate=cost(1),
-    )(low, high, *through)
+    )(in_hbm(low), in_hbm(high), *after)
 
 
 def panel_of(x_ref, index, panel):
@@ -236,13 +250,19 @@
     return jnp.concatenate(parts, axis=1)
 
 
-def correlated(left, right):
-    return lax.dot_general(
+def correlated(by_row, moving, fixed):
+    panel = moving.shape[0]
+    left, right = (fixed, moving) if by_row else (moving, fixed)
+    result = lax.dot_general(
         left, right, (((1,), (1,)), ((), ())), preferred_element_type=F32
     ) * (1.0 / (NCH * 8))
-
-
-def far_kernel(place_ref, own_ref, prev_ref, next_ref, lo_ref, hi_ref, re_ref, im_ref, x_ref, r_ref):
+    if by_row:
+        return result[:panel], result[panel:]
+    return result[:, :panel], result[:, panel:]
+
+
+def far_kernel(by_row, place_ref, own_ref, prev_ref, next_ref, lo_ref, hi_ref, *refs):
+    re_ref, im_ref, x_ref, r_ref = refs[-4:]
     fixed, ring = place_ref[0], place_ref[1]
     blocks, _, inputs, lanes = own_ref.shape
     half = blocks // 2 * inputs
@@ -254,13 +274,13 @@
     panel = re_ref.shape[1]
     mine = panel_of(x_ref, fixed, panel)
     r_ref[0, :panel] = mine
-    r_ref[0, panel:] = turned_panel(mine, lanes, -1.0)
-    result = correlated(panel_of(x_ref, lax.rem(ring + 2, 4), panel), r_ref[0])
-    re_ref[0] = result[:, :panel].astype(BF16)
-    im_ref[0] = result[:, panel:].astype(BF16)
-
-
-def far_products(place, slots):
+    r_ref[0, panel:] = turned_panel(mine, lanes, 1.0 if by_row else -1.0)
+    re, im = correlated(by_row, panel_of(x_ref, lax.rem(ring + 2, 4), panel), r_ref[0])
+    re_ref[0] = re.astype(BF16)
+    im_ref[0] = im.astype(BF16)
+
+
+def far_products(place, slots, by_row, after=()):
     own = slots[0]
     blocks, size, inputs, lanes = own.shape
     total = blocks * inputs
@@ -273,10 +293,10 @@
         return pl.BlockSpec((1, rows, width), lambda k, c: (k, 0, 0))
 
     def shape(rows, width):
-        return jax.ShapeDtypeStruct((size, rows, width), BF16)
-
-    return pl.pallas_call(
-        far_kernel,
+        return pltpu.HBM((size, rows, width), BF16)
+
+    return pl.pallas_call(
+        functools.partial(far_kernel, by_row),
         out_shape=[
             shape(panel, panel),
             shape(panel, panel),
@@ -286,7 +306,7 @@
         grid_spec=pltpu.PrefetchScalarGridSpec(
             num_scalar_prefetch=1,
             grid=(size,),
-            in_specs=[data(blocks)] * 3 + [data(blocks // 2)] * 2,
+            in_specs=[data(blocks)] * 3 + [data(blocks // 2)] * 2 + [ANY] * len(after),
             out_specs=[
                 whole(panel, panel),
                 whole(panel, panel),
@@ -294,29 +314,56 @@
                 whole(2 * panel, 4 * lanes),
             ],
         ),
-        compiler_params=limit(20),
+        compiler_params=limit(62),
         cost_estimate=cost(4),
-    )(place, *slots)
-
-
-def near_kernel(
-    first, place_ref, x_ref, r_ref, w_hbm, own_ref, up_ref, down_ref, beam_ref, w_ref, sem
-):
+    )(place, *[in_hbm(slot) for slot in slots[:3]], *slots[3:], *after)
+
+
+def formed(parts, lanes):
+    beams = parts.shape[0] // 2
+    low = lax.broadcasted_iota(jnp.int32, (beams, lanes), 1) < lanes // 2
+    turned = pltpu.roll(parts[beams:], lanes // 2, axis=1)
+    value = parts[:beams] + jnp.where(low, -turned, turned)
+    return value * value
+
+
+def pooled(power, bins, first):
+    lanes = power.shape[1]
+    lane = lax.broadcasted_iota(jnp.int32, (bins, lanes), 1)
+    place = lax.broadcasted_iota(jnp.int32, (bins, lanes), 0)
+    wanted = first + lax.rem(lane, lanes // 2) // INTEG
+    pool = jnp.where(place == wanted, 1.0 / INTEG, 0.0).astype(F32)
+    return lax.dot_general(
+        pool,
+        power,
+        (((1,), (1,)), ((), ())),
+        precision=lax.Precision.HIGHEST,
+        preferred_element_type=F32,
+    )
+
+
+def near_kernel(by_row, place_ref, x_ref, r_ref, *refs):
     fixed, ring = place_ref[0], place_ref[1]
-    k = pl.program_id(0)
-    size = w_ref.shape[1]
-    copy = pltpu.make_async_copy(w_hbm.at[:, first : first + size], w_ref, sem)
-
-    @pl.when(k == 0)
-    def _():
-        copy.start()
+    if by_row:
+        own_ref, up_ref, down_ref = refs
+    else:
+        w_hbm, own_ref, up_ref, down_ref, beam_ref, w_ref, sem = refs
+        k = pl.program_id(0)
+        copy = pltpu.make_async_copy(w_hbm.at[:, : w_ref.shape[1]], w_ref, sem)
+
+        @pl.when(k == 0)
+        def _():
+            copy.start()
 
     panel = own_ref.shape[2]
     lanes = x_ref.shape[2] // 4
     for step, ref in ((1, up_ref), (3, down_ref), (0, own_ref)):
-        result = correlated(panel_of(x_ref, lax.rem(ring + step, 4), panel), r_ref[0])
-        ref[0, 0] = result[:, :panel].astype(ref.dtype)
-        ref[1, 0] = result[:, panel:].astype(ref.dtype)
+        target = panel_of(x_ref, lax.rem(ring + step, 4), panel)
+        re, im = correlated(by_row, target, r_ref[0])
+        ref[0, 0] = re.astype(ref.dtype)
+        ref[1, 0] = im.astype(ref.dtype)
+    if by_row:
+        return
 
     @pl.when(k == 0)
     def _():
@@ -327,79 +374,99 @@
     parts = lax.dot_general(
         weights, x_ref[0], (((1,), (0,)), ((), ())), preferred_element_type=F32
     )
-    low = lax.broadcasted_iota(jnp.int32, (beams, lanes), 1) < lanes // 2
     bins = lanes // 2 // INTEG
     power = jnp.zeros((4 * bins, beams), F32)
     for s, shift in enumerate((0, 3, 1, 2)):
-        piece = parts[:, s * lanes : (s + 1) * lanes]
-        turned = pltpu.roll(piece[beams:], lanes // 2, axis=1)
-        value = piece[:beams] + jnp.where(low, -turned, turned)
-        lane = lax.broadcasted_iota(jnp.int32, (4 * bins, lanes), 1)
-        place = lax.broadcasted_iota(jnp.int32, (4 * bins, lanes), 0)
-        wanted = lax.rem(fixed + shift, 4) * bins + lax.rem(lane, lanes // 2) // INTEG
-        pool = jnp.where(place == wanted, 1.0 / INTEG, 0.0).astype(F32)
-        power = power + lax.dot_general(
-            pool,
-            value * value,
-            (((1,), (1,)), ((), ())),
-            precision=lax.Precision.HIGHEST,
-            preferred_element_type=F32,
-        )
+        squared = formed(parts[:, s * lanes : (s + 1) * lanes], lanes)
+        power = power + pooled(squared, 4 * bins, lax.rem(fixed + shift, 4) * bins)
     beam_ref[0] = power
 
 
-def near_products(place, x, r, weights, first):
+def near_products(place, x, r, by_row, weights=None):
     size, total, width = x.shape
     panel = total // 4
-    beams = weights.shape[2]
-    bins = width // 2 // INTEG
     block = pl.BlockSpec((2, 1, panel, panel), lambda k, c: (0, k, 0, 0))
-    return pl.pallas_call(
-        functools.partial(near_kernel, first),
-        out_shape=[
-            jax.ShapeDtypeStruct((2, size, panel, panel), F32),
-            jax.ShapeDtypeStruct((2, size, panel, panel), BF16),
-            jax.ShapeDtypeStruct((2, size, panel, panel), BF16),
-            jax.ShapeDtypeStruct((size, bins, beams), F32),
-        ],
+    shape = (2, size, panel, panel)
+    shapes = [pltpu.HBM(shape, F32), pltpu.HBM(shape, BF16), pltpu.HBM(shape, BF16)]
+    specs = [block] * 3
+    args = [x, r]
+    scratch = []
+    if not by_row:
+        beams = weights.shape[2]
+        bins = width // 2 // INTEG
+        shapes.append(jax.ShapeDtypeStruct((size, bins, beams), F32))
+        specs.append(pl.BlockSpec((1, bins, beams), lambda k, c: (k, 0, 0)))
+        args.append(weights)
+        scratch = [pltpu.VMEM((2, size) + weights.shape[2:], BF16), pltpu.SemaphoreType.DMA]
+    args = [in_hbm(arg) for arg in args]
+    return pl.pallas_call(
+        functools.partial(near_kernel, by_row),
+        out_shape=shapes,
         grid_spec=pltpu.PrefetchScalarGridSpec(
             num_scalar_prefetch=1,
             grid=(size,),
             in_specs=[
                 pl.BlockSpec((1, total, width), lambda k, c: (k, 0, 0)),
                 pl.BlockSpec((1, 2 * panel, width), lambda k, c: (k, 0, 0)),
-                ANY,
-            ],
-            out_specs=[block] * 3 + [pl.BlockSpec((1, bins, beams), lambda k, c: (k, 0, 0))],
-            scratch_shapes=[
-                pltpu.VMEM((2, size) + weights.shape[2:], BF16),
-                pltpu.SemaphoreType.DMA,
-            ],
+            ]
+            + [HBM] * (len(args) - 2),
+            out_specs=specs,
+            scratch_shapes=scratch,
         ),
-        compiler_params=limit(20),
+        compiler_params=limit(62),
         cost_estimate=cost(7),
-    )(place, x, r, weights)
+    )(place, *args)
+
+
+def beam_kernel(own_ref, w_ref, out_ref):
+    blocks, _, inputs, lanes = own_ref.shape
+    owners, _, _, beams, total = w_ref.shape
+    x = own_ref[:, 0].reshape(blocks * inputs, lanes)
+    weights = w_ref[:, :, 0].reshape(owners * 2 * beams, total)
+    parts = lax.dot_general(weights, x, (((1,), (0,)), ((), ())), preferred_element_type=F32)
+    for owner in range(owners):
+        squared = formed(parts[owner * 2 * beams : (owner + 1) * 2 * beams], lanes)
+        out_ref[owner, 0] = pooled(squared, lanes // 2 // INTEG, 0)
+
+
+def own_beams(own, weights):
+    blocks, size, inputs, lanes = own.shape
+    owners, _, _, beams, total = weights.shape
+    bins = lanes // 2 // INTEG
+    return pl.pallas_call(
+        beam_kernel,
+        out_shape=jax.ShapeDtypeStruct((owners, size, bins, beams), F32),
+        grid=(size,),
+        in_specs=[
+            pl.BlockSpec((blocks, 1, inputs, lanes), lambda k: (0, k, 0, 0)),
+            pl.BlockSpec((owners, 2, 1, beams, total), lambda k: (0, 0, k, 0, 0)),
+        ],
+        out_specs=pl.BlockSpec((owners, 1, bins, beams), lambda k: (0, k, 0, 0)),
+        compiler_params=limit(62),
+        cost_estimate=cost(4),
+    )(in_hbm(own), in_hbm(weights))
 
 
 def add_kernel(up_ref, down_ref, low_ref, high_ref, *refs):
     up_out, down_out = refs[-2:]
-    up_out[0, 0] = (up_ref[0, 0].astype(F32) + low_ref[0].astype(F32)).astype(BF16)
-    down_out[0, 0] = (down_ref[0, 0].astype(F32) + high_ref[0].astype(F32)).astype(BF16)
+    up_out[0] = (up_ref[0].astype(F32) + low_ref[...].astype(F32)).astype(BF16)
+    down_out[0] = (down_ref[0].astype(F32) + high_ref[...].astype(F32)).astype(BF16)
 
 
 def added(up, down, low, high, after=()):
     _, size, panel, _ = up.shape
-    real = pl.BlockSpec((1, 1, panel, panel), lambda k: (0, k, 0, 0))
-    imag = pl.BlockSpec((1, 1, panel, panel), lambda k: (1, k, 0, 0))
-    one = pl.BlockSpec((1, panel, panel), lambda k: (k, 0, 0))
-    shape = jax.ShapeDtypeStruct(up.shape, BF16)
+    real = pl.BlockSpec((1, size, panel, panel), lambda n: (0, 0, 0, 0))
+    imag = pl.BlockSpec((1, size, panel, panel), lambda n: (1, 0, 0, 0))
+    one = pl.BlockSpec((size, panel, panel), lambda n: (0, 0, 0))
+    shape = pltpu.HBM(up.shape, BF16)
     return pl.pallas_call(
         add_kernel,
         out_shape=[shape, shape],
-        grid=(size,),
+        grid=(1,),
         in_specs=[real, imag, one, one] + [ANY] * len(after),
         out_specs=[real, imag],
         input_output_aliases={0: 0, 1: 1},
+        compiler_params=limit(62),
         cost_estimate=cost(1),
     )(up, down, low, high, *after)
 
@@ -410,17 +477,19 @@
 
 def finished(own, from_prev, from_next, first, channels, out):
     _, size, panel, _ = own.shape
-    block = pl.BlockSpec((1, 1, panel, panel), lambda p, k: (p, k, 0, 0))
+    step = math.gcd(first, size) if first else size
+    block = pl.BlockSpec((1, step, panel, panel), lambda p, k: (p, k, 0, 0))
     extra = [] if out is None else [out]
     return pl.pallas_call(
         final_kernel,
         out_shape=jax.ShapeDtypeStruct((2, channels, panel, panel), F32),
-        grid=(2, size),
+        grid=(2, size // step),
         in_specs=[block] * 3 + [ANY] * len(extra),
-        out_specs=pl.BlockSpec((1, 1, panel, panel), lambda p, k: (p, first + k, 0, 0)),
+        out_specs=pl.BlockSpec((1, step, panel, panel), lambda p, k: (p, first // step + k, 0, 0)),
         input_output_aliases={3: 0} if extra else {},
+        compiler_params=limit(62),
         cost_estimate=cost(2),
-    )(own, from_prev, from_next, *extra)
+    )(in_hbm(own), from_prev, from_next, *extra)
 
 
 def along(value, axis, step):
@@ -433,36 +502,41 @@
 
 
 def on_device(voltages, input_flags, channel_order, beam_weights):
+    size_a, size_b = CHUNKS
+    channels = size_a + size_b
     history = passed_along(voltages[:, :, voltages.shape[2] - (TAPS - 1) * NCH :], ("row", "col"), 1)
-    place = jnp.stack([lax.axis_index("col"), lax.axis_index("row")]).astype(jnp.int32)
-    pieces = spectra(voltages, history, input_flags, channel_order, CHUNKS)
-    channels = sum(CHUNKS)
-
-    def turn(piece):
-        return lax.all_to_all(piece, "chan", split_axis=0, concat_axis=0, tiled=True)
-
-    own0 = turn(pieces[0])
-    near0 = both_ways(own0, own0, "col")
-    own1 = turn(pieces[1])
-    low0, high0, own1 = halves(*near0, [own1])
-    far0 = both_ways(low0, high0, "col")
-    near1 = both_ways(own1, own1, "col")
-
-    re0, im0, x0, r0 = far_products(place, (own0, *near0, *far0))
-    got0 = both_ways(re0, im0, "row")
-    mine0, up0, down0, beam0 = near_products(place, x0, r0, beam_weights, 0)
-    low1, high1 = halves(*near1)
-    far1 = both_ways(low1, high1, "col")
-    sent0 = both_ways(*added(up0, down0, *got0), "row")
-
-    re1, im1, x1, r1 = far_products(place, (own1, *near1, *far1))
-    got1 = both_ways(re1, im1, "row")
-    mine1, up1, down1, beam1 = near_products(place, x1, r1, beam_weights, CHUNKS[0])
-    sent1 = both_ways(*added(up1, down1, *got1), "row")
-
-    out = finished(mine0, *sent0, 0, channels, None)
-    visibility = finished(mine1, *sent1, CHUNKS[0], channels, out)
-    power = jnp.concatenate([beam0, beam1], axis=0)
+    row = lax.axis_index("row").astype(jnp.int32)
+    col = lax.axis_index("col").astype(jnp.int32)
+    place_a = jnp.stack([col, row])
+    place_b = jnp.stack([row, col])
+    weights_b = lax.all_gather(beam_weights[:, size_a:], "col", axis=0)
+    piece_a, piece_b = spectra(voltages, history, input_flags, channel_order, CHUNKS)
+
+    def turn(piece, axis):
+        return lax.all_to_all(piece, axis, split_axis=0, concat_axis=0, tiled=True)
+
+    own_a = turn(piece_a, "chan")
+    near_a = both_ways(own_a, own_a, "col")
+    own_b = turn(piece_b, "chan")
+    near_b = both_ways(own_b, own_b, "row")
+    far_b = both_ways(*halves(*near_b, [own_a]), "row")
+    far_a = both_ways(*halves(*near_a), "col")
+    beam_b = own_beams(own_b, weights_b)
+
+    re_b, im_b, x_b, r_b = far_products(place_b, (own_b, *near_b, *far_b), True, [beam_b])
+    got_b = both_ways(re_b, im_b, "col")
+    mine_b, up_b, down_b = near_products(place_b, x_b, r_b, True)
+    sent_b = both_ways(*added(up_b, down_b, *got_b), "col")
+
+    re_a, im_a, x_a, r_a = far_products(place_a, (own_a, *near_a, *far_a), False, [mine_b])
+    got_a = both_ways(re_a, im_a, "row")
+    mine_a, up_a, down_a, power_a = near_products(place_a, x_a, r_a, False, beam_weights)
+    sent_a = both_ways(*added(up_a, down_a, *got_a), "row")
+
+    power_b = jnp.transpose(turn(beam_b, "col"), (1, 0, 2, 3)).reshape(size_b, -1, beam_b.shape[3])
+    out = finished(mine_a, *sent_a, 0, channels, None)
+    visibility = finished(mine_b, *sent_b, size_a, channels, out)
+    power = jnp.concatenate([power_a, power_b], axis=0)
     return (visibility, jnp.transpose(power, (0, 2, 1)))
 
 

time: 250 us -> 271 us (1.084)
  Pallas kernels: 61.6 us -> 130 us
  waiting for transfers between devices: 92.1 us -> 27.9 us
  local copies, waits for them, and re-layouts: 28.7 us -> 6.79 us
  blocking collectives: 35.6 us -> 56.8 us
  between operations: 0.81 us -> 14.2 us
    pallas_call x8 -> x9, Pallas kernels: 37.2 us -> 109 us  [the longest x2 65.8 us: halves(): pl.pallas_call(halves_kernel, out_shape=[jax.ShapeDtypeStruct(shape, BF16...]
    ppermute x16, waiting for transfers between devices: 67.6 us -> 3.34 us  [along(): lax.ppermute(value, axis, [(i, (i + step) % count) for i in range(count)])]
    unnamed x62 -> x20, local copies, waits for them, and re-layouts: 27.8 us -> 2.99 us
    all_to_all x1 -> x2, blocking collectives: 35.6 us -> 56.8 us  [turn(): return lax.all_to_all(piece, axis, split_axis=0, concat_axis=0, tiled=True)]
    pallas_call x2, Pallas kernels: 12.2 us -> 6.53 us  [finished(): pl.pallas_call(final_kernel, out_shape=jax.ShapeDtypeStruct((2, channels,...]
  transfers between devices with their start and end apart: 18 -> 19, of which waited for: 7 -> 3; matrix products, arithmetic and copies ran while one was open for 0% -> 2% of each run, Pallas kernels for 18% -> 47%
where the time goes in v3:
time: 271 us; the launch traced here: 268 us
  Pallas kernels  130 us (48%)
  blocking collectives  56.8 us (21%)
  starting transfers between devices  29 us (11%)
  waiting for transfers between devices  27.9 us (10%)
  between operations  14.2 us (5%)
  local copies, waits for them, and re-layouts  6.79 us (3%)
    pallas_call x2, Pallas kernels, halves(): pl.pallas_call(halves_kernel, out_shape=[jax.ShapeDtypeStruct(shape, BF16...  65.8 us
    all_to_all x2, blocking collectives, turn(): return lax.all_to_all(piece, axis, split_axis=0, concat_axis=0, tiled=True)  56.8 us
    all_to_all x1, waiting for transfers between devices, turn(): return lax.all_to_all(piece, axis, split_axis=0, concat_axis=0, tiled=True)  24.5 us
    ppermute x16, starting transfers between devices, along(): lax.ppermute(value, axis, [(i, (i + step) % count) for i in range(count)])  21.3 us
    pallas_call x2, Pallas kernels, near_products(): pl.pallas_call(functools.partial(near_kernel, by_row), out_shape=shapes,...  17.9 us
    pallas_call x2, Pallas kernels, far_products(): pl.pallas_call(functools.partial(far_kernel, by_row), out_shape=[shape(pa...  14 us
    pallas_call x1, Pallas kernels, spectra(): pl.pallas_call(functools.partial(spectrum_kernel, chunks), out_shape=[jax...  7.98 us
    pallas_call x1, Pallas kernels, own_beams(): pl.pallas_call(beam_kernel, out_shape=jax.ShapeDtypeStruct((owners, size,...  6.61 us
  transfers between devices with their start and end apart: 19, of which 3 were waited for; matrix products, arithmetic and copies ran while one was open for 2% of the time, Pallas kernels for 47%

profile of v3, /device:TPU:6, one launch (start us, length us, event | category | flops | bytes accessed | tf_op | source)
XLA Modules:
  0.0 267.9 jit_solution(1199704010133184999)
XLA Ops:
  7.2 0.0 all-gather.3.cloned.1.call-start
  7.2 2.4 slice.7
  9.6 0.0 all-gather.3.cloned.1.call-update
  9.6 0.9 slice.6
  10.5 3.5 %collective-permute-start = (bf16[2,64,384]{2,1,0:T(8,128)(2,1)S(1)}, bf16[2,64,384]{2,1,0:T(8,128)(2,1)S(1)}, u32[]{:S(2)}, u32[]{:S(2)}) collective-permute-start(bf16[2,64,384]{2,1,0:T(8,128)(2,1)S(1)} %slice.6), channel_id=1, source_target_pairs={{0,1},{1,2},{2,3},{3,4},{4,5},{5,6},{6,7},{7,8},{8,9},{9,10},{10,1... | collective-permute-start | bytes 294920 | tf_op jit(solution)/shard_map/ppermute | solution.py:56
  14.0 6.4 %shard_map.77.filt_ref = f32[2,4096,128]{2,1,0:T(8,128)S(1)} custom-call(bf16[2,64,8192]{2,1,0:T(8,128)(2,1)} %v_hbm.1, s32[1,64]{1,0:T(1,128)} %bitcast.13, f32[4,128]{1,0:T(4,128)} %constant.11.clone.coeff_hbm), custom_call_target="tpu_custom_call" | custom-call | flops 5500000256 | bytes 1 | tf_op jit(solution)/shard_map/pallas_call | solution.py:176
  20.5 0.0 collective-permute-done.halo_ref
  20.5 8.0 %shard_map.78 = (bf16[16,4,64,128]{3,2,1,0:T(8,128)(2,1)}, bf16[16,4,64,128]{3,2,1,0:T(8,128)(2,1)S(1)}) custom-call(f32[2,4096,128]{2,1,0:T(8,128)S(1)} %shard_map.77.filt_ref, bf16[2,64,384]{2,1,0:T(8,128)(2,1)S(1)} %collective-permute-done.halo_ref, s32[1,64]{1,0:T(1,128)} %bitcast.14, s32[1,128]{1,0:T(1,128)} %bitcast.15, ...), custom_call_target="tpu_custom_call" | custom-call | flops 6600000000 | bytes 1 | tf_op jit(solution)/shard_map/pallas_call | solution.py:191
  28.5 35.6 %all_to_all.15.own_ref = bf16[16,4,64,128]{3,2,1,0:T(8,128)(2,1)S(1)} all-to-all(bf16[16,4,64,128]{3,2,1,0:T(8,128)(2,1)S(1)} %get-tuple-element.27), channel_id=1, replica_groups=mesh['chan'=16,'row'=4,'col'=4] {'chan'}, dimensions={0} | all-to-all | bytes 2097152 | tf_op jit(solution)/shard_map/all_to_all | solution.py:516
  64.1 4.2 %all-to-all-start.1 = ((bf16[16,4,64,128]{3,2,1,0:T(8,128)(2,1)}), bf16[16,4,64,128]{3,2,1,0:T(8,128)(2,1)S(1)}, u32[]{:S(2)}, u32[]{:S(2)}) async-start(bf16[16,4,64,128]{3,2,1,0:T(8,128)(2,1)} %get-tuple-element.28), calls=%async_computation.1 | async-start | bytes 2097152 | tf_op jit(solution)/shard_map/all_to_all | solution.py:516
  68.3 0.6 collective-permute-start.1
  68.9 1.5 collective-permute-start.2
  70.4 24.5 %all-to-all-done.1.refs_0_.own_ref = bf16[16,4,64,128]{3,2,1,0:T(8,128)(2,1)S(1)} async-done(((bf16[16,4,64,128]{3,2,1,0:T(8,128)(2,1)}), bf16[16,4,64,128]{3,2,1,0:T(8,128)(2,1)S(1)}, u32[]{:S(2)}, u32[]{:S(2)}) %all-to-all-start.1) | async-done | bytes 1048608 | tf_op jit(solution)/shard_map/all_to_all | solution.py:516
  95.0 1.6 collective-permute-start.9
  96.5 1.7 collective-permute-start.10
  98.2 0.7 pad_add_fusion.place_ref
  98.9 0.0 collective-permute-done.1.low_ref.prev_ref
  98.9 0.0 collective-permute-done.2.high_ref.next_ref
  98.9 32.9 %shard_map.79 = (bf16[8,4,64,128]{3,2,1,0:T(8,128)(2,1)}, bf16[8,4,64,128]{3,2,1,0:T(8,128)(2,1)}) custom-call(bf16[16,4,64,128]{3,2,1,0:T(8,128)(2,1)} %collective-permute-done.1.low_ref.prev_ref, bf16[16,4,64,128]{3,2,1,0:T(8,128)(2,1)} %collective-permute-done.2.high_ref.next_ref, bf16[16,4,64,128]{3,2,1,0:T(8,128)(2,1)} %copy-done.1), custom_call_target="tpu_custom_call" | custom-call | flops 1100000000 | bytes 1 | tf_op jit(solution)/shard_map/pallas_call | solution.py:229
  131.8 0.6 collective-permute-start.3
  132.3 1.5 collective-permute-start.4
  133.9 0.6 pad_add_fusion.1.place_ref
  134.5 0.0 collective-permute-done.9.low_ref.prev_ref
  134.5 0.0 collective-permute-done.10.high_ref.next_ref
  134.5 32.9 %shard_map.84 = (bf16[8,4,64,128]{3,2,1,0:T(8,128)(2,1)}, bf16[8,4,64,128]{3,2,1,0:T(8,128)(2,1)}) custom-call(bf16[16,4,64,128]{3,2,1,0:T(8,128)(2,1)} %collective-permute-done.9.low_ref.prev_ref, bf16[16,4,64,128]{3,2,1,0:T(8,128)(2,1)} %collective-permute-done.10.high_ref.next_ref), custom_call_target="tpu_custom_call" | custom-call | flops 1100000000 | bytes 1 | tf_op jit(solution)/shard_map/pallas_call | solution.py:229
  167.4 0.4 collective-permute-start.11
  167.8 2.9 %collective-permute-start.12 = (bf16[8,4,64,128]{3,2,1,0:T(8,128)(2,1)}, bf16[8,4,64,128]{3,2,1,0:T(8,128)(2,1)}, u32[]{:S(2)}, u32[]{:S(2)}) collective-permute-start(bf16[8,4,64,128]{3,2,1,0:T(8,128)(2,1)} %get-tuple-element.41), channel_id=1, source_target_pairs={{0,3},{1,0},{2,1},{3,2},{4,7},{5,4},{6,5},{7,6},{8,11},{9,8},{10,9... | collective-permute-start | bytes 1572872 | tf_op jit(solution)/shard_map/ppermute | solution.py:497
  170.7 6.6 %shard_map.80.refs_0_ = f32[4,4,8,64]{3,2,1,0:T(8,128)} custom-call(bf16[16,4,64,128]{3,2,1,0:T(8,128)(2,1)} %copy-done.2, bf16[4,2,4,64,1024]{4,3,2,1,0:T(8,128)(2,1)} %bitcast.12), custom_call_target="tpu_custom_call" | custom-call | flops 4400000000 | bytes 1 | tf_op jit(solution)/shard_map/pallas_call | solution.py:436
  177.3 0.0 collective-permute-done.3.lo_ref
  177.3 0.0 collective-permute-done.4.hi_ref
  177.3 6.9 %shard_map.81 = (bf16[4,256,256]{2,1,0:T(8,128)(2,1)}, bf16[4,256,256]{2,1,0:T(8,128)(2,1)}, bf16[4,1024,512]{2,1,0:T(8,128)(2,1)}, bf16[4,512,512]{2,1,0:T(8,128)(2,1)}) custom-call(s32[2]{0:T(128)} %pad_add_fusion.place_ref, bf16[16,4,64,128]{3,2,1,0:T(8,128)(2,1)} %copy-done.2, bf16[16,4,64,128]{3,2,1,0:T(8,128)(2,1)} %collective-permute-done.1.low_ref.prev_ref, ...), custom_call_target="tpu_custom_call" | custom-call | flops 4400000000 | bytes 1 | tf_op jit(solution)/shard_map/pallas_call | solution.py:298
  184.3 0.0 collective-permute-start.5
  184.3 3.2 %collective-permute-start.6 = (bf16[4,256,256]{2,1,0:T(8,128)(2,1)}, bf16[4,256,256]{2,1,0:T(8,128)(2,1)S(1)}, u32[]{:S(2)}, u32[]{:S(2)}) collective-permute-start(bf16[4,256,256]{2,1,0:T(8,128)(2,1)} %get-tuple-element.37), channel_id=1, source_target_pairs={{0,3},{1,0},{2,1},{3,2},{4,7},{5,4},{6,5},{7,6},{8,11},{9,8},{10,9... | collective-permute-start | bytes 1572872 | tf_op jit(solution)/shard_map/ppermute | solution.py:497
  187.5 7.0 %shard_map.82 = (f32[2,4,256,256]{3,2,1,0:T(8,128)}, bf16[2,4,256,256]{3,2,1,0:T(8,128)(2,1)}, bf16[2,4,256,256]{3,2,1,0:T(8,128)(2,1)}) custom-call(s32[2]{0:T(128)} %pad_add_fusion.place_ref, bf16[4,1024,512]{2,1,0:T(8,128)(2,1)} %get-tuple-element.31.x_ref, bf16[4,512,512]{2,1,0:T(8,128)(2,1)} %get-tuple-element.32.r_ref), custom_call_target="tpu_custom_call" | custom-call | flops 7699999744 | bytes 1 | tf_op jit(solution)/shard_map/pallas_call | solution.py:402
  194.6 0.8 copy-done.7
  195.3 7.0 %shard_map.85 = (bf16[4,256,256]{2,1,0:T(8,128)(2,1)}, bf16[4,256,256]{2,1,0:T(8,128)(2,1)}, bf16[4,1024,512]{2,1,0:T(8,128)(2,1)}, bf16[4,512,512]{2,1,0:T(8,128)(2,1)}) custom-call(s32[2]{0:T(128)} %pad_add_fusion.1.place_ref, bf16[16,4,64,128]{3,2,1,0:T(8,128)(2,1)} %copy-done.1, bf16[16,4,64,128]{3,2,1,0:T(8,128)(2,1)} %collective-permute-done.9.low_ref.prev_ref, ...), custom_call_target="tpu_custom_call" | custom-call | flops 4400000000 | bytes 1 | tf_op jit(solution)/shard_map/pallas_call | solution.py:298
  202.4 1.7 collective-permute-start.13
  204.1 0.3 collective-permute-start.14
  204.4 10.9 %shard_map.86 = (f32[2,4,256,256]{3,2,1,0:T(8,128)}, bf16[2,4,256,256]{3,2,1,0:T(8,128)(2,1)}, bf16[2,4,256,256]{3,2,1,0:T(8,128)(2,1)}, f32[4,32,64]{2,1,0:T(8,128)}) custom-call(s32[2]{0:T(128)} %pad_add_fusion.1.place_ref, bf16[4,1024,512]{2,1,0:T(8,128)(2,1)} %get-tuple-element.42.x_ref, bf16[4,512,512]{2,1,0:T(8,128)(2,1)} %get-tuple-element.43.r_ref, ...), custom_call_target="tpu_custom_call" | custom-call | flops 7699999744 | bytes 1 | tf_op jit(solution)/shard_map/pallas_call | solution.py:402
  215.3 0.0 copy-start.3
  215.3 0.6 collective-permute-done.13.low_ref
  215.9 2.7 %collective-permute-done.14.high_ref = bf16[4,256,256]{2,1,0:T(8,128)(2,1)} collective-permute-done((bf16[4,256,256]{2,1,0:T(8,128)(2,1)}, bf16[4,256,256]{2,1,0:T(8,128)(2,1)}, u32[]{:S(2)}, u32[]{:S(2)}) %collective-permute-start.14) | collective-permute-done | bytes 524320 | tf_op jit(solution)/shard_map/ppermute | solution.py:497
  218.6 2.6 shard_map.87
  221.3 1.0 collective-permute-start.15
  222.2 1.1 collective-permute-start.16
  223.3 0.0 collective-permute-done.5.low_ref
  223.3 0.0 collective-permute-done.6.high_ref
  223.3 0.8 copy-done.5
  224.1 0.2 copy-done.6
  224.3 2.6 shard_map.83
  226.9 0.0 collective-permute-start.7
  226.9 3.2 %collective-permute-start.8 = (bf16[2,4,256,256]{3,2,1,0:T(8,128)(2,1)}, bf16[2,4,256,256]{3,2,1,0:T(8,128)(2,1)}, u32[]{:S(2)}, u32[]{:S(2)}) collective-permute-start(bf16[2,4,256,256]{3,2,1,0:T(8,128)(2,1)} %get-tuple-element.39), channel_id=1, source_target_pairs={{0,3},{1,0},{2,1},{3,2},{4,7},{5,4},{6,5},{7,6},{8,11},{9,8},{10,9... | collective-permute-start | bytes 3145736 | tf_op jit(solution)/shard_map/ppermute | solution.py:497
  230.2 0.1 reshape.17
  230.3 21.2 %all_to_all.16 = f32[4,1,2048]{2,1,0:T(1,128)S(1)} all-to-all(f32[4,1,2048]{2,1,0:T(1,128)S(1)} %reshape.17), channel_id=1, replica_groups=mesh['chan'=16,'row'=4,'col'=4] {'col'}, dimensions={0} | all-to-all | bytes 65536 | tf_op jit(solution)/shard_map/all_to_all | solution.py:516
  251.5 0.5 broadcast
  252.0 0.7 reduce
  252.7 0.1 reshape.18
  252.8 0.7 maximum_bitcast_fusion
  253.5 0.0 collective-permute-done.16.next_ref
  253.5 3.3 %shard_map.88.refs_0_ = f32[2,8,256,256]{3,2,1,0:T(8,128)} custom-call(f32[2,4,256,256]{3,2,1,0:T(8,128)} %get-tuple-element.44.own_ref, bf16[2,4,256,256]{3,2,1,0:T(8,128)(2,1)} %collective-permute-done.15.prev_ref, bf16[2,4,256,256]{3,2,1,0:T(8,128)(2,1)} %collective-permute-done.16.next_ref), custom_call_target="tpu_custom_call" | custom-call | flops 2200000000 | bytes 1 | tf_op jit(solution)/shard_map/pallas_call | solution.py:483
  256.8 0.0 collective-permute-done.7.prev_ref
  256.8 0.0 collective-permute-done.8.next_ref
  256.8 1.0 copy-done
  257.8 3.3 %shard_map.89 = f32[2,8,256,256]{3,2,1,0:T(8,128)} custom-call(f32[2,4,256,256]{3,2,1,0:T(8,128)} %get-tuple-element.33.refs_0_.own_ref, bf16[2,4,256,256]{3,2,1,0:T(8,128)(2,1)} %copy-done, bf16[2,4,256,256]{3,2,1,0:T(8,128)(2,1)} %collective-permute-done.8.next_ref, f32[2,8,256,256]{3,2,1,0:T(8,128)} %shard_map.88.refs_0_), custom_call_target="tpu_custom_call", output_to_operand_aliasing={{}: (3, {})} | custom-call | flops 2200000000 | bytes 1 | tf_op jit(solution)/shard_map/pallas_call | solution.py:483
  (18 shorter events, 0.0 us)
Async XLA Ops:
  7.2 163.6 %all-gather.3.cloned.1.call-start = ((), (), s32[]{:S(2)}) async-start(), calls=%async_computation.3 | async-start | bytes 5242880 | tf_op jit(solution)/shard_map/all_gather | solution.py:512
  10.5 9.9 %collective-permute-start = (bf16[2,64,384]{2,1,0:T(8,128)(2,1)S(1)}, bf16[2,64,384]{2,1,0:T(8,128)(2,1)S(1)}, u32[]{:S(2)}, u32[]{:S(2)}) collective-permute-start(bf16[2,64,384]{2,1,0:T(8,128)(2,1)S(1)} %slice.6), channel_id=1, source_target_pairs={{0,1},{1,2},{2,3},{3,4},{4,5},{5,6},{6,7},{7,8},{8,9},{9,10},{10,1... | collective-permute-start | bytes 294920 | tf_op jit(solution)/shard_map/ppermute | solution.py:56
  64.1 30.8 %copy-start.2 = (bf16[16,4,64,128]{3,2,1,0:T(8,128)(2,1)}, bf16[16,4,64,128]{3,2,1,0:T(8,128)(2,1)S(1)}, u32[]{:S(2)}) copy-start(bf16[16,4,64,128]{3,2,1,0:T(8,128)(2,1)S(1)} %all_to_all.15.own_ref) | copy-start | bytes 3145732
  64.1 30.8 %all-to-all-start.1 = ((bf16[16,4,64,128]{3,2,1,0:T(8,128)(2,1)}), bf16[16,4,64,128]{3,2,1,0:T(8,128)(2,1)S(1)}, u32[]{:S(2)}, u32[]{:S(2)}) async-start(bf16[16,4,64,128]{3,2,1,0:T(8,128)(2,1)} %get-tuple-element.28), calls=%async_computation.1 | async-start | bytes 2097152 | tf_op jit(solution)/shard_map/all_to_all | solution.py:516
  68.3 30.6 %collective-permute-start.1 = (bf16[16,4,64,128]{3,2,1,0:T(8,128)(2,1)S(1)}, bf16[16,4,64,128]{3,2,1,0:T(8,128)(2,1)}, u32[]{:S(2)}, u32[]{:S(2)}) collective-permute-start(bf16[16,4,64,128]{3,2,1,0:T(8,128)(2,1)S(1)} %all_to_all.15.own_ref), channel_id=1, source_target_pairs={{0,4},{4,8},{8,12},{12,0},{1,5},{5,9},{9,13},{13,1},{2,6},{6,10},{... | collective-permute-start | bytes 3145736 | tf_op jit(solution)/shard_map/ppermute | solution.py:497
  68.9 30.0 %collective-permute-start.2 = (bf16[16,4,64,128]{3,2,1,0:T(8,128)(2,1)S(1)}, bf16[16,4,64,128]{3,2,1,0:T(8,128)(2,1)}, u32[]{:S(2)}, u32[]{:S(2)}) collective-permute-start(bf16[16,4,64,128]{3,2,1,0:T(8,128)(2,1)S(1)} %all_to_all.15.own_ref), channel_id=1, source_target_pairs={{0,12},{4,0},{8,4},{12,8},{1,13},{5,1},{9,5},{13,9},{2,14},{6,2},{... | collective-permute-start | bytes 3145736 | tf_op jit(solution)/shard_map/ppermute | solution.py:497
  94.9 3.9 %copy-start.1 = (bf16[16,4,64,128]{3,2,1,0:T(8,128)(2,1)}, bf16[16,4,64,128]{3,2,1,0:T(8,128)(2,1)S(1)}, u32[]{:S(2)}) copy-start(bf16[16,4,64,128]{3,2,1,0:T(8,128)(2,1)S(1)} %all-to-all-done.1.refs_0_.own_ref) | copy-start | bytes 3145732
  95.0 39.6 %collective-permute-start.9 = (bf16[16,4,64,128]{3,2,1,0:T(8,128)(2,1)S(1)}, bf16[16,4,64,128]{3,2,1,0:T(8,128)(2,1)}, u32[]{:S(2)}, u32[]{:S(2)}) collective-permute-start(bf16[16,4,64,128]{3,2,1,0:T(8,128)(2,1)S(1)} %all-to-all-done.1.refs_0_.own_ref), channel_id=1, source_target_pairs={{0,1},{1,2},{2,3},{3,0},{4,5},{5,6},{6,7},{7,4},{8,9},{9,10},{10,1... | collective-permute-start | bytes 3145736 | tf_op jit(solution)/shard_map/ppermute | solution.py:497
  96.5 38.0 %collective-permute-start.10 = (bf16[16,4,64,128]{3,2,1,0:T(8,128)(2,1)S(1)}, bf16[16,4,64,128]{3,2,1,0:T(8,128)(2,1)}, u32[]{:S(2)}, u32[]{:S(2)}) collective-permute-start(bf16[16,4,64,128]{3,2,1,0:T(8,128)(2,1)S(1)} %all-to-all-done.1.refs_0_.own_ref), channel_id=1, source_target_pairs={{0,3},{1,0},{2,1},{3,2},{4,7},{5,4},{6,5},{7,6},{8,11},{9,8},{10,9... | collective-permute-start | bytes 3145736 | tf_op jit(solution)/shard_map/ppermute | solution.py:497
  131.8 45.6 %collective-permute-start.3 = (bf16[8,4,64,128]{3,2,1,0:T(8,128)(2,1)}, bf16[8,4,64,128]{3,2,1,0:T(8,128)(2,1)}, u32[]{:S(2)}, u32[]{:S(2)}) collective-permute-start(bf16[8,4,64,128]{3,2,1,0:T(8,128)(2,1)} %get-tuple-element.29), channel_id=1, source_target_pairs={{0,4},{4,8},{8,12},{12,0},{1,5},{5,9},{9,13},{13,1},{2,6},{6,10},{... | collective-permute-start | bytes 1572872 | tf_op jit(solution)/shard_map/ppermute | solution.py:497
  132.3 45.0 %collective-permute-start.4 = (bf16[8,4,64,128]{3,2,1,0:T(8,128)(2,1)}, bf16[8,4,64,128]{3,2,1,0:T(8,128)(2,1)}, u32[]{:S(2)}, u32[]{:S(2)}) collective-permute-start(bf16[8,4,64,128]{3,2,1,0:T(8,128)(2,1)} %get-tuple-element.30), channel_id=1, source_target_pairs={{0,12},{4,0},{8,4},{12,8},{1,13},{5,1},{9,5},{13,9},{2,14},{6,2},{... | collective-permute-start | bytes 1572872 | tf_op jit(solution)/shard_map/ppermute | solution.py:497
  167.4 27.1 %collective-permute-start.11 = (bf16[8,4,64,128]{3,2,1,0:T(8,128)(2,1)}, bf16[8,4,64,128]{3,2,1,0:T(8,128)(2,1)S(1)}, u32[]{:S(2)}, u32[]{:S(2)}) collective-permute-start(bf16[8,4,64,128]{3,2,1,0:T(8,128)(2,1)} %get-tuple-element.40), channel_id=1, source_target_pairs={{0,1},{1,2},{2,3},{3,0},{4,5},{5,6},{6,7},{7,4},{8,9},{9,10},{10,1... | collective-permute-start | bytes 1572872 | tf_op jit(solution)/shard_map/ppermute | solution.py:497
  167.8 26.7 %collective-permute-start.12 = (bf16[8,4,64,128]{3,2,1,0:T(8,128)(2,1)}, bf16[8,4,64,128]{3,2,1,0:T(8,128)(2,1)}, u32[]{:S(2)}, u32[]{:S(2)}) collective-permute-start(bf16[8,4,64,128]{3,2,1,0:T(8,128)(2,1)} %get-tuple-element.41), channel_id=1, source_target_pairs={{0,3},{1,0},{2,1},{3,2},{4,7},{5,4},{6,5},{7,6},{8,11},{9,8},{10,9... | collective-permute-start | bytes 1572872 | tf_op jit(solution)/shard_map/ppermute | solution.py:497
  184.3 39.0 %collective-permute-start.5 = (bf16[4,256,256]{2,1,0:T(8,128)(2,1)}, bf16[4,256,256]{2,1,0:T(8,128)(2,1)S(1)}, u32[]{:S(2)}, u32[]{:S(2)}) collective-permute-start(bf16[4,256,256]{2,1,0:T(8,128)(2,1)} %get-tuple-element.36), channel_id=1, source_target_pairs={{0,1},{1,2},{2,3},{3,0},{4,5},{5,6},{6,7},{7,4},{8,9},{9,10},{10,1... | collective-permute-start | bytes 1572872 | tf_op jit(solution)/shard_map/ppermute | solution.py:497
  184.3 39.0 %collective-permute-start.6 = (bf16[4,256,256]{2,1,0:T(8,128)(2,1)}, bf16[4,256,256]{2,1,0:T(8,128)(2,1)S(1)}, u32[]{:S(2)}, u32[]{:S(2)}) collective-permute-start(bf16[4,256,256]{2,1,0:T(8,128)(2,1)} %get-tuple-element.37), channel_id=1, source_target_pairs={{0,3},{1,0},{2,1},{3,2},{4,7},{5,4},{6,5},{7,6},{8,11},{9,8},{10,9... | collective-permute-start | bytes 1572872 | tf_op jit(solution)/shard_map/ppermute | solution.py:497
  194.5 0.8 copy-start.7
  202.4 13.5 %collective-permute-start.13 = (bf16[4,256,256]{2,1,0:T(8,128)(2,1)}, bf16[4,256,256]{2,1,0:T(8,128)(2,1)S(1)}, u32[]{:S(2)}, u32[]{:S(2)}) collective-permute-start(bf16[4,256,256]{2,1,0:T(8,128)(2,1)} %get-tuple-element.47), channel_id=1, source_target_pairs={{0,4},{4,8},{8,12},{12,0},{1,5},{5,9},{9,13},{13,1},{2,6},{6,10},{... | collective-permute-start | bytes 1572872 | tf_op jit(solution)/shard_map/ppermute | solution.py:497
  204.1 14.5 %collective-permute-start.14 = (bf16[4,256,256]{2,1,0:T(8,128)(2,1)}, bf16[4,256,256]{2,1,0:T(8,128)(2,1)}, u32[]{:S(2)}, u32[]{:S(2)}) collective-permute-start(bf16[4,256,256]{2,1,0:T(8,128)(2,1)} %get-tuple-element.48), channel_id=1, source_target_pairs={{0,12},{4,0},{8,4},{12,8},{1,13},{5,1},{9,5},{13,9},{2,14},{6,2},{... | collective-permute-start | bytes 1572872 | tf_op jit(solution)/shard_map/ppermute | solution.py:497
  215.3 14.9 %copy-start.3 = (f32[4,4,8,64]{3,2,1,0:T(8,128)S(1)}, f32[4,4,8,64]{3,2,1,0:T(8,128)}, u32[]{:S(2)}) copy-start(f32[4,4,8,64]{3,2,1,0:T(8,128)} %shard_map.80.refs_0_) | copy-start | bytes 98308
  215.9 2.7 %copy-start.8 = (bf16[4,256,256]{2,1,0:T(8,128)(2,1)}, bf16[4,256,256]{2,1,0:T(8,128)(2,1)S(1)}, u32[]{:S(2)}) copy-start(bf16[4,256,256]{2,1,0:T(8,128)(2,1)S(1)} %collective-permute-done.13.low_ref) | copy-start | bytes 1572868
  218.6 34.2 %copy-start.4 = (f32[4,32,64]{2,1,0:T(8,128)S(1)}, f32[4,32,64]{2,1,0:T(8,128)}, u32[]{:S(2)}) copy-start(f32[4,32,64]{2,1,0:T(8,128)} %get-tuple-element.51) | copy-start | bytes 98308
  221.3 32.2 %collective-permute-start.15 = (bf16[2,4,256,256]{3,2,1,0:T(8,128)(2,1)}, bf16[2,4,256,256]{3,2,1,0:T(8,128)(2,1)}, u32[]{:S(2)}, u32[]{:S(2)}) collective-permute-start(bf16[2,4,256,256]{3,2,1,0:T(8,128)(2,1)} %get-tuple-element.49), channel_id=1, source_target_pairs={{0,4},{4,8},{8,12},{12,0},{1,5},{5,9},{9,13},{13,1},{2,6},{6,10},{... | collective-permute-start | bytes 3145736 | tf_op jit(solution)/shard_map/ppermute | solution.py:497
  222.2 31.3 %collective-permute-start.16 = (bf16[2,4,256,256]{3,2,1,0:T(8,128)(2,1)}, bf16[2,4,256,256]{3,2,1,0:T(8,128)(2,1)}, u32[]{:S(2)}, u32[]{:S(2)}) collective-permute-start(bf16[2,4,256,256]{3,2,1,0:T(8,128)(2,1)} %get-tuple-element.50), channel_id=1, source_target_pairs={{0,12},{4,0},{8,4},{12,8},{1,13},{5,1},{9,5},{13,9},{2,14},{6,2},{... | collective-permute-start | bytes 3145736 | tf_op jit(solution)/shard_map/ppermute | solution.py:497
  223.3 0.8 copy-start.5
  223.3 1.0 copy-start.6
  226.9 29.8 %collective-permute-start.7 = (bf16[2,4,256,256]{3,2,1,0:T(8,128)(2,1)}, bf16[2,4,256,256]{3,2,1,0:T(8,128)(2,1)S(1)}, u32[]{:S(2)}, u32[]{:S(2)}) collective-permute-start(bf16[2,4,256,256]{3,2,1,0:T(8,128)(2,1)} %get-tuple-element.38), channel_id=1, source_target_pairs={{0,1},{1,2},{2,3},{3,0},{4,5},{5,6},{6,7},{7,4},{8,9},{9,10},{10,1... | collective-permute-start | bytes 3145736 | tf_op jit(solution)/shard_map/ppermute | solution.py:497
  226.9 29.8 %collective-permute-start.8 = (bf16[2,4,256,256]{3,2,1,0:T(8,128)(2,1)}, bf16[2,4,256,256]{3,2,1,0:T(8,128)(2,1)}, u32[]{:S(2)}, u32[]{:S(2)}) collective-permute-start(bf16[2,4,256,256]{3,2,1,0:T(8,128)(2,1)} %get-tuple-element.39), channel_id=1, source_target_pairs={{0,3},{1,0},{2,1},{3,2},{4,7},{5,4},{6,5},{7,6},{8,11},{9,8},{10,9... | collective-permute-start | bytes 3145736 | tf_op jit(solution)/shard_map/ppermute | solution.py:497
  256.8 1.0 copy-start
Sparse Core Ops, SparseCore 0:
  9.8 53.7 all-gather.2

commit v4 on v3

--- a/solution.py
+++ b/solution.py
@@ -12,7 +12,7 @@
 NCH = 128
 TAPS = 4
 INTEG = 8
-CHUNKS = (4, 4)
+CHUNKS = (5, 3)
 
 F32 = jnp.float32
 BF16 = jnp.bfloat16
@@ -212,33 +212,25 @@
 
 
 def halves_kernel(low_ref, high_ref, *refs):
-    low_out, high_out, sems = refs[-3:]
-    half = low_out.shape[0]
-    copies = [
-        pltpu.make_async_copy(low_ref.at[:half], low_out, sems.at[0]),
-        pltpu.make_async_copy(high_ref.at[half:], high_out, sems.at[1]),
-    ]
-    for copy in copies:
-        copy.start()
-    for copy in copies:
-        copy.wait()
+    low_out, high_out = refs[-2:]
+    low_out[...] = low_ref[...]
+    high_out[...] = high_ref[...]
 
 
 def halves(low, high, after=()):
-    shape = (low.shape[0] // 2,) + low.shape[1:]
+    blocks = low.shape[0] // 2
+    block = (blocks // 2,) + low.shape[1:]
+    first = pl.BlockSpec(block, lambda n: (n, 0, 0, 0))
+    second = pl.BlockSpec(block, lambda n: (2 + n, 0, 0, 0))
     return pl.pallas_call(
         halves_kernel,
-        out_shape=[jax.ShapeDtypeStruct(shape, BF16)] * 2,
-        in_specs=[ANY] * (2 + len(after)),
-        out_specs=[ANY] * 2,
-        scratch_shapes=[pltpu.SemaphoreType.DMA((2,))],
+        out_shape=[pltpu.HBM((blocks,) + low.shape[1:], BF16)] * 2,
+        grid=(2,),
+        in_specs=[first, second] + [ANY] * len(after),
+        out_specs=[first, first],
         compiler_params=limit(62),
         cost_estimate=cost(1),
-    )(in_hbm(low), in_hbm(high), *after)
-
-
-def panel_of(x_ref, index, panel):
-    return x_ref[0, pl.ds(pl.multiple_of(index * panel, panel), panel), :]
+    )(low, high, *after)
 
 
 def turned_panel(panel, lanes, low_sign):
@@ -261,21 +253,22 @@
     return result[:, :panel], result[:, panel:]
 
 
-def far_kernel(by_row, place_ref, own_ref, prev_ref, next_ref, lo_ref, hi_ref, *refs):
-    re_ref, im_ref, x_ref, r_ref = refs[-4:]
-    fixed, ring = place_ref[0], place_ref[1]
-    blocks, _, inputs, lanes = own_ref.shape
-    half = blocks // 2 * inputs
-    total = blocks * inputs
-    for s, ref in enumerate((own_ref, prev_ref, next_ref)):
-        x_ref[0, :, s * lanes : (s + 1) * lanes] = ref[:, 0].reshape(total, lanes)
-    x_ref[0, :half, 3 * lanes :] = lo_ref[:, 0].reshape(half, lanes)
-    x_ref[0, half:, 3 * lanes :] = hi_ref[:, 0].reshape(half, lanes)
-    panel = re_ref.shape[1]
-    mine = panel_of(x_ref, fixed, panel)
-    r_ref[0, :panel] = mine
-    r_ref[0, panel:] = turned_panel(mine, lanes, 1.0 if by_row else -1.0)
-    re, im = correlated(by_row, panel_of(x_ref, lax.rem(ring + 2, 4), panel), r_ref[0])
+def stacked(by_row, panel, lanes):
+    return jnp.concatenate([panel, turned_panel(panel, lanes, 1.0 if by_row else -1.0)], axis=0)
+
+
+def far_kernel(by_row, place_ref, *refs):
+    re_ref, im_ref = refs[-2:]
+    lanes = refs[0].shape[3]
+
+    def panel(parts, index):
+        near = [part[:, 0].reshape(-1, lanes) for part in parts[:3]]
+        low, high = [part[:, 0].reshape(-1, lanes) for part in parts[3:]]
+        return jnp.concatenate(near + [jnp.where(index < 2, low, high)], axis=1)
+
+    mine = panel(refs[:5], place_ref[0])
+    other = panel(refs[5:10], lax.rem(place_ref[1] + 2, 4))
+    re, im = correlated(by_row, other, stacked(by_row, mine, lanes))
     re_ref[0] = re.astype(BF16)
     im_ref[0] = im.astype(BF16)
 
@@ -283,40 +276,42 @@
 def far_products(place, slots, by_row, after=()):
     own = slots[0]
     blocks, size, inputs, lanes = own.shape
-    total = blocks * inputs
-    panel = total // 4
-
-    def data(count):
-        return pl.BlockSpec((count, 1, inputs, lanes), lambda k, c: (0, k, 0, 0))
-
-    def whole(rows, width):
-        return pl.BlockSpec((1, rows, width), lambda k, c: (k, 0, 0))
-
-    def shape(rows, width):
-        return pltpu.HBM((size, rows, width), BF16)
-
+    quarter = blocks // 4
+    panel = quarter * inputs
+
+    def fixed(k, c):
+        return (c[0], k, 0, 0)
+
+    def fixed_half(k, c):
+        return (lax.rem(c[0], 2), k, 0, 0)
+
+    def other(k, c):
+        return (lax.rem(c[1] + 2, 4), k, 0, 0)
+
+    def other_half(k, c):
+        return (lax.rem(c[1], 2), k, 0, 0)
+
+    def data(index):
+        return pl.BlockSpec((quarter, 1, inputs, lanes), index)
+
+    whole = pl.BlockSpec((1, panel, panel), lambda k, c: (k, 0, 0))
+    slots = [in_hbm(slot) for slot in slots[:3]] + list(slots[3:])
     return pl.pallas_call(
         functools.partial(far_kernel, by_row),
-        out_shape=[
-            shape(panel, panel),
-            shape(panel, panel),
-            shape(total, 4 * lanes),
-            shape(2 * panel, 4 * lanes),
-        ],
+        out_shape=[pltpu.HBM((size, panel, panel), BF16)] * 2,
         grid_spec=pltpu.PrefetchScalarGridSpec(
             num_scalar_prefetch=1,
             grid=(size,),
-            in_specs=[data(blocks)] * 3 + [data(blocks // 2)] * 2 + [ANY] * len(after),
-            out_specs=[
-                whole(panel, panel),
-                whole(panel, panel),
-                whole(total, 4 * lanes),
-                whole(2 * panel, 4 * lanes),
-            ],
+            in_specs=[data(fixed)] * 3
+            + [data(fixed_half)] * 2
+            + [data(other)] * 3
+            + [data(other_half)] * 2
+            + [ANY] * len(after),
+            out_specs=[whole, whole],
         ),
         compiler_params=limit(62),
         cost_estimate=cost(4),
-    )(place, *[in_hbm(slot) for slot in slots[:3]], *slots[3:], *after)
+    )(place, *slots, *slots, *after)
 
 
 def formed(parts, lanes):
@@ -342,24 +337,35 @@
     )
 
 
-def near_kernel(by_row, place_ref, x_ref, r_ref, *refs):
+def near_kernel(by_row, first, place_ref, own_ref, prev_ref, next_ref, low_ref, high_ref, *refs):
     fixed, ring = place_ref[0], place_ref[1]
     if by_row:
-        own_ref, up_ref, down_ref = refs
+        out_ref, up_ref, down_ref, x_ref = refs[-4:]
     else:
-        w_hbm, own_ref, up_ref, down_ref, beam_ref, w_ref, sem = refs
+        w_hbm = refs[0]
+        out_ref, up_ref, down_ref, beam_ref, x_ref, w_ref, sem = refs[-7:]
         k = pl.program_id(0)
-        copy = pltpu.make_async_copy(w_hbm.at[:, : w_ref.shape[1]], w_ref, sem)
+        copy = pltpu.make_async_copy(w_hbm.at[:, first : first + w_ref.shape[1]], w_ref, sem)
 
         @pl.when(k == 0)
         def _():
             copy.start()
 
-    panel = own_ref.shape[2]
-    lanes = x_ref.shape[2] // 4
-    for step, ref in ((1, up_ref), (3, down_ref), (0, own_ref)):
-        target = panel_of(x_ref, lax.rem(ring + step, 4), panel)
-        re, im = correlated(by_row, target, r_ref[0])
+    blocks, _, inputs, lanes = own_ref.shape
+    half = blocks // 2 * inputs
+    total = blocks * inputs
+    panel = total // 4
+    for s, ref in enumerate((own_ref, prev_ref, next_ref)):
+        x_ref[:, s * lanes : (s + 1) * lanes] = ref[:, 0].reshape(total, lanes)
+    x_ref[:half, 3 * lanes :] = low_ref[:, 0].reshape(half, lanes)
+    x_ref[half:, 3 * lanes :] = high_ref[:, 0].reshape(half, lanes)
+
+    def panel_of(index):
+        return x_ref[pl.ds(pl.multiple_of(index * panel, panel), panel), :]
+
+    stack = stacked(by_row, panel_of(fixed), lanes)
+    for step, ref in ((1, up_ref), (3, down_ref), (0, out_ref)):
+        re, im = correlated(by_row, panel_of(lax.rem(ring + step, 4)), stack)
         ref[0, 0] = re.astype(ref.dtype)
         ref[1, 0] = im.astype(ref.dtype)
     if by_row:
@@ -370,9 +376,9 @@
         copy.wait()
 
     beams = w_ref.shape[2]
-    weights = w_ref[:, k].reshape(2 * beams, w_ref.shape[3])
+    weights = w_ref[:, k].reshape(2 * beams, total)
     parts = lax.dot_general(
-        weights, x_ref[0], (((1,), (0,)), ((), ())), preferred_element_type=F32
+        weights, x_ref[...], (((1,), (0,)), ((), ())), preferred_element_type=F32
     )
     bins = lanes // 2 // INTEG
     power = jnp.zeros((4 * bins, beams), F32)
@@ -382,34 +388,35 @@
     beam_ref[0] = power
 
 
-def near_products(place, x, r, by_row, weights=None):
-    size, total, width = x.shape
+def near_products(place, slots, by_row, first=0, weights=None, after=()):
+    blocks, size, inputs, lanes = slots[0].shape
+    total = blocks * inputs
     panel = total // 4
+
+    def data(count):
+        return pl.BlockSpec((count, 1, inputs, lanes), lambda k, c: (0, k, 0, 0))
+
     block = pl.BlockSpec((2, 1, panel, panel), lambda k, c: (0, k, 0, 0))
     shape = (2, size, panel, panel)
     shapes = [pltpu.HBM(shape, F32), pltpu.HBM(shape, BF16), pltpu.HBM(shape, BF16)]
     specs = [block] * 3
-    args = [x, r]
-    scratch = []
+    args = [in_hbm(slot) for slot in slots[:3]] + list(slots[3:])
+    scratch = [pltpu.VMEM((total, 4 * lanes), BF16)]
     if not by_row:
         beams = weights.shape[2]
-        bins = width // 2 // INTEG
+        bins = 4 * (lanes // 2 // INTEG)
         shapes.append(jax.ShapeDtypeStruct((size, bins, beams), F32))
         specs.append(pl.BlockSpec((1, bins, beams), lambda k, c: (k, 0, 0)))
-        args.append(weights)
-        scratch = [pltpu.VMEM((2, size) + weights.shape[2:], BF16), pltpu.SemaphoreType.DMA]
-    args = [in_hbm(arg) for arg in args]
-    return pl.pallas_call(
-        functools.partial(near_kernel, by_row),
+        args.append(in_hbm(weights))
+        scratch += [pltpu.VMEM((2, size) + weights.shape[2:], BF16), pltpu.SemaphoreType.DMA]
+    args += after
+    return pl.pallas_call(
+        functools.partial(near_kernel, by_row, first),
         out_shape=shapes,
         grid_spec=pltpu.PrefetchScalarGridSpec(
             num_scalar_prefetch=1,
             grid=(size,),
-            in_specs=[
-                pl.BlockSpec((1, total, width), lambda k, c: (k, 0, 0)),
-                pl.BlockSpec((1, 2 * panel, width), lambda k, c: (k, 0, 0)),
-            ]
-            + [HBM] * (len(args) - 2),
+            in_specs=[data(blocks)] * 3 + [data(blocks // 2)] * 2 + [ANY] * (len(args) - 5),
             out_specs=specs,
             scratch_shapes=scratch,
         ),
@@ -502,41 +509,44 @@
 
 
 def on_device(voltages, input_flags, channel_order, beam_weights):
-    size_a, size_b = CHUNKS
+    size_b, size_a = CHUNKS
     channels = size_a + size_b
     history = passed_along(voltages[:, :, voltages.shape[2] - (TAPS - 1) * NCH :], ("row", "col"), 1)
     row = lax.axis_index("row").astype(jnp.int32)
     col = lax.axis_index("col").astype(jnp.int32)
     place_a = jnp.stack([col, row])
     place_b = jnp.stack([row, col])
-    weights_b = lax.all_gather(beam_weights[:, size_a:], "col", axis=0)
-    piece_a, piece_b = spectra(voltages, history, input_flags, channel_order, CHUNKS)
+    weights = lax.all_gather(beam_weights, "col", axis=0)
+    piece_b, piece_a = spectra(voltages, history, input_flags, channel_order, CHUNKS)
 
     def turn(piece, axis):
         return lax.all_to_all(piece, axis, split_axis=0, concat_axis=0, tiled=True)
 
+    own_b = turn(piece_b, "chan")
+    near_b = both_ways(own_b, own_b, "row")
     own_a = turn(piece_a, "chan")
     near_a = both_ways(own_a, own_a, "col")
-    own_b = turn(piece_b, "chan")
-    near_b = both_ways(own_b, own_b, "row")
     far_b = both_ways(*halves(*near_b, [own_a]), "row")
-    far_a = both_ways(*halves(*near_a), "col")
-    beam_b = own_beams(own_b, weights_b)
-
-    re_b, im_b, x_b, r_b = far_products(place_b, (own_b, *near_b, *far_b), True, [beam_b])
+    beam_b = own_beams(own_b, weights)
+    slots_b = (own_b, *near_b, *far_b)
+    re_b, im_b = far_products(place_b, slots_b, True, [beam_b])
     got_b = both_ways(re_b, im_b, "col")
-    mine_b, up_b, down_b = near_products(place_b, x_b, r_b, True)
-    sent_b = both_ways(*added(up_b, down_b, *got_b), "col")
-
-    re_a, im_a, x_a, r_a = far_products(place_a, (own_a, *near_a, *far_a), False, [mine_b])
+    half_a = halves(*near_a, [re_b])
+    far_a = both_ways(*half_a, "col")
+    slots_a = (own_a, *near_a, *far_a)
+    mine_b, up_b, down_b = near_products(place_b, slots_b, True, after=[half_a[0]])
+    sum_b = added(up_b, down_b, *got_b)
+    sent_b = both_ways(*sum_b, "col")
+    re_a, im_a = far_products(place_a, slots_a, False, [sum_b[0]])
     got_a = both_ways(re_a, im_a, "row")
-    mine_a, up_a, down_a, power_a = near_products(place_a, x_a, r_a, False, beam_weights)
-    sent_a = both_ways(*added(up_a, down_a, *got_a), "row")
+    mine_a, up_a, down_a, power_a = near_products(place_a, slots_a, False, size_b, beam_weights)
+    sum_a = added(up_a, down_a, *got_a)
+    sent_a = both_ways(*sum_a, "row")
 
     power_b = jnp.transpose(turn(beam_b, "col"), (1, 0, 2, 3)).reshape(size_b, -1, beam_b.shape[3])
-    out = finished(mine_a, *sent_a, 0, channels, None)
-    visibility = finished(mine_b, *sent_b, size_a, channels, out)
-    power = jnp.concatenate([power_a, power_b], axis=0)
+    out = finished(mine_b, *sent_b, 0, channels, None)
+    visibility = finished(mine_a, *sent_a, size_b, channels, out)
+    power = jnp.concatenate([power_b, power_a], axis=0)
     return (visibility, jnp.transpose(power, (0, 2, 1)))
 
 

time: 271 us -> 216 us (0.80)
  Pallas kernels: 130 us -> 68.8 us
  waiting for transfers between devices: 27.9 us -> 45.8 us
  blocking collectives: 56.8 us -> 51.3 us
  starting transfers between devices: 29 us -> 25.1 us
    pallas_call x6, Pallas kernels: 97.6 us -> 32.6 us  [the longest x2 17.8 us: near_products(): pl.pallas_call(functools.partial(near_kernel, by_row, first), out_shape=s...]
    ppermute x16, waiting for transfers between devices: 3.34 us -> 27.6 us  [along(): lax.ppermute(value, axis, [(i, (i + step) % count) for i in range(count)])]
    all_to_all x1, waiting for transfers between devices: 24.5 us -> 17.6 us  [turn(): return lax.all_to_all(piece, axis, split_axis=0, concat_axis=0, tiled=True)]
    all_to_all x2, blocking collectives: 56.8 us -> 51.3 us  [turn(): return lax.all_to_all(piece, axis, split_axis=0, concat_axis=0, tiled=True)]
    ppermute x16, starting transfers between devices: 21.3 us -> 18 us  [along(): lax.ppermute(value, axis, [(i, (i + step) % count) for i in range(count)])]
  transfers between devices with their start and end apart: 19 -> 19, of which waited for: 3 -> 8; matrix products, arithmetic and copies ran while one was open for 2% -> 2% of each run, Pallas kernels for 47% -> 30%
where the time goes in v4:
time: 216 us; the launch traced here: 213 us
  Pallas kernels  68.8 us (32%)
  blocking collectives  51.3 us (24%)
  waiting for transfers between devices  45.8 us (21%)
  starting transfers between devices  25.1 us (12%)
  between operations  14.2 us (7%)
  local copies, waits for them, and re-layouts  5.29 us (2%)
  other arithmetic  2.73 us (1%)
    all_to_all x2, blocking collectives, turn(): return lax.all_to_all(piece, axis, split_axis=0, concat_axis=0, tiled=True)  51.3 us
    ppermute x16, waiting for transfers between devices, along(): lax.ppermute(value, axis, [(i, (i + step) % count) for i in range(count)])  27.6 us
    ppermute x16, starting transfers between devices, along(): lax.ppermute(value, axis, [(i, (i + step) % count) for i in range(count)])  18 us
    pallas_call x2, Pallas kernels, near_products(): pl.pallas_call(functools.partial(near_kernel, by_row, first), out_shape=s...  17.8 us
    all_to_all x1, waiting for transfers between devices, turn(): return lax.all_to_all(piece, axis, split_axis=0, concat_axis=0, tiled=True)  17.6 us
    pallas_call x2, Pallas kernels, far_products(): pl.pallas_call(functools.partial(far_kernel, by_row), out_shape=[pltpu.HB...  10.5 us
    pallas_call x2, Pallas kernels, finished(): pl.pallas_call(final_kernel, out_shape=jax.ShapeDtypeStruct((2, channels,...  8.6 us
    pallas_call x1, Pallas kernels, own_beams(): pl.pallas_call(beam_kernel, out_shape=jax.ShapeDtypeStruct((owners, size,...  7.88 us
  transfers between devices with their start and end apart: 19, of which 8 were waited for; matrix products, arithmetic and copies ran while one was open for 2% of the time, Pallas kernels for 30%

profile of v4, /device:TPU:6, one launch (start us, length us, event | category | flops | bytes accessed | tf_op | source)
XLA Modules:
  0.0 213.2 jit_solution(11987240781181365218)
XLA Ops:
  7.2 0.0 all-gather.3.cloned.1.call-start
  7.2 0.7 all-gather.3.cloned.1.call-update
  7.9 0.9 slice.3
  8.8 3.5 %collective-permute-start = (bf16[2,64,384]{2,1,0:T(8,128)(2,1)S(1)}, bf16[2,64,384]{2,1,0:T(8,128)(2,1)S(1)}, u32[]{:S(2)}, u32[]{:S(2)}) collective-permute-start(bf16[2,64,384]{2,1,0:T(8,128)(2,1)S(1)} %slice.3), channel_id=1, source_target_pairs={{0,1},{1,2},{2,3},{3,4},{4,5},{5,6},{6,7},{7,8},{8,9},{9,10},{10,1... | collective-permute-start | bytes 294920 | tf_op jit(solution)/shard_map/ppermute | solution.py:56
  12.3 6.4 %shard_map.77.filt_ref = f32[2,4096,128]{2,1,0:T(8,128)S(1)} custom-call(bf16[2,64,8192]{2,1,0:T(8,128)(2,1)} %v_hbm.1, s32[1,64]{1,0:T(1,128)} %bitcast.13, f32[4,128]{1,0:T(4,128)} %constant.11.clone.coeff_hbm), custom_call_target="tpu_custom_call" | custom-call | flops 5500000256 | bytes 1 | tf_op jit(solution)/shard_map/pallas_call | solution.py:176
  18.8 0.0 collective-permute-done.halo_ref
  18.8 7.9 %shard_map.78 = (bf16[16,5,64,128]{3,2,1,0:T(8,128)(2,1)S(1)}, bf16[16,3,64,128]{3,2,1,0:T(8,128)(2,1)}) custom-call(f32[2,4096,128]{2,1,0:T(8,128)S(1)} %shard_map.77.filt_ref, bf16[2,64,384]{2,1,0:T(8,128)(2,1)S(1)} %collective-permute-done.halo_ref, s32[1,64]{1,0:T(1,128)} %bitcast.14, s32[1,128]{1,0:T(1,128)} %bitcast.15, ...), custom_call_target="tpu_custom_call" | custom-call | flops 6600000000 | bytes 1 | tf_op jit(solution)/shard_map/pallas_call | solution.py:191
  26.7 42.0 %all_to_all.15.own_ref.refs_0_.refs_5_ = bf16[16,5,64,128]{3,2,1,0:T(8,128)(2,1)S(1)} all-to-all(bf16[16,5,64,128]{3,2,1,0:T(8,128)(2,1)S(1)} %get-tuple-element.24), channel_id=1, replica_groups=mesh['chan'=16,'row'=4,'col'=4] {'chan'}, dimensions={0} | all-to-all | bytes 2621440 | tf_op jit(solution)/shard_map/all_to_all | solution.py:523
  68.7 3.6 %all-to-all-start = ((bf16[16,3,64,128]{3,2,1,0:T(8,128)(2,1)}), bf16[16,3,64,128]{3,2,1,0:T(8,128)(2,1)S(1)}, u32[]{:S(2)}, u32[]{:S(2)}) async-start(bf16[16,3,64,128]{3,2,1,0:T(8,128)(2,1)} %get-tuple-element.23), calls=%async_computation | async-start | bytes 1572864 | tf_op jit(solution)/shard_map/all_to_all | solution.py:523
  72.3 0.9 collective-permute-start.4
  73.2 2.4 %collective-permute-start.3 = (bf16[16,5,64,128]{3,2,1,0:T(8,128)(2,1)S(1)}, bf16[16,5,64,128]{3,2,1,0:T(8,128)(2,1)}, u32[]{:S(2)}, u32[]{:S(2)}) collective-permute-start(bf16[16,5,64,128]{3,2,1,0:T(8,128)(2,1)S(1)} %all_to_all.15.own_ref.refs_0_.refs_5_), channel_id=1, source_target_pairs={{0,4},{4,8},{8,12},{12,0},{1,5},{5,9},{9,13},{13,1},{2,6},{6,10},{... | collective-permute-start | bytes 3932168 | tf_op jit(solution)/shard_map/ppermute | solution.py:504
  75.6 17.6 %all-to-all-done.refs_0_.own_ref.refs_5_ = bf16[16,3,64,128]{3,2,1,0:T(8,128)(2,1)S(1)} async-done(((bf16[16,3,64,128]{3,2,1,0:T(8,128)(2,1)}), bf16[16,3,64,128]{3,2,1,0:T(8,128)(2,1)S(1)}, u32[]{:S(2)}, u32[]{:S(2)}) %all-to-all-start) | async-done | bytes 786464 | tf_op jit(solution)/shard_map/all_to_all | solution.py:523
  93.2 12.0 %collective-permute-done.4.high_ref.refs_2_.refs_7_.next_ref = bf16[16,5,64,128]{3,2,1,0:T(8,128)(2,1)} collective-permute-done((bf16[16,5,64,128]{3,2,1,0:T(8,128)(2,1)S(1)}, bf16[16,5,64,128]{3,2,1,0:T(8,128)(2,1)}, u32[]{:S(2)}, u32[]{:S(2)}) %collective-permute-start.4) | collective-permute-done | bytes 1310752 | tf_op jit(solution)/shard_map/ppermute | solution.py:504
  105.2 0.0 collective-permute-done.3.low_ref.refs_1_.refs_6_.prev_ref
  105.2 2.3 %shard_map.79 = (bf16[8,5,64,128]{3,2,1,0:T(8,128)(2,1)}, bf16[8,5,64,128]{3,2,1,0:T(8,128)(2,1)}) custom-call(bf16[16,5,64,128]{3,2,1,0:T(8,128)(2,1)} %collective-permute-done.3.low_ref.refs_1_.refs_6_.prev_ref, bf16[16,5,64,128]{3,2,1,0:T(8,128)(2,1)} %collective-permute-done.4.high_ref.refs_2_.refs_7_.next_ref, bf16[16,3,64,128]{3,2,1,0:T(8,128)(2,1)} %copy-done.2), custom_call_target="tpu_custom_call" | custom-call | flops 1100000000 | bytes 1 | tf_op jit(solution)/shard_map/pallas_call | solution.py:225
  107.5 2.9 %collective-permute-start.5 = (bf16[8,5,64,128]{3,2,1,0:T(8,128)(2,1)}, bf16[8,5,64,128]{3,2,1,0:T(8,128)(2,1)}, u32[]{:S(2)}, u32[]{:S(2)}) collective-permute-start(bf16[8,5,64,128]{3,2,1,0:T(8,128)(2,1)} %get-tuple-element.25), channel_id=1, source_target_pairs={{0,4},{4,8},{8,12},{12,0},{1,5},{5,9},{9,13},{13,1},{2,6},{6,10},{... | collective-permute-start | bytes 1966088 | tf_op jit(solution)/shard_map/ppermute | solution.py:504
  110.4 0.0 collective-permute-start.6
  110.4 0.7 pad_add_fusion.1.place_ref
  111.1 0.6 pad_add_fusion.place_ref
  111.7 0.8 collective-permute-start.2
  112.5 1.2 collective-permute-start.1
  113.8 7.9 %shard_map.80.refs_10_ = f32[4,5,8,64]{3,2,1,0:T(8,128)} custom-call(bf16[16,5,64,128]{3,2,1,0:T(8,128)(2,1)} %copy-done.1, bf16[4,2,8,64,1024]{4,3,2,1,0:T(8,128)(2,1)} %bitcast.12), custom_call_target="tpu_custom_call" | custom-call | flops 4400000000 | bytes 1 | tf_op jit(solution)/shard_map/pallas_call | solution.py:443
  121.6 3.0 %collective-permute-done.5.refs_3_.refs_8_.low_ref = bf16[8,5,64,128]{3,2,1,0:T(8,128)(2,1)} collective-permute-done((bf16[8,5,64,128]{3,2,1,0:T(8,128)(2,1)}, bf16[8,5,64,128]{3,2,1,0:T(8,128)(2,1)}, u32[]{:S(2)}, u32[]{:S(2)}) %collective-permute-start.5) | collective-permute-done | bytes 655392 | tf_op jit(solution)/shard_map/ppermute | solution.py:504
  124.7 3.4 %collective-permute-done.6.refs_4_.refs_9_.high_ref = bf16[8,5,64,128]{3,2,1,0:T(8,128)(2,1)} collective-permute-done((bf16[8,5,64,128]{3,2,1,0:T(8,128)(2,1)}, bf16[8,5,64,128]{3,2,1,0:T(8,128)(2,1)}, u32[]{:S(2)}, u32[]{:S(2)}) %collective-permute-start.6) | collective-permute-done | bytes 655392 | tf_op jit(solution)/shard_map/ppermute | solution.py:504
  128.1 6.0 %shard_map.81 = (bf16[5,256,256]{2,1,0:T(8,128)(2,1)}, bf16[5,256,256]{2,1,0:T(8,128)(2,1)}) custom-call(s32[2]{0:T(128)} %pad_add_fusion.1.place_ref, bf16[16,5,64,128]{3,2,1,0:T(8,128)(2,1)} %copy-done.1, bf16[16,5,64,128]{3,2,1,0:T(8,128)(2,1)} %collective-permute-done.3.low_ref.refs_1_.refs_6_.prev_ref, ...), custom_call_target="tpu_custom_call" | custom-call | flops 4400000000 | bytes 1 | tf_op jit(solution)/shard_map/pallas_call | solution.py:299
  134.0 0.9 collective-permute-start.10
  134.9 1.2 collective-permute-start.9
  136.1 0.0 collective-permute-done.2.high_ref.next_ref.refs_2_.refs_7_
  136.1 0.0 collective-permute-done.1.low_ref.prev_ref.refs_1_.refs_6_
  136.2 0.9 copy-done.5
  137.1 0.9 copy-done.6
  138.0 2.0 shard_map.82
  140.0 2.0 collective-permute-start.8
  142.0 0.0 collective-permute-start.7
  142.0 8.5 %shard_map.84 = (f32[2,5,256,256]{3,2,1,0:T(8,128)}, bf16[2,5,256,256]{3,2,1,0:T(8,128)(2,1)}, bf16[2,5,256,256]{3,2,1,0:T(8,128)(2,1)}) custom-call(s32[2]{0:T(128)} %pad_add_fusion.1.place_ref, bf16[16,5,64,128]{3,2,1,0:T(8,128)(2,1)} %copy-done.1, bf16[16,5,64,128]{3,2,1,0:T(8,128)(2,1)} %collective-permute-done.3.low_ref.refs_1_.refs_6_.prev_ref, ...), custom_call_target="tpu_custom_call" | custom-call | flops 7699999744 | bytes 1 | tf_op jit(solution)/shard_map/pallas_call | solution.py:413
  150.5 1.6 collective-permute-done.10.high_ref
  152.1 2.0 collective-permute-done.9.low_ref
  154.1 3.0 %shard_map.85 = (bf16[2,5,256,256]{3,2,1,0:T(8,128)(2,1)}, bf16[2,5,256,256]{3,2,1,0:T(8,128)(2,1)}) custom-call(bf16[2,5,256,256]{3,2,1,0:T(8,128)(2,1)} %get-tuple-element.33.up_ref, bf16[2,5,256,256]{3,2,1,0:T(8,128)(2,1)} %get-tuple-element.34.down_ref, ...), custom_call_target="tpu_custom_call", output_to_operand_aliasing={{0}: (0, {}), {1}: (1, {})} | custom-call | flops 1100000000 | bytes 1 | tf_op jit(solution)/shard_map/pallas_call | solution.py:469
  157.1 0.0 collective-permute-start.15
  157.1 0.9 collective-permute-done.8.high_ref.refs_4_.refs_9_
  158.0 4.6 %collective-permute-done.7.low_ref.refs_3_.refs_8_ = bf16[8,3,64,128]{3,2,1,0:T(8,128)(2,1)} collective-permute-done((bf16[8,3,64,128]{3,2,1,0:T(8,128)(2,1)}, bf16[8,3,64,128]{3,2,1,0:T(8,128)(2,1)}, u32[]{:S(2)}, u32[]{:S(2)}) %collective-permute-start.7) | collective-permute-done | bytes 393248 | tf_op jit(solution)/shard_map/ppermute | solution.py:504
  162.6 4.5 %shard_map.86 = (bf16[3,256,256]{2,1,0:T(8,128)(2,1)}, bf16[3,256,256]{2,1,0:T(8,128)(2,1)}) custom-call(s32[2]{0:T(128)} %pad_add_fusion.place_ref, bf16[16,3,64,128]{3,2,1,0:T(8,128)(2,1)} %copy-done.2, bf16[16,3,64,128]{3,2,1,0:T(8,128)(2,1)} %copy-done.6, bf16[16,3,64,128]{3,2,1,0:T(8,128)(2,1)} %copy-done.5, ...), custom_call_target="tpu_custom_call" | custom-call | flops 4400000000 | bytes 1 | tf_op jit(solution)/shard_map/pallas_call | solution.py:299
  167.1 0.4 collective-permute-start.11
  167.5 1.7 collective-permute-start.12
  169.2 1.4 collective-permute-start.16
  170.6 9.4 %shard_map.83 = (f32[2,3,256,256]{3,2,1,0:T(8,128)}, bf16[2,3,256,256]{3,2,1,0:T(8,128)(2,1)}, bf16[2,3,256,256]{3,2,1,0:T(8,128)(2,1)}, f32[3,32,64]{2,1,0:T(8,128)}) custom-call(s32[2]{0:T(128)} %pad_add_fusion.place_ref, bf16[16,3,64,128]{3,2,1,0:T(8,128)(2,1)} %copy-done.2, bf16[16,3,64,128]{3,2,1,0:T(8,128)(2,1)} %copy-done.6, ...), custom_call_target="tpu_custom_call" | custom-call | flops 7699999744 | bytes 1 | tf_op jit(solution)/shard_map/pallas_call | solution.py:413
  180.0 0.0 collective-permute-done.11.low_ref
  180.0 0.0 copy-start.8
  180.1 0.0 collective-permute-done.12.high_ref
  180.1 0.7 copy-done.8
  180.8 2.4 %shard_map.87 = (bf16[2,3,256,256]{3,2,1,0:T(8,128)(2,1)}, bf16[2,3,256,256]{3,2,1,0:T(8,128)(2,1)}) custom-call(bf16[2,3,256,256]{3,2,1,0:T(8,128)(2,1)} %get-tuple-element.31.up_ref, bf16[2,3,256,256]{3,2,1,0:T(8,128)(2,1)} %get-tuple-element.32.down_ref, bf16[3,256,256]{2,1,0:T(8,128)(2,1)} %copy-done.8, ...), custom_call_target="tpu_custom_call", output_to_operand_aliasing={{0}: (0, {}), {1}: (1, {})} | custom-call | flops 1100000000 | bytes 1 | tf_op jit(solution)/shard_map/pallas_call | solution.py:469
  183.2 1.5 collective-permute-start.13
  184.7 0.5 collective-permute-start.14
  185.2 0.1 reshape.17
  185.3 9.3 %all_to_all.16 = f32[4,1,2560]{2,1,0:T(1,128)S(1)} all-to-all(f32[4,1,2560]{2,1,0:T(1,128)S(1)} %reshape.17), channel_id=1, replica_groups=mesh['chan'=16,'row'=4,'col'=4] {'col'}, dimensions={0} | all-to-all | bytes 81920 | tf_op jit(solution)/shard_map/all_to_all | solution.py:523
  194.6 0.5 broadcast
  195.1 0.8 reduce
  195.8 0.1 reshape.18
  195.9 0.7 maximum_bitcast_fusion
  196.6 0.0 collective-permute-done.16.next_ref
  196.6 0.0 collective-permute-done.15.prev_ref
  196.6 1.1 copy-done
  197.7 3.7 %shard_map.88.refs_0_ = f32[2,8,256,256]{3,2,1,0:T(8,128)} custom-call(f32[2,5,256,256]{3,2,1,0:T(8,128)} %get-tuple-element.41.own_ref, bf16[2,5,256,256]{3,2,1,0:T(8,128)(2,1)} %copy-done, bf16[2,5,256,256]{3,2,1,0:T(8,128)(2,1)} %collective-permute-done.16.next_ref), custom_call_target="tpu_custom_call" | custom-call | flops 2200000000 | bytes 1 | tf_op jit(solution)/shard_map/pallas_call | solution.py:490
  201.4 4.9 %shard_map.89 = f32[2,8,256,256]{3,2,1,0:T(8,128)} custom-call(f32[2,3,256,256]{3,2,1,0:T(8,128)} %get-tuple-element.30.own_ref, bf16[2,3,256,256]{3,2,1,0:T(8,128)(2,1)} %collective-permute-done.13.prev_ref, bf16[2,3,256,256]{3,2,1,0:T(8,128)(2,1)} %collective-permute-done.14.next_ref, ...), custom_call_target="tpu_custom_call", output_to_operand_aliasing={{}: (3, {})} | custom-call | flops 2200000000 | bytes 1 | tf_op jit(solution)/shard_map/pallas_call | solution.py:490
  (17 shorter events, 0.0 us)
Async XLA Ops:
  7.2 106.6 %all-gather.3.cloned.1.call-start = ((), (), s32[]{:S(2)}) async-start(), calls=%async_computation.3 | async-start | bytes 10485760 | tf_op jit(solution)/shard_map/all_gather | solution.py:519
  8.8 9.9 %collective-permute-start = (bf16[2,64,384]{2,1,0:T(8,128)(2,1)S(1)}, bf16[2,64,384]{2,1,0:T(8,128)(2,1)S(1)}, u32[]{:S(2)}, u32[]{:S(2)}) collective-permute-start(bf16[2,64,384]{2,1,0:T(8,128)(2,1)S(1)} %slice.3), channel_id=1, source_target_pairs={{0,1},{1,2},{2,3},{3,4},{4,5},{5,6},{6,7},{7,8},{8,9},{9,10},{10,1... | collective-permute-start | bytes 294920 | tf_op jit(solution)/shard_map/ppermute | solution.py:56
  68.7 38.8 %copy-start.1 = (bf16[16,5,64,128]{3,2,1,0:T(8,128)(2,1)}, bf16[16,5,64,128]{3,2,1,0:T(8,128)(2,1)S(1)}, u32[]{:S(2)}) copy-start(bf16[16,5,64,128]{3,2,1,0:T(8,128)(2,1)S(1)} %all_to_all.15.own_ref.refs_0_.refs_5_) | copy-start | bytes 3932164
  68.7 24.5 %all-to-all-start = ((bf16[16,3,64,128]{3,2,1,0:T(8,128)(2,1)}), bf16[16,3,64,128]{3,2,1,0:T(8,128)(2,1)S(1)}, u32[]{:S(2)}, u32[]{:S(2)}) async-start(bf16[16,3,64,128]{3,2,1,0:T(8,128)(2,1)} %get-tuple-element.23), calls=%async_computation | async-start | bytes 1572864 | tf_op jit(solution)/shard_map/all_to_all | solution.py:523
  72.3 32.9 %collective-permute-start.4 = (bf16[16,5,64,128]{3,2,1,0:T(8,128)(2,1)S(1)}, bf16[16,5,64,128]{3,2,1,0:T(8,128)(2,1)}, u32[]{:S(2)}, u32[]{:S(2)}) collective-permute-start(bf16[16,5,64,128]{3,2,1,0:T(8,128)(2,1)S(1)} %all_to_all.15.own_ref.refs_0_.refs_5_), channel_id=1, source_target_pairs={{0,12},{4,0},{8,4},{12,8},{1,13},{5,1},{9,5},{13,9},{2,14},{6,2},{... | collective-permute-start | bytes 3932168 | tf_op jit(solution)/shard_map/ppermute | solution.py:504
  73.2 32.0 %collective-permute-start.3 = (bf16[16,5,64,128]{3,2,1,0:T(8,128)(2,1)S(1)}, bf16[16,5,64,128]{3,2,1,0:T(8,128)(2,1)}, u32[]{:S(2)}, u32[]{:S(2)}) collective-permute-start(bf16[16,5,64,128]{3,2,1,0:T(8,128)(2,1)S(1)} %all_to_all.15.own_ref.refs_0_.refs_5_), channel_id=1, source_target_pairs={{0,4},{4,8},{8,12},{12,0},{1,5},{5,9},{9,13},{13,1},{2,6},{6,10},{... | collective-permute-start | bytes 3932168 | tf_op jit(solution)/shard_map/ppermute | solution.py:504
  93.2 12.0 %copy-start.2 = (bf16[16,3,64,128]{3,2,1,0:T(8,128)(2,1)}, bf16[16,3,64,128]{3,2,1,0:T(8,128)(2,1)S(1)}, u32[]{:S(2)}) copy-start(bf16[16,3,64,128]{3,2,1,0:T(8,128)(2,1)S(1)} %all-to-all-done.refs_0_.own_ref.refs_5_) | copy-start | bytes 2359300
  107.5 17.2 %collective-permute-start.5 = (bf16[8,5,64,128]{3,2,1,0:T(8,128)(2,1)}, bf16[8,5,64,128]{3,2,1,0:T(8,128)(2,1)}, u32[]{:S(2)}, u32[]{:S(2)}) collective-permute-start(bf16[8,5,64,128]{3,2,1,0:T(8,128)(2,1)} %get-tuple-element.25), channel_id=1, source_target_pairs={{0,4},{4,8},{8,12},{12,0},{1,5},{5,9},{9,13},{13,1},{2,6},{6,10},{... | collective-permute-start | bytes 1966088 | tf_op jit(solution)/shard_map/ppermute | solution.py:504
  110.4 17.7 %collective-permute-start.6 = (bf16[8,5,64,128]{3,2,1,0:T(8,128)(2,1)}, bf16[8,5,64,128]{3,2,1,0:T(8,128)(2,1)}, u32[]{:S(2)}, u32[]{:S(2)}) collective-permute-start(bf16[8,5,64,128]{3,2,1,0:T(8,128)(2,1)} %get-tuple-element.26), channel_id=1, source_target_pairs={{0,12},{4,0},{8,4},{12,8},{1,13},{5,1},{9,5},{13,9},{2,14},{6,2},{... | collective-permute-start | bytes 1966088 | tf_op jit(solution)/shard_map/ppermute | solution.py:504
  111.7 24.4 %collective-permute-start.2 = (bf16[16,3,64,128]{3,2,1,0:T(8,128)(2,1)}, bf16[16,3,64,128]{3,2,1,0:T(8,128)(2,1)S(1)}, u32[]{:S(2)}, u32[]{:S(2)}) collective-permute-start(bf16[16,3,64,128]{3,2,1,0:T(8,128)(2,1)} %copy-done.2), channel_id=1, source_target_pairs={{0,3},{1,0},{2,1},{3,2},{4,7},{5,4},{6,5},{7,6},{8,11},{9,8},{10,9... | collective-permute-start | bytes 2359304 | tf_op jit(solution)/shard_map/ppermute | solution.py:504
  112.5 23.6 %collective-permute-start.1 = (bf16[16,3,64,128]{3,2,1,0:T(8,128)(2,1)}, bf16[16,3,64,128]{3,2,1,0:T(8,128)(2,1)S(1)}, u32[]{:S(2)}, u32[]{:S(2)}) collective-permute-start(bf16[16,3,64,128]{3,2,1,0:T(8,128)(2,1)} %copy-done.2), channel_id=1, source_target_pairs={{0,1},{1,2},{2,3},{3,0},{4,5},{5,6},{6,7},{7,4},{8,9},{9,10},{10,1... | collective-permute-start | bytes 2359304 | tf_op jit(solution)/shard_map/ppermute | solution.py:504
  134.0 18.1 %collective-permute-start.10 = (bf16[5,256,256]{2,1,0:T(8,128)(2,1)}, bf16[5,256,256]{2,1,0:T(8,128)(2,1)}, u32[]{:S(2)}, u32[]{:S(2)}) collective-permute-start(bf16[5,256,256]{2,1,0:T(8,128)(2,1)} %get-tuple-element.35), channel_id=1, source_target_pairs={{0,3},{1,0},{2,1},{3,2},{4,7},{5,4},{6,5},{7,6},{8,11},{9,8},{10,9... | collective-permute-start | bytes 1966088 | tf_op jit(solution)/shard_map/ppermute | solution.py:504
  134.9 19.2 %collective-permute-start.9 = (bf16[5,256,256]{2,1,0:T(8,128)(2,1)}, bf16[5,256,256]{2,1,0:T(8,128)(2,1)}, u32[]{:S(2)}, u32[]{:S(2)}) collective-permute-start(bf16[5,256,256]{2,1,0:T(8,128)(2,1)} %get-tuple-element.27.refs_0_), channel_id=1, source_target_pairs={{0,1},{1,2},{2,3},{3,0},{4,5},{5,6},{6,7},{7,4},{8,9},{9,10},{10,1... | collective-permute-start | bytes 1966088 | tf_op jit(solution)/shard_map/ppermute | solution.py:504
  136.1 0.9 copy-start.5
  137.1 0.9 copy-start.6
  140.0 18.0 %collective-permute-start.8 = (bf16[8,3,64,128]{3,2,1,0:T(8,128)(2,1)}, bf16[8,3,64,128]{3,2,1,0:T(8,128)(2,1)S(1)}, u32[]{:S(2)}, u32[]{:S(2)}) collective-permute-start(bf16[8,3,64,128]{3,2,1,0:T(8,128)(2,1)} %get-tuple-element.29), channel_id=1, source_target_pairs={{0,3},{1,0},{2,1},{3,2},{4,7},{5,4},{6,5},{7,6},{8,11},{9,8},{10,9... | collective-permute-start | bytes 1179656 | tf_op jit(solution)/shard_map/ppermute | solution.py:504
  142.0 20.5 %collective-permute-start.7 = (bf16[8,3,64,128]{3,2,1,0:T(8,128)(2,1)}, bf16[8,3,64,128]{3,2,1,0:T(8,128)(2,1)}, u32[]{:S(2)}, u32[]{:S(2)}) collective-permute-start(bf16[8,3,64,128]{3,2,1,0:T(8,128)(2,1)} %get-tuple-element.28.refs_0_), channel_id=1, source_target_pairs={{0,1},{1,2},{2,3},{3,0},{4,5},{5,6},{6,7},{7,4},{8,9},{9,10},{10,1... | collective-permute-start | bytes 1179656 | tf_op jit(solution)/shard_map/ppermute | solution.py:504
  157.1 39.5 %collective-permute-start.15 = (bf16[2,5,256,256]{3,2,1,0:T(8,128)(2,1)}, bf16[2,5,256,256]{3,2,1,0:T(8,128)(2,1)S(1)}, u32[]{:S(2)}, u32[]{:S(2)}) collective-permute-start(bf16[2,5,256,256]{3,2,1,0:T(8,128)(2,1)} %get-tuple-element.36.refs_10_), channel_id=1, source_target_pairs={{0,1},{1,2},{2,3},{3,0},{4,5},{5,6},{6,7},{7,4},{8,9},{9,10},{10,1... | collective-permute-start | bytes 3932168 | tf_op jit(solution)/shard_map/ppermute | solution.py:504
  158.0 4.6 %copy-start.7 = (bf16[8,3,64,128]{3,2,1,0:T(8,128)(2,1)}, bf16[8,3,64,128]{3,2,1,0:T(8,128)(2,1)S(1)}, u32[]{:S(2)}) copy-start(bf16[8,3,64,128]{3,2,1,0:T(8,128)(2,1)S(1)} %collective-permute-done.8.high_ref.refs_4_.refs_9_) | copy-start | bytes 1179652
  167.1 12.9 %collective-permute-start.11 = (bf16[3,256,256]{2,1,0:T(8,128)(2,1)}, bf16[3,256,256]{2,1,0:T(8,128)(2,1)S(1)}, u32[]{:S(2)}, u32[]{:S(2)}) collective-permute-start(bf16[3,256,256]{2,1,0:T(8,128)(2,1)} %get-tuple-element.37), channel_id=1, source_target_pairs={{0,4},{4,8},{8,12},{12,0},{1,5},{5,9},{9,13},{13,1},{2,6},{6,10},{... | collective-permute-start | bytes 1179656 | tf_op jit(solution)/shard_map/ppermute | solution.py:504
  167.5 12.6 %collective-permute-start.12 = (bf16[3,256,256]{2,1,0:T(8,128)(2,1)}, bf16[3,256,256]{2,1,0:T(8,128)(2,1)}, u32[]{:S(2)}, u32[]{:S(2)}) collective-permute-start(bf16[3,256,256]{2,1,0:T(8,128)(2,1)} %get-tuple-element.38), channel_id=1, source_target_pairs={{0,12},{4,0},{8,4},{12,8},{1,13},{5,1},{9,5},{13,9},{2,14},{6,2},{... | collective-permute-start | bytes 1179656 | tf_op jit(solution)/shard_map/ppermute | solution.py:504
  169.2 27.4 %collective-permute-start.16 = (bf16[2,5,256,256]{3,2,1,0:T(8,128)(2,1)}, bf16[2,5,256,256]{3,2,1,0:T(8,128)(2,1)}, u32[]{:S(2)}, u32[]{:S(2)}) collective-permute-start(bf16[2,5,256,256]{3,2,1,0:T(8,128)(2,1)} %get-tuple-element.42), channel_id=1, source_target_pairs={{0,3},{1,0},{2,1},{3,2},{4,7},{5,4},{6,5},{7,6},{8,11},{9,8},{10,9... | collective-permute-start | bytes 3932168 | tf_op jit(solution)/shard_map/ppermute | solution.py:504
  180.0 0.7 copy-start.8
  180.8 4.4 %copy-start.3 = (f32[4,5,8,64]{3,2,1,0:T(8,128)S(1)}, f32[4,5,8,64]{3,2,1,0:T(8,128)}, u32[]{:S(2)}) copy-start(f32[4,5,8,64]{3,2,1,0:T(8,128)} %shard_map.80.refs_10_) | copy-start | bytes 122884
  180.8 15.1 %copy-start.4 = (f32[3,32,64]{2,1,0:T(8,128)S(1)}, f32[3,32,64]{2,1,0:T(8,128)}, u32[]{:S(2)}) copy-start(f32[3,32,64]{2,1,0:T(8,128)} %get-tuple-element.43) | copy-start | bytes 73732
  183.2 18.2 %collective-permute-start.13 = (bf16[2,3,256,256]{3,2,1,0:T(8,128)(2,1)}, bf16[2,3,256,256]{3,2,1,0:T(8,128)(2,1)}, u32[]{:S(2)}, u32[]{:S(2)}) collective-permute-start(bf16[2,3,256,256]{3,2,1,0:T(8,128)(2,1)} %get-tuple-element.39), channel_id=1, source_target_pairs={{0,4},{4,8},{8,12},{12,0},{1,5},{5,9},{9,13},{13,1},{2,6},{6,10},{... | collective-permute-start | bytes 2359304 | tf_op jit(solution)/shard_map/ppermute | solution.py:504
  184.7 16.8 %collective-permute-start.14 = (bf16[2,3,256,256]{3,2,1,0:T(8,128)(2,1)}, bf16[2,3,256,256]{3,2,1,0:T(8,128)(2,1)}, u32[]{:S(2)}, u32[]{:S(2)}) collective-permute-start(bf16[2,3,256,256]{3,2,1,0:T(8,128)(2,1)} %get-tuple-element.40), channel_id=1, source_target_pairs={{0,12},{4,0},{8,4},{12,8},{1,13},{5,1},{9,5},{13,9},{2,14},{6,2},{... | collective-permute-start | bytes 2359304 | tf_op jit(solution)/shard_map/ppermute | solution.py:504
  196.6 1.1 copy-start
Sparse Core Ops, SparseCore 0:
  9.8 88.6 all-gather.2

commit v5 on v4

--- a/solution.py
+++ b/solution.py
@@ -91,7 +91,7 @@
             return window[1:]
 
         zero = v_ref[part, :, :NCH].astype(F32) * 0.0
-        lax.fori_loop(0, frames, frame_step, (zero,) * (TAPS - 1), unroll=4)
+        lax.fori_loop(0, frames, frame_step, (zero,) * (TAPS - 1), unroll=8)
 
 
 def spectrum_kernel(chunks, filt_ref, halo_ref, flags_hbm, order_hbm, coeff_hbm, table_hbm, *rest):
@@ -153,7 +153,7 @@
             ]
         return carry
 
-    lax.fori_loop(0, inputs // 2, input_step, 0, unroll=2)
+    lax.fori_loop(0, inputs // 2, input_step, 0, unroll=4)
     per_block = sum(chunks)
 
     def copy_step(block, carry):
@@ -229,7 +229,7 @@
         in_specs=[first, second] + [ANY] * len(after),
         out_specs=[first, first],
         compiler_params=limit(62),
-        cost_estimate=cost(1),
+        cost_estimate=cost(0.1),
     )(low, high, *after)
 
 
@@ -310,31 +310,41 @@
             out_specs=[whole, whole],
         ),
         compiler_params=limit(62),
-        cost_estimate=cost(4),
+        cost_estimate=cost(0.1),
     )(place, *slots, *slots, *after)
 
 
 def formed(parts, lanes):
     beams = parts.shape[0] // 2
+    values = []
     low = lax.broadcasted_iota(jnp.int32, (beams, lanes), 1) < lanes // 2
-    turned = pltpu.roll(parts[beams:], lanes // 2, axis=1)
-    value = parts[:beams] + jnp.where(low, -turned, turned)
-    return value * value
-
-
-def pooled(power, bins, first):
-    lanes = power.shape[1]
-    lane = lax.broadcasted_iota(jnp.int32, (bins, lanes), 1)
-    place = lax.broadcasted_iota(jnp.int32, (bins, lanes), 0)
-    wanted = first + lax.rem(lane, lanes // 2) // INTEG
-    pool = jnp.where(place == wanted, 1.0 / INTEG, 0.0).astype(F32)
-    return lax.dot_general(
-        pool,
-        power,
-        (((1,), (1,)), ((), ())),
-        precision=lax.Precision.HIGHEST,
-        preferred_element_type=F32,
-    )
+    for s in range(parts.shape[1] // lanes):
+        piece = parts[:, s * lanes : (s + 1) * lanes]
+        turned = pltpu.roll(piece[beams:], lanes // 2, axis=1)
+        value = piece[:beams] + jnp.where(low, -turned, turned)
+        values.append(value * value)
+    return jnp.concatenate(values, axis=1) if len(values) > 1 else values[0]
+
+
+def pooled(power, lanes, bins, sources):
+    width = power.shape[1]
+    pools = []
+    for source in sources:
+        lane = lax.broadcasted_iota(jnp.int32, (bins, lanes), 1)
+        place = lax.broadcasted_iota(jnp.int32, (bins, lanes), 0)
+        wanted = source * (lanes // 2 // INTEG) + lax.rem(lane, lanes // 2) // INTEG
+        pools.append(jnp.where(place == wanted, 1.0 / INTEG, 0.0).astype(BF16))
+    pool = jnp.concatenate(pools, axis=1) if len(pools) > 1 else pools[0]
+    high = power.astype(BF16)
+    rest = power - high.astype(F32)
+    middle = rest.astype(BF16)
+    low = (rest - middle.astype(F32)).astype(BF16)
+    total = jnp.zeros((bins, power.shape[0]), F32)
+    for term in (low, middle, high):
+        total = total + lax.dot_general(
+            pool, term, (((1,), (1,)), ((), ())), preferred_element_type=F32
+        )
+    return total
 
 
 def near_kernel(by_row, first, place_ref, own_ref, prev_ref, next_ref, low_ref, high_ref, *refs):
@@ -381,11 +391,8 @@
         weights, x_ref[...], (((1,), (0,)), ((), ())), preferred_element_type=F32
     )
     bins = lanes // 2 // INTEG
-    power = jnp.zeros((4 * bins, beams), F32)
-    for s, shift in enumerate((0, 3, 1, 2)):
-        squared = formed(parts[:, s * lanes : (s + 1) * lanes], lanes)
-        power = power + pooled(squared, 4 * bins, lax.rem(fixed + shift, 4) * bins)
-    beam_ref[0] = power
+    sources = [lax.rem(fixed + shift, 4) for shift in (0, 3, 1, 2)]
+    beam_ref[0] = pooled(formed(parts, lanes), lanes, 4 * bins, sources)
 
 
 def near_products(place, slots, by_row, first=0, weights=None, after=()):
@@ -421,7 +428,7 @@
             scratch_shapes=scratch,
         ),
         compiler_params=limit(62),
-        cost_estimate=cost(7),
+        cost_estimate=cost(0.1),
     )(place, *args)
 
 
@@ -429,14 +436,16 @@
     blocks, _, inputs, lanes = own_ref.shape
     owners, _, _, beams, total = w_ref.shape
     x = own_ref[:, 0].reshape(blocks * inputs, lanes)
-    weights = w_ref[:, :, 0].reshape(owners * 2 * beams, total)
+    weights = jnp.concatenate(
+        [w_ref[:, part, 0].reshape(owners * beams, total) for part in range(2)], axis=0
+    )
     parts = lax.dot_general(weights, x, (((1,), (0,)), ((), ())), preferred_element_type=F32)
+    power = pooled(formed(parts, lanes), lanes, lanes // 2 // INTEG, [0])
     for owner in range(owners):
-        squared = formed(parts[owner * 2 * beams : (owner + 1) * 2 * beams], lanes)
-        out_ref[owner, 0] = pooled(squared, lanes // 2 // INTEG, 0)
-
-
-def own_beams(own, weights):
+        out_ref[owner, 0] = power[:, owner * beams : (owner + 1) * beams]
+
+
+def own_beams(own, weights, first=0):
     blocks, size, inputs, lanes = own.shape
     owners, _, _, beams, total = weights.shape
     bins = lanes // 2 // INTEG
@@ -446,11 +455,11 @@
         grid=(size,),
         in_specs=[
             pl.BlockSpec((blocks, 1, inputs, lanes), lambda k: (0, k, 0, 0)),
-            pl.BlockSpec((owners, 2, 1, beams, total), lambda k: (0, 0, k, 0, 0)),
+            pl.BlockSpec((owners, 2, 1, beams, total), lambda k: (0, 0, first + k, 0, 0)),
         ],
         out_specs=pl.BlockSpec((owners, 1, bins, beams), lambda k: (0, k, 0, 0)),
         compiler_params=limit(62),
-        cost_estimate=cost(4),
+        cost_estimate=cost(0.1),
     )(in_hbm(own), in_hbm(weights))
 
 
@@ -474,28 +483,50 @@
         out_specs=[real, imag],
         input_output_aliases={0: 0, 1: 1},
         compiler_params=limit(62),
-        cost_estimate=cost(1),
+        cost_estimate=cost(0.1),
     )(up, down, low, high, *after)
 
 
-def final_kernel(own_ref, prev_ref, next_ref, *refs):
-    refs[-1][...] = own_ref[...] + prev_ref[...].astype(F32) + next_ref[...].astype(F32)
+def final_kernel(first, own_ref, prev_ref, next_ref, *refs):
+    out_hbm, held, sems = refs[-3:]
+    size = own_ref.shape[1]
+    p = pl.program_id(0)
+
+    def copy(part):
+        return pltpu.make_async_copy(
+            held.at[part], out_hbm.at[part, first : first + size], sems.at[part]
+        )
+
+    for part in range(2):
+
+        @pl.when(p == part)
+        def _(part=part):
+            held[part] = own_ref[0] + prev_ref[0].astype(F32) + next_ref[0].astype(F32)
+            copy(part).start()
+
+    @pl.when(p == 1)
+    def _():
+        copy(0).wait()
+        copy(1).wait()
 
 
 def finished(own, from_prev, from_next, first, channels, out):
     _, size, panel, _ = own.shape
-    step = math.gcd(first, size) if first else size
-    block = pl.BlockSpec((1, step, panel, panel), lambda p, k: (p, k, 0, 0))
+    block = pl.BlockSpec((1, size, panel, panel), lambda p: (p, 0, 0, 0))
     extra = [] if out is None else [out]
     return pl.pallas_call(
-        final_kernel,
+        functools.partial(final_kernel, first),
         out_shape=jax.ShapeDtypeStruct((2, channels, panel, panel), F32),
-        grid=(2, size // step),
+        grid=(2,),
         in_specs=[block] * 3 + [ANY] * len(extra),
-        out_specs=pl.BlockSpec((1, step, panel, panel), lambda p, k: (p, first // step + k, 0, 0)),
+        out_specs=HBM,
         input_output_aliases={3: 0} if extra else {},
+        scratch_shapes=[
+            pltpu.VMEM((2, size, panel, panel), F32),
+            pltpu.SemaphoreType.DMA((2,)),
+        ],
         compiler_params=limit(62),
-        cost_estimate=cost(2),
+        cost_estimate=cost(0.1),
     )(in_hbm(own), from_prev, from_next, *extra)
 
 
@@ -526,10 +557,10 @@
     near_b = both_ways(own_b, own_b, "row")
     own_a = turn(piece_a, "chan")
     near_a = both_ways(own_a, own_a, "col")
-    far_b = both_ways(*halves(*near_b, [own_a]), "row")
     beam_b = own_beams(own_b, weights)
+    far_b = both_ways(*halves(*near_b, [own_a, beam_b]), "row")
     slots_b = (own_b, *near_b, *far_b)
-    re_b, im_b = far_products(place_b, slots_b, True, [beam_b])
+    re_b, im_b = far_products(place_b, slots_b, True)
     got_b = both_ways(re_b, im_b, "col")
     half_a = halves(*near_a, [re_b])
     far_a = both_ways(*half_a, "col")

time: 216 us -> 210 us (0.972)
  Pallas kernels: 68.8 us -> 63.2 us
    all_gather x1, waiting for transfers between devices: 0.01 us -> 23.5 us  [on_device(): weights = lax.all_gather(beam_weights, 'col', axis=0)]
    all_to_all x1, waiting for transfers between devices: 17.6 us -> 0.01 us  [turn(): return lax.all_to_all(piece, axis, split_axis=0, concat_axis=0, tiled=True)]
    ppermute x16, waiting for transfers between devices: 27.6 us -> 21.3 us  [along(): lax.ppermute(value, axis, [(i, (i + step) % count) for i in range(count)])]
    unnamed x20 -> x24, local copies, waits for them, and re-layouts: 3.86 us -> 4.54 us
  transfers between devices with their start and end apart: 19 -> 19, of which waited for: 8 -> 8; matrix products, arithmetic and copies ran while one was open for 2% -> 2% of each run, Pallas kernels for 30% -> 28%
where the time goes in v5:
time: 210 us; the launch traced here: 208 us
  Pallas kernels  63.2 us (30%)
  blocking collectives  51 us (24%)
  waiting for transfers between devices  45.5 us (22%)
  starting transfers between devices  25.5 us (12%)
  between operations  14.2 us (7%)
  local copies, waits for them, and re-layouts  5.97 us (3%)
  other arithmetic  2.71 us (1%)
    all_to_all x2, blocking collectives, turn(): return lax.all_to_all(piece, axis, split_axis=0, concat_axis=0, tiled=True)  51 us
    all_gather x1, waiting for transfers between devices, on_device(): weights = lax.all_gather(beam_weights, 'col', axis=0)  23.5 us
    ppermute x16, waiting for transfers between devices, along(): lax.ppermute(value, axis, [(i, (i + step) % count) for i in range(count)])  21.3 us
    ppermute x16, starting transfers between devices, along(): lax.ppermute(value, axis, [(i, (i + step) % count) for i in range(count)])  17.6 us
    pallas_call x2, Pallas kernels, near_products(): pl.pallas_call(functools.partial(near_kernel, by_row, first), out_shape=s...  16.7 us
    pallas_call x2, Pallas kernels, far_products(): pl.pallas_call(functools.partial(far_kernel, by_row), out_shape=[pltpu.HB...  10.5 us
    pallas_call x1, Pallas kernels, own_beams(): pl.pallas_call(beam_kernel, out_shape=jax.ShapeDtypeStruct((owners, size,...  7 us
    pallas_call x1, Pallas kernels, spectra(): pl.pallas_call(functools.partial(spectrum_kernel, chunks), out_shape=[jax...  6.55 us
  transfers between devices with their start and end apart: 19, of which 8 were waited for; matrix products, arithmetic and copies ran while one was open for 2% of the time, Pallas kernels for 28%

profile of v5, /device:TPU:6, one launch (start us, length us, event | category | flops | bytes accessed | tf_op | source)
XLA Modules:
  0.0 208.1 jit_solution(16514075815060403664)
XLA Ops:
  7.2 0.0 all-gather.3.cloned.1.call-start
  7.2 0.7 all-gather.3.cloned.1.call-update
  7.9 0.9 slice.3
  8.8 3.5 %collective-permute-start = (bf16[2,64,384]{2,1,0:T(8,128)(2,1)S(1)}, bf16[2,64,384]{2,1,0:T(8,128)(2,1)S(1)}, u32[]{:S(2)}, u32[]{:S(2)}) collective-permute-start(bf16[2,64,384]{2,1,0:T(8,128)(2,1)S(1)} %slice.3), channel_id=1, source_target_pairs={{0,1},{1,2},{2,3},{3,4},{4,5},{5,6},{6,7},{7,8},{8,9},{9,10},{10,1... | collective-permute-start | bytes 294920 | tf_op jit(solution)/shard_map/ppermute | solution.py:56
  12.3 6.4 %shard_map.77.filt_ref = f32[2,4096,128]{2,1,0:T(8,128)S(1)} custom-call(bf16[2,64,8192]{2,1,0:T(8,128)(2,1)} %v_hbm.1, s32[1,64]{1,0:T(1,128)} %bitcast.13, f32[4,128]{1,0:T(4,128)} %constant.11.clone.coeff_hbm), custom_call_target="tpu_custom_call" | custom-call | flops 5500000256 | bytes 1 | tf_op jit(solution)/shard_map/pallas_call | solution.py:176
  18.8 6.6 %shard_map.78 = (bf16[16,5,64,128]{3,2,1,0:T(8,128)(2,1)S(1)}, bf16[16,3,64,128]{3,2,1,0:T(8,128)(2,1)}) custom-call(f32[2,4096,128]{2,1,0:T(8,128)S(1)} %shard_map.77.filt_ref, bf16[2,64,384]{2,1,0:T(8,128)(2,1)S(1)} %collective-permute-done.halo_ref, s32[1,64]{1,0:T(1,128)} %bitcast.14, s32[1,128]{1,0:T(1,128)} %bitcast.15, ...), custom_call_target="tpu_custom_call" | custom-call | flops 6600000000 | bytes 1 | tf_op jit(solution)/shard_map/pallas_call | solution.py:191
  25.3 42.0 %all_to_all.15.own_ref.refs_0_.refs_5_ = bf16[16,5,64,128]{3,2,1,0:T(8,128)(2,1)S(1)} all-to-all(bf16[16,5,64,128]{3,2,1,0:T(8,128)(2,1)S(1)} %get-tuple-element.24), channel_id=1, replica_groups=mesh['chan'=16,'row'=4,'col'=4] {'chan'}, dimensions={0} | all-to-all | bytes 2621440 | tf_op jit(solution)/shard_map/all_to_all | solution.py:554
  67.3 4.3 %all-to-all-start = ((bf16[16,3,64,128]{3,2,1,0:T(8,128)(2,1)}), bf16[16,3,64,128]{3,2,1,0:T(8,128)(2,1)}, u32[]{:S(2)}, u32[]{:S(2)}) async-start(bf16[16,3,64,128]{3,2,1,0:T(8,128)(2,1)} %get-tuple-element.23), calls=%async_computation | async-start | bytes 1572864 | tf_op jit(solution)/shard_map/all_to_all | solution.py:554
  71.6 0.9 collective-permute-start.4
  72.5 2.4 %collective-permute-start.3 = (bf16[16,5,64,128]{3,2,1,0:T(8,128)(2,1)S(1)}, bf16[16,5,64,128]{3,2,1,0:T(8,128)(2,1)}, u32[]{:S(2)}, u32[]{:S(2)}) collective-permute-start(bf16[16,5,64,128]{3,2,1,0:T(8,128)(2,1)S(1)} %all_to_all.15.own_ref.refs_0_.refs_5_), channel_id=1, source_target_pairs={{0,4},{4,8},{8,12},{12,0},{1,5},{5,9},{9,13},{13,1},{2,6},{6,10},{... | collective-permute-start | bytes 3932168 | tf_op jit(solution)/shard_map/ppermute | solution.py:535
  74.9 23.5 %all-gather.3.cloned.1.call-done = bf16[8,8,64,1024]{3,2,1,0:T(8,128)(2,1)} async-done(((bf16[2,8,64,1024]{3,2,1,0:T(8,128)(2,1)}), bf16[8,8,64,1024]{3,2,1,0:T(8,128)(2,1)}) %all-gather.3.cloned.1.call-update) | async-done | bytes 8388624 | tf_op jit(solution)/shard_map/all_gather | solution.py:550
  98.5 7.0 %shard_map.79.refs_1_ = f32[4,5,8,64]{3,2,1,0:T(8,128)} custom-call(bf16[16,5,64,128]{3,2,1,0:T(8,128)(2,1)} %copy-done, bf16[4,2,8,64,1024]{4,3,2,1,0:T(8,128)(2,1)} %bitcast.12), custom_call_target="tpu_custom_call" | custom-call | flops 110000000 | bytes 1 | tf_op jit(solution)/shard_map/pallas_call | solution.py:452
  105.5 0.0 collective-permute-done.4.high_ref.refs_2_.refs_7_.next_ref
  105.5 0.0 collective-permute-done.3.low_ref.refs_1_.refs_6_.prev_ref
  105.5 2.2 %shard_map.80 = (bf16[8,5,64,128]{3,2,1,0:T(8,128)(2,1)}, bf16[8,5,64,128]{3,2,1,0:T(8,128)(2,1)}) custom-call(bf16[16,5,64,128]{3,2,1,0:T(8,128)(2,1)} %collective-permute-done.3.low_ref.refs_1_.refs_6_.prev_ref, bf16[16,5,64,128]{3,2,1,0:T(8,128)(2,1)} %collective-permute-done.4.high_ref.refs_2_.refs_7_.next_ref, ...), custom_call_target="tpu_custom_call" | custom-call | flops 110000000 | bytes 1 | tf_op jit(solution)/shard_map/pallas_call | solution.py:225
  107.7 2.0 collective-permute-start.5
  109.7 0.0 collective-permute-start.6
  109.7 1.7 collective-permute-start.2
  111.5 0.3 collective-permute-start.1
  111.8 0.6 pad_add_fusion.1.place_ref
  112.4 12.1 %collective-permute-done.5.refs_3_.refs_8_.low_ref = bf16[8,5,64,128]{3,2,1,0:T(8,128)(2,1)} collective-permute-done((bf16[8,5,64,128]{3,2,1,0:T(8,128)(2,1)}, bf16[8,5,64,128]{3,2,1,0:T(8,128)(2,1)}, u32[]{:S(2)}, u32[]{:S(2)}) %collective-permute-start.5) | collective-permute-done | bytes 655392 | tf_op jit(solution)/shard_map/ppermute | solution.py:535
  124.5 2.9 %collective-permute-done.6.refs_4_.refs_9_.high_ref = bf16[8,5,64,128]{3,2,1,0:T(8,128)(2,1)} collective-permute-done((bf16[8,5,64,128]{3,2,1,0:T(8,128)(2,1)}, bf16[8,5,64,128]{3,2,1,0:T(8,128)(2,1)}, u32[]{:S(2)}, u32[]{:S(2)}) %collective-permute-start.6) | collective-permute-done | bytes 655392 | tf_op jit(solution)/shard_map/ppermute | solution.py:535
  127.4 6.0 %shard_map.81 = (bf16[5,256,256]{2,1,0:T(8,128)(2,1)}, bf16[5,256,256]{2,1,0:T(8,128)(2,1)}) custom-call(s32[2]{0:T(128)} %pad_add_fusion.1.place_ref, bf16[16,5,64,128]{3,2,1,0:T(8,128)(2,1)} %copy-done, bf16[16,5,64,128]{3,2,1,0:T(8,128)(2,1)} %collective-permute-done.3.low_ref.refs_1_.refs_6_.prev_ref, ...), custom_call_target="tpu_custom_call" | custom-call | flops 110000000 | bytes 1 | tf_op jit(solution)/shard_map/pallas_call | solution.py:299
  133.3 0.9 collective-permute-start.10
  134.2 1.2 collective-permute-start.9
  135.4 0.0 collective-permute-done.2.high_ref.next_ref.refs_2_.refs_7_
  135.5 0.0 collective-permute-done.1.low_ref.prev_ref.refs_1_.refs_6_
  135.5 0.9 copy-done.1
  136.3 0.9 copy-done.2
  137.2 2.0 shard_map.82
  139.3 2.0 collective-permute-start.8
  141.3 8.4 %shard_map.84 = (f32[2,5,256,256]{3,2,1,0:T(8,128)}, bf16[2,5,256,256]{3,2,1,0:T(8,128)(2,1)}, bf16[2,5,256,256]{3,2,1,0:T(8,128)(2,1)}) custom-call(s32[2]{0:T(128)} %pad_add_fusion.1.place_ref, bf16[16,5,64,128]{3,2,1,0:T(8,128)(2,1)} %copy-done, bf16[16,5,64,128]{3,2,1,0:T(8,128)(2,1)} %collective-permute-done.3.low_ref.refs_1_.refs_6_.prev_ref, ...), custom_call_target="tpu_custom_call" | custom-call | flops 110000000 | bytes 1 | tf_op jit(solution)/shard_map/pallas_call | solution.py:420
  149.7 1.7 collective-permute-done.10.high_ref
  151.4 2.0 collective-permute-done.9.low_ref
  153.4 2.9 %shard_map.85 = (bf16[2,5,256,256]{3,2,1,0:T(8,128)(2,1)}, bf16[2,5,256,256]{3,2,1,0:T(8,128)(2,1)}) custom-call(bf16[2,5,256,256]{3,2,1,0:T(8,128)(2,1)} %get-tuple-element.33.up_ref, bf16[2,5,256,256]{3,2,1,0:T(8,128)(2,1)} %get-tuple-element.34.down_ref, ...), custom_call_target="tpu_custom_call", output_to_operand_aliasing={{0}: (0, {}), {1}: (1, {})} | custom-call | flops 110000000 | bytes 1 | tf_op jit(solution)/shard_map/pallas_call | solution.py:478
  156.3 1.4 collective-permute-start.16
  157.8 0.6 collective-permute-start.15
  158.4 0.6 pad_add_fusion.place_ref
  159.0 0.7 collective-permute-done.8.high_ref.refs_4_.refs_9_
  159.7 1.2 collective-permute-done.7.low_ref.refs_3_.refs_8_
  161.0 0.7 copy-done.4
  161.7 4.5 %shard_map.86 = (bf16[3,256,256]{2,1,0:T(8,128)(2,1)}, bf16[3,256,256]{2,1,0:T(8,128)(2,1)}) custom-call(s32[2]{0:T(128)} %pad_add_fusion.place_ref, bf16[16,3,64,128]{3,2,1,0:T(8,128)(2,1)} %all-to-all-done.refs_0_.own_ref.refs_5_, bf16[16,3,64,128]{3,2,1,0:T(8,128)(2,1)} %copy-done.2, bf16[16,3,64,128]{3,2,1,0:T(8,128)(2,1)} %copy-done.1, ...), custom_call_target="tpu_custom_call" | custom-call | flops 110000000 | bytes 1 | tf_op jit(solution)/shard_map/pallas_call | solution.py:299
  166.2 0.7 collective-permute-start.11
  166.9 1.4 collective-permute-start.12
  168.3 8.2 %shard_map.83 = (f32[2,3,256,256]{3,2,1,0:T(8,128)}, bf16[2,3,256,256]{3,2,1,0:T(8,128)(2,1)}, bf16[2,3,256,256]{3,2,1,0:T(8,128)(2,1)}, f32[3,32,64]{2,1,0:T(8,128)}) custom-call(s32[2]{0:T(128)} %pad_add_fusion.place_ref, bf16[16,3,64,128]{3,2,1,0:T(8,128)(2,1)} %all-to-all-done.refs_0_.own_ref.refs_5_, bf16[16,3,64,128]{3,2,1,0:T(8,128)(2,1)} %copy-done.2, ...), custom_call_target="tpu_custom_call" | custom-call | flops 110000000 | bytes 1 | tf_op jit(solution)/shard_map/pallas_call | solution.py:420
  176.6 0.0 copy-start.7
  176.6 0.0 collective-permute-done.11.low_ref
  176.6 0.0 copy-start.8
  176.6 0.7 copy-done.8
  177.4 0.2 copy-done.9
  177.5 2.4 %shard_map.87 = (bf16[2,3,256,256]{3,2,1,0:T(8,128)(2,1)}, bf16[2,3,256,256]{3,2,1,0:T(8,128)(2,1)}) custom-call(bf16[2,3,256,256]{3,2,1,0:T(8,128)(2,1)} %get-tuple-element.31.up_ref, bf16[2,3,256,256]{3,2,1,0:T(8,128)(2,1)} %get-tuple-element.32.down_ref, bf16[3,256,256]{2,1,0:T(8,128)(2,1)} %copy-done.8, ...), custom_call_target="tpu_custom_call", output_to_operand_aliasing={{0}: (0, {}), {1}: (1, {})} | custom-call | flops 110000000 | bytes 1 | tf_op jit(solution)/shard_map/pallas_call | solution.py:478
  179.9 1.8 collective-permute-start.13
  181.7 0.2 collective-permute-start.14
  181.9 0.1 reshape.17
  182.0 9.0 %all_to_all.16 = f32[4,1,2560]{2,1,0:T(1,128)S(1)} all-to-all(f32[4,1,2560]{2,1,0:T(1,128)S(1)} %reshape.17), channel_id=1, replica_groups=mesh['chan'=16,'row'=4,'col'=4] {'col'}, dimensions={0} | all-to-all | bytes 81920 | tf_op jit(solution)/shard_map/all_to_all | solution.py:554
  191.0 0.5 broadcast
  191.5 0.8 reduce
  192.3 0.1 reshape.18
  192.4 0.7 maximum_bitcast_fusion
  193.1 3.7 %shard_map.88.refs_0_ = f32[2,8,256,256]{3,2,1,0:T(8,128)} custom-call(f32[2,5,256,256]{3,2,1,0:T(8,128)} %get-tuple-element.41.own_ref, bf16[2,5,256,256]{3,2,1,0:T(8,128)(2,1)} %collective-permute-done.15.prev_ref, bf16[2,5,256,256]{3,2,1,0:T(8,128)(2,1)} %collective-permute-done.16.next_ref), custom_call_target="tpu_custom_call" | custom-call | flops 110000000 | bytes 1 | tf_op jit(solution)/shard_map/pallas_call | solution.py:517
  196.8 0.7 collective-permute-done.14.next_ref
  197.5 0.2 copy-done.5
  197.7 0.7 copy-done.6
  198.4 2.8 %shard_map.89 = f32[2,8,256,256]{3,2,1,0:T(8,128)} custom-call(f32[2,3,256,256]{3,2,1,0:T(8,128)} %get-tuple-element.30.own_ref, bf16[2,3,256,256]{3,2,1,0:T(8,128)(2,1)} %copy-done.5, bf16[2,3,256,256]{3,2,1,0:T(8,128)(2,1)} %copy-done.6, f32[2,8,256,256]{3,2,1,0:T(8,128)} %shard_map.88.refs_0_), custom_call_target="tpu_custom_call", output_to_operand_aliasing={{}: (3, {})} | custom-call | flops 110000000 | bytes 1 | tf_op jit(solution)/shard_map/pallas_call | solution.py:517
  (21 shorter events, 0.1 us)
Async XLA Ops:
  7.2 91.3 %all-gather.3.cloned.1.call-start = ((), (), s32[]{:S(2)}) async-start(), calls=%async_computation.3 | async-start | bytes 10485760 | tf_op jit(solution)/shard_map/all_gather | solution.py:550
  8.8 9.9 %collective-permute-start = (bf16[2,64,384]{2,1,0:T(8,128)(2,1)S(1)}, bf16[2,64,384]{2,1,0:T(8,128)(2,1)S(1)}, u32[]{:S(2)}, u32[]{:S(2)}) collective-permute-start(bf16[2,64,384]{2,1,0:T(8,128)(2,1)S(1)} %slice.3), channel_id=1, source_target_pairs={{0,1},{1,2},{2,3},{3,4},{4,5},{5,6},{6,7},{7,8},{8,9},{9,10},{10,1... | collective-permute-start | bytes 294920 | tf_op jit(solution)/shard_map/ppermute | solution.py:56
  67.3 31.1 %copy-start = (bf16[16,5,64,128]{3,2,1,0:T(8,128)(2,1)}, bf16[16,5,64,128]{3,2,1,0:T(8,128)(2,1)S(1)}, u32[]{:S(2)}) copy-start(bf16[16,5,64,128]{3,2,1,0:T(8,128)(2,1)S(1)} %all_to_all.15.own_ref.refs_0_.refs_5_) | copy-start | bytes 3932164
  67.3 38.1 %all-to-all-start = ((bf16[16,3,64,128]{3,2,1,0:T(8,128)(2,1)}), bf16[16,3,64,128]{3,2,1,0:T(8,128)(2,1)}, u32[]{:S(2)}, u32[]{:S(2)}) async-start(bf16[16,3,64,128]{3,2,1,0:T(8,128)(2,1)} %get-tuple-element.23), calls=%async_computation | async-start | bytes 1572864 | tf_op jit(solution)/shard_map/all_to_all | solution.py:554
  71.6 33.8 %collective-permute-start.4 = (bf16[16,5,64,128]{3,2,1,0:T(8,128)(2,1)S(1)}, bf16[16,5,64,128]{3,2,1,0:T(8,128)(2,1)}, u32[]{:S(2)}, u32[]{:S(2)}) collective-permute-start(bf16[16,5,64,128]{3,2,1,0:T(8,128)(2,1)S(1)} %all_to_all.15.own_ref.refs_0_.refs_5_), channel_id=1, source_target_pairs={{0,12},{4,0},{8,4},{12,8},{1,13},{5,1},{9,5},{13,9},{2,14},{6,2},{... | collective-permute-start | bytes 3932168 | tf_op jit(solution)/shard_map/ppermute | solution.py:535
  72.5 32.9 %collective-permute-start.3 = (bf16[16,5,64,128]{3,2,1,0:T(8,128)(2,1)S(1)}, bf16[16,5,64,128]{3,2,1,0:T(8,128)(2,1)}, u32[]{:S(2)}, u32[]{:S(2)}) collective-permute-start(bf16[16,5,64,128]{3,2,1,0:T(8,128)(2,1)S(1)} %all_to_all.15.own_ref.refs_0_.refs_5_), channel_id=1, source_target_pairs={{0,4},{4,8},{8,12},{12,0},{1,5},{5,9},{9,13},{13,1},{2,6},{6,10},{... | collective-permute-start | bytes 3932168 | tf_op jit(solution)/shard_map/ppermute | solution.py:535
  107.7 16.8 %collective-permute-start.5 = (bf16[8,5,64,128]{3,2,1,0:T(8,128)(2,1)}, bf16[8,5,64,128]{3,2,1,0:T(8,128)(2,1)}, u32[]{:S(2)}, u32[]{:S(2)}) collective-permute-start(bf16[8,5,64,128]{3,2,1,0:T(8,128)(2,1)} %get-tuple-element.25), channel_id=1, source_target_pairs={{0,4},{4,8},{8,12},{12,0},{1,5},{5,9},{9,13},{13,1},{2,6},{6,10},{... | collective-permute-start | bytes 1966088 | tf_op jit(solution)/shard_map/ppermute | solution.py:535
  109.7 17.7 %collective-permute-start.6 = (bf16[8,5,64,128]{3,2,1,0:T(8,128)(2,1)}, bf16[8,5,64,128]{3,2,1,0:T(8,128)(2,1)}, u32[]{:S(2)}, u32[]{:S(2)}) collective-permute-start(bf16[8,5,64,128]{3,2,1,0:T(8,128)(2,1)} %get-tuple-element.26), channel_id=1, source_target_pairs={{0,12},{4,0},{8,4},{12,8},{1,13},{5,1},{9,5},{13,9},{2,14},{6,2},{... | collective-permute-start | bytes 1966088 | tf_op jit(solution)/shard_map/ppermute | solution.py:535
  109.7 25.7 %collective-permute-start.2 = (bf16[16,3,64,128]{3,2,1,0:T(8,128)(2,1)}, bf16[16,3,64,128]{3,2,1,0:T(8,128)(2,1)S(1)}, u32[]{:S(2)}, u32[]{:S(2)}) collective-permute-start(bf16[16,3,64,128]{3,2,1,0:T(8,128)(2,1)} %all-to-all-done.refs_0_.own_ref.refs_5_), channel_id=1, source_target_pairs={{0,3},{1,0},{2,1},{3,2},{4,7},{5,4},{6,5},{7,6},{8,11},{9,8},{10,9... | collective-permute-start | bytes 2359304 | tf_op jit(solution)/shard_map/ppermute | solution.py:535
  111.5 24.0 %collective-permute-start.1 = (bf16[16,3,64,128]{3,2,1,0:T(8,128)(2,1)}, bf16[16,3,64,128]{3,2,1,0:T(8,128)(2,1)S(1)}, u32[]{:S(2)}, u32[]{:S(2)}) collective-permute-start(bf16[16,3,64,128]{3,2,1,0:T(8,128)(2,1)} %all-to-all-done.refs_0_.own_ref.refs_5_), channel_id=1, source_target_pairs={{0,1},{1,2},{2,3},{3,0},{4,5},{5,6},{6,7},{7,4},{8,9},{9,10},{10,1... | collective-permute-start | bytes 2359304 | tf_op jit(solution)/shard_map/ppermute | solution.py:535
  133.3 18.1 %collective-permute-start.10 = (bf16[5,256,256]{2,1,0:T(8,128)(2,1)}, bf16[5,256,256]{2,1,0:T(8,128)(2,1)}, u32[]{:S(2)}, u32[]{:S(2)}) collective-permute-start(bf16[5,256,256]{2,1,0:T(8,128)(2,1)} %get-tuple-element.35), channel_id=1, source_target_pairs={{0,3},{1,0},{2,1},{3,2},{4,7},{5,4},{6,5},{7,6},{8,11},{9,8},{10,9... | collective-permute-start | bytes 1966088 | tf_op jit(solution)/shard_map/ppermute | solution.py:535
  134.2 19.2 %collective-permute-start.9 = (bf16[5,256,256]{2,1,0:T(8,128)(2,1)}, bf16[5,256,256]{2,1,0:T(8,128)(2,1)}, u32[]{:S(2)}, u32[]{:S(2)}) collective-permute-start(bf16[5,256,256]{2,1,0:T(8,128)(2,1)} %get-tuple-element.27.refs_0_), channel_id=1, source_target_pairs={{0,1},{1,2},{2,3},{3,0},{4,5},{5,6},{6,7},{7,4},{8,9},{9,10},{10,1... | collective-permute-start | bytes 1966088 | tf_op jit(solution)/shard_map/ppermute | solution.py:535
  135.4 0.9 copy-start.1
  136.3 0.9 copy-start.2
  139.3 20.5 %collective-permute-start.8 = (bf16[8,3,64,128]{3,2,1,0:T(8,128)(2,1)}, bf16[8,3,64,128]{3,2,1,0:T(8,128)(2,1)S(1)}, u32[]{:S(2)}, u32[]{:S(2)}) collective-permute-start(bf16[8,3,64,128]{3,2,1,0:T(8,128)(2,1)} %get-tuple-element.29), channel_id=1, source_target_pairs={{0,3},{1,0},{2,1},{3,2},{4,7},{5,4},{6,5},{7,6},{8,11},{9,8},{10,9... | collective-permute-start | bytes 1179656 | tf_op jit(solution)/shard_map/ppermute | solution.py:535
  141.3 19.7 %collective-permute-start.7 = (bf16[8,3,64,128]{3,2,1,0:T(8,128)(2,1)}, bf16[8,3,64,128]{3,2,1,0:T(8,128)(2,1)S(1)}, u32[]{:S(2)}, u32[]{:S(2)}) collective-permute-start(bf16[8,3,64,128]{3,2,1,0:T(8,128)(2,1)} %get-tuple-element.28.refs_0_), channel_id=1, source_target_pairs={{0,1},{1,2},{2,3},{3,0},{4,5},{5,6},{6,7},{7,4},{8,9},{9,10},{10,1... | collective-permute-start | bytes 1179656 | tf_op jit(solution)/shard_map/ppermute | solution.py:535
  156.3 36.8 %collective-permute-start.16 = (bf16[2,5,256,256]{3,2,1,0:T(8,128)(2,1)}, bf16[2,5,256,256]{3,2,1,0:T(8,128)(2,1)}, u32[]{:S(2)}, u32[]{:S(2)}) collective-permute-start(bf16[2,5,256,256]{3,2,1,0:T(8,128)(2,1)} %get-tuple-element.42), channel_id=1, source_target_pairs={{0,3},{1,0},{2,1},{3,2},{4,7},{5,4},{6,5},{7,6},{8,11},{9,8},{10,9... | collective-permute-start | bytes 3932168 | tf_op jit(solution)/shard_map/ppermute | solution.py:535
  157.8 35.3 %collective-permute-start.15 = (bf16[2,5,256,256]{3,2,1,0:T(8,128)(2,1)}, bf16[2,5,256,256]{3,2,1,0:T(8,128)(2,1)}, u32[]{:S(2)}, u32[]{:S(2)}) collective-permute-start(bf16[2,5,256,256]{3,2,1,0:T(8,128)(2,1)} %get-tuple-element.36.refs_10_), channel_id=1, source_target_pairs={{0,1},{1,2},{2,3},{3,0},{4,5},{5,6},{6,7},{7,4},{8,9},{9,10},{10,1... | collective-permute-start | bytes 3932168 | tf_op jit(solution)/shard_map/ppermute | solution.py:535
  159.7 1.2 copy-start.3
  161.0 0.7 copy-start.4
  166.2 10.4 %collective-permute-start.11 = (bf16[3,256,256]{2,1,0:T(8,128)(2,1)}, bf16[3,256,256]{2,1,0:T(8,128)(2,1)S(1)}, u32[]{:S(2)}, u32[]{:S(2)}) collective-permute-start(bf16[3,256,256]{2,1,0:T(8,128)(2,1)} %get-tuple-element.37), channel_id=1, source_target_pairs={{0,4},{4,8},{8,12},{12,0},{1,5},{5,9},{9,13},{13,1},{2,6},{6,10},{... | collective-permute-start | bytes 1179656 | tf_op jit(solution)/shard_map/ppermute | solution.py:535
  166.9 9.7 %collective-permute-start.12 = (bf16[3,256,256]{2,1,0:T(8,128)(2,1)}, bf16[3,256,256]{2,1,0:T(8,128)(2,1)S(1)}, u32[]{:S(2)}, u32[]{:S(2)}) collective-permute-start(bf16[3,256,256]{2,1,0:T(8,128)(2,1)} %get-tuple-element.38), channel_id=1, source_target_pairs={{0,12},{4,0},{8,4},{12,8},{1,13},{5,1},{9,5},{13,9},{2,14},{6,2},{... | collective-permute-start | bytes 1179656 | tf_op jit(solution)/shard_map/ppermute | solution.py:535
  176.6 5.3 %copy-start.7 = (f32[4,5,8,64]{3,2,1,0:T(8,128)S(1)}, f32[4,5,8,64]{3,2,1,0:T(8,128)}, u32[]{:S(2)}) copy-start(f32[4,5,8,64]{3,2,1,0:T(8,128)} %shard_map.79.refs_1_) | copy-start | bytes 122884
  176.6 0.7 copy-start.8
  176.6 0.9 copy-start.9
  177.5 14.9 %copy-start.10 = (f32[3,32,64]{2,1,0:T(8,128)S(1)}, f32[3,32,64]{2,1,0:T(8,128)}, u32[]{:S(2)}) copy-start(f32[3,32,64]{2,1,0:T(8,128)} %get-tuple-element.43) | copy-start | bytes 73732
  179.9 16.9 %collective-permute-start.13 = (bf16[2,3,256,256]{3,2,1,0:T(8,128)(2,1)}, bf16[2,3,256,256]{3,2,1,0:T(8,128)(2,1)S(1)}, u32[]{:S(2)}, u32[]{:S(2)}) collective-permute-start(bf16[2,3,256,256]{3,2,1,0:T(8,128)(2,1)} %get-tuple-element.39), channel_id=1, source_target_pairs={{0,4},{4,8},{8,12},{12,0},{1,5},{5,9},{9,13},{13,1},{2,6},{6,10},{... | collective-permute-start | bytes 2359304 | tf_op jit(solution)/shard_map/ppermute | solution.py:535
  181.7 15.8 %collective-permute-start.14 = (bf16[2,3,256,256]{3,2,1,0:T(8,128)(2,1)}, bf16[2,3,256,256]{3,2,1,0:T(8,128)(2,1)S(1)}, u32[]{:S(2)}, u32[]{:S(2)}) collective-permute-start(bf16[2,3,256,256]{3,2,1,0:T(8,128)(2,1)} %get-tuple-element.40), channel_id=1, source_target_pairs={{0,12},{4,0},{8,4},{12,8},{1,13},{5,1},{9,5},{13,9},{2,14},{6,2},{... | collective-permute-start | bytes 2359304 | tf_op jit(solution)/shard_map/ppermute | solution.py:535
  196.8 0.9 copy-start.5
  197.5 0.9 copy-start.6
Sparse Core Ops, SparseCore 0:
  9.8 88.6 all-gather.2

commit v6 on v5

--- a/solution.py
+++ b/solution.py
@@ -12,7 +12,7 @@
 NCH = 128
 TAPS = 4
 INTEG = 8
-CHUNKS = (5, 3)
+CHUNKS = (3, 3, 2)
 
 F32 = jnp.float32
 BF16 = jnp.bfloat16
@@ -64,22 +64,31 @@
     return jnp.broadcast_to(jnp.sum(held, axis=1, keepdims=True), (inputs, NCH))
 
 
-def filter_kernel(v_hbm, flags_hbm, coeff_hbm, filt_ref, v_ref, flags_ref, coeff_ref, sems):
-    copies = [
-        pltpu.make_async_copy(src, dst, sems.at[n])
-        for n, (src, dst) in enumerate(
-            ((v_hbm, v_ref), (flags_hbm, flags_ref), (coeff_hbm, coeff_ref))
-        )
-    ]
-    for copy in copies:
+def filter_kernel(
+    first, v_hbm, flags_hbm, coeff_hbm, w_hbm, filt_ref, cut_hbm, v_ref, flags_ref, coeff_ref, w_ref, sems
+):
+    pairs = (
+        (v_hbm.at[0], v_ref.at[0]),
+        (flags_hbm, flags_ref),
+        (coeff_hbm, coeff_ref),
+        (v_hbm.at[1], v_ref.at[1]),
+        (w_hbm.at[:, first : first + w_ref.shape[1]], w_ref),
+        (w_ref, cut_hbm),
+    )
+    copies = [pltpu.make_async_copy(src, dst, sems.at[n]) for n, (src, dst) in enumerate(pairs)]
+    for copy in copies[:5]:
         copy.start()
-    for copy in copies:
+    for copy in copies[:3]:
         copy.wait()
     inputs = v_ref.shape[1]
     frames = v_ref.shape[2] // NCH
     mask = flag_column(flags_ref[...], inputs)
     taps = [jnp.broadcast_to(coeff_ref[t : t + 1, :], (inputs, NCH)) * mask for t in range(TAPS)]
     for part in range(2):
+        if part == 1:
+            copies[3].wait()
+            copies[4].wait()
+            copies[5].start()
 
         def frame_step(f, past, part=part):
             lanes = pl.ds(pl.multiple_of(f * NCH, NCH), NCH)
@@ -92,6 +101,7 @@
 
         zero = v_ref[part, :, :NCH].astype(F32) * 0.0
         lax.fori_loop(0, frames, frame_step, (zero,) * (TAPS - 1), unroll=8)
+    copies[5].wait()
 
 
 def spectrum_kernel(chunks, filt_ref, halo_ref, flags_hbm, order_hbm, coeff_hbm, table_hbm, *rest):
@@ -168,27 +178,29 @@
     lax.fori_loop(0, NCH // per_block, copy_step, 0)
 
 
-def spectra(voltages, history, flags, order, chunks):
+def spectra(voltages, history, flags, order, weights, chunks):
     inputs = voltages.shape[1]
     frames = voltages.shape[2] // NCH
     flags = flags.reshape(1, inputs)
     coeff = jnp.asarray(prototype(TAPS, NCH))
-    filtered = pl.pallas_call(
-        filter_kernel,
-        out_shape=jax.ShapeDtypeStruct((2, inputs * frames, NCH), F32),
-        in_specs=[HBM] * 3,
-        out_specs=VMEM,
+    held = (2, chunks[1]) + weights.shape[2:]
+    filtered, cut = pl.pallas_call(
+        functools.partial(filter_kernel, chunks[0]),
+        out_shape=[jax.ShapeDtypeStruct((2, inputs * frames, NCH), F32), pltpu.HBM(held, BF16)],
+        in_specs=[HBM] * 4,
+        out_specs=[VMEM, HBM],
         scratch_shapes=[
             pltpu.VMEM(voltages.shape, BF16),
             pltpu.VMEM((1, inputs), jnp.int32),
             pltpu.VMEM((TAPS, NCH), F32),
-            pltpu.SemaphoreType.DMA((3,)),
+            pltpu.VMEM(held, BF16),
+            pltpu.SemaphoreType.DMA((6,)),
         ],
         compiler_params=limit(16),
         cost_estimate=cost(5),
-    )(in_hbm(voltages), in_hbm(flags), in_hbm(coeff))
+    )(in_hbm(voltages), in_hbm(flags), in_hbm(coeff), in_hbm(weights))
     blocks = NCH // sum(chunks)
-    return pl.pallas_call(
+    pieces = pl.pallas_call(
         functools.partial(spectrum_kernel, chunks),
         out_shape=[jax.ShapeDtypeStruct((blocks, size, inputs, 2 * frames), BF16) for size in chunks],
         in_specs=[VMEM, VMEM] + [HBM] * 4,
@@ -209,6 +221,7 @@
         history,
         *[in_hbm(x) for x in (flags, order.reshape(1, NCH), coeff, jnp.asarray(dft_table(NCH)))],
     )
+    return pieces, cut
 
 
 def halves_kernel(low_ref, high_ref, *refs):
@@ -432,7 +445,8 @@
     )(place, *args)
 
 
-def beam_kernel(own_ref, w_ref, out_ref):
+def beam_kernel(own_ref, w_ref, *refs):
+    out_ref = refs[-1]
     blocks, _, inputs, lanes = own_ref.shape
     owners, _, _, beams, total = w_ref.shape
     x = own_ref[:, 0].reshape(blocks * inputs, lanes)
@@ -445,7 +459,7 @@
         out_ref[owner, 0] = power[:, owner * beams : (owner + 1) * beams]
 
 
-def own_beams(own, weights, first=0):
+def own_beams(own, weights, first=0, after=()):
     blocks, size, inputs, lanes = own.shape
     owners, _, _, beams, total = weights.shape
     bins = lanes // 2 // INTEG
@@ -456,11 +470,12 @@
         in_specs=[
             pl.BlockSpec((blocks, 1, inputs, lanes), lambda k: (0, k, 0, 0)),
             pl.BlockSpec((owners, 2, 1, beams, total), lambda k: (0, 0, first + k, 0, 0)),
-        ],
+        ]
+        + [ANY] * len(after),
         out_specs=pl.BlockSpec((owners, 1, bins, beams), lambda k: (0, k, 0, 0)),
         compiler_params=limit(62),
         cost_estimate=cost(0.1),
-    )(in_hbm(own), in_hbm(weights))
+    )(in_hbm(own), in_hbm(weights), *after)
 
 
 def add_kernel(up_ref, down_ref, low_ref, high_ref, *refs):
@@ -488,7 +503,8 @@
 
 
 def final_kernel(first, own_ref, prev_ref, next_ref, *refs):
-    out_hbm, held, sems = refs[-3:]
+    out_hbm, token_ref, held, sems = refs[-4:]
+    token_ref[...] = jnp.zeros_like(token_ref)
     size = own_ref.shape[1]
     p = pl.program_id(0)
 
@@ -510,16 +526,19 @@
         copy(1).wait()
 
 
-def finished(own, from_prev, from_next, first, channels, out):
+def finished(own, from_prev, from_next, first, channels, out, after=()):
     _, size, panel, _ = own.shape
     block = pl.BlockSpec((1, size, panel, panel), lambda p: (p, 0, 0, 0))
     extra = [] if out is None else [out]
     return pl.pallas_call(
         functools.partial(final_kernel, first),
-        out_shape=jax.ShapeDtypeStruct((2, channels, panel, panel), F32),
+        out_shape=[
+            jax.ShapeDtypeStruct((2, channels, panel, panel), F32),
+            jax.ShapeDtypeStruct((8, NCH), F32),
+        ],
         grid=(2,),
-        in_specs=[block] * 3 + [ANY] * len(extra),
-        out_specs=HBM,
+        in_specs=[block] * 3 + [ANY] * (len(extra) + len(after)),
+        out_specs=[HBM, pl.BlockSpec((8, NCH), lambda p: (0, 0))],
         input_output_aliases={3: 0} if extra else {},
         scratch_shapes=[
             pltpu.VMEM((2, size, panel, panel), F32),
@@ -527,7 +546,7 @@
         ],
         compiler_params=limit(62),
         cost_estimate=cost(0.1),
-    )(in_hbm(own), from_prev, from_next, *extra)
+    )(in_hbm(own), from_prev, from_next, *extra, *after)
 
 
 def along(value, axis, step):
@@ -540,45 +559,61 @@
 
 
 def on_device(voltages, input_flags, channel_order, beam_weights):
-    size_b, size_a = CHUNKS
-    channels = size_a + size_b
+    firsts = [sum(CHUNKS[:n]) for n in range(len(CHUNKS))]
     history = passed_along(voltages[:, :, voltages.shape[2] - (TAPS - 1) * NCH :], ("row", "col"), 1)
     row = lax.axis_index("row").astype(jnp.int32)
     col = lax.axis_index("col").astype(jnp.int32)
-    place_a = jnp.stack([col, row])
-    place_b = jnp.stack([row, col])
-    weights = lax.all_gather(beam_weights, "col", axis=0)
-    piece_b, piece_a = spectra(voltages, history, input_flags, channel_order, CHUNKS)
+    by_row = (False, True, False)
+    places = [jnp.stack([row, col]) if turned else jnp.stack([col, row]) for turned in by_row]
+    gather = [("row" if turned else "col") for turned in by_row]
+    reduce = [("col" if turned else "row") for turned in by_row]
+    pieces, cut = spectra(voltages, history, input_flags, channel_order, beam_weights, CHUNKS)
+    weights = lax.all_gather(cut, "col", axis=0)
 
     def turn(piece, axis):
         return lax.all_to_all(piece, axis, split_axis=0, concat_axis=0, tiled=True)
 
-    own_b = turn(piece_b, "chan")
-    near_b = both_ways(own_b, own_b, "row")
-    own_a = turn(piece_a, "chan")
-    near_a = both_ways(own_a, own_a, "col")
-    beam_b = own_beams(own_b, weights)
-    far_b = both_ways(*halves(*near_b, [own_a, beam_b]), "row")
-    slots_b = (own_b, *near_b, *far_b)
-    re_b, im_b = far_products(place_b, slots_b, True)
-    got_b = both_ways(re_b, im_b, "col")
-    half_a = halves(*near_a, [re_b])
-    far_a = both_ways(*half_a, "col")
-    slots_a = (own_a, *near_a, *far_a)
-    mine_b, up_b, down_b = near_products(place_b, slots_b, True, after=[half_a[0]])
-    sum_b = added(up_b, down_b, *got_b)
-    sent_b = both_ways(*sum_b, "col")
-    re_a, im_a = far_products(place_a, slots_a, False, [sum_b[0]])
-    got_a = both_ways(re_a, im_a, "row")
-    mine_a, up_a, down_a, power_a = near_products(place_a, slots_a, False, size_b, beam_weights)
-    sum_a = added(up_a, down_a, *got_a)
-    sent_a = both_ways(*sum_a, "row")
-
-    power_b = jnp.transpose(turn(beam_b, "col"), (1, 0, 2, 3)).reshape(size_b, -1, beam_b.shape[3])
-    out = finished(mine_b, *sent_b, 0, channels, None)
-    visibility = finished(mine_a, *sent_a, size_b, channels, out)
-    power = jnp.concatenate([power_b, power_a], axis=0)
-    return (visibility, jnp.transpose(power, (0, 2, 1)))
+    own = [turn(piece, "chan") for piece in pieces]
+    near = [both_ways(x, x, axis) for x, axis in zip(own, gather)]
+
+    def spread(n, after):
+        half = halves(*near[n], after)
+        return half, (own[n], *near[n], *both_ways(*half, gather[n]))
+
+    def far(n, slots, after):
+        sides = far_products(places[n], slots, by_row[n], after)
+        return sides, both_ways(*sides, reduce[n])
+
+    def near_by(n, slots, after):
+        given = None if by_row[n] else beam_weights
+        return near_products(places[n], slots, by_row[n], firsts[n], given, after)
+
+    def send(n, results, got, after):
+        sums = added(results[1], results[2], *got, after)
+        return sums, both_ways(*sums, reduce[n])
+
+    def close(n, result, sent, out, after):
+        return finished(result[0], *sent, firsts[n], sum(CHUNKS), out, after)
+
+    half, slots0 = spread(0, [])
+    sides, got0 = far(0, slots0, [])
+    result0 = near_by(0, slots0, [sides[0]])
+    half, slots1 = spread(1, [result0[0]])
+    sums, sent0 = send(0, result0, got0, [half[0]])
+    beam1 = own_beams(own[1], weights, after=[sums[0]])
+    sides, got1 = far(1, slots1, [beam1])
+    half, slots2 = spread(2, [sides[0]])
+    result1 = near_by(1, slots1, [half[0]])
+    sums, sent1 = send(1, result1, got1, [])
+    out, token = close(0, result0, sent0, None, [sums[0]])
+    sides, got2 = far(2, slots2, [token])
+    result2 = near_by(2, slots2, [sides[0]])
+    sums, sent2 = send(2, result2, got2, [])
+    power1 = jnp.transpose(turn(beam1, "col"), (1, 0, 2, 3)).reshape(CHUNKS[1], -1, beam1.shape[3])
+    out, token = close(1, result1, sent1, out, [sums[0]])
+    out, token = close(2, result2, sent2, out, [])
+    power = jnp.concatenate([result0[3], power1, result2[3]], axis=0)
+    return (out, jnp.transpose(power, (0, 2, 1)))
 
 
 def solution(mesh):

time: 210 us -> 226 us (1.076)
  starting transfers between devices: 25.5 us -> 43.6 us
  blocking collectives: 51 us -> 40.5 us
  Pallas kernels: 63.2 us -> 73.6 us
  waiting for transfers between devices: 45.5 us -> 37.7 us
  local copies, waits for them, and re-layouts: 5.97 us -> 11.3 us
    all_gather x1, waiting for transfers between devices: 23.5 us -> 0.01 us  [on_device(): weights = lax.all_gather(cut, 'col', axis=0)]
    all_to_all x1 -> x2, waiting for transfers between devices: 0.01 us -> 18.8 us  [turn(): return lax.all_to_all(piece, axis, split_axis=0, concat_axis=0, tiled=True)]
    ppermute x16 -> x24, starting transfers between devices: 17.6 us -> 31.5 us  [along(): lax.ppermute(value, axis, [(i, (i + step) % count) for i in range(count)])]
    all_to_all x2, blocking collectives: 51 us -> 40.5 us  [turn(): return lax.all_to_all(piece, axis, split_axis=0, concat_axis=0, tiled=True)]
    unnamed x24 -> x38, local copies, waits for them, and re-layouts: 4.54 us -> 9.84 us
    pallas_call x2 -> x3, Pallas kernels: 16.7 us -> 20.9 us  [near_products(): pl.pallas_call(functools.partial(near_kernel, by_row, first), out_shape=s...]
    all_to_all x1 -> x2, starting transfers between devices: 4.29 us -> 8.53 us  [turn(): return lax.all_to_all(piece, axis, split_axis=0, concat_axis=0, tiled=True)]
    pallas_call x3 -> x4, Pallas kernels: 13 us -> 16 us  [the longest x3 9.9 us: finished(): pl.pallas_call(functools.partial(final_kernel, first), out_shape=[jax.Sha...]
  transfers between devices with their start and end apart: 19 -> 28, of which waited for: 8 -> 5; matrix products, arithmetic and copies ran while one was open for 2% -> 2% of each run, Pallas kernels for 28% -> 30%
where the time goes in v6:
time: 226 us; the launch traced here: 225 us
  Pallas kernels  73.6 us (33%)
  starting transfers between devices  43.6 us (19%)
  blocking collectives  40.5 us (18%)
  waiting for transfers between devices  37.7 us (17%)
  between operations  14.4 us (6%)
  local copies, waits for them, and re-layouts  11.3 us (5%)
  other arithmetic  3.46 us (2%)
    all_to_all x2, blocking collectives, turn(): return lax.all_to_all(piece, axis, split_axis=0, concat_axis=0, tiled=True)  40.5 us
    ppermute x24, starting transfers between devices, along(): lax.ppermute(value, axis, [(i, (i + step) % count) for i in range(count)])  31.5 us
    pallas_call x3, Pallas kernels, near_products(): pl.pallas_call(functools.partial(near_kernel, by_row, first), out_shape=s...  20.9 us
    ppermute x24, waiting for transfers between devices, along(): lax.ppermute(value, axis, [(i, (i + step) % count) for i in range(count)])  18.9 us
    all_to_all x2, waiting for transfers between devices, turn(): return lax.all_to_all(piece, axis, split_axis=0, concat_axis=0, tiled=True)  18.8 us
    pallas_call x3, Pallas kernels, far_products(): pl.pallas_call(functools.partial(far_kernel, by_row), out_shape=[pltpu.HB...  12.5 us
    pallas_call x3, Pallas kernels, finished(): pl.pallas_call(functools.partial(final_kernel, first), out_shape=[jax.Sha...  9.9 us
    unnamed x38, local copies, waits for them, and re-layouts  9.84 us
  transfers between devices with their start and end apart: 28, of which 5 were waited for; matrix products, arithmetic and copies ran while one was open for 2% of the time, Pallas kernels for 30%

profile of v6, /device:TPU:6, one launch (start us, length us, event | category | flops | bytes accessed | tf_op | source)
XLA Modules:
  0.0 224.6 jit_solution(15621122565179573008)
XLA Ops:
  7.2 0.9 slice.3
  8.1 3.5 %collective-permute-start = (bf16[2,64,384]{2,1,0:T(8,128)(2,1)S(1)}, bf16[2,64,384]{2,1,0:T(8,128)(2,1)S(1)}, u32[]{:S(2)}, u32[]{:S(2)}) collective-permute-start(bf16[2,64,384]{2,1,0:T(8,128)(2,1)S(1)} %slice.3), channel_id=1, source_target_pairs={{0,1},{1,2},{2,3},{3,4},{4,5},{5,6},{6,7},{7,8},{8,9},{9,10},{10,1... | collective-permute-start | bytes 294920 | tf_op jit(solution)/shard_map/ppermute | solution.py:56
  11.6 6.1 %shard_map.77 = (f32[2,4096,128]{2,1,0:T(8,128)S(1)}, bf16[2,3,64,1024]{3,2,1,0:T(8,128)(2,1)}) custom-call(bf16[2,64,8192]{2,1,0:T(8,128)(2,1)} %v_hbm.1, s32[1,64]{1,0:T(1,128)} %bitcast.13, f32[4,128]{1,0:T(4,128)} %constant.11.clone.coeff_hbm, bf16[2,8,64,1024]{3,2,1,0:T(8,128)(2,1)} %refs_0_.3), custom_call_target="tpu_custom_call" | custom-call | flops 5500000256 | bytes 1 | tf_op jit(solution)/shard_map/pallas_call | solution.py:187
  17.7 2.0 copy-done
  19.8 2.2 copy-done.1
  22.0 6.7 %shard_map.78 = (bf16[16,3,64,128]{3,2,1,0:T(8,128)(2,1)S(1)}, bf16[16,3,64,128]{3,2,1,0:T(8,128)(2,1)}, bf16[16,2,64,128]{3,2,1,0:T(8,128)(2,1)}) custom-call(f32[2,4096,128]{2,1,0:T(8,128)S(1)} %copy-done.1, bf16[2,64,384]{2,1,0:T(8,128)(2,1)S(1)} %collective-permute-done.halo_ref, s32[1,64]{1,0:T(1,128)} %bitcast.14, s32[1,128]{1,0:T(1,128)} %bitcast.15, ...), custom_call_target="tpu_custom_call" | custom-call | flops 6600000000 | bytes 1 | tf_op jit(solution)/shard_map/pallas_call | solution.py:203
  28.7 30.8 %all_to_all.20.refs_0_.refs_5_.own_ref = bf16[16,3,64,128]{3,2,1,0:T(8,128)(2,1)S(1)} all-to-all(bf16[16,3,64,128]{3,2,1,0:T(8,128)(2,1)S(1)} %get-tuple-element.43), channel_id=1, replica_groups=mesh['chan'=16,'row'=4,'col'=4] {'chan'}, dimensions={0} | all-to-all | bytes 1572864 | tf_op jit(solution)/shard_map/all_to_all | solution.py:574
  59.5 3.6 %all-to-all-start.1 = ((bf16[16,3,64,128]{3,2,1,0:T(8,128)(2,1)}), bf16[16,3,64,128]{3,2,1,0:T(8,128)(2,1)S(1)}, u32[]{:S(2)}, u32[]{:S(2)}) async-start(bf16[16,3,64,128]{3,2,1,0:T(8,128)(2,1)} %get-tuple-element.42), calls=%async_computation.1 | async-start | bytes 1572864 | tf_op jit(solution)/shard_map/all_to_all | solution.py:574
  63.1 0.9 collective-permute-start.6
  64.0 1.2 collective-permute-start.5
  65.2 18.8 %all-to-all-done.1.own_ref.refs_0_.refs_5_ = bf16[16,3,64,128]{3,2,1,0:T(8,128)(2,1)S(1)} async-done(((bf16[16,3,64,128]{3,2,1,0:T(8,128)(2,1)}), bf16[16,3,64,128]{3,2,1,0:T(8,128)(2,1)S(1)}, u32[]{:S(2)}, u32[]{:S(2)}) %all-to-all-start.1) | async-done | bytes 786464 | tf_op jit(solution)/shard_map/all_to_all | solution.py:574
  84.0 0.8 collective-permute-start.4
  84.8 2.4 %collective-permute-start.3 = (bf16[16,3,64,128]{3,2,1,0:T(8,128)(2,1)S(1)}, bf16[16,3,64,128]{3,2,1,0:T(8,128)(2,1)}, u32[]{:S(2)}, u32[]{:S(2)}) collective-permute-start(bf16[16,3,64,128]{3,2,1,0:T(8,128)(2,1)S(1)} %all-to-all-done.1.own_ref.refs_0_.refs_5_), channel_id=1, source_target_pairs={{0,4},{4,8},{8,12},{12,0},{1,5},{5,9},{9,13},{13,1},{2,6},{6,10},{... | collective-permute-start | bytes 2359304 | tf_op jit(solution)/shard_map/ppermute | solution.py:554
  87.2 4.9 %all-to-all-start = ((bf16[16,2,64,128]{3,2,1,0:T(8,128)(2,1)}), bf16[16,2,64,128]{3,2,1,0:T(8,128)(2,1)}, u32[]{:S(2)}, u32[]{:S(2)}) async-start(bf16[16,2,64,128]{3,2,1,0:T(8,128)(2,1)} %get-tuple-element.41), calls=%async_computation | async-start | bytes 1048576 | tf_op jit(solution)/shard_map/all_to_all | solution.py:574
  92.2 2.0 shard_map.79
  94.2 1.6 collective-permute-start.7
  95.8 1.7 collective-permute-start.8
  97.4 0.6 pad_add_fusion.place_ref
  98.0 9.2 %collective-permute-done.7.refs_3_.refs_8_.low_ref = bf16[8,3,64,128]{3,2,1,0:T(8,128)(2,1)S(1)} collective-permute-done((bf16[8,3,64,128]{3,2,1,0:T(8,128)(2,1)}, bf16[8,3,64,128]{3,2,1,0:T(8,128)(2,1)S(1)}, u32[]{:S(2)}, u32[]{:S(2)}) %collective-permute-start.7) | collective-permute-done | bytes 393248 | tf_op jit(solution)/shard_map/ppermute | solution.py:554
  107.3 0.2 collective-permute-done.8.refs_4_.refs_9_.high_ref
  107.5 0.6 copy-done.7
  108.0 4.5 %shard_map.80 = (bf16[3,256,256]{2,1,0:T(8,128)(2,1)}, bf16[3,256,256]{2,1,0:T(8,128)(2,1)}) custom-call(s32[2]{0:T(128)} %pad_add_fusion.place_ref, bf16[16,3,64,128]{3,2,1,0:T(8,128)(2,1)} %copy-done.4, bf16[16,3,64,128]{3,2,1,0:T(8,128)(2,1)} %collective-permute-done.5.low_ref.refs_1_.refs_6_.prev_ref, ...), custom_call_target="tpu_custom_call" | custom-call | flops 110000000 | bytes 1 | tf_op jit(solution)/shard_map/pallas_call | solution.py:312
  112.7 3.2 %collective-permute-start.11 = (bf16[3,256,256]{2,1,0:T(8,128)(2,1)}, bf16[3,256,256]{2,1,0:T(8,128)(2,1)}, u32[]{:S(2)}, u32[]{:S(2)}) collective-permute-start(bf16[3,256,256]{2,1,0:T(8,128)(2,1)} %get-tuple-element.46.refs_1_), channel_id=1, source_target_pairs={{0,4},{4,8},{8,12},{12,0},{1,5},{5,9},{9,13},{13,1},{2,6},{6,10},{... | collective-permute-start | bytes 1179656 | tf_op jit(solution)/shard_map/ppermute | solution.py:554
  115.9 8.3 %shard_map.81 = (f32[2,3,256,256]{3,2,1,0:T(8,128)}, bf16[2,3,256,256]{3,2,1,0:T(8,128)(2,1)}, bf16[2,3,256,256]{3,2,1,0:T(8,128)(2,1)}, f32[3,32,64]{2,1,0:T(8,128)}) custom-call(s32[2]{0:T(128)} %pad_add_fusion.place_ref, bf16[16,3,64,128]{3,2,1,0:T(8,128)(2,1)} %copy-done.4, ...), custom_call_target="tpu_custom_call" | custom-call | flops 110000000 | bytes 1 | tf_op jit(solution)/shard_map/pallas_call | solution.py:433
  124.2 0.9 copy-done.3
  125.1 2.0 shard_map.82
  127.1 3.2 %collective-permute-start.9 = (bf16[8,3,64,128]{3,2,1,0:T(8,128)(2,1)}, bf16[8,3,64,128]{3,2,1,0:T(8,128)(2,1)S(1)}, u32[]{:S(2)}, u32[]{:S(2)}) collective-permute-start(bf16[8,3,64,128]{3,2,1,0:T(8,128)(2,1)} %get-tuple-element.48.refs_0_), channel_id=1, source_target_pairs={{0,4},{4,8},{8,12},{12,0},{1,5},{5,9},{9,13},{13,1},{2,6},{6,10},{... | collective-permute-start | bytes 1179656 | tf_op jit(solution)/shard_map/ppermute | solution.py:554
  130.4 2.3 %collective-permute-start.2 = (bf16[16,2,64,128]{3,2,1,0:T(8,128)(2,1)}, bf16[16,2,64,128]{3,2,1,0:T(8,128)(2,1)S(1)}, u32[]{:S(2)}, u32[]{:S(2)}) collective-permute-start(bf16[16,2,64,128]{3,2,1,0:T(8,128)(2,1)} %all-to-all-done.refs_0_.refs_5_.own_ref), channel_id=1, source_target_pairs={{0,3},{1,0},{2,1},{3,2},{4,7},{5,4},{6,5},{7,6},{8,11},{9,8},{10,9... | collective-permute-start | bytes 1572872 | tf_op jit(solution)/shard_map/ppermute | solution.py:554
  132.7 2.3 %shard_map.83 = (bf16[2,3,256,256]{3,2,1,0:T(8,128)(2,1)}, bf16[2,3,256,256]{3,2,1,0:T(8,128)(2,1)}) custom-call(bf16[2,3,256,256]{3,2,1,0:T(8,128)(2,1)} %get-tuple-element.51.up_ref, bf16[2,3,256,256]{3,2,1,0:T(8,128)(2,1)} %get-tuple-element.52.down_ref, ...), custom_call_target="tpu_custom_call", output_to_operand_aliasing={{0}: (0, {}), {1}: (1, {})} | custom-call | flops 110000000 | bytes 1 | tf_op jit(solution)/shard_map/pallas_call | solution.py:493
  135.1 5.5 %collective-permute-done.10.refs_4_.refs_9_.high_ref = bf16[8,3,64,128]{3,2,1,0:T(8,128)(2,1)S(1)} collective-permute-done((bf16[8,3,64,128]{3,2,1,0:T(8,128)(2,1)}, bf16[8,3,64,128]{3,2,1,0:T(8,128)(2,1)S(1)}, u32[]{:S(2)}, u32[]{:S(2)}) %collective-permute-start.10) | collective-permute-done | bytes 393248 | tf_op jit(solution)/shard_map/ppermute | solution.py:554
  140.5 0.7 pad_add_fusion.1.place_ref
  141.2 4.8 %shard_map.84.refs_10_ = f32[4,3,8,64]{3,2,1,0:T(8,128)} custom-call(bf16[16,3,64,128]{3,2,1,0:T(8,128)(2,1)} %copy-done.2, bf16[4,2,3,64,1024]{4,3,2,1,0:T(8,128)(2,1)} %bitcast.12, bf16[2,3,256,256]{3,2,1,0:T(8,128)(2,1)} %get-tuple-element.54.refs_0_), custom_call_target="tpu_custom_call" | custom-call | flops 110000000 | bytes 1 | tf_op jit(solution)/shard_map/pallas_call | solution.py:466
  146.1 0.7 copy-done.9
  146.8 4.5 %shard_map.85 = (bf16[3,256,256]{2,1,0:T(8,128)(2,1)}, bf16[3,256,256]{2,1,0:T(8,128)(2,1)}) custom-call(s32[2]{0:T(128)} %pad_add_fusion.1.place_ref, bf16[16,3,64,128]{3,2,1,0:T(8,128)(2,1)} %copy-done.2, bf16[16,3,64,128]{3,2,1,0:T(8,128)(2,1)} %collective-permute-done.3.low_ref.refs_1_.refs_6_.prev_ref, bf16[16,3,64,128]{3,2,1,0:T(8,128)(2,1)} %copy-done.3, ...), custom_call_target="tpu_custom_call" | custom-call | flops 110000000 | bytes 1 | tf_op jit(solution)/shard_map/pallas_call | solution.py:312
  151.3 1.1 collective-permute-start.18
  152.4 1.0 collective-permute-start.17
  153.4 0.8 copy-done.6
  154.2 1.8 shard_map.86
  156.1 2.2 collective-permute-start.14
  158.3 3.9 %collective-permute-done.18.high_ref = bf16[3,256,256]{2,1,0:T(8,128)(2,1)S(1)} collective-permute-done((bf16[3,256,256]{2,1,0:T(8,128)(2,1)}, bf16[3,256,256]{2,1,0:T(8,128)(2,1)S(1)}, u32[]{:S(2)}, u32[]{:S(2)}) %collective-permute-start.18) | collective-permute-done | bytes 393248 | tf_op jit(solution)/shard_map/ppermute | solution.py:554
  162.2 0.7 collective-permute-start.13
  162.9 6.1 %shard_map.87 = (f32[2,3,256,256]{3,2,1,0:T(8,128)}, bf16[2,3,256,256]{3,2,1,0:T(8,128)(2,1)}, bf16[2,3,256,256]{3,2,1,0:T(8,128)(2,1)}) custom-call(s32[2]{0:T(128)} %pad_add_fusion.1.place_ref, bf16[16,3,64,128]{3,2,1,0:T(8,128)(2,1)} %copy-done.2, bf16[16,3,64,128]{3,2,1,0:T(8,128)(2,1)} %collective-permute-done.3.low_ref.refs_1_.refs_6_.prev_ref, ...), custom_call_target="tpu_custom_call" | custom-call | flops 110000000 | bytes 1 | tf_op jit(solution)/shard_map/pallas_call | solution.py:433
  169.0 2.3 %shard_map.88 = (bf16[2,3,256,256]{3,2,1,0:T(8,128)(2,1)}, bf16[2,3,256,256]{3,2,1,0:T(8,128)(2,1)}) custom-call(bf16[2,3,256,256]{3,2,1,0:T(8,128)(2,1)} %get-tuple-element.59.up_ref, bf16[2,3,256,256]{3,2,1,0:T(8,128)(2,1)} %get-tuple-element.60.down_ref, ...), custom_call_target="tpu_custom_call", output_to_operand_aliasing={{0}: (0, {}), {1}: (1, {})} | custom-call | flops 110000000 | bytes 1 | tf_op jit(solution)/shard_map/pallas_call | solution.py:493
  171.3 3.5 %shard_map.89 = (f32[2,8,256,256]{3,2,1,0:T(8,128)}, f32[8,128]{1,0:T(8,128)}) custom-call(f32[2,3,256,256]{3,2,1,0:T(8,128)} %get-tuple-element.47.refs_0_.own_ref, bf16[2,3,256,256]{3,2,1,0:T(8,128)(2,1)} %collective-permute-done.15.prev_ref, bf16[2,3,256,256]{3,2,1,0:T(8,128)(2,1)} %collective-permute-done.16.next_ref, ...), custom_call_target="tpu_custom_call" | custom-call | flops 110000000 | bytes 1 | tf_op jit(solution)/shard_map/pallas_call | solution.py:533
  174.9 0.7 copy-done.11
  175.5 0.1 copy-done.12
  175.7 3.5 %shard_map.90 = (bf16[2,256,256]{2,1,0:T(8,128)(2,1)}, bf16[2,256,256]{2,1,0:T(8,128)(2,1)}) custom-call(s32[2]{0:T(128)} %pad_add_fusion.place_ref, bf16[16,2,64,128]{3,2,1,0:T(8,128)(2,1)} %all-to-all-done.refs_0_.refs_5_.own_ref, bf16[16,2,64,128]{3,2,1,0:T(8,128)(2,1)} %copy-done.6, bf16[16,2,64,128]{3,2,1,0:T(8,128)(2,1)} %copy-done.5, ...), custom_call_target="tpu_custom_call" | custom-call | flops 110000000 | bytes 1 | tf_op jit(solution)/shard_map/pallas_call | solution.py:312
  179.1 2.0 collective-permute-start.20
  181.1 1.3 collective-permute-start.19
  182.5 2.6 %collective-permute-start.24 = (bf16[2,3,256,256]{3,2,1,0:T(8,128)(2,1)}, bf16[2,3,256,256]{3,2,1,0:T(8,128)(2,1)S(1)}, u32[]{:S(2)}, u32[]{:S(2)}) collective-permute-start(bf16[2,3,256,256]{3,2,1,0:T(8,128)(2,1)} %get-tuple-element.72), channel_id=1, source_target_pairs={{0,3},{1,0},{2,1},{3,2},{4,7},{5,4},{6,5},{7,6},{8,11},{9,8},{10,9... | collective-permute-start | bytes 2359304 | tf_op jit(solution)/shard_map/ppermute | solution.py:554
  185.0 6.6 %shard_map.91 = (f32[2,2,256,256]{3,2,1,0:T(8,128)}, bf16[2,2,256,256]{3,2,1,0:T(8,128)(2,1)}, bf16[2,2,256,256]{3,2,1,0:T(8,128)(2,1)}, f32[2,32,64]{2,1,0:T(8,128)}) custom-call(s32[2]{0:T(128)} %pad_add_fusion.place_ref, bf16[16,2,64,128]{3,2,1,0:T(8,128)(2,1)} %all-to-all-done.refs_0_.refs_5_.own_ref, bf16[16,2,64,128]{3,2,1,0:T(8,128)(2,1)} %copy-done.6, ...), custom_call_target="tpu_custom_call" | custom-call | flops 110000000 | bytes 1 | tf_op jit(solution)/shard_map/pallas_call | solution.py:433
  191.6 0.7 copy-done.16
  192.3 2.1 shard_map.92
  194.4 0.7 collective-permute-start.22
  195.2 2.5 %collective-permute-start.21 = (bf16[2,2,256,256]{3,2,1,0:T(8,128)(2,1)}, bf16[2,2,256,256]{3,2,1,0:T(8,128)(2,1)}, u32[]{:S(2)}, u32[]{:S(2)}) collective-permute-start(bf16[2,2,256,256]{3,2,1,0:T(8,128)(2,1)} %get-tuple-element.69.refs_1_), channel_id=1, source_target_pairs={{0,4},{4,8},{8,12},{12,0},{1,5},{5,9},{9,13},{13,1},{2,6},{6,10},{... | collective-permute-start | bytes 1572872 | tf_op jit(solution)/shard_map/ppermute | solution.py:554
  197.7 0.1 reshape.17
  197.8 9.7 %all_to_all.21 = f32[4,1,1536]{2,1,0:T(1,128)S(1)} all-to-all(f32[4,1,1536]{2,1,0:T(1,128)S(1)} %reshape.17), channel_id=1, replica_groups=mesh['chan'=16,'row'=4,'col'=4] {'col'}, dimensions={0} | all-to-all | bytes 49152 | tf_op jit(solution)/shard_map/all_to_all | solution.py:574
  207.5 0.6 broadcast
  208.1 0.8 reduce
  208.8 0.1 reshape.18
  208.9 1.4 maximum_bitcast_fusion
  210.4 0.9 copy-done.13
  211.3 3.4 %shard_map.93 = (f32[2,8,256,256]{3,2,1,0:T(8,128)}, f32[8,128]{1,0:T(8,128)}) custom-call(f32[2,3,256,256]{3,2,1,0:T(8,128)} %get-tuple-element.71.own_ref, bf16[2,3,256,256]{3,2,1,0:T(8,128)(2,1)} %collective-permute-done.23.prev_ref, bf16[2,3,256,256]{3,2,1,0:T(8,128)(2,1)} %copy-done.13, ...), custom_call_target="tpu_custom_call", output_to_operand_aliasing={{0}: (3, {})} | custom-call | flops 110000000 | bytes 1 | tf_op jit(solution)/shard_map/pallas_call | solution.py:533
  214.7 3.0 %shard_map.94 = (f32[2,8,256,256]{3,2,1,0:T(8,128)}, f32[8,128]{1,0:T(8,128)}) custom-call(f32[2,2,256,256]{3,2,1,0:T(8,128)} %get-tuple-element.65.own_ref, bf16[2,2,256,256]{3,2,1,0:T(8,128)(2,1)} %collective-permute-done.21.prev_ref, bf16[2,2,256,256]{3,2,1,0:T(8,128)(2,1)} %collective-permute-done.22.next_ref, ...), custom_call_target="tpu_custom_call", output_to_operand_aliasing={{0}: (3, {})} | custom-call | flops 110000000 | bytes 1 | tf_op jit(solution)/shard_map/pallas_call | solution.py:533
  (58 shorter events, 0.3 us)
Async XLA Ops:
  7.2 134.1 %all-gather.3.cloned.1.call-start = ((), (), s32[]{:S(2)}) async-start(), calls=%async_computation.4 | async-start | bytes 3932160 | tf_op jit(solution)/shard_map/all_gather | solution.py:571
  8.1 11.6 %collective-permute-start = (bf16[2,64,384]{2,1,0:T(8,128)(2,1)S(1)}, bf16[2,64,384]{2,1,0:T(8,128)(2,1)S(1)}, u32[]{:S(2)}, u32[]{:S(2)}) collective-permute-start(bf16[2,64,384]{2,1,0:T(8,128)(2,1)S(1)} %slice.3), channel_id=1, source_target_pairs={{0,1},{1,2},{2,3},{3,4},{4,5},{5,6},{6,7},{7,8},{8,9},{9,10},{10,1... | collective-permute-start | bytes 294920 | tf_op jit(solution)/shard_map/ppermute | solution.py:56
  17.7 2.0 copy-start
  19.8 2.2 copy-start.1
  59.5 24.5 %copy-start.4 = (bf16[16,3,64,128]{3,2,1,0:T(8,128)(2,1)}, bf16[16,3,64,128]{3,2,1,0:T(8,128)(2,1)S(1)}, u32[]{:S(2)}) copy-start(bf16[16,3,64,128]{3,2,1,0:T(8,128)(2,1)S(1)} %all_to_all.20.refs_0_.refs_5_.own_ref) | copy-start | bytes 2359300
  59.5 24.5 %all-to-all-start.1 = ((bf16[16,3,64,128]{3,2,1,0:T(8,128)(2,1)}), bf16[16,3,64,128]{3,2,1,0:T(8,128)(2,1)S(1)}, u32[]{:S(2)}, u32[]{:S(2)}) async-start(bf16[16,3,64,128]{3,2,1,0:T(8,128)(2,1)} %get-tuple-element.42), calls=%async_computation.1 | async-start | bytes 1572864 | tf_op jit(solution)/shard_map/all_to_all | solution.py:574
  63.1 29.0 %collective-permute-start.6 = (bf16[16,3,64,128]{3,2,1,0:T(8,128)(2,1)S(1)}, bf16[16,3,64,128]{3,2,1,0:T(8,128)(2,1)}, u32[]{:S(2)}, u32[]{:S(2)}) collective-permute-start(bf16[16,3,64,128]{3,2,1,0:T(8,128)(2,1)S(1)} %all_to_all.20.refs_0_.refs_5_.own_ref), channel_id=1, source_target_pairs={{0,3},{1,0},{2,1},{3,2},{4,7},{5,4},{6,5},{7,6},{8,11},{9,8},{10,9... | collective-permute-start | bytes 2359304 | tf_op jit(solution)/shard_map/ppermute | solution.py:554
  64.0 28.2 %collective-permute-start.5 = (bf16[16,3,64,128]{3,2,1,0:T(8,128)(2,1)S(1)}, bf16[16,3,64,128]{3,2,1,0:T(8,128)(2,1)}, u32[]{:S(2)}, u32[]{:S(2)}) collective-permute-start(bf16[16,3,64,128]{3,2,1,0:T(8,128)(2,1)S(1)} %all_to_all.20.refs_0_.refs_5_.own_ref), channel_id=1, source_target_pairs={{0,1},{1,2},{2,3},{3,0},{4,5},{5,6},{6,7},{7,4},{8,9},{9,10},{10,1... | collective-permute-start | bytes 2359304 | tf_op jit(solution)/shard_map/ppermute | solution.py:554
  84.0 28.6 %copy-start.2 = (bf16[16,3,64,128]{3,2,1,0:T(8,128)(2,1)}, bf16[16,3,64,128]{3,2,1,0:T(8,128)(2,1)S(1)}, u32[]{:S(2)}) copy-start(bf16[16,3,64,128]{3,2,1,0:T(8,128)(2,1)S(1)} %all-to-all-done.1.own_ref.refs_0_.refs_5_) | copy-start | bytes 2359300
  84.0 40.2 %collective-permute-start.4 = (bf16[16,3,64,128]{3,2,1,0:T(8,128)(2,1)S(1)}, bf16[16,3,64,128]{3,2,1,0:T(8,128)(2,1)S(1)}, u32[]{:S(2)}, u32[]{:S(2)}) collective-permute-start(bf16[16,3,64,128]{3,2,1,0:T(8,128)(2,1)S(1)} %all-to-all-done.1.own_ref.refs_0_.refs_5_), channel_id=1, source_target_pairs={{0,12},{4,0},{8,4},{12,8},{1,13},{5,1},{9,5},{13,9},{2,14},{6,2},{... | collective-permute-start | bytes 2359304 | tf_op jit(solution)/shard_map/ppermute | solution.py:554
  84.8 39.4 %collective-permute-start.3 = (bf16[16,3,64,128]{3,2,1,0:T(8,128)(2,1)S(1)}, bf16[16,3,64,128]{3,2,1,0:T(8,128)(2,1)}, u32[]{:S(2)}, u32[]{:S(2)}) collective-permute-start(bf16[16,3,64,128]{3,2,1,0:T(8,128)(2,1)S(1)} %all-to-all-done.1.own_ref.refs_0_.refs_5_), channel_id=1, source_target_pairs={{0,4},{4,8},{8,12},{12,0},{1,5},{5,9},{9,13},{13,1},{2,6},{6,10},{... | collective-permute-start | bytes 2359304 | tf_op jit(solution)/shard_map/ppermute | solution.py:554
  87.2 43.2 %all-to-all-start = ((bf16[16,2,64,128]{3,2,1,0:T(8,128)(2,1)}), bf16[16,2,64,128]{3,2,1,0:T(8,128)(2,1)}, u32[]{:S(2)}, u32[]{:S(2)}) async-start(bf16[16,2,64,128]{3,2,1,0:T(8,128)(2,1)} %get-tuple-element.41), calls=%async_computation | async-start | bytes 1048576 | tf_op jit(solution)/shard_map/all_to_all | solution.py:574
  94.2 13.1 %collective-permute-start.7 = (bf16[8,3,64,128]{3,2,1,0:T(8,128)(2,1)}, bf16[8,3,64,128]{3,2,1,0:T(8,128)(2,1)S(1)}, u32[]{:S(2)}, u32[]{:S(2)}) collective-permute-start(bf16[8,3,64,128]{3,2,1,0:T(8,128)(2,1)} %get-tuple-element.44), channel_id=1, source_target_pairs={{0,1},{1,2},{2,3},{3,0},{4,5},{5,6},{6,7},{7,4},{8,9},{9,10},{10,1... | collective-permute-start | bytes 1179656 | tf_op jit(solution)/shard_map/ppermute | solution.py:554
  95.8 11.7 %collective-permute-start.8 = (bf16[8,3,64,128]{3,2,1,0:T(8,128)(2,1)}, bf16[8,3,64,128]{3,2,1,0:T(8,128)(2,1)}, u32[]{:S(2)}, u32[]{:S(2)}) collective-permute-start(bf16[8,3,64,128]{3,2,1,0:T(8,128)(2,1)} %get-tuple-element.45), channel_id=1, source_target_pairs={{0,3},{1,0},{2,1},{3,2},{4,7},{5,4},{6,5},{7,6},{8,11},{9,8},{10,9... | collective-permute-start | bytes 1179656 | tf_op jit(solution)/shard_map/ppermute | solution.py:554
  107.3 0.7 copy-start.7
  112.6 20.1 %collective-permute-start.12 = (bf16[3,256,256]{2,1,0:T(8,128)(2,1)}, bf16[3,256,256]{2,1,0:T(8,128)(2,1)}, u32[]{:S(2)}, u32[]{:S(2)}) collective-permute-start(bf16[3,256,256]{2,1,0:T(8,128)(2,1)} %get-tuple-element.53), channel_id=1, source_target_pairs={{0,12},{4,0},{8,4},{12,8},{1,13},{5,1},{9,5},{13,9},{2,14},{6,2},{... | collective-permute-start | bytes 1179656 | tf_op jit(solution)/shard_map/ppermute | solution.py:554
  112.7 20.0 %collective-permute-start.11 = (bf16[3,256,256]{2,1,0:T(8,128)(2,1)}, bf16[3,256,256]{2,1,0:T(8,128)(2,1)}, u32[]{:S(2)}, u32[]{:S(2)}) collective-permute-start(bf16[3,256,256]{2,1,0:T(8,128)(2,1)} %get-tuple-element.46.refs_1_), channel_id=1, source_target_pairs={{0,4},{4,8},{8,12},{12,0},{1,5},{5,9},{9,13},{13,1},{2,6},{6,10},{... | collective-permute-start | bytes 1179656 | tf_op jit(solution)/shard_map/ppermute | solution.py:554
  124.2 1.0 copy-start.3
  127.1 13.4 %collective-permute-start.10 = (bf16[8,3,64,128]{3,2,1,0:T(8,128)(2,1)}, bf16[8,3,64,128]{3,2,1,0:T(8,128)(2,1)S(1)}, u32[]{:S(2)}, u32[]{:S(2)}) collective-permute-start(bf16[8,3,64,128]{3,2,1,0:T(8,128)(2,1)} %get-tuple-element.49), channel_id=1, source_target_pairs={{0,12},{4,0},{8,4},{12,8},{1,13},{5,1},{9,5},{13,9},{2,14},{6,2},{... | collective-permute-start | bytes 1179656 | tf_op jit(solution)/shard_map/ppermute | solution.py:554
  127.1 19.0 %collective-permute-start.9 = (bf16[8,3,64,128]{3,2,1,0:T(8,128)(2,1)}, bf16[8,3,64,128]{3,2,1,0:T(8,128)(2,1)S(1)}, u32[]{:S(2)}, u32[]{:S(2)}) collective-permute-start(bf16[8,3,64,128]{3,2,1,0:T(8,128)(2,1)} %get-tuple-element.48.refs_0_), channel_id=1, source_target_pairs={{0,4},{4,8},{8,12},{12,0},{1,5},{5,9},{9,13},{13,1},{2,6},{6,10},{... | collective-permute-start | bytes 1179656 | tf_op jit(solution)/shard_map/ppermute | solution.py:554
  130.4 22.0 %collective-permute-start.2 = (bf16[16,2,64,128]{3,2,1,0:T(8,128)(2,1)}, bf16[16,2,64,128]{3,2,1,0:T(8,128)(2,1)S(1)}, u32[]{:S(2)}, u32[]{:S(2)}) collective-permute-start(bf16[16,2,64,128]{3,2,1,0:T(8,128)(2,1)} %all-to-all-done.refs_0_.refs_5_.own_ref), channel_id=1, source_target_pairs={{0,3},{1,0},{2,1},{3,2},{4,7},{5,4},{6,5},{7,6},{8,11},{9,8},{10,9... | collective-permute-start | bytes 1572872 | tf_op jit(solution)/shard_map/ppermute | solution.py:554
  132.7 20.7 %collective-permute-start.1 = (bf16[16,2,64,128]{3,2,1,0:T(8,128)(2,1)}, bf16[16,2,64,128]{3,2,1,0:T(8,128)(2,1)S(1)}, u32[]{:S(2)}, u32[]{:S(2)}) collective-permute-start(bf16[16,2,64,128]{3,2,1,0:T(8,128)(2,1)} %all-to-all-done.refs_0_.refs_5_.own_ref), channel_id=1, source_target_pairs={{0,1},{1,2},{2,3},{3,0},{4,5},{5,6},{6,7},{7,4},{8,9},{9,10},{10,1... | collective-permute-start | bytes 1572872 | tf_op jit(solution)/shard_map/ppermute | solution.py:554
  135.1 36.3 %collective-permute-start.16 = (bf16[2,3,256,256]{3,2,1,0:T(8,128)(2,1)}, bf16[2,3,256,256]{3,2,1,0:T(8,128)(2,1)}, u32[]{:S(2)}, u32[]{:S(2)}) collective-permute-start(bf16[2,3,256,256]{3,2,1,0:T(8,128)(2,1)} %get-tuple-element.58), channel_id=1, source_target_pairs={{0,12},{4,0},{8,4},{12,8},{1,13},{5,1},{9,5},{13,9},{2,14},{6,2},{... | collective-permute-start | bytes 2359304 | tf_op jit(solution)/shard_map/ppermute | solution.py:554
  140.5 5.6 %copy-start.8 = (bf16[8,3,64,128]{3,2,1,0:T(8,128)(2,1)}, bf16[8,3,64,128]{3,2,1,0:T(8,128)(2,1)S(1)}, u32[]{:S(2)}) copy-start(bf16[8,3,64,128]{3,2,1,0:T(8,128)(2,1)S(1)} %collective-permute-done.10.refs_4_.refs_9_.high_ref) | copy-start | bytes 1179652
  140.5 30.8 %collective-permute-start.15 = (bf16[2,3,256,256]{3,2,1,0:T(8,128)(2,1)}, bf16[2,3,256,256]{3,2,1,0:T(8,128)(2,1)}, u32[]{:S(2)}, u32[]{:S(2)}) collective-permute-start(bf16[2,3,256,256]{3,2,1,0:T(8,128)(2,1)} %get-tuple-element.54.refs_0_), channel_id=1, source_target_pairs={{0,4},{4,8},{8,12},{12,0},{1,5},{5,9},{9,13},{13,1},{2,6},{6,10},{... | collective-permute-start | bytes 2359304 | tf_op jit(solution)/shard_map/ppermute | solution.py:554
  146.1 0.8 copy-start.9
  151.3 10.9 %collective-permute-start.18 = (bf16[3,256,256]{2,1,0:T(8,128)(2,1)}, bf16[3,256,256]{2,1,0:T(8,128)(2,1)S(1)}, u32[]{:S(2)}, u32[]{:S(2)}) collective-permute-start(bf16[3,256,256]{2,1,0:T(8,128)(2,1)} %get-tuple-element.61), channel_id=1, source_target_pairs={{0,3},{1,0},{2,1},{3,2},{4,7},{5,4},{6,5},{7,6},{8,11},{9,8},{10,9... | collective-permute-start | bytes 1179656 | tf_op jit(solution)/shard_map/ppermute | solution.py:554
  152.4 1.0 copy-start.5
  152.4 16.6 %collective-permute-start.17 = (bf16[3,256,256]{2,1,0:T(8,128)(2,1)}, bf16[3,256,256]{2,1,0:T(8,128)(2,1)}, u32[]{:S(2)}, u32[]{:S(2)}) collective-permute-start(bf16[3,256,256]{2,1,0:T(8,128)(2,1)} %get-tuple-element.55.refs_0_), channel_id=1, source_target_pairs={{0,1},{1,2},{2,3},{3,0},{4,5},{5,6},{6,7},{7,4},{8,9},{9,10},{10,1... | collective-permute-start | bytes 1179656 | tf_op jit(solution)/shard_map/ppermute | solution.py:554
  153.4 0.8 copy-start.6
  156.1 18.8 %collective-permute-start.14 = (bf16[8,2,64,128]{3,2,1,0:T(8,128)(2,1)}, bf16[8,2,64,128]{3,2,1,0:T(8,128)(2,1)S(1)}, u32[]{:S(2)}, u32[]{:S(2)}) collective-permute-start(bf16[8,2,64,128]{3,2,1,0:T(8,128)(2,1)} %get-tuple-element.57), channel_id=1, source_target_pairs={{0,3},{1,0},{2,1},{3,2},{4,7},{5,4},{6,5},{7,6},{8,11},{9,8},{10,9... | collective-permute-start | bytes 786440 | tf_op jit(solution)/shard_map/ppermute | solution.py:554
  162.2 6.8 %copy-start.15 = (bf16[3,256,256]{2,1,0:T(8,128)(2,1)}, bf16[3,256,256]{2,1,0:T(8,128)(2,1)S(1)}, u32[]{:S(2)}) copy-start(bf16[3,256,256]{2,1,0:T(8,128)(2,1)S(1)} %collective-permute-done.18.high_ref) | copy-start | bytes 1179652
  162.2 12.7 %collective-permute-start.13 = (bf16[8,2,64,128]{3,2,1,0:T(8,128)(2,1)}, bf16[8,2,64,128]{3,2,1,0:T(8,128)(2,1)S(1)}, u32[]{:S(2)}, u32[]{:S(2)}) collective-permute-start(bf16[8,2,64,128]{3,2,1,0:T(8,128)(2,1)} %get-tuple-element.56.refs_0_), channel_id=1, source_target_pairs={{0,1},{1,2},{2,3},{3,0},{4,5},{5,6},{6,7},{7,4},{8,9},{9,10},{10,1... | collective-permute-start | bytes 786440 | tf_op jit(solution)/shard_map/ppermute | solution.py:554
  171.3 13.7 %copy-start.10 = (bf16[2,3,256,256]{3,2,1,0:T(8,128)(2,1)S(1)}, bf16[2,3,256,256]{3,2,1,0:T(8,128)(2,1)}, u32[]{:S(2)}) copy-start(bf16[2,3,256,256]{3,2,1,0:T(8,128)(2,1)} %get-tuple-element.62.refs_0_) | copy-start | bytes 2359300
  174.8 0.7 copy-start.11
  174.9 0.8 copy-start.12
  179.1 18.6 %copy-start.14 = (f32[4,3,8,64]{3,2,1,0:T(8,128)S(1)}, f32[4,3,8,64]{3,2,1,0:T(8,128)}, u32[]{:S(2)}) copy-start(f32[4,3,8,64]{3,2,1,0:T(8,128)} %shard_map.84.refs_10_) | copy-start | bytes 73732
  179.1 12.5 %collective-permute-start.20 = (bf16[2,256,256]{2,1,0:T(8,128)(2,1)}, bf16[2,256,256]{2,1,0:T(8,128)(2,1)S(1)}, u32[]{:S(2)}, u32[]{:S(2)}) collective-permute-start(bf16[2,256,256]{2,1,0:T(8,128)(2,1)} %get-tuple-element.68), channel_id=1, source_target_pairs={{0,12},{4,0},{8,4},{12,8},{1,13},{5,1},{9,5},{13,9},{2,14},{6,2},{... | collective-permute-start | bytes 786440 | tf_op jit(solution)/shard_map/ppermute | solution.py:554
  181.1 10.5 %collective-permute-start.19 = (bf16[2,256,256]{2,1,0:T(8,128)(2,1)}, bf16[2,256,256]{2,1,0:T(8,128)(2,1)}, u32[]{:S(2)}, u32[]{:S(2)}) collective-permute-start(bf16[2,256,256]{2,1,0:T(8,128)(2,1)} %get-tuple-element.64.refs_1_), channel_id=1, source_target_pairs={{0,4},{4,8},{8,12},{12,0},{1,5},{5,9},{9,13},{13,1},{2,6},{6,10},{... | collective-permute-start | bytes 786440 | tf_op jit(solution)/shard_map/ppermute | solution.py:554
  182.5 26.5 %copy-start.17 = (f32[3,32,64]{2,1,0:T(8,128)S(1)}, f32[3,32,64]{2,1,0:T(8,128)}, u32[]{:S(2)}) copy-start(f32[3,32,64]{2,1,0:T(8,128)} %get-tuple-element.76) | copy-start | bytes 73732
  182.5 27.9 %collective-permute-start.24 = (bf16[2,3,256,256]{3,2,1,0:T(8,128)(2,1)}, bf16[2,3,256,256]{3,2,1,0:T(8,128)(2,1)S(1)}, u32[]{:S(2)}, u32[]{:S(2)}) collective-permute-start(bf16[2,3,256,256]{3,2,1,0:T(8,128)(2,1)} %get-tuple-element.72), channel_id=1, source_target_pairs={{0,3},{1,0},{2,1},{3,2},{4,7},{5,4},{6,5},{7,6},{8,11},{9,8},{10,9... | collective-permute-start | bytes 2359304 | tf_op jit(solution)/shard_map/ppermute | solution.py:554
  185.0 25.4 %collective-permute-start.23 = (bf16[2,3,256,256]{3,2,1,0:T(8,128)(2,1)S(1)}, bf16[2,3,256,256]{3,2,1,0:T(8,128)(2,1)}, u32[]{:S(2)}, u32[]{:S(2)}) collective-permute-start(bf16[2,3,256,256]{3,2,1,0:T(8,128)(2,1)S(1)} %copy-done.10), channel_id=1, source_target_pairs={{0,1},{1,2},{2,3},{3,0},{4,5},{5,6},{6,7},{7,4},{8,9},{9,10},{10,1... | collective-permute-start | bytes 2359304 | tf_op jit(solution)/shard_map/ppermute | solution.py:554
  191.6 0.7 copy-start.16
  194.4 20.2 %collective-permute-start.22 = (bf16[2,2,256,256]{3,2,1,0:T(8,128)(2,1)}, bf16[2,2,256,256]{3,2,1,0:T(8,128)(2,1)}, u32[]{:S(2)}, u32[]{:S(2)}) collective-permute-start(bf16[2,2,256,256]{3,2,1,0:T(8,128)(2,1)} %get-tuple-element.70), channel_id=1, source_target_pairs={{0,12},{4,0},{8,4},{12,8},{1,13},{5,1},{9,5},{13,9},{2,14},{6,2},{... | collective-permute-start | bytes 1572872 | tf_op jit(solution)/shard_map/ppermute | solution.py:554
  195.2 19.5 %collective-permute-start.21 = (bf16[2,2,256,256]{3,2,1,0:T(8,128)(2,1)}, bf16[2,2,256,256]{3,2,1,0:T(8,128)(2,1)}, u32[]{:S(2)}, u32[]{:S(2)}) collective-permute-start(bf16[2,2,256,256]{3,2,1,0:T(8,128)(2,1)} %get-tuple-element.69.refs_1_), channel_id=1, source_target_pairs={{0,4},{4,8},{8,12},{12,0},{1,5},{5,9},{9,13},{13,1},{2,6},{6,10},{... | collective-permute-start | bytes 1572872 | tf_op jit(solution)/shard_map/ppermute | solution.py:554
  210.4 0.9 copy-start.13
Sparse Core Ops, SparseCore 0:
  19.9 44.7 all-gather.2

commit v7 on v5

--- a/solution.py
+++ b/solution.py
@@ -12,7 +12,7 @@
 NCH = 128
 TAPS = 4
 INTEG = 8
-CHUNKS = (5, 3)
+CHUNKS = (4, 4)
 
 F32 = jnp.float32
 BF16 = jnp.bfloat16
@@ -432,7 +432,8 @@
     )(place, *args)
 
 
-def beam_kernel(own_ref, w_ref, out_ref):
+def beam_kernel(own_ref, w_ref, *refs):
+    out_ref = refs[-1]
     blocks, _, inputs, lanes = own_ref.shape
     owners, _, _, beams, total = w_ref.shape
     x = own_ref[:, 0].reshape(blocks * inputs, lanes)
@@ -445,7 +446,7 @@
         out_ref[owner, 0] = power[:, owner * beams : (owner + 1) * beams]
 
 
-def own_beams(own, weights, first=0):
+def own_beams(own, weights, after):
     blocks, size, inputs, lanes = own.shape
     owners, _, _, beams, total = weights.shape
     bins = lanes // 2 // INTEG
@@ -455,12 +456,13 @@
         grid=(size,),
         in_specs=[
             pl.BlockSpec((blocks, 1, inputs, lanes), lambda k: (0, k, 0, 0)),
-            pl.BlockSpec((owners, 2, 1, beams, total), lambda k: (0, 0, first + k, 0, 0)),
-        ],
+            pl.BlockSpec((owners, 2, 1, beams, total), lambda k: (0, 0, k, 0, 0)),
+        ]
+        + [ANY] * len(after),
         out_specs=pl.BlockSpec((owners, 1, bins, beams), lambda k: (0, k, 0, 0)),
         compiler_params=limit(62),
         cost_estimate=cost(0.1),
-    )(in_hbm(own), in_hbm(weights))
+    )(in_hbm(own), in_hbm(weights), *after)
 
 
 def add_kernel(up_ref, down_ref, low_ref, high_ref, *refs):
@@ -557,10 +559,11 @@
     near_b = both_ways(own_b, own_b, "row")
     own_a = turn(piece_a, "chan")
     near_a = both_ways(own_a, own_a, "col")
-    beam_b = own_beams(own_b, weights)
-    far_b = both_ways(*halves(*near_b, [own_a, beam_b]), "row")
+    half_b = halves(*near_b, [own_a])
+    far_b = both_ways(*half_b, "row")
+    beam_b = own_beams(own_b, weights, half_b[:1])
     slots_b = (own_b, *near_b, *far_b)
-    re_b, im_b = far_products(place_b, slots_b, True)
+    re_b, im_b = far_products(place_b, slots_b, True, [beam_b])
     got_b = both_ways(re_b, im_b, "col")
     half_a = halves(*near_a, [re_b])
     far_a = both_ways(*half_a, "col")

time: 210 us -> 210 us (level)
  waiting for transfers between devices: 45.5 us -> 53.9 us
  blocking collectives: 51 us -> 43.4 us
  starting transfers between devices: 25.5 us -> 28 us
  local copies, waits for them, and re-layouts: 5.97 us -> 3.53 us
    all_to_all x1, waiting for transfers between devices: 0.01 us -> 24.5 us  [turn(): return lax.all_to_all(piece, axis, split_axis=0, concat_axis=0, tiled=True)]
    all_gather x1, waiting for transfers between devices: 23.5 us -> 0.01 us  [on_device(): weights = lax.all_gather(beam_weights, 'col', axis=0)]
    all_to_all x2, blocking collectives: 51 us -> 43.4 us  [turn(): return lax.all_to_all(piece, axis, split_axis=0, concat_axis=0, tiled=True)]
    ppermute x16, waiting for transfers between devices: 21.3 us -> 28.7 us  [along(): lax.ppermute(value, axis, [(i, (i + step) % count) for i in range(count)])]
    ppermute x16, starting transfers between devices: 17.6 us -> 20.3 us  [along(): lax.ppermute(value, axis, [(i, (i + step) % count) for i in range(count)])]
    unnamed x24 -> x22, local copies, waits for them, and re-layouts: 4.54 us -> 2.11 us
  transfers between devices with their start and end apart: 19 -> 19, of which waited for: 8 -> 8; matrix products, arithmetic and copies ran while one was open for 2% -> 2% of each run, Pallas kernels for 28% -> 26%
where the time goes in v7:
time: 210 us; the launch traced here: 208 us
  Pallas kernels  61.9 us (29%)
  waiting for transfers between devices  53.9 us (26%)
  blocking collectives  43.4 us (21%)
  starting transfers between devices  28 us (13%)
  between operations  14.2 us (7%)
  other arithmetic  3.56 us (2%)
  local copies, waits for them, and re-layouts  3.53 us (2%)
    all_to_all x2, blocking collectives, turn(): return lax.all_to_all(piece, axis, split_axis=0, concat_axis=0, tiled=True)  43.4 us
    ppermute x16, waiting for transfers between devices, along(): lax.ppermute(value, axis, [(i, (i + step) % count) for i in range(count)])  28.7 us
    all_to_all x1, waiting for transfers between devices, turn(): return lax.all_to_all(piece, axis, split_axis=0, concat_axis=0, tiled=True)  24.5 us
    ppermute x16, starting transfers between devices, along(): lax.ppermute(value, axis, [(i, (i + step) % count) for i in range(count)])  20.3 us
    pallas_call x2, Pallas kernels, near_products(): pl.pallas_call(functools.partial(near_kernel, by_row, first), out_shape=s...  16.8 us
    pallas_call x2, Pallas kernels, far_products(): pl.pallas_call(functools.partial(far_kernel, by_row), out_shape=[pltpu.HB...  10.2 us
    pallas_call x1, Pallas kernels, spectra(): pl.pallas_call(functools.partial(spectrum_kernel, chunks), out_shape=[jax...  6.65 us
    pallas_call x2, Pallas kernels, finished(): pl.pallas_call(functools.partial(final_kernel, first), out_shape=jax.Shap...  6.56 us
  transfers between devices with their start and end apart: 19, of which 8 were waited for; matrix products, arithmetic and copies ran while one was open for 2% of the time, Pallas kernels for 26%

profile of v7, /device:TPU:6, one launch (start us, length us, event | category | flops | bytes accessed | tf_op | source)
XLA Modules:
  0.0 208.4 jit_solution(6777207412958808654)
XLA Ops:
  7.2 0.0 all-gather.3.cloned.1.call-start
  7.2 0.7 all-gather.3.cloned.1.call-update
  7.9 0.9 slice.3
  8.8 3.5 %collective-permute-start = (bf16[2,64,384]{2,1,0:T(8,128)(2,1)S(1)}, bf16[2,64,384]{2,1,0:T(8,128)(2,1)S(1)}, u32[]{:S(2)}, u32[]{:S(2)}) collective-permute-start(bf16[2,64,384]{2,1,0:T(8,128)(2,1)S(1)} %slice.3), channel_id=1, source_target_pairs={{0,1},{1,2},{2,3},{3,4},{4,5},{5,6},{6,7},{7,8},{8,9},{9,10},{10,1... | collective-permute-start | bytes 294920 | tf_op jit(solution)/shard_map/ppermute | solution.py:56
  12.3 6.4 %shard_map.77.filt_ref = f32[2,4096,128]{2,1,0:T(8,128)S(1)} custom-call(bf16[2,64,8192]{2,1,0:T(8,128)(2,1)} %v_hbm.1, s32[1,64]{1,0:T(1,128)} %bitcast.13, f32[4,128]{1,0:T(4,128)} %constant.11.clone.coeff_hbm), custom_call_target="tpu_custom_call" | custom-call | flops 5500000256 | bytes 1 | tf_op jit(solution)/shard_map/pallas_call | solution.py:176
  18.7 0.0 collective-permute-done.halo_ref
  18.8 6.6 %shard_map.78 = (bf16[16,4,64,128]{3,2,1,0:T(8,128)(2,1)S(1)}, bf16[16,4,64,128]{3,2,1,0:T(8,128)(2,1)}) custom-call(f32[2,4096,128]{2,1,0:T(8,128)S(1)} %shard_map.77.filt_ref, bf16[2,64,384]{2,1,0:T(8,128)(2,1)S(1)} %collective-permute-done.halo_ref, s32[1,64]{1,0:T(1,128)} %bitcast.14, s32[1,128]{1,0:T(1,128)} %bitcast.15, ...), custom_call_target="tpu_custom_call" | custom-call | flops 6600000000 | bytes 1 | tf_op jit(solution)/shard_map/pallas_call | solution.py:191
  25.4 35.6 %all_to_all.15.own_ref.refs_0_.refs_5_ = bf16[16,4,64,128]{3,2,1,0:T(8,128)(2,1)S(1)} all-to-all(bf16[16,4,64,128]{3,2,1,0:T(8,128)(2,1)S(1)} %get-tuple-element.24), channel_id=1, replica_groups=mesh['chan'=16,'row'=4,'col'=4] {'chan'}, dimensions={0} | all-to-all | bytes 2097152 | tf_op jit(solution)/shard_map/all_to_all | solution.py:556
  61.0 4.2 %all-to-all-start = ((bf16[16,4,64,128]{3,2,1,0:T(8,128)(2,1)}), bf16[16,4,64,128]{3,2,1,0:T(8,128)(2,1)S(1)}, u32[]{:S(2)}, u32[]{:S(2)}) async-start(bf16[16,4,64,128]{3,2,1,0:T(8,128)(2,1)} %get-tuple-element.23), calls=%async_computation | async-start | bytes 2097152 | tf_op jit(solution)/shard_map/all_to_all | solution.py:556
  65.2 0.6 collective-permute-start.3
  65.8 1.5 collective-permute-start.4
  67.3 24.5 %all-to-all-done.refs_0_.own_ref.refs_5_ = bf16[16,4,64,128]{3,2,1,0:T(8,128)(2,1)S(1)} async-done(((bf16[16,4,64,128]{3,2,1,0:T(8,128)(2,1)}), bf16[16,4,64,128]{3,2,1,0:T(8,128)(2,1)S(1)}, u32[]{:S(2)}, u32[]{:S(2)}) %all-to-all-start) | async-done | bytes 1048608 | tf_op jit(solution)/shard_map/all_to_all | solution.py:556
  91.9 1.6 collective-permute-start.1
  93.5 1.7 collective-permute-start.2
  95.1 0.0 collective-permute-done.3.low_ref.refs_1_.refs_6_.prev_ref
  95.1 0.0 collective-permute-done.4.high_ref.refs_2_.refs_7_.next_ref
  95.1 2.1 shard_map.79
  97.2 0.5 collective-permute-start.5
  97.7 1.5 collective-permute-start.6
  99.2 0.7 pad_add_fusion.1.place_ref
  99.9 5.8 %shard_map.80.refs_10_ = f32[4,4,8,64]{3,2,1,0:T(8,128)} custom-call(bf16[16,4,64,128]{3,2,1,0:T(8,128)(2,1)} %copy-done.1, bf16[4,2,8,64,1024]{4,3,2,1,0:T(8,128)(2,1)} %bitcast.12, bf16[8,4,64,128]{3,2,1,0:T(8,128)(2,1)} %get-tuple-element.25.refs_0_), custom_call_target="tpu_custom_call" | custom-call | flops 110000000 | bytes 1 | tf_op jit(solution)/shard_map/pallas_call | solution.py:453
  105.7 6.4 %collective-permute-done.5.refs_3_.refs_8_.low_ref = bf16[8,4,64,128]{3,2,1,0:T(8,128)(2,1)S(1)} collective-permute-done((bf16[8,4,64,128]{3,2,1,0:T(8,128)(2,1)}, bf16[8,4,64,128]{3,2,1,0:T(8,128)(2,1)S(1)}, u32[]{:S(2)}, u32[]{:S(2)}) %collective-permute-start.5) | collective-permute-done | bytes 524320 | tf_op jit(solution)/shard_map/ppermute | solution.py:537
  112.1 1.9 collective-permute-done.6.refs_4_.refs_9_.high_ref
  113.9 5.0 %shard_map.81 = (bf16[4,256,256]{2,1,0:T(8,128)(2,1)}, bf16[4,256,256]{2,1,0:T(8,128)(2,1)}) custom-call(s32[2]{0:T(128)} %pad_add_fusion.1.place_ref, bf16[16,4,64,128]{3,2,1,0:T(8,128)(2,1)} %copy-done.1, bf16[16,4,64,128]{3,2,1,0:T(8,128)(2,1)} %collective-permute-done.3.low_ref.refs_1_.refs_6_.prev_ref, ...), custom_call_target="tpu_custom_call" | custom-call | flops 110000000 | bytes 1 | tf_op jit(solution)/shard_map/pallas_call | solution.py:299
  118.9 1.4 collective-permute-start.10
  120.4 0.7 collective-permute-start.9
  121.0 0.0 collective-permute-done.1.low_ref.prev_ref.refs_1_.refs_6_
  121.0 0.0 collective-permute-done.2.high_ref.next_ref.refs_2_.refs_7_
  121.0 2.1 shard_map.82
  123.1 0.9 collective-permute-start.7
  124.0 2.3 %collective-permute-start.8 = (bf16[8,4,64,128]{3,2,1,0:T(8,128)(2,1)}, bf16[8,4,64,128]{3,2,1,0:T(8,128)(2,1)S(1)}, u32[]{:S(2)}, u32[]{:S(2)}) collective-permute-start(bf16[8,4,64,128]{3,2,1,0:T(8,128)(2,1)} %get-tuple-element.29), channel_id=1, source_target_pairs={{0,3},{1,0},{2,1},{3,2},{4,7},{5,4},{6,5},{7,6},{8,11},{9,8},{10,9... | collective-permute-start | bytes 1572872 | tf_op jit(solution)/shard_map/ppermute | solution.py:537
  126.4 0.7 pad_add_fusion.place_ref
  127.0 7.0 %shard_map.84 = (f32[2,4,256,256]{3,2,1,0:T(8,128)}, bf16[2,4,256,256]{3,2,1,0:T(8,128)(2,1)}, bf16[2,4,256,256]{3,2,1,0:T(8,128)(2,1)}) custom-call(s32[2]{0:T(128)} %pad_add_fusion.1.place_ref, bf16[16,4,64,128]{3,2,1,0:T(8,128)(2,1)} %copy-done.1, bf16[16,4,64,128]{3,2,1,0:T(8,128)(2,1)} %collective-permute-done.3.low_ref.refs_1_.refs_6_.prev_ref, ...), custom_call_target="tpu_custom_call" | custom-call | flops 110000000 | bytes 1 | tf_op jit(solution)/shard_map/pallas_call | solution.py:420
  134.0 0.0 collective-permute-done.10.high_ref
  134.0 2.7 %collective-permute-done.9.low_ref = bf16[4,256,256]{2,1,0:T(8,128)(2,1)} collective-permute-done((bf16[4,256,256]{2,1,0:T(8,128)(2,1)}, bf16[4,256,256]{2,1,0:T(8,128)(2,1)}, u32[]{:S(2)}, u32[]{:S(2)}) %collective-permute-start.9) | collective-permute-done | bytes 524320 | tf_op jit(solution)/shard_map/ppermute | solution.py:537
  136.7 2.6 %shard_map.85 = (bf16[2,4,256,256]{3,2,1,0:T(8,128)(2,1)}, bf16[2,4,256,256]{3,2,1,0:T(8,128)(2,1)}) custom-call(bf16[2,4,256,256]{3,2,1,0:T(8,128)(2,1)} %get-tuple-element.33.up_ref, bf16[2,4,256,256]{3,2,1,0:T(8,128)(2,1)} %get-tuple-element.34.down_ref, ...), custom_call_target="tpu_custom_call", output_to_operand_aliasing={{0}: (0, {}), {1}: (1, {})} | custom-call | flops 110000000 | bytes 1 | tf_op jit(solution)/shard_map/pallas_call | solution.py:480
  139.4 7.2 %collective-permute-done.7.low_ref.refs_3_.refs_8_ = bf16[8,4,64,128]{3,2,1,0:T(8,128)(2,1)S(1)} collective-permute-done((bf16[8,4,64,128]{3,2,1,0:T(8,128)(2,1)}, bf16[8,4,64,128]{3,2,1,0:T(8,128)(2,1)S(1)}, u32[]{:S(2)}, u32[]{:S(2)}) %collective-permute-start.7) | collective-permute-done | bytes 524320 | tf_op jit(solution)/shard_map/ppermute | solution.py:537
  146.6 0.0 collective-permute-done.8.high_ref.refs_4_.refs_9_
  146.6 0.8 copy-done.3
  147.4 0.2 copy-done.4
  147.6 5.1 %shard_map.86 = (bf16[4,256,256]{2,1,0:T(8,128)(2,1)}, bf16[4,256,256]{2,1,0:T(8,128)(2,1)}) custom-call(s32[2]{0:T(128)} %pad_add_fusion.place_ref, bf16[16,4,64,128]{3,2,1,0:T(8,128)(2,1)} %copy-done, bf16[16,4,64,128]{3,2,1,0:T(8,128)(2,1)} %collective-permute-done.1.low_ref.prev_ref.refs_1_.refs_6_, ...), custom_call_target="tpu_custom_call" | custom-call | flops 110000000 | bytes 1 | tf_op jit(solution)/shard_map/pallas_call | solution.py:299
  152.7 1.1 collective-permute-start.11
  153.8 1.0 collective-permute-start.12
  154.8 0.0 collective-permute-start.15
  154.8 3.2 %collective-permute-start.16 = (bf16[2,4,256,256]{3,2,1,0:T(8,128)(2,1)}, bf16[2,4,256,256]{3,2,1,0:T(8,128)(2,1)}, u32[]{:S(2)}, u32[]{:S(2)}) collective-permute-start(bf16[2,4,256,256]{3,2,1,0:T(8,128)(2,1)} %get-tuple-element.42), channel_id=1, source_target_pairs={{0,3},{1,0},{2,1},{3,2},{4,7},{5,4},{6,5},{7,6},{8,11},{9,8},{10,9... | collective-permute-start | bytes 3145736 | tf_op jit(solution)/shard_map/ppermute | solution.py:537
  158.0 9.9 %shard_map.83 = (f32[2,4,256,256]{3,2,1,0:T(8,128)}, bf16[2,4,256,256]{3,2,1,0:T(8,128)(2,1)}, bf16[2,4,256,256]{3,2,1,0:T(8,128)(2,1)}, f32[4,32,64]{2,1,0:T(8,128)}) custom-call(s32[2]{0:T(128)} %pad_add_fusion.place_ref, bf16[16,4,64,128]{3,2,1,0:T(8,128)(2,1)} %copy-done, ...), custom_call_target="tpu_custom_call" | custom-call | flops 110000000 | bytes 1 | tf_op jit(solution)/shard_map/pallas_call | solution.py:420
  167.9 0.0 collective-permute-done.11.low_ref
  167.9 0.0 copy-start.8
  167.9 0.1 collective-permute-done.12.high_ref
  168.0 0.7 copy-done.8
  168.7 0.2 copy-done.9
  168.9 2.7 %shard_map.87 = (bf16[2,4,256,256]{3,2,1,0:T(8,128)(2,1)}, bf16[2,4,256,256]{3,2,1,0:T(8,128)(2,1)}) custom-call(bf16[2,4,256,256]{3,2,1,0:T(8,128)(2,1)} %get-tuple-element.31.up_ref, bf16[2,4,256,256]{3,2,1,0:T(8,128)(2,1)} %get-tuple-element.32.down_ref, bf16[4,256,256]{2,1,0:T(8,128)(2,1)} %copy-done.8, ...), custom_call_target="tpu_custom_call", output_to_operand_aliasing={{0}: (0, {}), {1}: (1, {})} | custom-call | flops 110000000 | bytes 1 | tf_op jit(solution)/shard_map/pallas_call | solution.py:480
  171.6 2.2 %collective-permute-start.13 = (bf16[2,4,256,256]{3,2,1,0:T(8,128)(2,1)}, bf16[2,4,256,256]{3,2,1,0:T(8,128)(2,1)S(1)}, u32[]{:S(2)}, u32[]{:S(2)}) collective-permute-start(bf16[2,4,256,256]{3,2,1,0:T(8,128)(2,1)} %get-tuple-element.39), channel_id=1, source_target_pairs={{0,4},{4,8},{8,12},{12,0},{1,5},{5,9},{9,13},{13,1},{2,6},{6,10},{... | collective-permute-start | bytes 3145736 | tf_op jit(solution)/shard_map/ppermute | solution.py:537
  173.8 0.1 reshape.17
  173.9 7.8 %all_to_all.16 = f32[4,1,2048]{2,1,0:T(1,128)S(1)} all-to-all(f32[4,1,2048]{2,1,0:T(1,128)S(1)} %reshape.17), channel_id=1, replica_groups=mesh['chan'=16,'row'=4,'col'=4] {'col'}, dimensions={0} | all-to-all | bytes 65536 | tf_op jit(solution)/shard_map/all_to_all | solution.py:556
  181.7 0.5 broadcast
  182.3 0.7 reduce
  183.0 0.1 reshape.18
  183.1 1.5 maximum_bitcast_fusion
  184.6 0.0 collective-permute-done.15.prev_ref
  184.6 3.3 %shard_map.88.refs_0_ = f32[2,8,256,256]{3,2,1,0:T(8,128)} custom-call(f32[2,4,256,256]{3,2,1,0:T(8,128)} %get-tuple-element.41.own_ref, bf16[2,4,256,256]{3,2,1,0:T(8,128)(2,1)} %collective-permute-done.15.prev_ref, bf16[2,4,256,256]{3,2,1,0:T(8,128)(2,1)} %collective-permute-done.16.next_ref), custom_call_target="tpu_custom_call" | custom-call | flops 110000000 | bytes 1 | tf_op jit(solution)/shard_map/pallas_call | solution.py:519
  187.9 7.0 %collective-permute-done.13.prev_ref = bf16[2,4,256,256]{3,2,1,0:T(8,128)(2,1)S(1)} collective-permute-done((bf16[2,4,256,256]{3,2,1,0:T(8,128)(2,1)}, bf16[2,4,256,256]{3,2,1,0:T(8,128)(2,1)S(1)}, u32[]{:S(2)}, u32[]{:S(2)}) %collective-permute-start.13) | collective-permute-done | bytes 1048608 | tf_op jit(solution)/shard_map/ppermute | solution.py:537
  194.9 3.3 %collective-permute-done.14.next_ref = bf16[2,4,256,256]{3,2,1,0:T(8,128)(2,1)} collective-permute-done((bf16[2,4,256,256]{3,2,1,0:T(8,128)(2,1)}, bf16[2,4,256,256]{3,2,1,0:T(8,128)(2,1)}, u32[]{:S(2)}, u32[]{:S(2)}) %collective-permute-start.14) | collective-permute-done | bytes 1048608 | tf_op jit(solution)/shard_map/ppermute | solution.py:537
  198.3 3.3 %shard_map.89 = f32[2,8,256,256]{3,2,1,0:T(8,128)} custom-call(f32[2,4,256,256]{3,2,1,0:T(8,128)} %get-tuple-element.30.own_ref, bf16[2,4,256,256]{3,2,1,0:T(8,128)(2,1)} %copy-done.5, bf16[2,4,256,256]{3,2,1,0:T(8,128)(2,1)} %collective-permute-done.14.next_ref, f32[2,8,256,256]{3,2,1,0:T(8,128)} %shard_map.88.refs_0_), custom_call_target="tpu_custom_call", output_to_operand_aliasing={{}: (3, {})} | custom-call | flops 110000000 | bytes 1 | tf_op jit(solution)/shard_map/pallas_call | solution.py:519
  (19 shorter events, 0.0 us)
Async XLA Ops:
  7.2 92.7 %all-gather.3.cloned.1.call-start = ((), (), s32[]{:S(2)}) async-start(), calls=%async_computation.3 | async-start | bytes 10485760 | tf_op jit(solution)/shard_map/all_gather | solution.py:552
  8.8 9.9 %collective-permute-start = (bf16[2,64,384]{2,1,0:T(8,128)(2,1)S(1)}, bf16[2,64,384]{2,1,0:T(8,128)(2,1)S(1)}, u32[]{:S(2)}, u32[]{:S(2)}) collective-permute-start(bf16[2,64,384]{2,1,0:T(8,128)(2,1)S(1)} %slice.3), channel_id=1, source_target_pairs={{0,1},{1,2},{2,3},{3,4},{4,5},{5,6},{6,7},{7,8},{8,9},{9,10},{10,1... | collective-permute-start | bytes 294920 | tf_op jit(solution)/shard_map/ppermute | solution.py:56
  61.0 30.8 %copy-start.1 = (bf16[16,4,64,128]{3,2,1,0:T(8,128)(2,1)}, bf16[16,4,64,128]{3,2,1,0:T(8,128)(2,1)S(1)}, u32[]{:S(2)}) copy-start(bf16[16,4,64,128]{3,2,1,0:T(8,128)(2,1)S(1)} %all_to_all.15.own_ref.refs_0_.refs_5_) | copy-start | bytes 3145732
  61.0 30.8 %all-to-all-start = ((bf16[16,4,64,128]{3,2,1,0:T(8,128)(2,1)}), bf16[16,4,64,128]{3,2,1,0:T(8,128)(2,1)S(1)}, u32[]{:S(2)}, u32[]{:S(2)}) async-start(bf16[16,4,64,128]{3,2,1,0:T(8,128)(2,1)} %get-tuple-element.23), calls=%async_computation | async-start | bytes 2097152 | tf_op jit(solution)/shard_map/all_to_all | solution.py:556
  65.2 29.9 %collective-permute-start.3 = (bf16[16,4,64,128]{3,2,1,0:T(8,128)(2,1)S(1)}, bf16[16,4,64,128]{3,2,1,0:T(8,128)(2,1)}, u32[]{:S(2)}, u32[]{:S(2)}) collective-permute-start(bf16[16,4,64,128]{3,2,1,0:T(8,128)(2,1)S(1)} %all_to_all.15.own_ref.refs_0_.refs_5_), channel_id=1, source_target_pairs={{0,4},{4,8},{8,12},{12,0},{1,5},{5,9},{9,13},{13,1},{2,6},{6,10},{... | collective-permute-start | bytes 3145736 | tf_op jit(solution)/shard_map/ppermute | solution.py:537
  65.8 29.3 %collective-permute-start.4 = (bf16[16,4,64,128]{3,2,1,0:T(8,128)(2,1)S(1)}, bf16[16,4,64,128]{3,2,1,0:T(8,128)(2,1)}, u32[]{:S(2)}, u32[]{:S(2)}) collective-permute-start(bf16[16,4,64,128]{3,2,1,0:T(8,128)(2,1)S(1)} %all_to_all.15.own_ref.refs_0_.refs_5_), channel_id=1, source_target_pairs={{0,12},{4,0},{8,4},{12,8},{1,13},{5,1},{9,5},{13,9},{2,14},{6,2},{... | collective-permute-start | bytes 3145736 | tf_op jit(solution)/shard_map/ppermute | solution.py:537
  91.9 3.2 %copy-start = (bf16[16,4,64,128]{3,2,1,0:T(8,128)(2,1)}, bf16[16,4,64,128]{3,2,1,0:T(8,128)(2,1)S(1)}, u32[]{:S(2)}) copy-start(bf16[16,4,64,128]{3,2,1,0:T(8,128)(2,1)S(1)} %all-to-all-done.refs_0_.own_ref.refs_5_) | copy-start | bytes 3145732
  91.9 29.1 %collective-permute-start.1 = (bf16[16,4,64,128]{3,2,1,0:T(8,128)(2,1)S(1)}, bf16[16,4,64,128]{3,2,1,0:T(8,128)(2,1)}, u32[]{:S(2)}, u32[]{:S(2)}) collective-permute-start(bf16[16,4,64,128]{3,2,1,0:T(8,128)(2,1)S(1)} %all-to-all-done.refs_0_.own_ref.refs_5_), channel_id=1, source_target_pairs={{0,1},{1,2},{2,3},{3,0},{4,5},{5,6},{6,7},{7,4},{8,9},{9,10},{10,1... | collective-permute-start | bytes 3145736 | tf_op jit(solution)/shard_map/ppermute | solution.py:537
  93.5 27.6 %collective-permute-start.2 = (bf16[16,4,64,128]{3,2,1,0:T(8,128)(2,1)S(1)}, bf16[16,4,64,128]{3,2,1,0:T(8,128)(2,1)}, u32[]{:S(2)}, u32[]{:S(2)}) collective-permute-start(bf16[16,4,64,128]{3,2,1,0:T(8,128)(2,1)S(1)} %all-to-all-done.refs_0_.own_ref.refs_5_), channel_id=1, source_target_pairs={{0,3},{1,0},{2,1},{3,2},{4,7},{5,4},{6,5},{7,6},{8,11},{9,8},{10,9... | collective-permute-start | bytes 3145736 | tf_op jit(solution)/shard_map/ppermute | solution.py:537
  97.2 14.8 %collective-permute-start.5 = (bf16[8,4,64,128]{3,2,1,0:T(8,128)(2,1)}, bf16[8,4,64,128]{3,2,1,0:T(8,128)(2,1)S(1)}, u32[]{:S(2)}, u32[]{:S(2)}) collective-permute-start(bf16[8,4,64,128]{3,2,1,0:T(8,128)(2,1)} %get-tuple-element.25.refs_0_), channel_id=1, source_target_pairs={{0,4},{4,8},{8,12},{12,0},{1,5},{5,9},{9,13},{13,1},{2,6},{6,10},{... | collective-permute-start | bytes 1572872 | tf_op jit(solution)/shard_map/ppermute | solution.py:537
  97.7 16.2 %collective-permute-start.6 = (bf16[8,4,64,128]{3,2,1,0:T(8,128)(2,1)}, bf16[8,4,64,128]{3,2,1,0:T(8,128)(2,1)}, u32[]{:S(2)}, u32[]{:S(2)}) collective-permute-start(bf16[8,4,64,128]{3,2,1,0:T(8,128)(2,1)} %get-tuple-element.26), channel_id=1, source_target_pairs={{0,12},{4,0},{8,4},{12,8},{1,13},{5,1},{9,5},{13,9},{2,14},{6,2},{... | collective-permute-start | bytes 1572872 | tf_op jit(solution)/shard_map/ppermute | solution.py:537
  112.1 1.9 copy-start.2
  118.9 15.1 %collective-permute-start.10 = (bf16[4,256,256]{2,1,0:T(8,128)(2,1)}, bf16[4,256,256]{2,1,0:T(8,128)(2,1)S(1)}, u32[]{:S(2)}, u32[]{:S(2)}) collective-permute-start(bf16[4,256,256]{2,1,0:T(8,128)(2,1)} %get-tuple-element.35), channel_id=1, source_target_pairs={{0,3},{1,0},{2,1},{3,2},{4,7},{5,4},{6,5},{7,6},{8,11},{9,8},{10,9... | collective-permute-start | bytes 1572872 | tf_op jit(solution)/shard_map/ppermute | solution.py:537
  120.4 16.4 %collective-permute-start.9 = (bf16[4,256,256]{2,1,0:T(8,128)(2,1)}, bf16[4,256,256]{2,1,0:T(8,128)(2,1)}, u32[]{:S(2)}, u32[]{:S(2)}) collective-permute-start(bf16[4,256,256]{2,1,0:T(8,128)(2,1)} %get-tuple-element.27.refs_0_), channel_id=1, source_target_pairs={{0,1},{1,2},{2,3},{3,0},{4,5},{5,6},{6,7},{7,4},{8,9},{9,10},{10,1... | collective-permute-start | bytes 1572872 | tf_op jit(solution)/shard_map/ppermute | solution.py:537
  123.1 23.5 %collective-permute-start.7 = (bf16[8,4,64,128]{3,2,1,0:T(8,128)(2,1)}, bf16[8,4,64,128]{3,2,1,0:T(8,128)(2,1)S(1)}, u32[]{:S(2)}, u32[]{:S(2)}) collective-permute-start(bf16[8,4,64,128]{3,2,1,0:T(8,128)(2,1)} %get-tuple-element.28.refs_0_), channel_id=1, source_target_pairs={{0,1},{1,2},{2,3},{3,0},{4,5},{5,6},{6,7},{7,4},{8,9},{9,10},{10,1... | collective-permute-start | bytes 1572872 | tf_op jit(solution)/shard_map/ppermute | solution.py:537
  124.0 22.6 %collective-permute-start.8 = (bf16[8,4,64,128]{3,2,1,0:T(8,128)(2,1)}, bf16[8,4,64,128]{3,2,1,0:T(8,128)(2,1)S(1)}, u32[]{:S(2)}, u32[]{:S(2)}) collective-permute-start(bf16[8,4,64,128]{3,2,1,0:T(8,128)(2,1)} %get-tuple-element.29), channel_id=1, source_target_pairs={{0,3},{1,0},{2,1},{3,2},{4,7},{5,4},{6,5},{7,6},{8,11},{9,8},{10,9... | collective-permute-start | bytes 1572872 | tf_op jit(solution)/shard_map/ppermute | solution.py:537
  134.0 2.7 %copy-start.7 = (bf16[4,256,256]{2,1,0:T(8,128)(2,1)}, bf16[4,256,256]{2,1,0:T(8,128)(2,1)S(1)}, u32[]{:S(2)}) copy-start(bf16[4,256,256]{2,1,0:T(8,128)(2,1)S(1)} %collective-permute-done.10.high_ref) | copy-start | bytes 1572868
  146.6 0.8 copy-start.3
  146.6 1.0 copy-start.4
  152.7 15.2 %collective-permute-start.11 = (bf16[4,256,256]{2,1,0:T(8,128)(2,1)}, bf16[4,256,256]{2,1,0:T(8,128)(2,1)S(1)}, u32[]{:S(2)}, u32[]{:S(2)}) collective-permute-start(bf16[4,256,256]{2,1,0:T(8,128)(2,1)} %get-tuple-element.37), channel_id=1, source_target_pairs={{0,4},{4,8},{8,12},{12,0},{1,5},{5,9},{9,13},{13,1},{2,6},{6,10},{... | collective-permute-start | bytes 1572872 | tf_op jit(solution)/shard_map/ppermute | solution.py:537
  153.8 14.2 %collective-permute-start.12 = (bf16[4,256,256]{2,1,0:T(8,128)(2,1)}, bf16[4,256,256]{2,1,0:T(8,128)(2,1)S(1)}, u32[]{:S(2)}, u32[]{:S(2)}) collective-permute-start(bf16[4,256,256]{2,1,0:T(8,128)(2,1)} %get-tuple-element.38), channel_id=1, source_target_pairs={{0,12},{4,0},{8,4},{12,8},{1,13},{5,1},{9,5},{13,9},{2,14},{6,2},{... | collective-permute-start | bytes 1572872 | tf_op jit(solution)/shard_map/ppermute | solution.py:537
  154.8 29.8 %collective-permute-start.15 = (bf16[2,4,256,256]{3,2,1,0:T(8,128)(2,1)}, bf16[2,4,256,256]{3,2,1,0:T(8,128)(2,1)}, u32[]{:S(2)}, u32[]{:S(2)}) collective-permute-start(bf16[2,4,256,256]{3,2,1,0:T(8,128)(2,1)} %get-tuple-element.36.refs_10_), channel_id=1, source_target_pairs={{0,1},{1,2},{2,3},{3,0},{4,5},{5,6},{6,7},{7,4},{8,9},{9,10},{10,1... | collective-permute-start | bytes 3145736 | tf_op jit(solution)/shard_map/ppermute | solution.py:537
  154.8 19.0 %copy-start.6 = (f32[4,4,8,64]{3,2,1,0:T(8,128)S(1)}, f32[4,4,8,64]{3,2,1,0:T(8,128)}, u32[]{:S(2)}) copy-start(f32[4,4,8,64]{3,2,1,0:T(8,128)} %shard_map.80.refs_10_) | copy-start | bytes 98308
  154.8 29.8 %collective-permute-start.16 = (bf16[2,4,256,256]{3,2,1,0:T(8,128)(2,1)}, bf16[2,4,256,256]{3,2,1,0:T(8,128)(2,1)}, u32[]{:S(2)}, u32[]{:S(2)}) collective-permute-start(bf16[2,4,256,256]{3,2,1,0:T(8,128)(2,1)} %get-tuple-element.42), channel_id=1, source_target_pairs={{0,3},{1,0},{2,1},{3,2},{4,7},{5,4},{6,5},{7,6},{8,11},{9,8},{10,9... | collective-permute-start | bytes 3145736 | tf_op jit(solution)/shard_map/ppermute | solution.py:537
  167.9 0.8 copy-start.8
  168.0 0.9 copy-start.9
  171.6 23.3 %collective-permute-start.13 = (bf16[2,4,256,256]{3,2,1,0:T(8,128)(2,1)}, bf16[2,4,256,256]{3,2,1,0:T(8,128)(2,1)S(1)}, u32[]{:S(2)}, u32[]{:S(2)}) collective-permute-start(bf16[2,4,256,256]{3,2,1,0:T(8,128)(2,1)} %get-tuple-element.39), channel_id=1, source_target_pairs={{0,4},{4,8},{8,12},{12,0},{1,5},{5,9},{9,13},{13,1},{2,6},{6,10},{... | collective-permute-start | bytes 3145736 | tf_op jit(solution)/shard_map/ppermute | solution.py:537
  173.8 24.4 %collective-permute-start.14 = (bf16[2,4,256,256]{3,2,1,0:T(8,128)(2,1)}, bf16[2,4,256,256]{3,2,1,0:T(8,128)(2,1)}, u32[]{:S(2)}, u32[]{:S(2)}) collective-permute-start(bf16[2,4,256,256]{3,2,1,0:T(8,128)(2,1)} %get-tuple-element.40), channel_id=1, source_target_pairs={{0,12},{4,0},{8,4},{12,8},{1,13},{5,1},{9,5},{13,9},{2,14},{6,2},{... | collective-permute-start | bytes 3145736 | tf_op jit(solution)/shard_map/ppermute | solution.py:537
  194.9 3.3 %copy-start.5 = (bf16[2,4,256,256]{3,2,1,0:T(8,128)(2,1)}, bf16[2,4,256,256]{3,2,1,0:T(8,128)(2,1)S(1)}, u32[]{:S(2)}) copy-start(bf16[2,4,256,256]{3,2,1,0:T(8,128)(2,1)S(1)} %collective-permute-done.13.prev_ref) | copy-start | bytes 3145732
Sparse Core Ops, SparseCore 0:
  9.8 90.0 all-gather.2

commit v8 on v7

--- a/solution.py
+++ b/solution.py
@@ -12,7 +12,7 @@
 NCH = 128
 TAPS = 4
 INTEG = 8
-CHUNKS = (4, 4)
+CHUNKS = (5, 3)
 
 F32 = jnp.float32
 BF16 = jnp.bfloat16
@@ -428,7 +428,7 @@
             scratch_shapes=scratch,
         ),
         compiler_params=limit(62),
-        cost_estimate=cost(0.1),
+        cost_estimate=cost(10 if by_row else 0.1),
     )(place, *args)
 
 
@@ -471,7 +471,7 @@
     down_out[0] = (down_ref[0].astype(F32) + high_ref[...].astype(F32)).astype(BF16)
 
 
-def added(up, down, low, high, after=()):
+def added(up, down, low, high, micros):
     _, size, panel, _ = up.shape
     real = pl.BlockSpec((1, size, panel, panel), lambda n: (0, 0, 0, 0))
     imag = pl.BlockSpec((1, size, panel, panel), lambda n: (1, 0, 0, 0))
@@ -481,12 +481,12 @@
         add_kernel,
         out_shape=[shape, shape],
         grid=(1,),
-        in_specs=[real, imag, one, one] + [ANY] * len(after),
+        in_specs=[real, imag, one, one],
         out_specs=[real, imag],
         input_output_aliases={0: 0, 1: 1},
         compiler_params=limit(62),
-        cost_estimate=cost(0.1),
-    )(up, down, low, high, *after)
+        cost_estimate=cost(micros),
+    )(up, down, low, high)
 
 
 def final_kernel(first, own_ref, prev_ref, next_ref, *refs):
@@ -562,19 +562,21 @@
     half_b = halves(*near_b, [own_a])
     far_b = both_ways(*half_b, "row")
     beam_b = own_beams(own_b, weights, half_b[:1])
+    half_a = halves(*near_a, [beam_b])
+    far_a = both_ways(*half_a, "col")
     slots_b = (own_b, *near_b, *far_b)
-    re_b, im_b = far_products(place_b, slots_b, True, [beam_b])
+    slots_a = (own_a, *near_a, *far_a)
+    re_b, im_b = far_products(place_b, slots_b, True, [half_a[0]])
     got_b = both_ways(re_b, im_b, "col")
-    half_a = halves(*near_a, [re_b])
-    far_a = both_ways(*half_a, "col")
-    slots_a = (own_a, *near_a, *far_a)
-    mine_b, up_b, down_b = near_products(place_b, slots_b, True, after=[half_a[0]])
-    sum_b = added(up_b, down_b, *got_b)
+    re_a, im_a = far_products(place_a, slots_a, False, [re_b])
+    got_a = both_ways(re_a, im_a, "row")
+    mine_b, up_b, down_b = near_products(place_b, slots_b, True, after=[re_a])
+    sum_b = added(up_b, down_b, *got_b, 0.1)
     sent_b = both_ways(*sum_b, "col")
-    re_a, im_a = far_products(place_a, slots_a, False, [sum_b[0]])
-    got_a = both_ways(re_a, im_a, "row")
-    mine_a, up_a, down_a, power_a = near_products(place_a, slots_a, False, size_b, beam_weights)
-    sum_a = added(up_a, down_a, *got_a)
+    mine_a, up_a, down_a, power_a = near_products(
+        place_a, slots_a, False, size_b, beam_weights, [sum_b[0]]
+    )
+    sum_a = added(up_a, down_a, *got_a, 20)
     sent_a = both_ways(*sum_a, "row")
 
     power_b = jnp.transpose(turn(beam_b, "col"), (1, 0, 2, 3)).reshape(size_b, -1, beam_b.shape[3])

time: 210 us -> 207 us (0.986)
  waiting for transfers between devices: 53.9 us -> 31.2 us
  blocking collectives: 43.4 us -> 56.8 us
  local copies, waits for them, and re-layouts: 3.53 us -> 6.72 us
    ppermute x16, waiting for transfers between devices: 28.7 us -> 11.7 us  [along(): lax.ppermute(value, axis, [(i, (i + step) % count) for i in range(count)])]
    all_to_all x2, blocking collectives: 43.4 us -> 56.8 us  [turn(): return lax.all_to_all(piece, axis, split_axis=0, concat_axis=0, tiled=True)]
    all_to_all x1, waiting for transfers between devices: 24.5 us -> 18.8 us  [turn(): return lax.all_to_all(piece, axis, split_axis=0, concat_axis=0, tiled=True)]
    unnamed x22, local copies, waits for them, and re-layouts: 2.11 us -> 5.29 us
  transfers between devices with their start and end apart: 19 -> 19, of which waited for: 8 -> 6; matrix products, arithmetic and copies ran while one was open for 2% -> 2% of each run, Pallas kernels for 26% -> 30%
where the time goes in v8:
time: 207 us; the launch traced here: 204 us
  Pallas kernels  63.5 us (31%)
  blocking collectives  56.8 us (27%)
  waiting for transfers between devices  31.2 us (15%)
  starting transfers between devices  28.6 us (14%)
  between operations  14.2 us (7%)
  local copies, waits for them, and re-layouts  6.72 us (3%)
  other arithmetic  2.61 us (1%)
    all_to_all x2, blocking collectives, turn(): return lax.all_to_all(piece, axis, split_axis=0, concat_axis=0, tiled=True)  56.8 us
    ppermute x16, starting transfers between devices, along(): lax.ppermute(value, axis, [(i, (i + step) % count) for i in range(count)])  20.8 us
    all_to_all x1, waiting for transfers between devices, turn(): return lax.all_to_all(piece, axis, split_axis=0, concat_axis=0, tiled=True)  18.8 us
    pallas_call x2, Pallas kernels, near_products(): pl.pallas_call(functools.partial(near_kernel, by_row, first), out_shape=s...  16.7 us
    ppermute x16, waiting for transfers between devices, along(): lax.ppermute(value, axis, [(i, (i + step) % count) for i in range(count)])  11.7 us
    pallas_call x2, Pallas kernels, far_products(): pl.pallas_call(functools.partial(far_kernel, by_row), out_shape=[pltpu.HB...  10.5 us
    pallas_call x1, Pallas kernels, own_beams(): pl.pallas_call(beam_kernel, out_shape=jax.ShapeDtypeStruct((owners, size,...  7 us
    pallas_call x1, Pallas kernels, spectra(): pl.pallas_call(functools.partial(spectrum_kernel, chunks), out_shape=[jax...  6.59 us
  transfers between devices with their start and end apart: 19, of which 6 were waited for; matrix products, arithmetic and copies ran while one was open for 2% of the time, Pallas kernels for 30%

profile of v8, /device:TPU:6, one launch (start us, length us, event | category | flops | bytes accessed | tf_op | source)
XLA Modules:
  0.0 203.7 jit_solution(14926737259234267548)
XLA Ops:
  7.2 0.0 all-gather.3.cloned.1.call-start
  7.2 0.7 all-gather.3.cloned.1.call-update
  7.9 0.9 slice.3
  8.8 3.5 %collective-permute-start = (bf16[2,64,384]{2,1,0:T(8,128)(2,1)S(1)}, bf16[2,64,384]{2,1,0:T(8,128)(2,1)S(1)}, u32[]{:S(2)}, u32[]{:S(2)}) collective-permute-start(bf16[2,64,384]{2,1,0:T(8,128)(2,1)S(1)} %slice.3), channel_id=1, source_target_pairs={{0,1},{1,2},{2,3},{3,4},{4,5},{5,6},{6,7},{7,8},{8,9},{9,10},{10,1... | collective-permute-start | bytes 294920 | tf_op jit(solution)/shard_map/ppermute | solution.py:56
  12.3 6.4 %shard_map.77.filt_ref = f32[2,4096,128]{2,1,0:T(8,128)S(1)} custom-call(bf16[2,64,8192]{2,1,0:T(8,128)(2,1)} %v_hbm.1, s32[1,64]{1,0:T(1,128)} %bitcast.13, f32[4,128]{1,0:T(4,128)} %constant.11.clone.coeff_hbm), custom_call_target="tpu_custom_call" | custom-call | flops 5500000256 | bytes 1 | tf_op jit(solution)/shard_map/pallas_call | solution.py:176
  18.7 0.0 collective-permute-done.halo_ref
  18.8 6.6 %shard_map.78 = (bf16[16,5,64,128]{3,2,1,0:T(8,128)(2,1)S(1)}, bf16[16,3,64,128]{3,2,1,0:T(8,128)(2,1)}) custom-call(f32[2,4096,128]{2,1,0:T(8,128)S(1)} %shard_map.77.filt_ref, bf16[2,64,384]{2,1,0:T(8,128)(2,1)S(1)} %collective-permute-done.halo_ref, s32[1,64]{1,0:T(1,128)} %bitcast.14, s32[1,128]{1,0:T(1,128)} %bitcast.15, ...), custom_call_target="tpu_custom_call" | custom-call | flops 6600000000 | bytes 1 | tf_op jit(solution)/shard_map/pallas_call | solution.py:191
  25.3 42.0 %all_to_all.15.own_ref.refs_0_.refs_5_ = bf16[16,5,64,128]{3,2,1,0:T(8,128)(2,1)S(1)} all-to-all(bf16[16,5,64,128]{3,2,1,0:T(8,128)(2,1)S(1)} %get-tuple-element.24), channel_id=1, replica_groups=mesh['chan'=16,'row'=4,'col'=4] {'chan'}, dimensions={0} | all-to-all | bytes 2621440 | tf_op jit(solution)/shard_map/all_to_all | solution.py:556
  67.4 4.3 %all-to-all-start = ((bf16[16,3,64,128]{3,2,1,0:T(8,128)(2,1)}), bf16[16,3,64,128]{3,2,1,0:T(8,128)(2,1)}, u32[]{:S(2)}, u32[]{:S(2)}) async-start(bf16[16,3,64,128]{3,2,1,0:T(8,128)(2,1)} %get-tuple-element.23), calls=%async_computation | async-start | bytes 1572864 | tf_op jit(solution)/shard_map/all_to_all | solution.py:556
  71.7 0.6 collective-permute-start.3
  72.2 1.5 collective-permute-start.4
  73.8 18.8 %all-to-all-done.refs_0_.refs_5_.own_ref = bf16[16,3,64,128]{3,2,1,0:T(8,128)(2,1)} async-done(((bf16[16,3,64,128]{3,2,1,0:T(8,128)(2,1)}), bf16[16,3,64,128]{3,2,1,0:T(8,128)(2,1)}, u32[]{:S(2)}, u32[]{:S(2)}) %all-to-all-start) | async-done | bytes 786464 | tf_op jit(solution)/shard_map/all_to_all | solution.py:556
  92.6 1.6 collective-permute-start.1
  94.2 1.7 collective-permute-start.2
  95.8 7.4 %collective-permute-done.3.low_ref.refs_1_.refs_6_.prev_ref = bf16[16,5,64,128]{3,2,1,0:T(8,128)(2,1)S(1)} collective-permute-done((bf16[16,5,64,128]{3,2,1,0:T(8,128)(2,1)S(1)}, bf16[16,5,64,128]{3,2,1,0:T(8,128)(2,1)S(1)}, u32[]{:S(2)}, u32[]{:S(2)}) %collective-permute-start.3) | collective-permute-done | bytes 1310752 | tf_op jit(solution)/shard_map/ppermute | solution.py:537
  103.3 1.1 copy-done.1
  104.3 0.5 collective-permute-done.4.high_ref.refs_2_.refs_7_.next_ref
  104.8 2.2 %shard_map.79 = (bf16[8,5,64,128]{3,2,1,0:T(8,128)(2,1)}, bf16[8,5,64,128]{3,2,1,0:T(8,128)(2,1)}) custom-call(bf16[16,5,64,128]{3,2,1,0:T(8,128)(2,1)} %copy-done.1, bf16[16,5,64,128]{3,2,1,0:T(8,128)(2,1)} %collective-permute-done.4.high_ref.refs_2_.refs_7_.next_ref, bf16[16,3,64,128]{3,2,1,0:T(8,128)(2,1)} %all-to-all-done.refs_0_.refs_5_.own_ref), custom_call_target="tpu_custom_call" | custom-call | flops 110000000 | bytes 1 | tf_op jit(solution)/shard_map/pallas_call | solution.py:225
  107.0 1.2 collective-permute-start.7
  108.2 0.8 collective-permute-start.8
  109.0 7.0 %shard_map.80.refs_0_ = f32[4,5,8,64]{3,2,1,0:T(8,128)} custom-call(bf16[16,5,64,128]{3,2,1,0:T(8,128)(2,1)} %copy-done, bf16[4,2,8,64,1024]{4,3,2,1,0:T(8,128)(2,1)} %bitcast.12, bf16[8,5,64,128]{3,2,1,0:T(8,128)(2,1)} %get-tuple-element.25.refs_0_), custom_call_target="tpu_custom_call" | custom-call | flops 110000000 | bytes 1 | tf_op jit(solution)/shard_map/pallas_call | solution.py:453
  116.0 0.0 collective-permute-done.1.low_ref.refs_1_.refs_6_.prev_ref
  116.0 0.0 collective-permute-done.2.high_ref.refs_2_.refs_7_.next_ref
  116.0 2.1 %shard_map.81 = (bf16[8,3,64,128]{3,2,1,0:T(8,128)(2,1)}, bf16[8,3,64,128]{3,2,1,0:T(8,128)(2,1)}) custom-call(bf16[16,3,64,128]{3,2,1,0:T(8,128)(2,1)} %collective-permute-done.1.low_ref.refs_1_.refs_6_.prev_ref, bf16[16,3,64,128]{3,2,1,0:T(8,128)(2,1)} %collective-permute-done.2.high_ref.refs_2_.refs_7_.next_ref, f32[4,5,8,64]{3,2,1,0:T(8,128)} %shard_map.80.refs_0_), custom_call_target="tpu_custom_call" | custom-call | flops 110000000 | bytes 1 | tf_op jit(solution)/shard_map/pallas_call | solution.py:225
  118.1 1.6 collective-permute-start.5
  119.6 1.7 collective-permute-start.6
  121.3 0.6 pad_add_fusion.1.place_ref
  121.9 0.6 pad_add_fusion.place_ref
  122.5 1.1 collective-permute-done.7.refs_3_.refs_8_.low_ref
  123.6 2.6 %collective-permute-done.8.refs_4_.refs_9_.high_ref = bf16[8,5,64,128]{3,2,1,0:T(8,128)(2,1)} collective-permute-done((bf16[8,5,64,128]{3,2,1,0:T(8,128)(2,1)}, bf16[8,5,64,128]{3,2,1,0:T(8,128)(2,1)}, u32[]{:S(2)}, u32[]{:S(2)}) %collective-permute-start.8) | collective-permute-done | bytes 655392 | tf_op jit(solution)/shard_map/ppermute | solution.py:537
  126.2 6.0 %shard_map.82 = (bf16[5,256,256]{2,1,0:T(8,128)(2,1)}, bf16[5,256,256]{2,1,0:T(8,128)(2,1)}) custom-call(s32[2]{0:T(128)} %pad_add_fusion.1.place_ref, bf16[16,5,64,128]{3,2,1,0:T(8,128)(2,1)} %copy-done, bf16[16,5,64,128]{3,2,1,0:T(8,128)(2,1)} %copy-done.1, bf16[16,5,64,128]{3,2,1,0:T(8,128)(2,1)} %collective-permute-done.4.high_ref.refs_2_.refs_7_.next_ref, ...), custom_call_target="tpu_custom_call" | custom-call | flops 110000000 | bytes 1 | tf_op jit(solution)/shard_map/pallas_call | solution.py:299
  132.1 2.7 %collective-permute-start.10 = (bf16[5,256,256]{2,1,0:T(8,128)(2,1)}, bf16[5,256,256]{2,1,0:T(8,128)(2,1)S(1)}, u32[]{:S(2)}, u32[]{:S(2)}) collective-permute-start(bf16[5,256,256]{2,1,0:T(8,128)(2,1)} %get-tuple-element.33), channel_id=1, source_target_pairs={{0,3},{1,0},{2,1},{3,2},{4,7},{5,4},{6,5},{7,6},{8,11},{9,8},{10,9... | collective-permute-start | bytes 1966088 | tf_op jit(solution)/shard_map/ppermute | solution.py:537
  134.8 0.0 collective-permute-start.9
  134.8 0.0 collective-permute-done.5.refs_3_.refs_8_.low_ref
  134.8 0.7 copy-done.2
  135.6 0.8 copy-done.3
  136.3 4.5 %shard_map.83 = (bf16[3,256,256]{2,1,0:T(8,128)(2,1)}, bf16[3,256,256]{2,1,0:T(8,128)(2,1)}) custom-call(s32[2]{0:T(128)} %pad_add_fusion.place_ref, bf16[16,3,64,128]{3,2,1,0:T(8,128)(2,1)} %all-to-all-done.refs_0_.refs_5_.own_ref, bf16[16,3,64,128]{3,2,1,0:T(8,128)(2,1)} %collective-permute-done.1.low_ref.refs_1_.refs_6_.prev_ref, ...), custom_call_target="tpu_custom_call" | custom-call | flops 110000000 | bytes 1 | tf_op jit(solution)/shard_map/pallas_call | solution.py:299
  140.9 1.1 collective-permute-start.11
  142.0 1.0 collective-permute-start.12
  143.0 8.5 %shard_map.84 = (f32[2,5,256,256]{3,2,1,0:T(8,128)}, bf16[2,5,256,256]{3,2,1,0:T(8,128)(2,1)}, bf16[2,5,256,256]{3,2,1,0:T(8,128)(2,1)}) custom-call(s32[2]{0:T(128)} %pad_add_fusion.1.place_ref, bf16[16,5,64,128]{3,2,1,0:T(8,128)(2,1)} %copy-done, bf16[16,5,64,128]{3,2,1,0:T(8,128)(2,1)} %copy-done.1, ...), custom_call_target="tpu_custom_call" | custom-call | flops 11000000512 | bytes 1 | tf_op jit(solution)/shard_map/pallas_call | solution.py:420
  151.5 0.0 collective-permute-done.10.high_ref
  151.5 0.1 collective-permute-done.9.low_ref
  151.6 0.7 copy-done.7
  152.3 3.0 %shard_map.85 = (bf16[2,5,256,256]{3,2,1,0:T(8,128)(2,1)}, bf16[2,5,256,256]{3,2,1,0:T(8,128)(2,1)}) custom-call(bf16[2,5,256,256]{3,2,1,0:T(8,128)(2,1)} %get-tuple-element.31.up_ref, bf16[2,5,256,256]{3,2,1,0:T(8,128)(2,1)} %get-tuple-element.32.down_ref, ...), custom_call_target="tpu_custom_call", output_to_operand_aliasing={{0}: (0, {}), {1}: (1, {})} | custom-call | flops 110000000 | bytes 1 | tf_op jit(solution)/shard_map/pallas_call | solution.py:480
  155.3 0.9 collective-permute-start.15
  156.2 2.3 %collective-permute-start.16 = (bf16[2,5,256,256]{3,2,1,0:T(8,128)(2,1)}, bf16[2,5,256,256]{3,2,1,0:T(8,128)(2,1)}, u32[]{:S(2)}, u32[]{:S(2)}) collective-permute-start(bf16[2,5,256,256]{3,2,1,0:T(8,128)(2,1)} %get-tuple-element.42), channel_id=1, source_target_pairs={{0,3},{1,0},{2,1},{3,2},{4,7},{5,4},{6,5},{7,6},{8,11},{9,8},{10,9... | collective-permute-start | bytes 3932168 | tf_op jit(solution)/shard_map/ppermute | solution.py:537
  158.5 8.2 %shard_map.86 = (f32[2,3,256,256]{3,2,1,0:T(8,128)}, bf16[2,3,256,256]{3,2,1,0:T(8,128)(2,1)}, bf16[2,3,256,256]{3,2,1,0:T(8,128)(2,1)}, f32[3,32,64]{2,1,0:T(8,128)}) custom-call(s32[2]{0:T(128)} %pad_add_fusion.place_ref, bf16[16,3,64,128]{3,2,1,0:T(8,128)(2,1)} %all-to-all-done.refs_0_.refs_5_.own_ref, ...), custom_call_target="tpu_custom_call" | custom-call | flops 110000000 | bytes 1 | tf_op jit(solution)/shard_map/pallas_call | solution.py:420
  166.8 0.0 collective-permute-done.11.low_ref
  166.8 0.0 copy-start.9
  166.8 0.7 copy-done.9
  167.5 2.4 %shard_map.87 = (bf16[2,3,256,256]{3,2,1,0:T(8,128)(2,1)}, bf16[2,3,256,256]{3,2,1,0:T(8,128)(2,1)}) custom-call(bf16[2,3,256,256]{3,2,1,0:T(8,128)(2,1)} %get-tuple-element.36.up_ref, bf16[2,3,256,256]{3,2,1,0:T(8,128)(2,1)} %get-tuple-element.37.down_ref, bf16[3,256,256]{2,1,0:T(8,128)(2,1)} %copy-done.9, ...), custom_call_target="tpu_custom_call", output_to_operand_aliasing={{0}: (0, {}), {1}: (1, {})} | custom-call | flops 22000001024 | bytes 1 | tf_op jit(solution)/shard_map/pallas_call | solution.py:480
  170.0 2.2 %collective-permute-start.13 = (bf16[2,3,256,256]{3,2,1,0:T(8,128)(2,1)}, bf16[2,3,256,256]{3,2,1,0:T(8,128)(2,1)}, u32[]{:S(2)}, u32[]{:S(2)}) collective-permute-start(bf16[2,3,256,256]{3,2,1,0:T(8,128)(2,1)} %get-tuple-element.39), channel_id=1, source_target_pairs={{0,4},{4,8},{8,12},{12,0},{1,5},{5,9},{9,13},{13,1},{2,6},{6,10},{... | collective-permute-start | bytes 2359304 | tf_op jit(solution)/shard_map/ppermute | solution.py:537
  172.2 0.0 collective-permute-start.14
  172.2 0.1 reshape.17
  172.3 14.8 %all_to_all.16 = f32[4,1,2560]{2,1,0:T(1,128)S(1)} all-to-all(f32[4,1,2560]{2,1,0:T(1,128)S(1)} %reshape.17), channel_id=1, replica_groups=mesh['chan'=16,'row'=4,'col'=4] {'col'}, dimensions={0} | all-to-all | bytes 81920 | tf_op jit(solution)/shard_map/all_to_all | solution.py:556
  187.1 0.5 broadcast
  187.6 0.8 reduce
  188.4 0.1 reshape.18
  188.5 0.7 maximum_bitcast_fusion
  189.2 0.0 collective-permute-done.15.prev_ref
  189.2 1.1 copy-done.5
  190.2 3.7 %shard_map.88.refs_0_ = f32[2,8,256,256]{3,2,1,0:T(8,128)} custom-call(f32[2,5,256,256]{3,2,1,0:T(8,128)} %get-tuple-element.41.own_ref, bf16[2,5,256,256]{3,2,1,0:T(8,128)(2,1)} %copy-done.5, bf16[2,5,256,256]{3,2,1,0:T(8,128)(2,1)} %collective-permute-done.16.next_ref), custom_call_target="tpu_custom_call" | custom-call | flops 110000000 | bytes 1 | tf_op jit(solution)/shard_map/pallas_call | solution.py:519
  194.0 0.0 collective-permute-done.13.prev_ref
  194.0 2.8 %shard_map.89 = f32[2,8,256,256]{3,2,1,0:T(8,128)} custom-call(f32[2,3,256,256]{3,2,1,0:T(8,128)} %get-tuple-element.35.own_ref, bf16[2,3,256,256]{3,2,1,0:T(8,128)(2,1)} %collective-permute-done.13.prev_ref, bf16[2,3,256,256]{3,2,1,0:T(8,128)(2,1)} %collective-permute-done.14.next_ref, ...), custom_call_target="tpu_custom_call", output_to_operand_aliasing={{}: (3, {})} | custom-call | flops 110000000 | bytes 1 | tf_op jit(solution)/shard_map/pallas_call | solution.py:519
  (19 shorter events, 0.0 us)
Async XLA Ops:
  7.2 101.8 %all-gather.3.cloned.1.call-start = ((), (), s32[]{:S(2)}) async-start(), calls=%async_computation.3 | async-start | bytes 10485760 | tf_op jit(solution)/shard_map/all_gather | solution.py:552
  8.8 9.9 %collective-permute-start = (bf16[2,64,384]{2,1,0:T(8,128)(2,1)S(1)}, bf16[2,64,384]{2,1,0:T(8,128)(2,1)S(1)}, u32[]{:S(2)}, u32[]{:S(2)}) collective-permute-start(bf16[2,64,384]{2,1,0:T(8,128)(2,1)S(1)} %slice.3), channel_id=1, source_target_pairs={{0,1},{1,2},{2,3},{3,4},{4,5},{5,6},{6,7},{7,8},{8,9},{9,10},{10,1... | collective-permute-start | bytes 294920 | tf_op jit(solution)/shard_map/ppermute | solution.py:56
  67.4 39.6 %copy-start = (bf16[16,5,64,128]{3,2,1,0:T(8,128)(2,1)}, bf16[16,5,64,128]{3,2,1,0:T(8,128)(2,1)S(1)}, u32[]{:S(2)}) copy-start(bf16[16,5,64,128]{3,2,1,0:T(8,128)(2,1)S(1)} %all_to_all.15.own_ref.refs_0_.refs_5_) | copy-start | bytes 3932164
  67.4 25.2 %all-to-all-start = ((bf16[16,3,64,128]{3,2,1,0:T(8,128)(2,1)}), bf16[16,3,64,128]{3,2,1,0:T(8,128)(2,1)}, u32[]{:S(2)}, u32[]{:S(2)}) async-start(bf16[16,3,64,128]{3,2,1,0:T(8,128)(2,1)} %get-tuple-element.23), calls=%async_computation | async-start | bytes 1572864 | tf_op jit(solution)/shard_map/all_to_all | solution.py:556
  71.7 31.6 %collective-permute-start.3 = (bf16[16,5,64,128]{3,2,1,0:T(8,128)(2,1)S(1)}, bf16[16,5,64,128]{3,2,1,0:T(8,128)(2,1)S(1)}, u32[]{:S(2)}, u32[]{:S(2)}) collective-permute-start(bf16[16,5,64,128]{3,2,1,0:T(8,128)(2,1)S(1)} %all_to_all.15.own_ref.refs_0_.refs_5_), channel_id=1, source_target_pairs={{0,4},{4,8},{8,12},{12,0},{1,5},{5,9},{9,13},{13,1},{2,6},{6,10},{... | collective-permute-start | bytes 3932168 | tf_op jit(solution)/shard_map/ppermute | solution.py:537
  72.2 32.6 %collective-permute-start.4 = (bf16[16,5,64,128]{3,2,1,0:T(8,128)(2,1)S(1)}, bf16[16,5,64,128]{3,2,1,0:T(8,128)(2,1)}, u32[]{:S(2)}, u32[]{:S(2)}) collective-permute-start(bf16[16,5,64,128]{3,2,1,0:T(8,128)(2,1)S(1)} %all_to_all.15.own_ref.refs_0_.refs_5_), channel_id=1, source_target_pairs={{0,12},{4,0},{8,4},{12,8},{1,13},{5,1},{9,5},{13,9},{2,14},{6,2},{... | collective-permute-start | bytes 3932168 | tf_op jit(solution)/shard_map/ppermute | solution.py:537
  92.6 23.4 %collective-permute-start.1 = (bf16[16,3,64,128]{3,2,1,0:T(8,128)(2,1)}, bf16[16,3,64,128]{3,2,1,0:T(8,128)(2,1)}, u32[]{:S(2)}, u32[]{:S(2)}) collective-permute-start(bf16[16,3,64,128]{3,2,1,0:T(8,128)(2,1)} %all-to-all-done.refs_0_.refs_5_.own_ref), channel_id=1, source_target_pairs={{0,1},{1,2},{2,3},{3,0},{4,5},{5,6},{6,7},{7,4},{8,9},{9,10},{10,1... | collective-permute-start | bytes 2359304 | tf_op jit(solution)/shard_map/ppermute | solution.py:537
  94.2 21.8 %collective-permute-start.2 = (bf16[16,3,64,128]{3,2,1,0:T(8,128)(2,1)}, bf16[16,3,64,128]{3,2,1,0:T(8,128)(2,1)}, u32[]{:S(2)}, u32[]{:S(2)}) collective-permute-start(bf16[16,3,64,128]{3,2,1,0:T(8,128)(2,1)} %all-to-all-done.refs_0_.refs_5_.own_ref), channel_id=1, source_target_pairs={{0,3},{1,0},{2,1},{3,2},{4,7},{5,4},{6,5},{7,6},{8,11},{9,8},{10,9... | collective-permute-start | bytes 2359304 | tf_op jit(solution)/shard_map/ppermute | solution.py:537
  103.3 1.1 copy-start.1
  107.0 16.6 %collective-permute-start.7 = (bf16[8,5,64,128]{3,2,1,0:T(8,128)(2,1)}, bf16[8,5,64,128]{3,2,1,0:T(8,128)(2,1)S(1)}, u32[]{:S(2)}, u32[]{:S(2)}) collective-permute-start(bf16[8,5,64,128]{3,2,1,0:T(8,128)(2,1)} %get-tuple-element.25.refs_0_), channel_id=1, source_target_pairs={{0,4},{4,8},{8,12},{12,0},{1,5},{5,9},{9,13},{13,1},{2,6},{6,10},{... | collective-permute-start | bytes 1966088 | tf_op jit(solution)/shard_map/ppermute | solution.py:537
  108.2 18.0 %collective-permute-start.8 = (bf16[8,5,64,128]{3,2,1,0:T(8,128)(2,1)}, bf16[8,5,64,128]{3,2,1,0:T(8,128)(2,1)}, u32[]{:S(2)}, u32[]{:S(2)}) collective-permute-start(bf16[8,5,64,128]{3,2,1,0:T(8,128)(2,1)} %get-tuple-element.28), channel_id=1, source_target_pairs={{0,12},{4,0},{8,4},{12,8},{1,13},{5,1},{9,5},{13,9},{2,14},{6,2},{... | collective-permute-start | bytes 1966088 | tf_op jit(solution)/shard_map/ppermute | solution.py:537
  118.1 16.8 %collective-permute-start.5 = (bf16[8,3,64,128]{3,2,1,0:T(8,128)(2,1)}, bf16[8,3,64,128]{3,2,1,0:T(8,128)(2,1)S(1)}, u32[]{:S(2)}, u32[]{:S(2)}) collective-permute-start(bf16[8,3,64,128]{3,2,1,0:T(8,128)(2,1)} %get-tuple-element.26.refs_10_), channel_id=1, source_target_pairs={{0,1},{1,2},{2,3},{3,0},{4,5},{5,6},{6,7},{7,4},{8,9},{9,10},{10,1... | collective-permute-start | bytes 1179656 | tf_op jit(solution)/shard_map/ppermute | solution.py:537
  119.6 15.2 %collective-permute-start.6 = (bf16[8,3,64,128]{3,2,1,0:T(8,128)(2,1)}, bf16[8,3,64,128]{3,2,1,0:T(8,128)(2,1)S(1)}, u32[]{:S(2)}, u32[]{:S(2)}) collective-permute-start(bf16[8,3,64,128]{3,2,1,0:T(8,128)(2,1)} %get-tuple-element.27), channel_id=1, source_target_pairs={{0,3},{1,0},{2,1},{3,2},{4,7},{5,4},{6,5},{7,6},{8,11},{9,8},{10,9... | collective-permute-start | bytes 1179656 | tf_op jit(solution)/shard_map/ppermute | solution.py:537
  123.6 2.6 %copy-start.4 = (bf16[8,5,64,128]{3,2,1,0:T(8,128)(2,1)}, bf16[8,5,64,128]{3,2,1,0:T(8,128)(2,1)S(1)}, u32[]{:S(2)}) copy-start(bf16[8,5,64,128]{3,2,1,0:T(8,128)(2,1)S(1)} %collective-permute-done.7.refs_3_.refs_8_.low_ref) | copy-start | bytes 1966084
  132.1 19.3 %collective-permute-start.10 = (bf16[5,256,256]{2,1,0:T(8,128)(2,1)}, bf16[5,256,256]{2,1,0:T(8,128)(2,1)S(1)}, u32[]{:S(2)}, u32[]{:S(2)}) collective-permute-start(bf16[5,256,256]{2,1,0:T(8,128)(2,1)} %get-tuple-element.33), channel_id=1, source_target_pairs={{0,3},{1,0},{2,1},{3,2},{4,7},{5,4},{6,5},{7,6},{8,11},{9,8},{10,9... | collective-permute-start | bytes 1966088 | tf_op jit(solution)/shard_map/ppermute | solution.py:537
  134.8 16.8 %collective-permute-start.9 = (bf16[5,256,256]{2,1,0:T(8,128)(2,1)}, bf16[5,256,256]{2,1,0:T(8,128)(2,1)}, u32[]{:S(2)}, u32[]{:S(2)}) collective-permute-start(bf16[5,256,256]{2,1,0:T(8,128)(2,1)} %get-tuple-element.29.refs_10_), channel_id=1, source_target_pairs={{0,1},{1,2},{2,3},{3,0},{4,5},{5,6},{6,7},{7,4},{8,9},{9,10},{10,1... | collective-permute-start | bytes 1966088 | tf_op jit(solution)/shard_map/ppermute | solution.py:537
  134.8 0.8 copy-start.2
  135.6 0.8 copy-start.3
  140.9 25.9 %collective-permute-start.11 = (bf16[3,256,256]{2,1,0:T(8,128)(2,1)}, bf16[3,256,256]{2,1,0:T(8,128)(2,1)S(1)}, u32[]{:S(2)}, u32[]{:S(2)}) collective-permute-start(bf16[3,256,256]{2,1,0:T(8,128)(2,1)} %get-tuple-element.30.refs_0_), channel_id=1, source_target_pairs={{0,4},{4,8},{8,12},{12,0},{1,5},{5,9},{9,13},{13,1},{2,6},{6,10},{... | collective-permute-start | bytes 1179656 | tf_op jit(solution)/shard_map/ppermute | solution.py:537
  142.0 24.8 %collective-permute-start.12 = (bf16[3,256,256]{2,1,0:T(8,128)(2,1)}, bf16[3,256,256]{2,1,0:T(8,128)(2,1)}, u32[]{:S(2)}, u32[]{:S(2)}) collective-permute-start(bf16[3,256,256]{2,1,0:T(8,128)(2,1)} %get-tuple-element.38), channel_id=1, source_target_pairs={{0,12},{4,0},{8,4},{12,8},{1,13},{5,1},{9,5},{13,9},{2,14},{6,2},{... | collective-permute-start | bytes 1179656 | tf_op jit(solution)/shard_map/ppermute | solution.py:537
  151.5 0.8 copy-start.7
  155.3 33.9 %collective-permute-start.15 = (bf16[2,5,256,256]{3,2,1,0:T(8,128)(2,1)}, bf16[2,5,256,256]{3,2,1,0:T(8,128)(2,1)S(1)}, u32[]{:S(2)}, u32[]{:S(2)}) collective-permute-start(bf16[2,5,256,256]{3,2,1,0:T(8,128)(2,1)} %get-tuple-element.34.refs_1_), channel_id=1, source_target_pairs={{0,1},{1,2},{2,3},{3,0},{4,5},{5,6},{6,7},{7,4},{8,9},{9,10},{10,1... | collective-permute-start | bytes 3932168 | tf_op jit(solution)/shard_map/ppermute | solution.py:537
  156.2 33.0 %collective-permute-start.16 = (bf16[2,5,256,256]{3,2,1,0:T(8,128)(2,1)}, bf16[2,5,256,256]{3,2,1,0:T(8,128)(2,1)}, u32[]{:S(2)}, u32[]{:S(2)}) collective-permute-start(bf16[2,5,256,256]{3,2,1,0:T(8,128)(2,1)} %get-tuple-element.42), channel_id=1, source_target_pairs={{0,3},{1,0},{2,1},{3,2},{4,7},{5,4},{6,5},{7,6},{8,11},{9,8},{10,9... | collective-permute-start | bytes 3932168 | tf_op jit(solution)/shard_map/ppermute | solution.py:537
  166.8 0.7 copy-start.9
  167.5 4.6 %copy-start.6 = (f32[4,5,8,64]{3,2,1,0:T(8,128)S(1)}, f32[4,5,8,64]{3,2,1,0:T(8,128)}, u32[]{:S(2)}) copy-start(f32[4,5,8,64]{3,2,1,0:T(8,128)} %shard_map.80.refs_0_) | copy-start | bytes 122884
  167.5 20.9 %copy-start.8 = (f32[3,32,64]{2,1,0:T(8,128)S(1)}, f32[3,32,64]{2,1,0:T(8,128)}, u32[]{:S(2)}) copy-start(f32[3,32,64]{2,1,0:T(8,128)} %get-tuple-element.43) | copy-start | bytes 73732
  170.0 24.0 %collective-permute-start.13 = (bf16[2,3,256,256]{3,2,1,0:T(8,128)(2,1)}, bf16[2,3,256,256]{3,2,1,0:T(8,128)(2,1)}, u32[]{:S(2)}, u32[]{:S(2)}) collective-permute-start(bf16[2,3,256,256]{3,2,1,0:T(8,128)(2,1)} %get-tuple-element.39), channel_id=1, source_target_pairs={{0,4},{4,8},{8,12},{12,0},{1,5},{5,9},{9,13},{13,1},{2,6},{6,10},{... | collective-permute-start | bytes 2359304 | tf_op jit(solution)/shard_map/ppermute | solution.py:537
  172.2 21.8 %collective-permute-start.14 = (bf16[2,3,256,256]{3,2,1,0:T(8,128)(2,1)}, bf16[2,3,256,256]{3,2,1,0:T(8,128)(2,1)}, u32[]{:S(2)}, u32[]{:S(2)}) collective-permute-start(bf16[2,3,256,256]{3,2,1,0:T(8,128)(2,1)} %get-tuple-element.40), channel_id=1, source_target_pairs={{0,12},{4,0},{8,4},{12,8},{1,13},{5,1},{9,5},{13,9},{2,14},{6,2},{... | collective-permute-start | bytes 2359304 | tf_op jit(solution)/shard_map/ppermute | solution.py:537
  189.2 1.1 copy-start.5
Sparse Core Ops, SparseCore 0:
  9.8 88.9 all-gather.2

commit v9 on v8

--- a/solution.py
+++ b/solution.py
@@ -465,13 +465,35 @@
     )(in_hbm(own), in_hbm(weights), *after)
 
 
+def keep_kernel(col_ref, *refs):
+    out_ref = refs[-1]
+    count = len(refs) - 1
+    col = col_ref[0]
+    for step, ref in enumerate(refs[:-1]):
+        bins = ref.shape[2]
+        at = pl.multiple_of(lax.rem(col + count - step, count) * bins, bins)
+        for k in range(ref.shape[1]):
+            out_ref[k, pl.ds(at, bins), :] = ref[col, k]
+
+
+def kept_beams(col, shared):
+    owners, size, bins, beams = shared[0].shape
+    return pl.pallas_call(
+        keep_kernel,
+        out_shape=jax.ShapeDtypeStruct((size, owners * bins, beams), F32),
+        in_specs=[SMEM] + [VMEM] * len(shared),
+        out_specs=VMEM,
+        cost_estimate=cost(0.1),
+    )(col, *shared)
+
+
 def add_kernel(up_ref, down_ref, low_ref, high_ref, *refs):
     up_out, down_out = refs[-2:]
     up_out[0] = (up_ref[0].astype(F32) + low_ref[...].astype(F32)).astype(BF16)
     down_out[0] = (down_ref[0].astype(F32) + high_ref[...].astype(F32)).astype(BF16)
 
 
-def added(up, down, low, high, micros):
+def added(up, down, low, high, micros, after=()):
     _, size, panel, _ = up.shape
     real = pl.BlockSpec((1, size, panel, panel), lambda n: (0, 0, 0, 0))
     imag = pl.BlockSpec((1, size, panel, panel), lambda n: (1, 0, 0, 0))
@@ -481,12 +503,12 @@
         add_kernel,
         out_shape=[shape, shape],
         grid=(1,),
-        in_specs=[real, imag, one, one],
+        in_specs=[real, imag, one, one] + [ANY] * len(after),
         out_specs=[real, imag],
         input_output_aliases={0: 0, 1: 1},
         compiler_params=limit(62),
         cost_estimate=cost(micros),
-    )(up, down, low, high)
+    )(up, down, low, high, *after)
 
 
 def final_kernel(first, own_ref, prev_ref, next_ref, *refs):
@@ -568,10 +590,10 @@
     slots_a = (own_a, *near_a, *far_a)
     re_b, im_b = far_products(place_b, slots_b, True, [half_a[0]])
     got_b = both_ways(re_b, im_b, "col")
-    re_a, im_a = far_products(place_a, slots_a, False, [re_b])
+    mine_b, up_b, down_b = near_products(place_b, slots_b, True, after=[re_b])
+    re_a, im_a = far_products(place_a, slots_a, False, [mine_b])
     got_a = both_ways(re_a, im_a, "row")
-    mine_b, up_b, down_b = near_products(place_b, slots_b, True, after=[re_a])
-    sum_b = added(up_b, down_b, *got_b, 0.1)
+    sum_b = added(up_b, down_b, *got_b, 0.1, [re_a])
     sent_b = both_ways(*sum_b, "col")
     mine_a, up_a, down_a, power_a = near_products(
         place_a, slots_a, False, size_b, beam_weights, [sum_b[0]]
@@ -579,7 +601,8 @@
     sum_a = added(up_a, down_a, *got_a, 20)
     sent_a = both_ways(*sum_a, "row")
 
-    power_b = jnp.transpose(turn(beam_b, "col"), (1, 0, 2, 3)).reshape(size_b, -1, beam_b.shape[3])
+    shared = [beam_b] + [along(beam_b, "col", step) for step in (1, 2, 3)]
+    power_b = kept_beams(col.reshape(1), shared)
     out = finished(mine_b, *sent_b, 0, channels, None)
     visibility = finished(mine_a, *sent_a, size_b, channels, out)
     power = jnp.concatenate([power_b, power_a], axis=0)

time: 207 us -> 219 us (1.058)
  waiting for transfers between devices: 31.2 us -> 54.2 us
  blocking collectives: 56.8 us -> 42 us
  starting transfers between devices: 28.6 us -> 31.7 us
    ppermute x16 -> x19, waiting for transfers between devices: 11.7 us -> 34.7 us  [along(): lax.ppermute(value, axis, [(i, (i + step) % count) for i in range(count)])]
    all_to_all x2 -> x1, blocking collectives: 56.8 us -> 42 us  [turn(): return lax.all_to_all(piece, axis, split_axis=0, concat_axis=0, tiled=True)]
    ppermute x16 -> x19, starting transfers between devices: 20.8 us -> 23.9 us  [along(): lax.ppermute(value, axis, [(i, (i + step) % count) for i in range(count)])]
    unnamed x22 -> x26, local copies, waits for them, and re-layouts: 5.29 us -> 4.76 us
  transfers between devices with their start and end apart: 19 -> 22, of which waited for: 6 -> 9; matrix products, arithmetic and copies ran while one was open for 2% -> 2% of each run, Pallas kernels for 30% -> 29%
where the time goes in v9:
time: 219 us; the launch traced here: 216 us
  Pallas kernels  65 us (30%)
  waiting for transfers between devices  54.2 us (25%)
  blocking collectives  42 us (19%)
  starting transfers between devices  31.7 us (14%)
  between operations  14.2 us (6%)
  local copies, waits for them, and re-layouts  5.67 us (3%)
  other arithmetic  2.77 us (1%)
    all_to_all x1, blocking collectives, turn(): return lax.all_to_all(piece, axis, split_axis=0, concat_axis=0, tiled=True)  42 us
    ppermute x19, waiting for transfers between devices, along(): lax.ppermute(value, axis, [(i, (i + step) % count) for i in range(count)])  34.7 us
    ppermute x19, starting transfers between devices, along(): lax.ppermute(value, axis, [(i, (i + step) % count) for i in range(count)])  23.9 us
    all_to_all x1, waiting for transfers between devices, turn(): return lax.all_to_all(piece, axis, split_axis=0, concat_axis=0, tiled=True)  18.8 us
    pallas_call x2, Pallas kernels, near_products(): pl.pallas_call(functools.partial(near_kernel, by_row, first), out_shape=s...  16.7 us
    pallas_call x2, Pallas kernels, far_products(): pl.pallas_call(functools.partial(far_kernel, by_row), out_shape=[pltpu.HB...  10.5 us
    pallas_call x1, Pallas kernels, own_beams(): pl.pallas_call(beam_kernel, out_shape=jax.ShapeDtypeStruct((owners, size,...  7 us
    pallas_call x1, Pallas kernels, spectra(): pl.pallas_call(functools.partial(spectrum_kernel, chunks), out_shape=[jax...  6.57 us
  transfers between devices with their start and end apart: 22, of which 9 were waited for; matrix products, arithmetic and copies ran while one was open for 2% of the time, Pallas kernels for 29%

profile of v9, /device:TPU:6, one launch (start us, length us, event | category | flops | bytes accessed | tf_op | source)
XLA Modules:
  0.0 215.6 jit_solution(12179747362703912946)
XLA Ops:
  7.2 0.0 all-gather.3.cloned.1.call-start
  7.2 0.7 all-gather.3.cloned.1.call-update
  7.9 0.9 slice.3
  8.8 3.5 %collective-permute-start = (bf16[2,64,384]{2,1,0:T(8,128)(2,1)S(1)}, bf16[2,64,384]{2,1,0:T(8,128)(2,1)S(1)}, u32[]{:S(2)}, u32[]{:S(2)}) collective-permute-start(bf16[2,64,384]{2,1,0:T(8,128)(2,1)S(1)} %slice.3), channel_id=1, source_target_pairs={{0,1},{1,2},{2,3},{3,4},{4,5},{5,6},{6,7},{7,8},{8,9},{9,10},{10,1... | collective-permute-start | bytes 294920 | tf_op jit(solution)/shard_map/ppermute | solution.py:56
  12.3 6.4 %shard_map.77.filt_ref = f32[2,4096,128]{2,1,0:T(8,128)S(1)} custom-call(bf16[2,64,8192]{2,1,0:T(8,128)(2,1)} %v_hbm.1, s32[1,64]{1,0:T(1,128)} %bitcast.8, f32[4,128]{1,0:T(4,128)} %constant.11.clone.coeff_hbm), custom_call_target="tpu_custom_call" | custom-call | flops 5500000256 | bytes 1 | tf_op jit(solution)/shard_map/pallas_call | solution.py:176
  18.7 0.0 collective-permute-done.halo_ref
  18.8 6.6 %shard_map.78 = (bf16[16,5,64,128]{3,2,1,0:T(8,128)(2,1)S(1)}, bf16[16,3,64,128]{3,2,1,0:T(8,128)(2,1)}) custom-call(f32[2,4096,128]{2,1,0:T(8,128)S(1)} %shard_map.77.filt_ref, bf16[2,64,384]{2,1,0:T(8,128)(2,1)S(1)} %collective-permute-done.halo_ref, s32[1,64]{1,0:T(1,128)} %bitcast.9, s32[1,128]{1,0:T(1,128)} %bitcast.10, ...), custom_call_target="tpu_custom_call" | custom-call | flops 6600000000 | bytes 1 | tf_op jit(solution)/shard_map/pallas_call | solution.py:191
  25.3 42.0 %all_to_all.10.own_ref.refs_0_.refs_5_ = bf16[16,5,64,128]{3,2,1,0:T(8,128)(2,1)S(1)} all-to-all(bf16[16,5,64,128]{3,2,1,0:T(8,128)(2,1)S(1)} %get-tuple-element.24), channel_id=1, replica_groups=mesh['chan'=16,'row'=4,'col'=4] {'chan'}, dimensions={0} | all-to-all | bytes 2621440 | tf_op jit(solution)/shard_map/all_to_all | solution.py:578
  67.3 4.3 %all-to-all-start = ((bf16[16,3,64,128]{3,2,1,0:T(8,128)(2,1)}), bf16[16,3,64,128]{3,2,1,0:T(8,128)(2,1)}, u32[]{:S(2)}, u32[]{:S(2)}) async-start(bf16[16,3,64,128]{3,2,1,0:T(8,128)(2,1)} %get-tuple-element.23), calls=%async_computation | async-start | bytes 1572864 | tf_op jit(solution)/shard_map/all_to_all | solution.py:578
  71.6 0.6 collective-permute-start.3
  72.2 1.5 collective-permute-start.4
  73.7 18.8 %all-to-all-done.refs_0_.refs_5_.own_ref = bf16[16,3,64,128]{3,2,1,0:T(8,128)(2,1)} async-done(((bf16[16,3,64,128]{3,2,1,0:T(8,128)(2,1)}), bf16[16,3,64,128]{3,2,1,0:T(8,128)(2,1)}, u32[]{:S(2)}, u32[]{:S(2)}) %all-to-all-start) | async-done | bytes 786464 | tf_op jit(solution)/shard_map/all_to_all | solution.py:578
  92.6 1.6 collective-permute-start.1
  94.1 1.7 collective-permute-start.2
  95.8 7.4 %collective-permute-done.3.low_ref.refs_1_.refs_6_.prev_ref = bf16[16,5,64,128]{3,2,1,0:T(8,128)(2,1)S(1)} collective-permute-done((bf16[16,5,64,128]{3,2,1,0:T(8,128)(2,1)S(1)}, bf16[16,5,64,128]{3,2,1,0:T(8,128)(2,1)S(1)}, u32[]{:S(2)}, u32[]{:S(2)}) %collective-permute-start.3) | collective-permute-done | bytes 1310752 | tf_op jit(solution)/shard_map/ppermute | solution.py:559
  103.2 1.1 copy-done.1
  104.3 0.4 collective-permute-done.4.high_ref.refs_2_.refs_7_.next_ref
  104.7 2.2 %shard_map.79 = (bf16[8,5,64,128]{3,2,1,0:T(8,128)(2,1)}, bf16[8,5,64,128]{3,2,1,0:T(8,128)(2,1)}) custom-call(bf16[16,5,64,128]{3,2,1,0:T(8,128)(2,1)} %copy-done.1, bf16[16,5,64,128]{3,2,1,0:T(8,128)(2,1)} %collective-permute-done.4.high_ref.refs_2_.refs_7_.next_ref, bf16[16,3,64,128]{3,2,1,0:T(8,128)(2,1)} %all-to-all-done.refs_0_.refs_5_.own_ref), custom_call_target="tpu_custom_call" | custom-call | flops 110000000 | bytes 1 | tf_op jit(solution)/shard_map/pallas_call | solution.py:225
  107.0 1.2 collective-permute-start.7
  108.2 0.8 collective-permute-start.8
  109.0 0.6 pad_add_fusion.1.place_ref
  109.5 0.7 pad_add_fusion.place_ref
  110.2 7.0 %shard_map.80.refs_0_ = f32[4,5,8,64]{3,2,1,0:T(8,128)} custom-call(bf16[16,5,64,128]{3,2,1,0:T(8,128)(2,1)} %copy-done, bf16[4,2,8,64,1024]{4,3,2,1,0:T(8,128)(2,1)} %bitcast.7, bf16[8,5,64,128]{3,2,1,0:T(8,128)(2,1)} %get-tuple-element.25.refs_0_), custom_call_target="tpu_custom_call" | custom-call | flops 110000000 | bytes 1 | tf_op jit(solution)/shard_map/pallas_call | solution.py:453
  117.2 0.0 collective-permute-done.1.low_ref.refs_1_.refs_6_.prev_ref
  117.2 0.0 collective-permute-done.2.high_ref.refs_2_.refs_7_.next_ref
  117.2 2.0 shard_map.81
  119.2 1.6 collective-permute-start.5
  120.8 1.7 collective-permute-start.6
  122.5 1.1 collective-permute-done.7.refs_3_.refs_8_.low_ref
  123.6 2.6 %collective-permute-done.8.refs_4_.refs_9_.high_ref = bf16[8,5,64,128]{3,2,1,0:T(8,128)(2,1)} collective-permute-done((bf16[8,5,64,128]{3,2,1,0:T(8,128)(2,1)}, bf16[8,5,64,128]{3,2,1,0:T(8,128)(2,1)}, u32[]{:S(2)}, u32[]{:S(2)}) %collective-permute-start.8) | collective-permute-done | bytes 655392 | tf_op jit(solution)/shard_map/ppermute | solution.py:559
  126.2 6.0 %shard_map.82 = (bf16[5,256,256]{2,1,0:T(8,128)(2,1)}, bf16[5,256,256]{2,1,0:T(8,128)(2,1)}) custom-call(s32[2]{0:T(128)} %pad_add_fusion.1.place_ref, bf16[16,5,64,128]{3,2,1,0:T(8,128)(2,1)} %copy-done, bf16[16,5,64,128]{3,2,1,0:T(8,128)(2,1)} %copy-done.1, bf16[16,5,64,128]{3,2,1,0:T(8,128)(2,1)} %collective-permute-done.4.high_ref.refs_2_.refs_7_.next_ref, ...), custom_call_target="tpu_custom_call" | custom-call | flops 110000000 | bytes 1 | tf_op jit(solution)/shard_map/pallas_call | solution.py:299
  132.1 2.7 %collective-permute-start.10 = (bf16[5,256,256]{2,1,0:T(8,128)(2,1)}, bf16[5,256,256]{2,1,0:T(8,128)(2,1)S(1)}, u32[]{:S(2)}, u32[]{:S(2)}) collective-permute-start(bf16[5,256,256]{2,1,0:T(8,128)(2,1)} %get-tuple-element.32), channel_id=1, source_target_pairs={{0,3},{1,0},{2,1},{3,2},{4,7},{5,4},{6,5},{7,6},{8,11},{9,8},{10,9... | collective-permute-start | bytes 1966088 | tf_op jit(solution)/shard_map/ppermute | solution.py:559
  134.8 8.4 %shard_map.83 = (f32[2,5,256,256]{3,2,1,0:T(8,128)}, bf16[2,5,256,256]{3,2,1,0:T(8,128)(2,1)}, bf16[2,5,256,256]{3,2,1,0:T(8,128)(2,1)}) custom-call(s32[2]{0:T(128)} %pad_add_fusion.1.place_ref, bf16[16,5,64,128]{3,2,1,0:T(8,128)(2,1)} %copy-done, bf16[16,5,64,128]{3,2,1,0:T(8,128)(2,1)} %copy-done.1, ...), custom_call_target="tpu_custom_call" | custom-call | flops 11000000512 | bytes 1 | tf_op jit(solution)/shard_map/pallas_call | solution.py:420
  143.2 0.8 copy-done.2
  144.0 0.2 copy-done.3
  144.2 4.6 %shard_map.84 = (bf16[3,256,256]{2,1,0:T(8,128)(2,1)}, bf16[3,256,256]{2,1,0:T(8,128)(2,1)}) custom-call(s32[2]{0:T(128)} %pad_add_fusion.place_ref, bf16[16,3,64,128]{3,2,1,0:T(8,128)(2,1)} %all-to-all-done.refs_0_.refs_5_.own_ref, bf16[16,3,64,128]{3,2,1,0:T(8,128)(2,1)} %collective-permute-done.1.low_ref.refs_1_.refs_6_.prev_ref, ...), custom_call_target="tpu_custom_call" | custom-call | flops 110000000 | bytes 1 | tf_op jit(solution)/shard_map/pallas_call | solution.py:299
  148.8 1.3 collective-permute-start.11
  150.1 1.0 collective-permute-start.12
  151.0 0.6 collective-permute-done.9.low_ref
  151.6 0.3 copy-done.7
  151.9 3.0 %shard_map.85 = (bf16[2,5,256,256]{3,2,1,0:T(8,128)(2,1)}, bf16[2,5,256,256]{3,2,1,0:T(8,128)(2,1)}) custom-call(bf16[2,5,256,256]{3,2,1,0:T(8,128)(2,1)} %get-tuple-element.30.up_ref, bf16[2,5,256,256]{3,2,1,0:T(8,128)(2,1)} %get-tuple-element.31.down_ref, ...), custom_call_target="tpu_custom_call", output_to_operand_aliasing={{0}: (0, {}), {1}: (1, {})} | custom-call | flops 110000000 | bytes 1 | tf_op jit(solution)/shard_map/pallas_call | solution.py:502
  154.8 0.9 collective-permute-start.15
  155.8 2.3 %collective-permute-start.16 = (bf16[2,5,256,256]{3,2,1,0:T(8,128)(2,1)}, bf16[2,5,256,256]{3,2,1,0:T(8,128)(2,1)}, u32[]{:S(2)}, u32[]{:S(2)}) collective-permute-start(bf16[2,5,256,256]{3,2,1,0:T(8,128)(2,1)} %get-tuple-element.42), channel_id=1, source_target_pairs={{0,3},{1,0},{2,1},{3,2},{4,7},{5,4},{6,5},{7,6},{8,11},{9,8},{10,9... | collective-permute-start | bytes 3932168 | tf_op jit(solution)/shard_map/ppermute | solution.py:559
  158.1 8.3 %shard_map.86 = (f32[2,3,256,256]{3,2,1,0:T(8,128)}, bf16[2,3,256,256]{3,2,1,0:T(8,128)(2,1)}, bf16[2,3,256,256]{3,2,1,0:T(8,128)(2,1)}, f32[3,32,64]{2,1,0:T(8,128)}) custom-call(s32[2]{0:T(128)} %pad_add_fusion.place_ref, bf16[16,3,64,128]{3,2,1,0:T(8,128)(2,1)} %all-to-all-done.refs_0_.refs_5_.own_ref, ...), custom_call_target="tpu_custom_call" | custom-call | flops 110000000 | bytes 1 | tf_op jit(solution)/shard_map/pallas_call | solution.py:420
  166.4 0.0 copy-start.12
  166.4 0.0 collective-permute-done.12.high_ref
  166.4 0.7 copy-done.12
  167.2 2.3 %shard_map.87 = (bf16[2,3,256,256]{3,2,1,0:T(8,128)(2,1)}, bf16[2,3,256,256]{3,2,1,0:T(8,128)(2,1)}) custom-call(bf16[2,3,256,256]{3,2,1,0:T(8,128)(2,1)} %get-tuple-element.37.up_ref, bf16[2,3,256,256]{3,2,1,0:T(8,128)(2,1)} %get-tuple-element.38.down_ref, bf16[3,256,256]{2,1,0:T(8,128)(2,1)} %copy-done.12, ...), custom_call_target="tpu_custom_call", output_to_operand_aliasing={{0}: (0, {}), {1}: (1, {})} | custom-call | flops 22000001024 | bytes 1 | tf_op jit(solution)/shard_map/pallas_call | solution.py:502
  169.5 2.3 %collective-permute-start.13 = (bf16[2,3,256,256]{3,2,1,0:T(8,128)(2,1)}, bf16[2,3,256,256]{3,2,1,0:T(8,128)(2,1)}, u32[]{:S(2)}, u32[]{:S(2)}) collective-permute-start(bf16[2,3,256,256]{3,2,1,0:T(8,128)(2,1)} %get-tuple-element.40), channel_id=1, source_target_pairs={{0,4},{4,8},{8,12},{12,0},{1,5},{5,9},{9,13},{13,1},{2,6},{6,10},{... | collective-permute-start | bytes 2359304 | tf_op jit(solution)/shard_map/ppermute | solution.py:559
  171.8 0.0 collective-permute-start.17
  171.8 15.0 %collective-permute-done.17.refs_1_ = f32[4,5,8,64]{3,2,1,0:T(8,128)S(1)} collective-permute-done((f32[4,5,8,64]{3,2,1,0:T(8,128)S(1)}, f32[4,5,8,64]{3,2,1,0:T(8,128)S(1)}, u32[]{:S(2)}, u32[]{:S(2)}) %collective-permute-start.17) | collective-permute-done | bytes 40992 | tf_op jit(solution)/shard_map/ppermute | solution.py:559
  186.8 0.7 collective-permute-start.18
  187.5 5.2 %collective-permute-done.18.refs_2_ = f32[4,5,8,64]{3,2,1,0:T(8,128)S(1)} collective-permute-done((f32[4,5,8,64]{3,2,1,0:T(8,128)S(1)}, f32[4,5,8,64]{3,2,1,0:T(8,128)S(1)}, u32[]{:S(2)}, u32[]{:S(2)}) %collective-permute-start.18) | collective-permute-done | bytes 40992 | tf_op jit(solution)/shard_map/ppermute | solution.py:559
  192.7 2.2 %collective-permute-start.19 = (f32[4,5,8,64]{3,2,1,0:T(8,128)S(1)}, f32[4,5,8,64]{3,2,1,0:T(8,128)S(1)}, u32[]{:S(2)}, u32[]{:S(2)}) collective-permute-start(f32[4,5,8,64]{3,2,1,0:T(8,128)S(1)} %copy-done.6), channel_id=1, source_target_pairs={{0,3},{1,0},{2,1},{3,2},{4,7},{5,4},{6,5},{7,6},{8,11},{9,8},{10,9... | collective-permute-start | bytes 122888 | tf_op jit(solution)/shard_map/ppermute | solution.py:559
  194.9 2.3 %collective-permute-done.19.refs_3_ = f32[4,5,8,64]{3,2,1,0:T(8,128)S(1)} collective-permute-done((f32[4,5,8,64]{3,2,1,0:T(8,128)S(1)}, f32[4,5,8,64]{3,2,1,0:T(8,128)S(1)}, u32[]{:S(2)}, u32[]{:S(2)}) %collective-permute-start.19) | collective-permute-done | bytes 40992 | tf_op jit(solution)/shard_map/ppermute | solution.py:559
  197.2 0.6 copy-done.10
  197.8 1.6 shard_map.90
  199.5 1.6 maximum_bitcast_fusion
  201.0 0.0 collective-permute-done.15.prev_ref
  201.0 0.0 collective-permute-done.16.next_ref
  201.0 1.1 copy-done.5
  202.1 3.7 %shard_map.88.refs_0_ = f32[2,8,256,256]{3,2,1,0:T(8,128)} custom-call(f32[2,5,256,256]{3,2,1,0:T(8,128)} %get-tuple-element.33.refs_10_.own_ref, bf16[2,5,256,256]{3,2,1,0:T(8,128)(2,1)} %copy-done.5, bf16[2,5,256,256]{3,2,1,0:T(8,128)(2,1)} %collective-permute-done.16.next_ref), custom_call_target="tpu_custom_call" | custom-call | flops 110000000 | bytes 1 | tf_op jit(solution)/shard_map/pallas_call | solution.py:541
  205.8 0.0 collective-permute-done.14.next_ref
  205.9 2.8 %shard_map.89 = f32[2,8,256,256]{3,2,1,0:T(8,128)} custom-call(f32[2,3,256,256]{3,2,1,0:T(8,128)} %get-tuple-element.36.own_ref, bf16[2,3,256,256]{3,2,1,0:T(8,128)(2,1)} %collective-permute-done.13.prev_ref, bf16[2,3,256,256]{3,2,1,0:T(8,128)(2,1)} %collective-permute-done.14.next_ref, ...), custom_call_target="tpu_custom_call", output_to_operand_aliasing={{}: (3, {})} | custom-call | flops 110000000 | bytes 1 | tf_op jit(solution)/shard_map/pallas_call | solution.py:541
  (26 shorter events, 0.1 us)
Async XLA Ops:
  7.2 103.0 %all-gather.3.cloned.1.call-start = ((), (), s32[]{:S(2)}) async-start(), calls=%async_computation.2 | async-start | bytes 10485760 | tf_op jit(solution)/shard_map/all_gather | solution.py:574
  8.8 9.9 %collective-permute-start = (bf16[2,64,384]{2,1,0:T(8,128)(2,1)S(1)}, bf16[2,64,384]{2,1,0:T(8,128)(2,1)S(1)}, u32[]{:S(2)}, u32[]{:S(2)}) collective-permute-start(bf16[2,64,384]{2,1,0:T(8,128)(2,1)S(1)} %slice.3), channel_id=1, source_target_pairs={{0,1},{1,2},{2,3},{3,4},{4,5},{5,6},{6,7},{7,8},{8,9},{9,10},{10,1... | collective-permute-start | bytes 294920 | tf_op jit(solution)/shard_map/ppermute | solution.py:56
  67.3 39.6 %copy-start = (bf16[16,5,64,128]{3,2,1,0:T(8,128)(2,1)}, bf16[16,5,64,128]{3,2,1,0:T(8,128)(2,1)S(1)}, u32[]{:S(2)}) copy-start(bf16[16,5,64,128]{3,2,1,0:T(8,128)(2,1)S(1)} %all_to_all.10.own_ref.refs_0_.refs_5_) | copy-start | bytes 3932164
  67.3 25.2 %all-to-all-start = ((bf16[16,3,64,128]{3,2,1,0:T(8,128)(2,1)}), bf16[16,3,64,128]{3,2,1,0:T(8,128)(2,1)}, u32[]{:S(2)}, u32[]{:S(2)}) async-start(bf16[16,3,64,128]{3,2,1,0:T(8,128)(2,1)} %get-tuple-element.23), calls=%async_computation | async-start | bytes 1572864 | tf_op jit(solution)/shard_map/all_to_all | solution.py:578
  71.6 31.6 %collective-permute-start.3 = (bf16[16,5,64,128]{3,2,1,0:T(8,128)(2,1)S(1)}, bf16[16,5,64,128]{3,2,1,0:T(8,128)(2,1)S(1)}, u32[]{:S(2)}, u32[]{:S(2)}) collective-permute-start(bf16[16,5,64,128]{3,2,1,0:T(8,128)(2,1)S(1)} %all_to_all.10.own_ref.refs_0_.refs_5_), channel_id=1, source_target_pairs={{0,4},{4,8},{8,12},{12,0},{1,5},{5,9},{9,13},{13,1},{2,6},{6,10},{... | collective-permute-start | bytes 3932168 | tf_op jit(solution)/shard_map/ppermute | solution.py:559
  72.2 32.6 %collective-permute-start.4 = (bf16[16,5,64,128]{3,2,1,0:T(8,128)(2,1)S(1)}, bf16[16,5,64,128]{3,2,1,0:T(8,128)(2,1)}, u32[]{:S(2)}, u32[]{:S(2)}) collective-permute-start(bf16[16,5,64,128]{3,2,1,0:T(8,128)(2,1)S(1)} %all_to_all.10.own_ref.refs_0_.refs_5_), channel_id=1, source_target_pairs={{0,12},{4,0},{8,4},{12,8},{1,13},{5,1},{9,5},{13,9},{2,14},{6,2},{... | collective-permute-start | bytes 3932168 | tf_op jit(solution)/shard_map/ppermute | solution.py:559
  92.6 24.6 %collective-permute-start.1 = (bf16[16,3,64,128]{3,2,1,0:T(8,128)(2,1)}, bf16[16,3,64,128]{3,2,1,0:T(8,128)(2,1)}, u32[]{:S(2)}, u32[]{:S(2)}) collective-permute-start(bf16[16,3,64,128]{3,2,1,0:T(8,128)(2,1)} %all-to-all-done.refs_0_.refs_5_.own_ref), channel_id=1, source_target_pairs={{0,1},{1,2},{2,3},{3,0},{4,5},{5,6},{6,7},{7,4},{8,9},{9,10},{10,1... | collective-permute-start | bytes 2359304 | tf_op jit(solution)/shard_map/ppermute | solution.py:559
  94.1 23.1 %collective-permute-start.2 = (bf16[16,3,64,128]{3,2,1,0:T(8,128)(2,1)}, bf16[16,3,64,128]{3,2,1,0:T(8,128)(2,1)}, u32[]{:S(2)}, u32[]{:S(2)}) collective-permute-start(bf16[16,3,64,128]{3,2,1,0:T(8,128)(2,1)} %all-to-all-done.refs_0_.refs_5_.own_ref), channel_id=1, source_target_pairs={{0,3},{1,0},{2,1},{3,2},{4,7},{5,4},{6,5},{7,6},{8,11},{9,8},{10,9... | collective-permute-start | bytes 2359304 | tf_op jit(solution)/shard_map/ppermute | solution.py:559
  103.2 1.1 copy-start.1
  107.0 16.6 %collective-permute-start.7 = (bf16[8,5,64,128]{3,2,1,0:T(8,128)(2,1)}, bf16[8,5,64,128]{3,2,1,0:T(8,128)(2,1)S(1)}, u32[]{:S(2)}, u32[]{:S(2)}) collective-permute-start(bf16[8,5,64,128]{3,2,1,0:T(8,128)(2,1)} %get-tuple-element.25.refs_0_), channel_id=1, source_target_pairs={{0,4},{4,8},{8,12},{12,0},{1,5},{5,9},{9,13},{13,1},{2,6},{6,10},{... | collective-permute-start | bytes 1966088 | tf_op jit(solution)/shard_map/ppermute | solution.py:559
  108.2 18.0 %collective-permute-start.8 = (bf16[8,5,64,128]{3,2,1,0:T(8,128)(2,1)}, bf16[8,5,64,128]{3,2,1,0:T(8,128)(2,1)}, u32[]{:S(2)}, u32[]{:S(2)}) collective-permute-start(bf16[8,5,64,128]{3,2,1,0:T(8,128)(2,1)} %get-tuple-element.28), channel_id=1, source_target_pairs={{0,12},{4,0},{8,4},{12,8},{1,13},{5,1},{9,5},{13,9},{2,14},{6,2},{... | collective-permute-start | bytes 1966088 | tf_op jit(solution)/shard_map/ppermute | solution.py:559
  119.2 24.0 %collective-permute-start.5 = (bf16[8,3,64,128]{3,2,1,0:T(8,128)(2,1)}, bf16[8,3,64,128]{3,2,1,0:T(8,128)(2,1)S(1)}, u32[]{:S(2)}, u32[]{:S(2)}) collective-permute-start(bf16[8,3,64,128]{3,2,1,0:T(8,128)(2,1)} %get-tuple-element.26.refs_10_), channel_id=1, source_target_pairs={{0,1},{1,2},{2,3},{3,0},{4,5},{5,6},{6,7},{7,4},{8,9},{9,10},{10,1... | collective-permute-start | bytes 1179656 | tf_op jit(solution)/shard_map/ppermute | solution.py:559
  120.8 22.4 %collective-permute-start.6 = (bf16[8,3,64,128]{3,2,1,0:T(8,128)(2,1)}, bf16[8,3,64,128]{3,2,1,0:T(8,128)(2,1)S(1)}, u32[]{:S(2)}, u32[]{:S(2)}) collective-permute-start(bf16[8,3,64,128]{3,2,1,0:T(8,128)(2,1)} %get-tuple-element.27), channel_id=1, source_target_pairs={{0,3},{1,0},{2,1},{3,2},{4,7},{5,4},{6,5},{7,6},{8,11},{9,8},{10,9... | collective-permute-start | bytes 1179656 | tf_op jit(solution)/shard_map/ppermute | solution.py:559
  123.6 2.6 %copy-start.4 = (bf16[8,5,64,128]{3,2,1,0:T(8,128)(2,1)}, bf16[8,5,64,128]{3,2,1,0:T(8,128)(2,1)S(1)}, u32[]{:S(2)}) copy-start(bf16[8,5,64,128]{3,2,1,0:T(8,128)(2,1)S(1)} %collective-permute-done.7.refs_3_.refs_8_.low_ref) | copy-start | bytes 1966084
  132.1 18.9 %collective-permute-start.10 = (bf16[5,256,256]{2,1,0:T(8,128)(2,1)}, bf16[5,256,256]{2,1,0:T(8,128)(2,1)S(1)}, u32[]{:S(2)}, u32[]{:S(2)}) collective-permute-start(bf16[5,256,256]{2,1,0:T(8,128)(2,1)} %get-tuple-element.32), channel_id=1, source_target_pairs={{0,3},{1,0},{2,1},{3,2},{4,7},{5,4},{6,5},{7,6},{8,11},{9,8},{10,9... | collective-permute-start | bytes 1966088 | tf_op jit(solution)/shard_map/ppermute | solution.py:559
  134.8 16.8 %collective-permute-start.9 = (bf16[5,256,256]{2,1,0:T(8,128)(2,1)}, bf16[5,256,256]{2,1,0:T(8,128)(2,1)}, u32[]{:S(2)}, u32[]{:S(2)}) collective-permute-start(bf16[5,256,256]{2,1,0:T(8,128)(2,1)} %get-tuple-element.29.refs_0_), channel_id=1, source_target_pairs={{0,1},{1,2},{2,3},{3,0},{4,5},{5,6},{6,7},{7,4},{8,9},{9,10},{10,1... | collective-permute-start | bytes 1966088 | tf_op jit(solution)/shard_map/ppermute | solution.py:559
  143.2 0.8 copy-start.2
  143.2 1.0 copy-start.3
  148.8 17.6 %collective-permute-start.11 = (bf16[3,256,256]{2,1,0:T(8,128)(2,1)}, bf16[3,256,256]{2,1,0:T(8,128)(2,1)S(1)}, u32[]{:S(2)}, u32[]{:S(2)}) collective-permute-start(bf16[3,256,256]{2,1,0:T(8,128)(2,1)} %get-tuple-element.34.refs_0_), channel_id=1, source_target_pairs={{0,4},{4,8},{8,12},{12,0},{1,5},{5,9},{9,13},{13,1},{2,6},{6,10},{... | collective-permute-start | bytes 1179656 | tf_op jit(solution)/shard_map/ppermute | solution.py:559
  150.1 16.4 %collective-permute-start.12 = (bf16[3,256,256]{2,1,0:T(8,128)(2,1)}, bf16[3,256,256]{2,1,0:T(8,128)(2,1)}, u32[]{:S(2)}, u32[]{:S(2)}) collective-permute-start(bf16[3,256,256]{2,1,0:T(8,128)(2,1)} %get-tuple-element.39), channel_id=1, source_target_pairs={{0,12},{4,0},{8,4},{12,8},{1,13},{5,1},{9,5},{13,9},{2,14},{6,2},{... | collective-permute-start | bytes 1179656 | tf_op jit(solution)/shard_map/ppermute | solution.py:559
  151.0 0.8 copy-start.7
  154.8 46.2 %collective-permute-start.15 = (bf16[2,5,256,256]{3,2,1,0:T(8,128)(2,1)}, bf16[2,5,256,256]{3,2,1,0:T(8,128)(2,1)S(1)}, u32[]{:S(2)}, u32[]{:S(2)}) collective-permute-start(bf16[2,5,256,256]{3,2,1,0:T(8,128)(2,1)} %get-tuple-element.35.refs_1_), channel_id=1, source_target_pairs={{0,1},{1,2},{2,3},{3,0},{4,5},{5,6},{6,7},{7,4},{8,9},{9,10},{10,1... | collective-permute-start | bytes 3932168 | tf_op jit(solution)/shard_map/ppermute | solution.py:559
  155.8 45.3 %collective-permute-start.16 = (bf16[2,5,256,256]{3,2,1,0:T(8,128)(2,1)}, bf16[2,5,256,256]{3,2,1,0:T(8,128)(2,1)}, u32[]{:S(2)}, u32[]{:S(2)}) collective-permute-start(bf16[2,5,256,256]{3,2,1,0:T(8,128)(2,1)} %get-tuple-element.42), channel_id=1, source_target_pairs={{0,3},{1,0},{2,1},{3,2},{4,7},{5,4},{6,5},{7,6},{8,11},{9,8},{10,9... | collective-permute-start | bytes 3932168 | tf_op jit(solution)/shard_map/ppermute | solution.py:559
  166.4 0.7 copy-start.12
  167.2 4.6 %copy-start.6 = (f32[4,5,8,64]{3,2,1,0:T(8,128)S(1)}, f32[4,5,8,64]{3,2,1,0:T(8,128)}, u32[]{:S(2)}) copy-start(f32[4,5,8,64]{3,2,1,0:T(8,128)} %shard_map.80.refs_0_) | copy-start | bytes 122884
  167.2 32.3 %copy-start.11 = (f32[3,32,64]{2,1,0:T(8,128)S(1)}, f32[3,32,64]{2,1,0:T(8,128)}, u32[]{:S(2)}) copy-start(f32[3,32,64]{2,1,0:T(8,128)} %get-tuple-element.43) | copy-start | bytes 73732
  169.5 36.3 %collective-permute-start.13 = (bf16[2,3,256,256]{3,2,1,0:T(8,128)(2,1)}, bf16[2,3,256,256]{3,2,1,0:T(8,128)(2,1)}, u32[]{:S(2)}, u32[]{:S(2)}) collective-permute-start(bf16[2,3,256,256]{3,2,1,0:T(8,128)(2,1)} %get-tuple-element.40), channel_id=1, source_target_pairs={{0,4},{4,8},{8,12},{12,0},{1,5},{5,9},{9,13},{13,1},{2,6},{6,10},{... | collective-permute-start | bytes 2359304 | tf_op jit(solution)/shard_map/ppermute | solution.py:559
  171.8 34.1 %collective-permute-start.14 = (bf16[2,3,256,256]{3,2,1,0:T(8,128)(2,1)}, bf16[2,3,256,256]{3,2,1,0:T(8,128)(2,1)}, u32[]{:S(2)}, u32[]{:S(2)}) collective-permute-start(bf16[2,3,256,256]{3,2,1,0:T(8,128)(2,1)} %get-tuple-element.41), channel_id=1, source_target_pairs={{0,12},{4,0},{8,4},{12,8},{1,13},{5,1},{9,5},{13,9},{2,14},{6,2},{... | collective-permute-start | bytes 2359304 | tf_op jit(solution)/shard_map/ppermute | solution.py:559
  171.8 15.0 %collective-permute-start.17 = (f32[4,5,8,64]{3,2,1,0:T(8,128)S(1)}, f32[4,5,8,64]{3,2,1,0:T(8,128)S(1)}, u32[]{:S(2)}, u32[]{:S(2)}) collective-permute-start(f32[4,5,8,64]{3,2,1,0:T(8,128)S(1)} %copy-done.6), channel_id=1, source_target_pairs={{0,1},{1,2},{2,3},{3,0},{4,5},{5,6},{6,7},{7,4},{8,9},{9,10},{10,1... | collective-permute-start | bytes 122888 | tf_op jit(solution)/shard_map/ppermute | solution.py:559
  186.8 10.4 %copy-start.8 = (f32[4,5,8,64]{3,2,1,0:T(8,128)}, f32[4,5,8,64]{3,2,1,0:T(8,128)S(1)}, u32[]{:S(2)}) copy-start(f32[4,5,8,64]{3,2,1,0:T(8,128)S(1)} %collective-permute-done.17.refs_1_) | copy-start | bytes 122884
  186.8 5.9 %collective-permute-start.18 = (f32[4,5,8,64]{3,2,1,0:T(8,128)S(1)}, f32[4,5,8,64]{3,2,1,0:T(8,128)S(1)}, u32[]{:S(2)}, u32[]{:S(2)}) collective-permute-start(f32[4,5,8,64]{3,2,1,0:T(8,128)S(1)} %copy-done.6), channel_id=1, source_target_pairs={{0,2},{1,3},{2,0},{3,1},{4,6},{5,7},{6,4},{7,5},{8,10},{9,11},{10,... | collective-permute-start | bytes 122888 | tf_op jit(solution)/shard_map/ppermute | solution.py:559
  192.7 4.4 %copy-start.9 = (f32[4,5,8,64]{3,2,1,0:T(8,128)}, f32[4,5,8,64]{3,2,1,0:T(8,128)S(1)}, u32[]{:S(2)}) copy-start(f32[4,5,8,64]{3,2,1,0:T(8,128)S(1)} %collective-permute-done.18.refs_2_) | copy-start | bytes 122884
  192.7 4.4 %collective-permute-start.19 = (f32[4,5,8,64]{3,2,1,0:T(8,128)S(1)}, f32[4,5,8,64]{3,2,1,0:T(8,128)S(1)}, u32[]{:S(2)}, u32[]{:S(2)}) collective-permute-start(f32[4,5,8,64]{3,2,1,0:T(8,128)S(1)} %copy-done.6), channel_id=1, source_target_pairs={{0,3},{1,0},{2,1},{3,2},{4,7},{5,4},{6,5},{7,6},{8,11},{9,8},{10,9... | collective-permute-start | bytes 122888 | tf_op jit(solution)/shard_map/ppermute | solution.py:559
  197.2 0.6 copy-start.10
  201.0 1.1 copy-start.5
Sparse Core Ops, SparseCore 0:
  9.8 88.9 all-gather.2

commit v10 on v8

--- a/solution.py
+++ b/solution.py
@@ -81,17 +81,22 @@
     taps = [jnp.broadcast_to(coeff_ref[t : t + 1, :], (inputs, NCH)) * mask for t in range(TAPS)]
     for part in range(2):
 
-        def frame_step(f, past, part=part):
-            lanes = pl.ds(pl.multiple_of(f * NCH, NCH), NCH)
-            window = past + (v_ref[part, :, lanes].astype(F32),)
-            total = taps[0] * window[0]
-            for t in range(1, TAPS):
-                total = total + taps[t] * window[t]
-            filt_ref[part, pl.ds(f, inputs, stride=frames), :] = total
-            return window[1:]
+        def frame_step(group, past, part=part):
+            totals = []
+            for f in range(8):
+                lanes = pl.ds(pl.multiple_of((group * 8 + f) * NCH, NCH), NCH)
+                window = past + (v_ref[part, :, lanes].astype(F32),)
+                total = taps[0] * window[0]
+                for t in range(1, TAPS):
+                    total = total + taps[t] * window[t]
+                totals.append(total)
+                past = window[1:]
+            at = pl.ds(pl.multiple_of(group * 8, 8), 8)
+            filt_ref[part, :, at, :] = jnp.transpose(jnp.stack(totals, axis=0), (1, 0, 2))
+            return past
 
         zero = v_ref[part, :, :NCH].astype(F32) * 0.0
-        lax.fori_loop(0, frames, frame_step, (zero,) * (TAPS - 1), unroll=8)
+        lax.fori_loop(0, frames // 8, frame_step, (zero,) * (TAPS - 1))
 
 
 def spectrum_kernel(chunks, filt_ref, halo_ref, flags_hbm, order_hbm, coeff_hbm, table_hbm, *rest):
@@ -113,7 +118,7 @@
     for copy in copies:
         copy.wait()
     inputs = halo_ref.shape[1]
-    frames = filt_ref.shape[1] // inputs
+    frames = filt_ref.shape[2]
     rows = 8
     mask = flag_column(flags_ref[...], inputs)
     taps = [jnp.broadcast_to(coeff_ref[t : t + 1, :], (inputs, NCH)) * mask for t in range(TAPS)]
@@ -131,37 +136,39 @@
         onehot.astype(BF16), table_ref[...], (((0,), (0,)), ((), ())), preferred_element_type=F32
     ).astype(BF16)
 
-    def input_step(pair, carry):
-        blocks = []
-        for which in range(2):
-            i = pair * 2 + which
-            both = []
-            for part in range(2):
-                block = filt_ref[part, pl.ds(pl.multiple_of(i * frames, frames), frames), :]
-                extra = corr_ref[part, pl.ds(pl.multiple_of(i * rows, rows), rows), :]
-                both.append(jnp.concatenate([block[:rows] + extra, block[rows:]], axis=0).astype(BF16))
-            re, im = both
-            blocks.append(jnp.concatenate([re, im], axis=1))
-            blocks.append(jnp.concatenate([im, -re], axis=1))
-        right = jnp.concatenate(blocks, axis=0)
-        result = lax.dot_general(
-            table, right, (((1,), (1,)), ((), ())), preferred_element_type=F32
-        )
-        for which in range(2):
-            spec_ref[pl.ds(pair * 2 + which, NCH, stride=inputs), :] = result[
-                :, which * NCH : (which + 1) * NCH
-            ]
+    def input_step(group, carry):
+        results = []
+        for pair in range(4):
+            blocks = []
+            for which in range(2):
+                i = group * 8 + pair * 2 + which
+                both = []
+                for part in range(2):
+                    block = filt_ref[part, i]
+                    extra = corr_ref[part, pl.ds(pl.multiple_of(i * rows, rows), rows), :]
+                    both.append(
+                        jnp.concatenate([block[:rows] + extra, block[rows:]], axis=0).astype(BF16)
+                    )
+                re, im = both
+                blocks.append(jnp.concatenate([re, im], axis=1))
+                blocks.append(jnp.concatenate([im, -re], axis=1))
+            right = jnp.concatenate(blocks, axis=0)
+            result = lax.dot_general(
+                table, right, (((1,), (1,)), ((), ())), preferred_element_type=F32
+            )
+            results += [result[:, :NCH], result[:, NCH:]]
+        at = pl.ds(pl.multiple_of(group * 8, 8), 8)
+        spec_ref[:, at, :] = jnp.transpose(jnp.stack(results, axis=0), (1, 0, 2))
         return carry
 
-    lax.fori_loop(0, inputs // 2, input_step, 0, unroll=4)
+    lax.fori_loop(0, inputs // 8, input_step, 0)
     per_block = sum(chunks)
 
     def copy_step(block, carry):
         first = 0
         for out, size in zip(outs, chunks):
             for k in range(size):
-                at = pl.multiple_of((block * per_block + first + k) * inputs, inputs)
-                out[block, k] = spec_ref[pl.ds(at, inputs), :].astype(BF16)
+                out[block, k] = spec_ref[block * per_block + first + k].astype(BF16)
             first += size
         return carry
 
@@ -175,7 +182,7 @@
     coeff = jnp.asarray(prototype(TAPS, NCH))
     filtered = pl.pallas_call(
         filter_kernel,
-        out_shape=jax.ShapeDtypeStruct((2, inputs * frames, NCH), F32),
+        out_shape=jax.ShapeDtypeStruct((2, inputs, frames, NCH), F32),
         in_specs=[HBM] * 3,
         out_specs=VMEM,
         scratch_shapes=[
@@ -199,7 +206,7 @@
             pltpu.VMEM((TAPS, NCH), F32),
             pltpu.VMEM((NCH, 2 * NCH), BF16),
             pltpu.VMEM((2, inputs * 8, NCH), F32),
-            pltpu.VMEM((NCH * inputs, 2 * frames), F32),
+            pltpu.VMEM((NCH, inputs, 2 * frames), F32),
             pltpu.SemaphoreType.DMA((4,)),
         ],
         compiler_params=limit(16),

time: 207 us -> 203 us (0.981)
  Pallas kernels: 63.5 us -> 59.3 us
    pallas_call x1, Pallas kernels: 6.43 us -> 3.64 us  [spectra(): pl.pallas_call(filter_kernel, out_shape=jax.ShapeDtypeStruct((2, inputs,...]
  transfers between devices with their start and end apart: 19 -> 19, of which waited for: 6 -> 6; matrix products, arithmetic and copies ran while one was open for 2% -> 2% of each run, Pallas kernels for 30% -> 28%
where the time goes in v10:
time: 203 us; the launch traced here: 200 us
  Pallas kernels  59.3 us (29%)
  blocking collectives  56.1 us (28%)
  waiting for transfers between devices  32.4 us (16%)
  starting transfers between devices  28.1 us (14%)
  between operations  14.2 us (7%)
  local copies, waits for them, and re-layouts  6.84 us (3%)
  other arithmetic  2.61 us (1%)
    all_to_all x2, blocking collectives, turn(): return lax.all_to_all(piece, axis, split_axis=0, concat_axis=0, tiled=True)  56.1 us
    ppermute x16, starting transfers between devices, along(): lax.ppermute(value, axis, [(i, (i + step) % count) for i in range(count)])  20.3 us
    all_to_all x1, waiting for transfers between devices, turn(): return lax.all_to_all(piece, axis, split_axis=0, concat_axis=0, tiled=True)  18.8 us
    pallas_call x2, Pallas kernels, near_products(): pl.pallas_call(functools.partial(near_kernel, by_row, first), out_shape=s...  16.7 us
    ppermute x16, waiting for transfers between devices, along(): lax.ppermute(value, axis, [(i, (i + step) % count) for i in range(count)])  11.4 us
    pallas_call x2, Pallas kernels, far_products(): pl.pallas_call(functools.partial(far_kernel, by_row), out_shape=[pltpu.HB...  10.5 us
    pallas_call x1, Pallas kernels, own_beams(): pl.pallas_call(beam_kernel, out_shape=jax.ShapeDtypeStruct((owners, size,...  7 us
    pallas_call x2, Pallas kernels, finished(): pl.pallas_call(functools.partial(final_kernel, first), out_shape=jax.Shap...  6.56 us
  transfers between devices with their start and end apart: 19, of which 6 were waited for; matrix products, arithmetic and copies ran while one was open for 2% of the time, Pallas kernels for 28%

profile of v10, /device:TPU:6, one launch (start us, length us, event | category | flops | bytes accessed | tf_op | source)
XLA Modules:
  0.0 199.6 jit_solution(18222860635760871283)
XLA Ops:
  7.2 0.0 all-gather.3.cloned.1.call-start
  7.2 0.7 all-gather.3.cloned.1.call-update
  7.9 0.9 slice.3
  8.8 3.5 %collective-permute-start = (bf16[2,64,384]{2,1,0:T(8,128)(2,1)S(1)}, bf16[2,64,384]{2,1,0:T(8,128)(2,1)S(1)}, u32[]{:S(2)}, u32[]{:S(2)}) collective-permute-start(bf16[2,64,384]{2,1,0:T(8,128)(2,1)S(1)} %slice.3), channel_id=1, source_target_pairs={{0,1},{1,2},{2,3},{3,4},{4,5},{5,6},{6,7},{7,8},{8,9},{9,10},{10,1... | collective-permute-start | bytes 294920 | tf_op jit(solution)/shard_map/ppermute | solution.py:56
  12.3 3.6 %shard_map.77.filt_ref = f32[2,64,64,128]{3,2,1,0:T(8,128)S(1)} custom-call(bf16[2,64,8192]{2,1,0:T(8,128)(2,1)} %v_hbm.1, s32[1,64]{1,0:T(1,128)} %bitcast.13, f32[4,128]{1,0:T(4,128)} %constant.11.clone.coeff_hbm), custom_call_target="tpu_custom_call" | custom-call | flops 5500000256 | bytes 1 | tf_op jit(solution)/shard_map/pallas_call | solution.py:183
  15.9 1.5 collective-permute-done.halo_ref
  17.4 5.3 %shard_map.78 = (bf16[16,5,64,128]{3,2,1,0:T(8,128)(2,1)S(1)}, bf16[16,3,64,128]{3,2,1,0:T(8,128)(2,1)}) custom-call(f32[2,64,64,128]{3,2,1,0:T(8,128)S(1)} %shard_map.77.filt_ref, bf16[2,64,384]{2,1,0:T(8,128)(2,1)S(1)} %collective-permute-done.halo_ref, s32[1,64]{1,0:T(1,128)} %bitcast.14, s32[1,128]{1,0:T(1,128)} %bitcast.15, ...), custom_call_target="tpu_custom_call" | custom-call | flops 6600000000 | bytes 1 | tf_op jit(solution)/shard_map/pallas_call | solution.py:198
  22.7 42.0 %all_to_all.15.own_ref.refs_0_.refs_5_ = bf16[16,5,64,128]{3,2,1,0:T(8,128)(2,1)S(1)} all-to-all(bf16[16,5,64,128]{3,2,1,0:T(8,128)(2,1)S(1)} %get-tuple-element.24), channel_id=1, replica_groups=mesh['chan'=16,'row'=4,'col'=4] {'chan'}, dimensions={0} | all-to-all | bytes 2621440 | tf_op jit(solution)/shard_map/all_to_all | solution.py:563
  64.7 4.3 %all-to-all-start = ((bf16[16,3,64,128]{3,2,1,0:T(8,128)(2,1)}), bf16[16,3,64,128]{3,2,1,0:T(8,128)(2,1)}, u32[]{:S(2)}, u32[]{:S(2)}) async-start(bf16[16,3,64,128]{3,2,1,0:T(8,128)(2,1)} %get-tuple-element.23), calls=%async_computation | async-start | bytes 1572864 | tf_op jit(solution)/shard_map/all_to_all | solution.py:563
  69.0 0.1 collective-permute-start.3
  69.1 2.0 %collective-permute-start.4 = (bf16[16,5,64,128]{3,2,1,0:T(8,128)(2,1)S(1)}, bf16[16,5,64,128]{3,2,1,0:T(8,128)(2,1)}, u32[]{:S(2)}, u32[]{:S(2)}) collective-permute-start(bf16[16,5,64,128]{3,2,1,0:T(8,128)(2,1)S(1)} %all_to_all.15.own_ref.refs_0_.refs_5_), channel_id=1, source_target_pairs={{0,12},{4,0},{8,4},{12,8},{1,13},{5,1},{9,5},{13,9},{2,14},{6,2},{... | collective-permute-start | bytes 3932168 | tf_op jit(solution)/shard_map/ppermute | solution.py:544
  71.1 18.8 %all-to-all-done.refs_0_.refs_5_.own_ref = bf16[16,3,64,128]{3,2,1,0:T(8,128)(2,1)} async-done(((bf16[16,3,64,128]{3,2,1,0:T(8,128)(2,1)}), bf16[16,3,64,128]{3,2,1,0:T(8,128)(2,1)}, u32[]{:S(2)}, u32[]{:S(2)}) %all-to-all-start) | async-done | bytes 786464 | tf_op jit(solution)/shard_map/all_to_all | solution.py:563
  90.0 0.1 collective-permute-start.1
  90.1 3.1 %collective-permute-start.2 = (bf16[16,3,64,128]{3,2,1,0:T(8,128)(2,1)}, bf16[16,3,64,128]{3,2,1,0:T(8,128)(2,1)}, u32[]{:S(2)}, u32[]{:S(2)}) collective-permute-start(bf16[16,3,64,128]{3,2,1,0:T(8,128)(2,1)} %all-to-all-done.refs_0_.refs_5_.own_ref), channel_id=1, source_target_pairs={{0,3},{1,0},{2,1},{3,2},{4,7},{5,4},{6,5},{7,6},{8,11},{9,8},{10,9... | collective-permute-start | bytes 2359304 | tf_op jit(solution)/shard_map/ppermute | solution.py:544
  93.2 7.4 %collective-permute-done.3.low_ref.refs_1_.refs_6_.prev_ref = bf16[16,5,64,128]{3,2,1,0:T(8,128)(2,1)S(1)} collective-permute-done((bf16[16,5,64,128]{3,2,1,0:T(8,128)(2,1)S(1)}, bf16[16,5,64,128]{3,2,1,0:T(8,128)(2,1)S(1)}, u32[]{:S(2)}, u32[]{:S(2)}) %collective-permute-start.3) | collective-permute-done | bytes 1310752 | tf_op jit(solution)/shard_map/ppermute | solution.py:544
  100.6 1.1 copy-done.1
  101.7 0.4 collective-permute-done.4.high_ref.refs_2_.refs_7_.next_ref
  102.0 2.2 %shard_map.79 = (bf16[8,5,64,128]{3,2,1,0:T(8,128)(2,1)}, bf16[8,5,64,128]{3,2,1,0:T(8,128)(2,1)}) custom-call(bf16[16,5,64,128]{3,2,1,0:T(8,128)(2,1)} %copy-done.1, bf16[16,5,64,128]{3,2,1,0:T(8,128)(2,1)} %collective-permute-done.4.high_ref.refs_2_.refs_7_.next_ref, bf16[16,3,64,128]{3,2,1,0:T(8,128)(2,1)} %all-to-all-done.refs_0_.refs_5_.own_ref), custom_call_target="tpu_custom_call" | custom-call | flops 110000000 | bytes 1 | tf_op jit(solution)/shard_map/pallas_call | solution.py:232
  104.2 0.9 collective-permute-start.7
  105.1 1.2 collective-permute-start.8
  106.3 7.0 %shard_map.80.refs_0_ = f32[4,5,8,64]{3,2,1,0:T(8,128)} custom-call(bf16[16,5,64,128]{3,2,1,0:T(8,128)(2,1)} %copy-done, bf16[4,2,8,64,1024]{4,3,2,1,0:T(8,128)(2,1)} %bitcast.12, bf16[8,5,64,128]{3,2,1,0:T(8,128)(2,1)} %get-tuple-element.25.refs_0_), custom_call_target="tpu_custom_call" | custom-call | flops 110000000 | bytes 1 | tf_op jit(solution)/shard_map/pallas_call | solution.py:460
  113.3 1.4 collective-permute-done.1.low_ref.refs_1_.refs_6_.prev_ref
  114.7 0.0 collective-permute-done.2.high_ref.refs_2_.refs_7_.next_ref
  114.7 2.0 %shard_map.81 = (bf16[8,3,64,128]{3,2,1,0:T(8,128)(2,1)}, bf16[8,3,64,128]{3,2,1,0:T(8,128)(2,1)}) custom-call(bf16[16,3,64,128]{3,2,1,0:T(8,128)(2,1)} %collective-permute-done.1.low_ref.refs_1_.refs_6_.prev_ref, bf16[16,3,64,128]{3,2,1,0:T(8,128)(2,1)} %collective-permute-done.2.high_ref.refs_2_.refs_7_.next_ref, f32[4,5,8,64]{3,2,1,0:T(8,128)} %shard_map.80.refs_0_), custom_call_target="tpu_custom_call" | custom-call | flops 110000000 | bytes 1 | tf_op jit(solution)/shard_map/pallas_call | solution.py:232
  116.7 1.5 collective-permute-start.5
  118.3 1.7 collective-permute-start.6
  120.0 0.6 pad_add_fusion.1.place_ref
  120.6 0.6 pad_add_fusion.place_ref
  121.2 0.0 collective-permute-done.7.refs_3_.refs_8_.low_ref
  121.2 2.1 %collective-permute-done.8.refs_4_.refs_9_.high_ref = bf16[8,5,64,128]{3,2,1,0:T(8,128)(2,1)} collective-permute-done((bf16[8,5,64,128]{3,2,1,0:T(8,128)(2,1)}, bf16[8,5,64,128]{3,2,1,0:T(8,128)(2,1)}, u32[]{:S(2)}, u32[]{:S(2)}) %collective-permute-start.8) | collective-permute-done | bytes 655392 | tf_op jit(solution)/shard_map/ppermute | solution.py:544
  123.3 6.0 %shard_map.82 = (bf16[5,256,256]{2,1,0:T(8,128)(2,1)}, bf16[5,256,256]{2,1,0:T(8,128)(2,1)}) custom-call(s32[2]{0:T(128)} %pad_add_fusion.1.place_ref, bf16[16,5,64,128]{3,2,1,0:T(8,128)(2,1)} %copy-done, bf16[16,5,64,128]{3,2,1,0:T(8,128)(2,1)} %copy-done.1, bf16[16,5,64,128]{3,2,1,0:T(8,128)(2,1)} %collective-permute-done.4.high_ref.refs_2_.refs_7_.next_ref, ...), custom_call_target="tpu_custom_call" | custom-call | flops 110000000 | bytes 1 | tf_op jit(solution)/shard_map/pallas_call | solution.py:306
  129.3 1.4 collective-permute-start.10
  130.7 0.7 collective-permute-start.9
  131.4 0.0 collective-permute-done.5.refs_3_.refs_8_.low_ref
  131.4 0.0 collective-permute-done.6.refs_4_.refs_9_.high_ref
  131.4 0.8 copy-done.2
  132.2 0.8 copy-done.3
  132.9 4.5 %shard_map.83 = (bf16[3,256,256]{2,1,0:T(8,128)(2,1)}, bf16[3,256,256]{2,1,0:T(8,128)(2,1)}) custom-call(s32[2]{0:T(128)} %pad_add_fusion.place_ref, bf16[16,3,64,128]{3,2,1,0:T(8,128)(2,1)} %all-to-all-done.refs_0_.refs_5_.own_ref, bf16[16,3,64,128]{3,2,1,0:T(8,128)(2,1)} %collective-permute-done.1.low_ref.refs_1_.refs_6_.prev_ref, ...), custom_call_target="tpu_custom_call" | custom-call | flops 110000000 | bytes 1 | tf_op jit(solution)/shard_map/pallas_call | solution.py:306
  137.5 1.1 collective-permute-start.11
  138.6 1.0 collective-permute-start.12
  139.6 8.5 %shard_map.84 = (f32[2,5,256,256]{3,2,1,0:T(8,128)}, bf16[2,5,256,256]{3,2,1,0:T(8,128)(2,1)}, bf16[2,5,256,256]{3,2,1,0:T(8,128)(2,1)}) custom-call(s32[2]{0:T(128)} %pad_add_fusion.1.place_ref, bf16[16,5,64,128]{3,2,1,0:T(8,128)(2,1)} %copy-done, bf16[16,5,64,128]{3,2,1,0:T(8,128)(2,1)} %copy-done.1, ...), custom_call_target="tpu_custom_call" | custom-call | flops 11000000512 | bytes 1 | tf_op jit(solution)/shard_map/pallas_call | solution.py:427
  148.1 0.0 collective-permute-done.10.high_ref
  148.1 0.0 collective-permute-done.9.low_ref
  148.1 0.8 copy-done.7
  148.9 3.0 %shard_map.85 = (bf16[2,5,256,256]{3,2,1,0:T(8,128)(2,1)}, bf16[2,5,256,256]{3,2,1,0:T(8,128)(2,1)}) custom-call(bf16[2,5,256,256]{3,2,1,0:T(8,128)(2,1)} %get-tuple-element.31.up_ref, bf16[2,5,256,256]{3,2,1,0:T(8,128)(2,1)} %get-tuple-element.32.down_ref, ...), custom_call_target="tpu_custom_call", output_to_operand_aliasing={{0}: (0, {}), {1}: (1, {})} | custom-call | flops 110000000 | bytes 1 | tf_op jit(solution)/shard_map/pallas_call | solution.py:487
  151.9 0.2 collective-permute-start.15
  152.1 3.0 %collective-permute-start.16 = (bf16[2,5,256,256]{3,2,1,0:T(8,128)(2,1)}, bf16[2,5,256,256]{3,2,1,0:T(8,128)(2,1)}, u32[]{:S(2)}, u32[]{:S(2)}) collective-permute-start(bf16[2,5,256,256]{3,2,1,0:T(8,128)(2,1)} %get-tuple-element.42), channel_id=1, source_target_pairs={{0,3},{1,0},{2,1},{3,2},{4,7},{5,4},{6,5},{7,6},{8,11},{9,8},{10,9... | collective-permute-start | bytes 3932168 | tf_op jit(solution)/shard_map/ppermute | solution.py:544
  155.1 8.2 %shard_map.86 = (f32[2,3,256,256]{3,2,1,0:T(8,128)}, bf16[2,3,256,256]{3,2,1,0:T(8,128)(2,1)}, bf16[2,3,256,256]{3,2,1,0:T(8,128)(2,1)}, f32[3,32,64]{2,1,0:T(8,128)}) custom-call(s32[2]{0:T(128)} %pad_add_fusion.place_ref, bf16[16,3,64,128]{3,2,1,0:T(8,128)(2,1)} %all-to-all-done.refs_0_.refs_5_.own_ref, ...), custom_call_target="tpu_custom_call" | custom-call | flops 110000000 | bytes 1 | tf_op jit(solution)/shard_map/pallas_call | solution.py:427
  163.4 0.0 collective-permute-done.11.low_ref
  163.4 0.0 copy-start.9
  163.4 0.7 copy-done.9
  164.1 2.4 %shard_map.87 = (bf16[2,3,256,256]{3,2,1,0:T(8,128)(2,1)}, bf16[2,3,256,256]{3,2,1,0:T(8,128)(2,1)}) custom-call(bf16[2,3,256,256]{3,2,1,0:T(8,128)(2,1)} %get-tuple-element.36.up_ref, bf16[2,3,256,256]{3,2,1,0:T(8,128)(2,1)} %get-tuple-element.37.down_ref, bf16[3,256,256]{2,1,0:T(8,128)(2,1)} %copy-done.9, ...), custom_call_target="tpu_custom_call", output_to_operand_aliasing={{0}: (0, {}), {1}: (1, {})} | custom-call | flops 22000001024 | bytes 1 | tf_op jit(solution)/shard_map/pallas_call | solution.py:487
  166.5 2.2 %collective-permute-start.13 = (bf16[2,3,256,256]{3,2,1,0:T(8,128)(2,1)}, bf16[2,3,256,256]{3,2,1,0:T(8,128)(2,1)}, u32[]{:S(2)}, u32[]{:S(2)}) collective-permute-start(bf16[2,3,256,256]{3,2,1,0:T(8,128)(2,1)} %get-tuple-element.39), channel_id=1, source_target_pairs={{0,4},{4,8},{8,12},{12,0},{1,5},{5,9},{9,13},{13,1},{2,6},{6,10},{... | collective-permute-start | bytes 2359304 | tf_op jit(solution)/shard_map/ppermute | solution.py:544
  168.8 0.0 collective-permute-start.14
  168.8 0.1 reshape.17
  168.9 14.1 %all_to_all.16 = f32[4,1,2560]{2,1,0:T(1,128)S(1)} all-to-all(f32[4,1,2560]{2,1,0:T(1,128)S(1)} %reshape.17), channel_id=1, replica_groups=mesh['chan'=16,'row'=4,'col'=4] {'col'}, dimensions={0} | all-to-all | bytes 81920 | tf_op jit(solution)/shard_map/all_to_all | solution.py:563
  183.0 0.5 broadcast
  183.5 0.8 reduce
  184.3 0.1 reshape.18
  184.4 0.7 maximum_bitcast_fusion
  185.1 1.1 copy-done.5
  186.1 3.7 %shard_map.88.refs_0_ = f32[2,8,256,256]{3,2,1,0:T(8,128)} custom-call(f32[2,5,256,256]{3,2,1,0:T(8,128)} %get-tuple-element.41.own_ref, bf16[2,5,256,256]{3,2,1,0:T(8,128)(2,1)} %copy-done.5, bf16[2,5,256,256]{3,2,1,0:T(8,128)(2,1)} %collective-permute-done.16.next_ref), custom_call_target="tpu_custom_call" | custom-call | flops 110000000 | bytes 1 | tf_op jit(solution)/shard_map/pallas_call | solution.py:526
  189.9 0.0 collective-permute-done.14.next_ref
  189.9 2.8 %shard_map.89 = f32[2,8,256,256]{3,2,1,0:T(8,128)} custom-call(f32[2,3,256,256]{3,2,1,0:T(8,128)} %get-tuple-element.35.own_ref, bf16[2,3,256,256]{3,2,1,0:T(8,128)(2,1)} %collective-permute-done.13.prev_ref, bf16[2,3,256,256]{3,2,1,0:T(8,128)(2,1)} %collective-permute-done.14.next_ref, ...), custom_call_target="tpu_custom_call", output_to_operand_aliasing={{}: (3, {})} | custom-call | flops 110000000 | bytes 1 | tf_op jit(solution)/shard_map/pallas_call | solution.py:526
  (19 shorter events, 0.0 us)
Async XLA Ops:
  7.2 99.1 %all-gather.3.cloned.1.call-start = ((), (), s32[]{:S(2)}) async-start(), calls=%async_computation.3 | async-start | bytes 10485760 | tf_op jit(solution)/shard_map/all_gather | solution.py:559
  8.8 8.6 %collective-permute-start = (bf16[2,64,384]{2,1,0:T(8,128)(2,1)S(1)}, bf16[2,64,384]{2,1,0:T(8,128)(2,1)S(1)}, u32[]{:S(2)}, u32[]{:S(2)}) collective-permute-start(bf16[2,64,384]{2,1,0:T(8,128)(2,1)S(1)} %slice.3), channel_id=1, source_target_pairs={{0,1},{1,2},{2,3},{3,4},{4,5},{5,6},{6,7},{7,8},{8,9},{9,10},{10,1... | collective-permute-start | bytes 294920 | tf_op jit(solution)/shard_map/ppermute | solution.py:56
  64.7 39.5 %copy-start = (bf16[16,5,64,128]{3,2,1,0:T(8,128)(2,1)}, bf16[16,5,64,128]{3,2,1,0:T(8,128)(2,1)S(1)}, u32[]{:S(2)}) copy-start(bf16[16,5,64,128]{3,2,1,0:T(8,128)(2,1)S(1)} %all_to_all.15.own_ref.refs_0_.refs_5_) | copy-start | bytes 3932164
  64.7 25.2 %all-to-all-start = ((bf16[16,3,64,128]{3,2,1,0:T(8,128)(2,1)}), bf16[16,3,64,128]{3,2,1,0:T(8,128)(2,1)}, u32[]{:S(2)}, u32[]{:S(2)}) async-start(bf16[16,3,64,128]{3,2,1,0:T(8,128)(2,1)} %get-tuple-element.23), calls=%async_computation | async-start | bytes 1572864 | tf_op jit(solution)/shard_map/all_to_all | solution.py:563
  69.0 31.6 %collective-permute-start.3 = (bf16[16,5,64,128]{3,2,1,0:T(8,128)(2,1)S(1)}, bf16[16,5,64,128]{3,2,1,0:T(8,128)(2,1)S(1)}, u32[]{:S(2)}, u32[]{:S(2)}) collective-permute-start(bf16[16,5,64,128]{3,2,1,0:T(8,128)(2,1)S(1)} %all_to_all.15.own_ref.refs_0_.refs_5_), channel_id=1, source_target_pairs={{0,4},{4,8},{8,12},{12,0},{1,5},{5,9},{9,13},{13,1},{2,6},{6,10},{... | collective-permute-start | bytes 3932168 | tf_op jit(solution)/shard_map/ppermute | solution.py:544
  69.1 32.9 %collective-permute-start.4 = (bf16[16,5,64,128]{3,2,1,0:T(8,128)(2,1)S(1)}, bf16[16,5,64,128]{3,2,1,0:T(8,128)(2,1)}, u32[]{:S(2)}, u32[]{:S(2)}) collective-permute-start(bf16[16,5,64,128]{3,2,1,0:T(8,128)(2,1)S(1)} %all_to_all.15.own_ref.refs_0_.refs_5_), channel_id=1, source_target_pairs={{0,12},{4,0},{8,4},{12,8},{1,13},{5,1},{9,5},{13,9},{2,14},{6,2},{... | collective-permute-start | bytes 3932168 | tf_op jit(solution)/shard_map/ppermute | solution.py:544
  90.0 24.7 %collective-permute-start.1 = (bf16[16,3,64,128]{3,2,1,0:T(8,128)(2,1)}, bf16[16,3,64,128]{3,2,1,0:T(8,128)(2,1)}, u32[]{:S(2)}, u32[]{:S(2)}) collective-permute-start(bf16[16,3,64,128]{3,2,1,0:T(8,128)(2,1)} %all-to-all-done.refs_0_.refs_5_.own_ref), channel_id=1, source_target_pairs={{0,1},{1,2},{2,3},{3,0},{4,5},{5,6},{6,7},{7,4},{8,9},{9,10},{10,1... | collective-permute-start | bytes 2359304 | tf_op jit(solution)/shard_map/ppermute | solution.py:544
  90.1 24.6 %collective-permute-start.2 = (bf16[16,3,64,128]{3,2,1,0:T(8,128)(2,1)}, bf16[16,3,64,128]{3,2,1,0:T(8,128)(2,1)}, u32[]{:S(2)}, u32[]{:S(2)}) collective-permute-start(bf16[16,3,64,128]{3,2,1,0:T(8,128)(2,1)} %all-to-all-done.refs_0_.refs_5_.own_ref), channel_id=1, source_target_pairs={{0,3},{1,0},{2,1},{3,2},{4,7},{5,4},{6,5},{7,6},{8,11},{9,8},{10,9... | collective-permute-start | bytes 2359304 | tf_op jit(solution)/shard_map/ppermute | solution.py:544
  100.6 1.1 copy-start.1
  104.2 16.9 %collective-permute-start.7 = (bf16[8,5,64,128]{3,2,1,0:T(8,128)(2,1)}, bf16[8,5,64,128]{3,2,1,0:T(8,128)(2,1)S(1)}, u32[]{:S(2)}, u32[]{:S(2)}) collective-permute-start(bf16[8,5,64,128]{3,2,1,0:T(8,128)(2,1)} %get-tuple-element.25.refs_0_), channel_id=1, source_target_pairs={{0,4},{4,8},{8,12},{12,0},{1,5},{5,9},{9,13},{13,1},{2,6},{6,10},{... | collective-permute-start | bytes 1966088 | tf_op jit(solution)/shard_map/ppermute | solution.py:544
  105.1 18.2 %collective-permute-start.8 = (bf16[8,5,64,128]{3,2,1,0:T(8,128)(2,1)}, bf16[8,5,64,128]{3,2,1,0:T(8,128)(2,1)}, u32[]{:S(2)}, u32[]{:S(2)}) collective-permute-start(bf16[8,5,64,128]{3,2,1,0:T(8,128)(2,1)} %get-tuple-element.28), channel_id=1, source_target_pairs={{0,12},{4,0},{8,4},{12,8},{1,13},{5,1},{9,5},{13,9},{2,14},{6,2},{... | collective-permute-start | bytes 1966088 | tf_op jit(solution)/shard_map/ppermute | solution.py:544
  116.7 14.7 %collective-permute-start.5 = (bf16[8,3,64,128]{3,2,1,0:T(8,128)(2,1)}, bf16[8,3,64,128]{3,2,1,0:T(8,128)(2,1)S(1)}, u32[]{:S(2)}, u32[]{:S(2)}) collective-permute-start(bf16[8,3,64,128]{3,2,1,0:T(8,128)(2,1)} %get-tuple-element.26.refs_10_), channel_id=1, source_target_pairs={{0,1},{1,2},{2,3},{3,0},{4,5},{5,6},{6,7},{7,4},{8,9},{9,10},{10,1... | collective-permute-start | bytes 1179656 | tf_op jit(solution)/shard_map/ppermute | solution.py:544
  118.3 13.1 %collective-permute-start.6 = (bf16[8,3,64,128]{3,2,1,0:T(8,128)(2,1)}, bf16[8,3,64,128]{3,2,1,0:T(8,128)(2,1)S(1)}, u32[]{:S(2)}, u32[]{:S(2)}) collective-permute-start(bf16[8,3,64,128]{3,2,1,0:T(8,128)(2,1)} %get-tuple-element.27), channel_id=1, source_target_pairs={{0,3},{1,0},{2,1},{3,2},{4,7},{5,4},{6,5},{7,6},{8,11},{9,8},{10,9... | collective-permute-start | bytes 1179656 | tf_op jit(solution)/shard_map/ppermute | solution.py:544
  121.2 2.2 %copy-start.4 = (bf16[8,5,64,128]{3,2,1,0:T(8,128)(2,1)}, bf16[8,5,64,128]{3,2,1,0:T(8,128)(2,1)S(1)}, u32[]{:S(2)}) copy-start(bf16[8,5,64,128]{3,2,1,0:T(8,128)(2,1)S(1)} %collective-permute-done.7.refs_3_.refs_8_.low_ref) | copy-start | bytes 1966084
  129.3 18.8 %collective-permute-start.10 = (bf16[5,256,256]{2,1,0:T(8,128)(2,1)}, bf16[5,256,256]{2,1,0:T(8,128)(2,1)S(1)}, u32[]{:S(2)}, u32[]{:S(2)}) collective-permute-start(bf16[5,256,256]{2,1,0:T(8,128)(2,1)} %get-tuple-element.33), channel_id=1, source_target_pairs={{0,3},{1,0},{2,1},{3,2},{4,7},{5,4},{6,5},{7,6},{8,11},{9,8},{10,9... | collective-permute-start | bytes 1966088 | tf_op jit(solution)/shard_map/ppermute | solution.py:544
  130.7 17.4 %collective-permute-start.9 = (bf16[5,256,256]{2,1,0:T(8,128)(2,1)}, bf16[5,256,256]{2,1,0:T(8,128)(2,1)}, u32[]{:S(2)}, u32[]{:S(2)}) collective-permute-start(bf16[5,256,256]{2,1,0:T(8,128)(2,1)} %get-tuple-element.29.refs_10_), channel_id=1, source_target_pairs={{0,1},{1,2},{2,3},{3,0},{4,5},{5,6},{6,7},{7,4},{8,9},{9,10},{10,1... | collective-permute-start | bytes 1966088 | tf_op jit(solution)/shard_map/ppermute | solution.py:544
  131.4 0.8 copy-start.2
  132.2 0.8 copy-start.3
  137.5 25.9 %collective-permute-start.11 = (bf16[3,256,256]{2,1,0:T(8,128)(2,1)}, bf16[3,256,256]{2,1,0:T(8,128)(2,1)S(1)}, u32[]{:S(2)}, u32[]{:S(2)}) collective-permute-start(bf16[3,256,256]{2,1,0:T(8,128)(2,1)} %get-tuple-element.30.refs_0_), channel_id=1, source_target_pairs={{0,4},{4,8},{8,12},{12,0},{1,5},{5,9},{9,13},{13,1},{2,6},{6,10},{... | collective-permute-start | bytes 1179656 | tf_op jit(solution)/shard_map/ppermute | solution.py:544
  138.6 24.8 %collective-permute-start.12 = (bf16[3,256,256]{2,1,0:T(8,128)(2,1)}, bf16[3,256,256]{2,1,0:T(8,128)(2,1)}, u32[]{:S(2)}, u32[]{:S(2)}) collective-permute-start(bf16[3,256,256]{2,1,0:T(8,128)(2,1)} %get-tuple-element.38), channel_id=1, source_target_pairs={{0,12},{4,0},{8,4},{12,8},{1,13},{5,1},{9,5},{13,9},{2,14},{6,2},{... | collective-permute-start | bytes 1179656 | tf_op jit(solution)/shard_map/ppermute | solution.py:544
  148.1 0.8 copy-start.7
  151.9 33.2 %collective-permute-start.15 = (bf16[2,5,256,256]{3,2,1,0:T(8,128)(2,1)}, bf16[2,5,256,256]{3,2,1,0:T(8,128)(2,1)S(1)}, u32[]{:S(2)}, u32[]{:S(2)}) collective-permute-start(bf16[2,5,256,256]{3,2,1,0:T(8,128)(2,1)} %get-tuple-element.34.refs_1_), channel_id=1, source_target_pairs={{0,1},{1,2},{2,3},{3,0},{4,5},{5,6},{6,7},{7,4},{8,9},{9,10},{10,1... | collective-permute-start | bytes 3932168 | tf_op jit(solution)/shard_map/ppermute | solution.py:544
  152.1 32.9 %collective-permute-start.16 = (bf16[2,5,256,256]{3,2,1,0:T(8,128)(2,1)}, bf16[2,5,256,256]{3,2,1,0:T(8,128)(2,1)}, u32[]{:S(2)}, u32[]{:S(2)}) collective-permute-start(bf16[2,5,256,256]{3,2,1,0:T(8,128)(2,1)} %get-tuple-element.42), channel_id=1, source_target_pairs={{0,3},{1,0},{2,1},{3,2},{4,7},{5,4},{6,5},{7,6},{8,11},{9,8},{10,9... | collective-permute-start | bytes 3932168 | tf_op jit(solution)/shard_map/ppermute | solution.py:544
  163.4 0.7 copy-start.9
  164.1 4.6 %copy-start.6 = (f32[4,5,8,64]{3,2,1,0:T(8,128)S(1)}, f32[4,5,8,64]{3,2,1,0:T(8,128)}, u32[]{:S(2)}) copy-start(f32[4,5,8,64]{3,2,1,0:T(8,128)} %shard_map.80.refs_0_) | copy-start | bytes 122884
  164.1 20.2 %copy-start.8 = (f32[3,32,64]{2,1,0:T(8,128)S(1)}, f32[3,32,64]{2,1,0:T(8,128)}, u32[]{:S(2)}) copy-start(f32[3,32,64]{2,1,0:T(8,128)} %get-tuple-element.43) | copy-start | bytes 73732
  166.5 23.3 %collective-permute-start.13 = (bf16[2,3,256,256]{3,2,1,0:T(8,128)(2,1)}, bf16[2,3,256,256]{3,2,1,0:T(8,128)(2,1)}, u32[]{:S(2)}, u32[]{:S(2)}) collective-permute-start(bf16[2,3,256,256]{3,2,1,0:T(8,128)(2,1)} %get-tuple-element.39), channel_id=1, source_target_pairs={{0,4},{4,8},{8,12},{12,0},{1,5},{5,9},{9,13},{13,1},{2,6},{6,10},{... | collective-permute-start | bytes 2359304 | tf_op jit(solution)/shard_map/ppermute | solution.py:544
  168.8 21.1 %collective-permute-start.14 = (bf16[2,3,256,256]{3,2,1,0:T(8,128)(2,1)}, bf16[2,3,256,256]{3,2,1,0:T(8,128)(2,1)}, u32[]{:S(2)}, u32[]{:S(2)}) collective-permute-start(bf16[2,3,256,256]{3,2,1,0:T(8,128)(2,1)} %get-tuple-element.40), channel_id=1, source_target_pairs={{0,12},{4,0},{8,4},{12,8},{1,13},{5,1},{9,5},{13,9},{2,14},{6,2},{... | collective-permute-start | bytes 2359304 | tf_op jit(solution)/shard_map/ppermute | solution.py:544
  185.1 1.1 copy-start.5
Sparse Core Ops, SparseCore 0:
  9.8 92.7 all-gather.2

commit v11 on v10

--- a/solution.py
+++ b/solution.py
@@ -435,7 +435,7 @@
             scratch_shapes=scratch,
         ),
         compiler_params=limit(62),
-        cost_estimate=cost(10 if by_row else 0.1),
+        cost_estimate=cost(10),
     )(place, *args)
 
 
@@ -575,15 +575,15 @@
     slots_a = (own_a, *near_a, *far_a)
     re_b, im_b = far_products(place_b, slots_b, True, [half_a[0]])
     got_b = both_ways(re_b, im_b, "col")
-    re_a, im_a = far_products(place_a, slots_a, False, [re_b])
-    got_a = both_ways(re_a, im_a, "row")
-    mine_b, up_b, down_b = near_products(place_b, slots_b, True, after=[re_a])
+    mine_b, up_b, down_b = near_products(place_b, slots_b, True, after=[re_b])
     sum_b = added(up_b, down_b, *got_b, 0.1)
     sent_b = both_ways(*sum_b, "col")
+    re_a, im_a = far_products(place_a, slots_a, False, [sum_b[0]])
+    got_a = both_ways(re_a, im_a, "row")
     mine_a, up_a, down_a, power_a = near_products(
-        place_a, slots_a, False, size_b, beam_weights, [sum_b[0]]
+        place_a, slots_a, False, size_b, beam_weights, [re_a]
     )
-    sum_a = added(up_a, down_a, *got_a, 20)
+    sum_a = added(up_a, down_a, *got_a, 0.1)
     sent_a = both_ways(*sum_a, "row")
 
     power_b = jnp.transpose(turn(beam_b, "col"), (1, 0, 2, 3)).reshape(size_b, -1, beam_b.shape[3])

time: 203 us -> 207 us (1.020)
  waiting for transfers between devices: 32.4 us -> 43.7 us
  blocking collectives: 56.1 us -> 50.3 us
    ppermute x16, waiting for transfers between devices: 11.4 us -> 22.7 us  [along(): lax.ppermute(value, axis, [(i, (i + step) % count) for i in range(count)])]
    all_to_all x2, blocking collectives: 56.1 us -> 50.3 us  [turn(): return lax.all_to_all(piece, axis, split_axis=0, concat_axis=0, tiled=True)]
    unnamed x22 -> x28, local copies, waits for them, and re-layouts: 5.42 us -> 5.14 us
  transfers between devices with their start and end apart: 19 -> 19, of which waited for: 6 -> 12; matrix products, arithmetic and copies ran while one was open for 2% -> 2% of each run, Pallas kernels for 28% -> 27%
where the time goes in v11:
time: 207 us; the launch traced here: 206 us
  Pallas kernels  59.2 us (29%)
  blocking collectives  50.3 us (24%)
  waiting for transfers between devices  43.7 us (21%)
  starting transfers between devices  29 us (14%)
  between operations  14.2 us (7%)
  local copies, waits for them, and re-layouts  6.57 us (3%)
  other arithmetic  2.68 us (1%)
    all_to_all x2, blocking collectives, turn(): return lax.all_to_all(piece, axis, split_axis=0, concat_axis=0, tiled=True)  50.3 us
    ppermute x16, waiting for transfers between devices, along(): lax.ppermute(value, axis, [(i, (i + step) % count) for i in range(count)])  22.7 us
    ppermute x16, starting transfers between devices, along(): lax.ppermute(value, axis, [(i, (i + step) % count) for i in range(count)])  21.2 us
    all_to_all x1, waiting for transfers between devices, turn(): return lax.all_to_all(piece, axis, split_axis=0, concat_axis=0, tiled=True)  18.8 us
    pallas_call x2, Pallas kernels, near_products(): pl.pallas_call(functools.partial(near_kernel, by_row, first), out_shape=s...  16.7 us
    pallas_call x2, Pallas kernels, far_products(): pl.pallas_call(functools.partial(far_kernel, by_row), out_shape=[pltpu.HB...  10.5 us
    pallas_call x1, Pallas kernels, own_beams(): pl.pallas_call(beam_kernel, out_shape=jax.ShapeDtypeStruct((owners, size,...  7 us
    pallas_call x2, Pallas kernels, finished(): pl.pallas_call(functools.partial(final_kernel, first), out_shape=jax.Shap...  6.55 us
  transfers between devices with their start and end apart: 19, of which 12 were waited for; matrix products, arithmetic and copies ran while one was open for 2% of the time, Pallas kernels for 27%

profile of v11, /device:TPU:6, one launch (start us, length us, event | category | flops | bytes accessed | tf_op | source)
XLA Modules:
  0.0 205.5 jit_solution(9009796379043661106)
XLA Ops:
  7.2 0.0 all-gather.3.cloned.1.call-start
  7.2 0.7 all-gather.3.cloned.1.call-update
  7.9 0.9 slice.3
  8.8 3.5 %collective-permute-start = (bf16[2,64,384]{2,1,0:T(8,128)(2,1)S(1)}, bf16[2,64,384]{2,1,0:T(8,128)(2,1)S(1)}, u32[]{:S(2)}, u32[]{:S(2)}) collective-permute-start(bf16[2,64,384]{2,1,0:T(8,128)(2,1)S(1)} %slice.3), channel_id=1, source_target_pairs={{0,1},{1,2},{2,3},{3,4},{4,5},{5,6},{6,7},{7,8},{8,9},{9,10},{10,1... | collective-permute-start | bytes 294920 | tf_op jit(solution)/shard_map/ppermute | solution.py:56
  12.3 3.6 %shard_map.77.filt_ref = f32[2,64,64,128]{3,2,1,0:T(8,128)S(1)} custom-call(bf16[2,64,8192]{2,1,0:T(8,128)(2,1)} %v_hbm.1, s32[1,64]{1,0:T(1,128)} %bitcast.13, f32[4,128]{1,0:T(4,128)} %constant.11.clone.coeff_hbm), custom_call_target="tpu_custom_call" | custom-call | flops 5500000256 | bytes 1 | tf_op jit(solution)/shard_map/pallas_call | solution.py:183
  15.9 1.5 collective-permute-done.halo_ref
  17.4 5.3 %shard_map.78 = (bf16[16,5,64,128]{3,2,1,0:T(8,128)(2,1)S(1)}, bf16[16,3,64,128]{3,2,1,0:T(8,128)(2,1)}) custom-call(f32[2,64,64,128]{3,2,1,0:T(8,128)S(1)} %shard_map.77.filt_ref, bf16[2,64,384]{2,1,0:T(8,128)(2,1)S(1)} %collective-permute-done.halo_ref, s32[1,64]{1,0:T(1,128)} %bitcast.14, s32[1,128]{1,0:T(1,128)} %bitcast.15, ...), custom_call_target="tpu_custom_call" | custom-call | flops 6600000000 | bytes 1 | tf_op jit(solution)/shard_map/pallas_call | solution.py:198
  22.7 42.0 %all_to_all.15.own_ref.refs_0_.refs_5_ = bf16[16,5,64,128]{3,2,1,0:T(8,128)(2,1)S(1)} all-to-all(bf16[16,5,64,128]{3,2,1,0:T(8,128)(2,1)S(1)} %get-tuple-element.24), channel_id=1, replica_groups=mesh['chan'=16,'row'=4,'col'=4] {'chan'}, dimensions={0} | all-to-all | bytes 2621440 | tf_op jit(solution)/shard_map/all_to_all | solution.py:563
  64.7 4.3 %all-to-all-start = ((bf16[16,3,64,128]{3,2,1,0:T(8,128)(2,1)}), bf16[16,3,64,128]{3,2,1,0:T(8,128)(2,1)}, u32[]{:S(2)}, u32[]{:S(2)}) async-start(bf16[16,3,64,128]{3,2,1,0:T(8,128)(2,1)} %get-tuple-element.23), calls=%async_computation | async-start | bytes 1572864 | tf_op jit(solution)/shard_map/all_to_all | solution.py:563
  69.0 0.1 collective-permute-start.3
  69.1 2.0 collective-permute-start.4
  71.1 18.8 %all-to-all-done.refs_0_.refs_5_.own_ref = bf16[16,3,64,128]{3,2,1,0:T(8,128)(2,1)} async-done(((bf16[16,3,64,128]{3,2,1,0:T(8,128)(2,1)}), bf16[16,3,64,128]{3,2,1,0:T(8,128)(2,1)}, u32[]{:S(2)}, u32[]{:S(2)}) %all-to-all-start) | async-done | bytes 786464 | tf_op jit(solution)/shard_map/all_to_all | solution.py:563
  89.9 0.1 collective-permute-start.1
  90.1 3.1 %collective-permute-start.2 = (bf16[16,3,64,128]{3,2,1,0:T(8,128)(2,1)}, bf16[16,3,64,128]{3,2,1,0:T(8,128)(2,1)}, u32[]{:S(2)}, u32[]{:S(2)}) collective-permute-start(bf16[16,3,64,128]{3,2,1,0:T(8,128)(2,1)} %all-to-all-done.refs_0_.refs_5_.own_ref), channel_id=1, source_target_pairs={{0,3},{1,0},{2,1},{3,2},{4,7},{5,4},{6,5},{7,6},{8,11},{9,8},{10,9... | collective-permute-start | bytes 2359304 | tf_op jit(solution)/shard_map/ppermute | solution.py:544
  93.2 7.4 %collective-permute-done.3.low_ref.refs_1_.refs_6_.prev_ref = bf16[16,5,64,128]{3,2,1,0:T(8,128)(2,1)S(1)} collective-permute-done((bf16[16,5,64,128]{3,2,1,0:T(8,128)(2,1)S(1)}, bf16[16,5,64,128]{3,2,1,0:T(8,128)(2,1)S(1)}, u32[]{:S(2)}, u32[]{:S(2)}) %collective-permute-start.3) | collective-permute-done | bytes 1310752 | tf_op jit(solution)/shard_map/ppermute | solution.py:544
  100.6 1.1 copy-done.1
  101.7 0.4 collective-permute-done.4.high_ref.refs_2_.refs_7_.next_ref
  102.0 2.2 %shard_map.79 = (bf16[8,5,64,128]{3,2,1,0:T(8,128)(2,1)}, bf16[8,5,64,128]{3,2,1,0:T(8,128)(2,1)}) custom-call(bf16[16,5,64,128]{3,2,1,0:T(8,128)(2,1)} %copy-done.1, bf16[16,5,64,128]{3,2,1,0:T(8,128)(2,1)} %collective-permute-done.4.high_ref.refs_2_.refs_7_.next_ref, bf16[16,3,64,128]{3,2,1,0:T(8,128)(2,1)} %all-to-all-done.refs_0_.refs_5_.own_ref), custom_call_target="tpu_custom_call" | custom-call | flops 110000000 | bytes 1 | tf_op jit(solution)/shard_map/pallas_call | solution.py:232
  104.3 0.9 collective-permute-start.7
  105.1 1.2 collective-permute-start.8
  106.3 0.6 pad_add_fusion.1.place_ref
  106.9 0.7 pad_add_fusion.place_ref
  107.6 7.0 %shard_map.80.refs_0_ = f32[4,5,8,64]{3,2,1,0:T(8,128)} custom-call(bf16[16,5,64,128]{3,2,1,0:T(8,128)(2,1)} %copy-done, bf16[4,2,8,64,1024]{4,3,2,1,0:T(8,128)(2,1)} %bitcast.12, bf16[8,5,64,128]{3,2,1,0:T(8,128)(2,1)} %get-tuple-element.25.refs_0_), custom_call_target="tpu_custom_call" | custom-call | flops 110000000 | bytes 1 | tf_op jit(solution)/shard_map/pallas_call | solution.py:460
  114.6 0.1 collective-permute-done.1.low_ref.refs_1_.refs_6_.prev_ref
  114.7 0.0 collective-permute-done.2.high_ref.refs_2_.refs_7_.next_ref
  114.7 2.0 shard_map.81
  116.7 1.5 collective-permute-start.5
  118.3 2.8 %collective-permute-done.7.refs_3_.refs_8_.low_ref = bf16[8,5,64,128]{3,2,1,0:T(8,128)(2,1)S(1)} collective-permute-done((bf16[8,5,64,128]{3,2,1,0:T(8,128)(2,1)}, bf16[8,5,64,128]{3,2,1,0:T(8,128)(2,1)S(1)}, u32[]{:S(2)}, u32[]{:S(2)}) %collective-permute-start.7) | collective-permute-done | bytes 655392 | tf_op jit(solution)/shard_map/ppermute | solution.py:544
  121.1 2.2 %collective-permute-done.8.refs_4_.refs_9_.high_ref = bf16[8,5,64,128]{3,2,1,0:T(8,128)(2,1)S(1)} collective-permute-done((bf16[8,5,64,128]{3,2,1,0:T(8,128)(2,1)}, bf16[8,5,64,128]{3,2,1,0:T(8,128)(2,1)S(1)}, u32[]{:S(2)}, u32[]{:S(2)}) %collective-permute-start.8) | collective-permute-done | bytes 655392 | tf_op jit(solution)/shard_map/ppermute | solution.py:544
  123.3 0.8 copy-done.3
  124.1 6.0 %shard_map.82 = (bf16[5,256,256]{2,1,0:T(8,128)(2,1)}, bf16[5,256,256]{2,1,0:T(8,128)(2,1)}) custom-call(s32[2]{0:T(128)} %pad_add_fusion.1.place_ref, bf16[16,5,64,128]{3,2,1,0:T(8,128)(2,1)} %copy-done, bf16[16,5,64,128]{3,2,1,0:T(8,128)(2,1)} %copy-done.1, bf16[16,5,64,128]{3,2,1,0:T(8,128)(2,1)} %collective-permute-done.4.high_ref.refs_2_.refs_7_.next_ref, ...), custom_call_target="tpu_custom_call" | custom-call | flops 110000000 | bytes 1 | tf_op jit(solution)/shard_map/pallas_call | solution.py:306
  130.1 1.4 collective-permute-start.10
  131.5 0.7 collective-permute-start.9
  132.2 2.5 %collective-permute-start.6 = (bf16[8,3,64,128]{3,2,1,0:T(8,128)(2,1)}, bf16[8,3,64,128]{3,2,1,0:T(8,128)(2,1)S(1)}, u32[]{:S(2)}, u32[]{:S(2)}) collective-permute-start(bf16[8,3,64,128]{3,2,1,0:T(8,128)(2,1)} %get-tuple-element.27), channel_id=1, source_target_pairs={{0,3},{1,0},{2,1},{3,2},{4,7},{5,4},{6,5},{7,6},{8,11},{9,8},{10,9... | collective-permute-start | bytes 1179656 | tf_op jit(solution)/shard_map/ppermute | solution.py:544
  134.7 8.4 %shard_map.83 = (f32[2,5,256,256]{3,2,1,0:T(8,128)}, bf16[2,5,256,256]{3,2,1,0:T(8,128)(2,1)}, bf16[2,5,256,256]{3,2,1,0:T(8,128)(2,1)}) custom-call(s32[2]{0:T(128)} %pad_add_fusion.1.place_ref, bf16[16,5,64,128]{3,2,1,0:T(8,128)(2,1)} %copy-done, bf16[16,5,64,128]{3,2,1,0:T(8,128)(2,1)} %copy-done.1, ...), custom_call_target="tpu_custom_call" | custom-call | flops 11000000512 | bytes 1 | tf_op jit(solution)/shard_map/pallas_call | solution.py:427
  143.1 4.9 %collective-permute-done.10.high_ref = bf16[5,256,256]{2,1,0:T(8,128)(2,1)S(1)} collective-permute-done((bf16[5,256,256]{2,1,0:T(8,128)(2,1)}, bf16[5,256,256]{2,1,0:T(8,128)(2,1)S(1)}, u32[]{:S(2)}, u32[]{:S(2)}) %collective-permute-start.10) | collective-permute-done | bytes 655392 | tf_op jit(solution)/shard_map/ppermute | solution.py:544
  148.0 0.3 collective-permute-done.9.low_ref
  148.3 0.6 copy-done.9
  148.9 2.9 %shard_map.84 = (bf16[2,5,256,256]{3,2,1,0:T(8,128)(2,1)}, bf16[2,5,256,256]{3,2,1,0:T(8,128)(2,1)}) custom-call(bf16[2,5,256,256]{3,2,1,0:T(8,128)(2,1)} %get-tuple-element.30.up_ref, bf16[2,5,256,256]{3,2,1,0:T(8,128)(2,1)} %get-tuple-element.31.down_ref, ...), custom_call_target="tpu_custom_call", output_to_operand_aliasing={{0}: (0, {}), {1}: (1, {})} | custom-call | flops 110000000 | bytes 1 | tf_op jit(solution)/shard_map/pallas_call | solution.py:487
  151.8 0.3 collective-permute-start.15
  152.1 2.9 %collective-permute-start.16 = (bf16[2,5,256,256]{3,2,1,0:T(8,128)(2,1)}, bf16[2,5,256,256]{3,2,1,0:T(8,128)(2,1)}, u32[]{:S(2)}, u32[]{:S(2)}) collective-permute-start(bf16[2,5,256,256]{3,2,1,0:T(8,128)(2,1)} %get-tuple-element.42), channel_id=1, source_target_pairs={{0,3},{1,0},{2,1},{3,2},{4,7},{5,4},{6,5},{7,6},{8,11},{9,8},{10,9... | collective-permute-start | bytes 3932168 | tf_op jit(solution)/shard_map/ppermute | solution.py:544
  155.0 1.4 collective-permute-done.6.refs_4_.refs_9_.high_ref
  156.4 0.8 copy-done.5
  157.2 4.5 %shard_map.85 = (bf16[3,256,256]{2,1,0:T(8,128)(2,1)}, bf16[3,256,256]{2,1,0:T(8,128)(2,1)}) custom-call(s32[2]{0:T(128)} %pad_add_fusion.place_ref, bf16[16,3,64,128]{3,2,1,0:T(8,128)(2,1)} %all-to-all-done.refs_0_.refs_5_.own_ref, bf16[16,3,64,128]{3,2,1,0:T(8,128)(2,1)} %collective-permute-done.1.low_ref.refs_1_.refs_6_.prev_ref, ...), custom_call_target="tpu_custom_call" | custom-call | flops 110000000 | bytes 1 | tf_op jit(solution)/shard_map/pallas_call | solution.py:306
  161.8 1.2 collective-permute-start.11
  162.9 0.9 collective-permute-start.12
  163.9 8.2 %shard_map.86 = (f32[2,3,256,256]{3,2,1,0:T(8,128)}, bf16[2,3,256,256]{3,2,1,0:T(8,128)(2,1)}, bf16[2,3,256,256]{3,2,1,0:T(8,128)(2,1)}, f32[3,32,64]{2,1,0:T(8,128)}) custom-call(s32[2]{0:T(128)} %pad_add_fusion.place_ref, bf16[16,3,64,128]{3,2,1,0:T(8,128)(2,1)} %all-to-all-done.refs_0_.refs_5_.own_ref, ...), custom_call_target="tpu_custom_call" | custom-call | flops 11000000512 | bytes 1 | tf_op jit(solution)/shard_map/pallas_call | solution.py:427
  172.1 0.0 copy-start.8
  172.1 0.0 copy-start.10
  172.1 0.1 collective-permute-done.12.high_ref
  172.3 0.6 copy-done.10
  172.9 0.2 copy-done.11
  173.1 2.4 %shard_map.87 = (bf16[2,3,256,256]{3,2,1,0:T(8,128)(2,1)}, bf16[2,3,256,256]{3,2,1,0:T(8,128)(2,1)}) custom-call(bf16[2,3,256,256]{3,2,1,0:T(8,128)(2,1)} %get-tuple-element.36.up_ref, bf16[2,3,256,256]{3,2,1,0:T(8,128)(2,1)} %get-tuple-element.37.down_ref, bf16[3,256,256]{2,1,0:T(8,128)(2,1)} %copy-done.10, ...), custom_call_target="tpu_custom_call", output_to_operand_aliasing={{0}: (0, {}), {1}: (1, {})} | custom-call | flops 110000000 | bytes 1 | tf_op jit(solution)/shard_map/pallas_call | solution.py:487
  175.4 2.3 %collective-permute-start.13 = (bf16[2,3,256,256]{3,2,1,0:T(8,128)(2,1)}, bf16[2,3,256,256]{3,2,1,0:T(8,128)(2,1)S(1)}, u32[]{:S(2)}, u32[]{:S(2)}) collective-permute-start(bf16[2,3,256,256]{3,2,1,0:T(8,128)(2,1)} %get-tuple-element.39), channel_id=1, source_target_pairs={{0,4},{4,8},{8,12},{12,0},{1,5},{5,9},{9,13},{13,1},{2,6},{6,10},{... | collective-permute-start | bytes 2359304 | tf_op jit(solution)/shard_map/ppermute | solution.py:544
  177.7 0.1 reshape.17
  177.8 8.2 %all_to_all.16 = f32[4,1,2560]{2,1,0:T(1,128)S(1)} all-to-all(f32[4,1,2560]{2,1,0:T(1,128)S(1)} %reshape.17), channel_id=1, replica_groups=mesh['chan'=16,'row'=4,'col'=4] {'col'}, dimensions={0} | all-to-all | bytes 81920 | tf_op jit(solution)/shard_map/all_to_all | solution.py:563
  186.1 0.5 broadcast
  186.6 0.8 reduce
  187.3 0.1 reshape.18
  187.5 0.7 maximum_bitcast_fusion
  188.1 3.7 %shard_map.88.refs_0_ = f32[2,8,256,256]{3,2,1,0:T(8,128)} custom-call(f32[2,5,256,256]{3,2,1,0:T(8,128)} %get-tuple-element.41.own_ref, bf16[2,5,256,256]{3,2,1,0:T(8,128)(2,1)} %collective-permute-done.15.prev_ref, bf16[2,5,256,256]{3,2,1,0:T(8,128)(2,1)} %collective-permute-done.16.next_ref), custom_call_target="tpu_custom_call" | custom-call | flops 110000000 | bytes 1 | tf_op jit(solution)/shard_map/pallas_call | solution.py:526
  191.9 3.1 %collective-permute-done.14.next_ref = bf16[2,3,256,256]{3,2,1,0:T(8,128)(2,1)S(1)} collective-permute-done((bf16[2,3,256,256]{3,2,1,0:T(8,128)(2,1)}, bf16[2,3,256,256]{3,2,1,0:T(8,128)(2,1)S(1)}, u32[]{:S(2)}, u32[]{:S(2)}) %collective-permute-start.14) | collective-permute-done | bytes 786464 | tf_op jit(solution)/shard_map/ppermute | solution.py:544
  194.9 0.9 copy-done.7
  195.8 2.8 %shard_map.89 = f32[2,8,256,256]{3,2,1,0:T(8,128)} custom-call(f32[2,3,256,256]{3,2,1,0:T(8,128)} %get-tuple-element.35.own_ref, bf16[2,3,256,256]{3,2,1,0:T(8,128)(2,1)} %copy-done.6, bf16[2,3,256,256]{3,2,1,0:T(8,128)(2,1)} %copy-done.7, f32[2,8,256,256]{3,2,1,0:T(8,128)} %shard_map.88.refs_0_), custom_call_target="tpu_custom_call", output_to_operand_aliasing={{}: (3, {})} | custom-call | flops 110000000 | bytes 1 | tf_op jit(solution)/shard_map/pallas_call | solution.py:526
  (25 shorter events, 0.1 us)
Async XLA Ops:
  7.2 100.4 %all-gather.3.cloned.1.call-start = ((), (), s32[]{:S(2)}) async-start(), calls=%async_computation.3 | async-start | bytes 10485760 | tf_op jit(solution)/shard_map/all_gather | solution.py:559
  8.8 8.6 %collective-permute-start = (bf16[2,64,384]{2,1,0:T(8,128)(2,1)S(1)}, bf16[2,64,384]{2,1,0:T(8,128)(2,1)S(1)}, u32[]{:S(2)}, u32[]{:S(2)}) collective-permute-start(bf16[2,64,384]{2,1,0:T(8,128)(2,1)S(1)} %slice.3), channel_id=1, source_target_pairs={{0,1},{1,2},{2,3},{3,4},{4,5},{5,6},{6,7},{7,8},{8,9},{9,10},{10,1... | collective-permute-start | bytes 294920 | tf_op jit(solution)/shard_map/ppermute | solution.py:56
  64.7 39.5 %copy-start = (bf16[16,5,64,128]{3,2,1,0:T(8,128)(2,1)}, bf16[16,5,64,128]{3,2,1,0:T(8,128)(2,1)S(1)}, u32[]{:S(2)}) copy-start(bf16[16,5,64,128]{3,2,1,0:T(8,128)(2,1)S(1)} %all_to_all.15.own_ref.refs_0_.refs_5_) | copy-start | bytes 3932164
  64.7 25.2 %all-to-all-start = ((bf16[16,3,64,128]{3,2,1,0:T(8,128)(2,1)}), bf16[16,3,64,128]{3,2,1,0:T(8,128)(2,1)}, u32[]{:S(2)}, u32[]{:S(2)}) async-start(bf16[16,3,64,128]{3,2,1,0:T(8,128)(2,1)} %get-tuple-element.23), calls=%async_computation | async-start | bytes 1572864 | tf_op jit(solution)/shard_map/all_to_all | solution.py:563
  69.0 31.6 %collective-permute-start.3 = (bf16[16,5,64,128]{3,2,1,0:T(8,128)(2,1)S(1)}, bf16[16,5,64,128]{3,2,1,0:T(8,128)(2,1)S(1)}, u32[]{:S(2)}, u32[]{:S(2)}) collective-permute-start(bf16[16,5,64,128]{3,2,1,0:T(8,128)(2,1)S(1)} %all_to_all.15.own_ref.refs_0_.refs_5_), channel_id=1, source_target_pairs={{0,4},{4,8},{8,12},{12,0},{1,5},{5,9},{9,13},{13,1},{2,6},{6,10},{... | collective-permute-start | bytes 3932168 | tf_op jit(solution)/shard_map/ppermute | solution.py:544
  69.1 32.9 %collective-permute-start.4 = (bf16[16,5,64,128]{3,2,1,0:T(8,128)(2,1)S(1)}, bf16[16,5,64,128]{3,2,1,0:T(8,128)(2,1)}, u32[]{:S(2)}, u32[]{:S(2)}) collective-permute-start(bf16[16,5,64,128]{3,2,1,0:T(8,128)(2,1)S(1)} %all_to_all.15.own_ref.refs_0_.refs_5_), channel_id=1, source_target_pairs={{0,12},{4,0},{8,4},{12,8},{1,13},{5,1},{9,5},{13,9},{2,14},{6,2},{... | collective-permute-start | bytes 3932168 | tf_op jit(solution)/shard_map/ppermute | solution.py:544
  89.9 24.7 %collective-permute-start.1 = (bf16[16,3,64,128]{3,2,1,0:T(8,128)(2,1)}, bf16[16,3,64,128]{3,2,1,0:T(8,128)(2,1)}, u32[]{:S(2)}, u32[]{:S(2)}) collective-permute-start(bf16[16,3,64,128]{3,2,1,0:T(8,128)(2,1)} %all-to-all-done.refs_0_.refs_5_.own_ref), channel_id=1, source_target_pairs={{0,1},{1,2},{2,3},{3,0},{4,5},{5,6},{6,7},{7,4},{8,9},{9,10},{10,1... | collective-permute-start | bytes 2359304 | tf_op jit(solution)/shard_map/ppermute | solution.py:544
  90.1 24.6 %collective-permute-start.2 = (bf16[16,3,64,128]{3,2,1,0:T(8,128)(2,1)}, bf16[16,3,64,128]{3,2,1,0:T(8,128)(2,1)}, u32[]{:S(2)}, u32[]{:S(2)}) collective-permute-start(bf16[16,3,64,128]{3,2,1,0:T(8,128)(2,1)} %all-to-all-done.refs_0_.refs_5_.own_ref), channel_id=1, source_target_pairs={{0,3},{1,0},{2,1},{3,2},{4,7},{5,4},{6,5},{7,6},{8,11},{9,8},{10,9... | collective-permute-start | bytes 2359304 | tf_op jit(solution)/shard_map/ppermute | solution.py:544
  100.6 1.1 copy-start.1
  104.3 16.8 %collective-permute-start.7 = (bf16[8,5,64,128]{3,2,1,0:T(8,128)(2,1)}, bf16[8,5,64,128]{3,2,1,0:T(8,128)(2,1)S(1)}, u32[]{:S(2)}, u32[]{:S(2)}) collective-permute-start(bf16[8,5,64,128]{3,2,1,0:T(8,128)(2,1)} %get-tuple-element.25.refs_0_), channel_id=1, source_target_pairs={{0,4},{4,8},{8,12},{12,0},{1,5},{5,9},{9,13},{13,1},{2,6},{6,10},{... | collective-permute-start | bytes 1966088 | tf_op jit(solution)/shard_map/ppermute | solution.py:544
  105.1 18.1 %collective-permute-start.8 = (bf16[8,5,64,128]{3,2,1,0:T(8,128)(2,1)}, bf16[8,5,64,128]{3,2,1,0:T(8,128)(2,1)S(1)}, u32[]{:S(2)}, u32[]{:S(2)}) collective-permute-start(bf16[8,5,64,128]{3,2,1,0:T(8,128)(2,1)} %get-tuple-element.28), channel_id=1, source_target_pairs={{0,12},{4,0},{8,4},{12,8},{1,13},{5,1},{9,5},{13,9},{2,14},{6,2},{... | collective-permute-start | bytes 1966088 | tf_op jit(solution)/shard_map/ppermute | solution.py:544
  116.7 38.3 %collective-permute-start.5 = (bf16[8,3,64,128]{3,2,1,0:T(8,128)(2,1)}, bf16[8,3,64,128]{3,2,1,0:T(8,128)(2,1)S(1)}, u32[]{:S(2)}, u32[]{:S(2)}) collective-permute-start(bf16[8,3,64,128]{3,2,1,0:T(8,128)(2,1)} %get-tuple-element.26.refs_10_), channel_id=1, source_target_pairs={{0,1},{1,2},{2,3},{3,0},{4,5},{5,6},{6,7},{7,4},{8,9},{9,10},{10,1... | collective-permute-start | bytes 1179656 | tf_op jit(solution)/shard_map/ppermute | solution.py:544
  121.1 2.2 %copy-start.2 = (bf16[8,5,64,128]{3,2,1,0:T(8,128)(2,1)}, bf16[8,5,64,128]{3,2,1,0:T(8,128)(2,1)S(1)}, u32[]{:S(2)}) copy-start(bf16[8,5,64,128]{3,2,1,0:T(8,128)(2,1)S(1)} %collective-permute-done.7.refs_3_.refs_8_.low_ref) | copy-start | bytes 1966084
  123.3 0.8 copy-start.3
  130.1 18.0 %collective-permute-start.10 = (bf16[5,256,256]{2,1,0:T(8,128)(2,1)}, bf16[5,256,256]{2,1,0:T(8,128)(2,1)S(1)}, u32[]{:S(2)}, u32[]{:S(2)}) collective-permute-start(bf16[5,256,256]{2,1,0:T(8,128)(2,1)} %get-tuple-element.32), channel_id=1, source_target_pairs={{0,3},{1,0},{2,1},{3,2},{4,7},{5,4},{6,5},{7,6},{8,11},{9,8},{10,9... | collective-permute-start | bytes 1966088 | tf_op jit(solution)/shard_map/ppermute | solution.py:544
  131.5 16.8 %collective-permute-start.9 = (bf16[5,256,256]{2,1,0:T(8,128)(2,1)}, bf16[5,256,256]{2,1,0:T(8,128)(2,1)}, u32[]{:S(2)}, u32[]{:S(2)}) collective-permute-start(bf16[5,256,256]{2,1,0:T(8,128)(2,1)} %get-tuple-element.29.refs_0_), channel_id=1, source_target_pairs={{0,1},{1,2},{2,3},{3,0},{4,5},{5,6},{6,7},{7,4},{8,9},{9,10},{10,1... | collective-permute-start | bytes 1966088 | tf_op jit(solution)/shard_map/ppermute | solution.py:544
  132.2 24.3 %collective-permute-start.6 = (bf16[8,3,64,128]{3,2,1,0:T(8,128)(2,1)}, bf16[8,3,64,128]{3,2,1,0:T(8,128)(2,1)S(1)}, u32[]{:S(2)}, u32[]{:S(2)}) collective-permute-start(bf16[8,3,64,128]{3,2,1,0:T(8,128)(2,1)} %get-tuple-element.27), channel_id=1, source_target_pairs={{0,3},{1,0},{2,1},{3,2},{4,7},{5,4},{6,5},{7,6},{8,11},{9,8},{10,9... | collective-permute-start | bytes 1179656 | tf_op jit(solution)/shard_map/ppermute | solution.py:544
  148.0 0.8 copy-start.9
  151.8 36.4 %collective-permute-start.15 = (bf16[2,5,256,256]{3,2,1,0:T(8,128)(2,1)}, bf16[2,5,256,256]{3,2,1,0:T(8,128)(2,1)}, u32[]{:S(2)}, u32[]{:S(2)}) collective-permute-start(bf16[2,5,256,256]{3,2,1,0:T(8,128)(2,1)} %get-tuple-element.33.refs_10_), channel_id=1, source_target_pairs={{0,1},{1,2},{2,3},{3,0},{4,5},{5,6},{6,7},{7,4},{8,9},{9,10},{10,1... | collective-permute-start | bytes 3932168 | tf_op jit(solution)/shard_map/ppermute | solution.py:544
  152.1 36.1 %collective-permute-start.16 = (bf16[2,5,256,256]{3,2,1,0:T(8,128)(2,1)}, bf16[2,5,256,256]{3,2,1,0:T(8,128)(2,1)}, u32[]{:S(2)}, u32[]{:S(2)}) collective-permute-start(bf16[2,5,256,256]{3,2,1,0:T(8,128)(2,1)} %get-tuple-element.42), channel_id=1, source_target_pairs={{0,3},{1,0},{2,1},{3,2},{4,7},{5,4},{6,5},{7,6},{8,11},{9,8},{10,9... | collective-permute-start | bytes 3932168 | tf_op jit(solution)/shard_map/ppermute | solution.py:544
  155.0 1.4 copy-start.4
  156.4 0.8 copy-start.5
  161.8 10.4 %collective-permute-start.11 = (bf16[3,256,256]{2,1,0:T(8,128)(2,1)}, bf16[3,256,256]{2,1,0:T(8,128)(2,1)S(1)}, u32[]{:S(2)}, u32[]{:S(2)}) collective-permute-start(bf16[3,256,256]{2,1,0:T(8,128)(2,1)} %get-tuple-element.34.refs_1_), channel_id=1, source_target_pairs={{0,4},{4,8},{8,12},{12,0},{1,5},{5,9},{9,13},{13,1},{2,6},{6,10},{... | collective-permute-start | bytes 1179656 | tf_op jit(solution)/shard_map/ppermute | solution.py:544
  162.9 9.4 %collective-permute-start.12 = (bf16[3,256,256]{2,1,0:T(8,128)(2,1)}, bf16[3,256,256]{2,1,0:T(8,128)(2,1)S(1)}, u32[]{:S(2)}, u32[]{:S(2)}) collective-permute-start(bf16[3,256,256]{2,1,0:T(8,128)(2,1)} %get-tuple-element.38), channel_id=1, source_target_pairs={{0,12},{4,0},{8,4},{12,8},{1,13},{5,1},{9,5},{13,9},{2,14},{6,2},{... | collective-permute-start | bytes 1179656 | tf_op jit(solution)/shard_map/ppermute | solution.py:544
  172.1 5.6 %copy-start.8 = (f32[4,5,8,64]{3,2,1,0:T(8,128)S(1)}, f32[4,5,8,64]{3,2,1,0:T(8,128)}, u32[]{:S(2)}) copy-start(f32[4,5,8,64]{3,2,1,0:T(8,128)} %shard_map.80.refs_0_) | copy-start | bytes 122884
  172.1 0.7 copy-start.10
  172.3 0.8 copy-start.11
  173.1 14.4 %copy-start.12 = (f32[3,32,64]{2,1,0:T(8,128)S(1)}, f32[3,32,64]{2,1,0:T(8,128)}, u32[]{:S(2)}) copy-start(f32[3,32,64]{2,1,0:T(8,128)} %get-tuple-element.43) | copy-start | bytes 73732
  175.4 16.4 %collective-permute-start.13 = (bf16[2,3,256,256]{3,2,1,0:T(8,128)(2,1)}, bf16[2,3,256,256]{3,2,1,0:T(8,128)(2,1)S(1)}, u32[]{:S(2)}, u32[]{:S(2)}) collective-permute-start(bf16[2,3,256,256]{3,2,1,0:T(8,128)(2,1)} %get-tuple-element.39), channel_id=1, source_target_pairs={{0,4},{4,8},{8,12},{12,0},{1,5},{5,9},{9,13},{13,1},{2,6},{6,10},{... | collective-permute-start | bytes 2359304 | tf_op jit(solution)/shard_map/ppermute | solution.py:544
  177.7 17.2 %collective-permute-start.14 = (bf16[2,3,256,256]{3,2,1,0:T(8,128)(2,1)}, bf16[2,3,256,256]{3,2,1,0:T(8,128)(2,1)S(1)}, u32[]{:S(2)}, u32[]{:S(2)}) collective-permute-start(bf16[2,3,256,256]{3,2,1,0:T(8,128)(2,1)} %get-tuple-element.40), channel_id=1, source_target_pairs={{0,12},{4,0},{8,4},{12,8},{1,13},{5,1},{9,5},{13,9},{2,14},{6,2},{... | collective-permute-start | bytes 2359304 | tf_op jit(solution)/shard_map/ppermute | solution.py:544
  191.9 3.1 %copy-start.6 = (bf16[2,3,256,256]{3,2,1,0:T(8,128)(2,1)}, bf16[2,3,256,256]{3,2,1,0:T(8,128)(2,1)S(1)}, u32[]{:S(2)}) copy-start(bf16[2,3,256,256]{3,2,1,0:T(8,128)(2,1)S(1)} %collective-permute-done.13.prev_ref) | copy-start | bytes 2359300
  194.9 0.9 copy-start.7
Sparse Core Ops, SparseCore 0:
  9.8 92.7 all-gather.2
